TPU v7x, 32 devices: a whole 2x2x4 slice. The times are simulated.
32 devices in a mesh: row: 8 (over y, x, core), col: 4 (over z).
Axes of the slice: x: 2, y: 2, z: 4, core: 2. Of those that a mesh axis runs over, the one named last changes fastest.
Arguments:
- kernel: float32 [4, 1024, 8, 512], P(None, 'row', None, 'col'), as said below
Outputs:
- factored: float32 [4, 1024, 8, 512], P(None, 'row', None, 'col')
Inputs may be any that keep to these rules, and one draw needn't show every extreme that they name: kernel is symmetric and positive definite.
All inputs are finite; a program needn't handle non-finite values.
Results may differ from a plain program's by a relative error of at most 0.0001.
Values sent between devices are 32-bit elements; how exact they have to be, the bound alone decides.
No kernel may reach another device: no remote copies, remote signals or barrier semaphores. Data moves between devices by JAX's collectives and lax.ppermute only.
A program may use at most 128 MiB of HBM per device.

v0:
```python
import jax
import jax.numpy as jnp
from jax import lax
from jax.sharding import PartitionSpec as P

PANELS = 2


def from_root(value, axis, source):
    kept = jnp.where(lax.axis_index(axis) == source, value, 0).astype(value.dtype)
    return lax.psum(kept, axis)


def solve_panel(column, panel_idx, grid_row, spread):
    blocks = column.shape[0]
    breadth = column.shape[1]
    diagonal = from_root(column[0], "row", panel_idx)
    factor = jnp.linalg.cholesky(diagonal)
    stacked = column.reshape(blocks * breadth, breadth)
    solved = jax.scipy.linalg.solve_triangular(factor, stacked.T, lower=True).T
    solved = solved.reshape(blocks, breadth, breadth)
    global_rows = jnp.arange(blocks, dtype=jnp.int32) * spread + grid_row
    solved = jnp.where((global_rows < panel_idx)[:, None, None], jnp.float32(0.0), solved)
    solved = jnp.where((global_rows == panel_idx)[:, None, None], factor[None], solved)
    return from_root(solved, "col", panel_idx)


def mirror(rows_part, grid_col):
    n_row = lax.axis_size("row")
    n_col = lax.axis_size("col")
    local_rows = rows_part.shape[0]
    breadth = rows_part.shape[1]
    extent = rows_part.shape[2]
    whole = lax.all_gather(rows_part, "row", axis=1, tiled=True)
    whole = whole.reshape(local_rows * n_row // n_col, n_col, breadth, extent)
    return lax.dynamic_index_in_dim(whole, grid_col, 1, keepdims=False)


def trailing(matrix, row_panel, col_panel):
    update = jnp.einsum("rib,cjb->ricj", row_panel, col_panel, precision=lax.Precision.HIGHEST)
    return matrix - update


def settle(matrix, panel_rows, panel_idx, global_rows, global_cols):
    col_mask = (global_cols == panel_idx)[None, None, :, None]
    matrix = jnp.where(col_mask, panel_rows[:, :, None, :], matrix)
    row_mask = (global_rows == panel_idx)[:, None, None, None] & (global_cols > panel_idx)[
        None, None, :, None
    ]
    return jnp.where(row_mask, jnp.float32(0.0), matrix)


def shards(kernel):
    grid_row = lax.axis_index("row")
    grid_col = lax.axis_index("col")
    n_row = lax.axis_size("row")
    n_col = lax.axis_size("col")
    global_rows = jnp.arange(kernel.shape[0], dtype=jnp.int32) * n_row + grid_row
    global_cols = jnp.arange(kernel.shape[2], dtype=jnp.int32) * n_col + grid_col
    matrix = kernel
    for panel_idx in range(PANELS):
        current = solve_panel(matrix[:, :, 0, :], panel_idx, grid_row, n_row)
        matrix = trailing(matrix, current, mirror(current, grid_col))
        matrix = settle(matrix, current, panel_idx, global_rows, global_cols)
    return matrix


def solution(mesh):
    in_specs = (P(None, "row", None, "col"),)
    out_specs = P(None, "row", None, "col")
    return jax.shard_map(shards, mesh=mesh, in_specs=in_specs, out_specs=out_specs, check_vma=False)
```

profile of v0, /device:TPU:0, one launch (start us, length us, event | category | flops | bytes accessed | tf_op | source)
XLA Modules:
  0.0 317.6 jit_solution(15762883483269014377)
XLA Ops:
  6.5 2.0 copy.14
  8.5 0.0 copy-start
  8.6 0.7 fusion.7
  9.3 0.0 all-reduce.5.cloned.1.call-update
  9.3 0.0 all-reduce.7.cloned.1.call-start
  9.4 56.2 %all-reduce.5.cloned.1.call-done = f32[128,128]{0,1:T(8,128)} async-done(((f32[128,128]{0,1:T(8,128)}), f32[128,128]{0,1:T(8,128)}) %all-reduce.5.cloned.1.call-update) | async-done | bytes 65552 | tf_op jit(solution)/shard_map/psum | solution.py:11
  65.6 0.9 copy.15
  66.5 0.9 fusion.11
  67.4 11.7 %cholesky.44 = f32[128,128]{1,0:T(8,128)S(1)} custom-call(f32[128,128]{1,0:T(8,128)S(1)} %fusion.11), custom_call_target="Cholesky" | custom-call | tf_op jit(solution)/shard_map/jit(cholesky)/cholesky | solution.py:18
  79.1 0.7 compare_reduce_fusion.1
  79.8 0.6 fusion.16
  80.5 9.8 %custom-call.6 = f32[1,128,128]{1,2,0:T(8,128)S(1)} custom-call(f32[1,128,128]{2,1,0:T(8,128)S(1)} %get-tuple-element.9), custom_call_target="InvertDiagBlocksLowerTriangular" | custom-call | tf_op jit(solution)/shard_map/jit(_solve_triangular)/triangular_solve | solution.py:20
  90.3 0.4 convolution_bitcast_fusion.1
  90.7 0.1 copy.31
  90.9 0.8 select_select_fusion.3
  91.7 0.0 all-reduce.7.cloned.1.call-update
  91.7 0.0 all-gather.3.cloned.1.call-start
  91.7 34.8 %all-reduce.7.cloned.1.call-done = f32[4,128,128]{2,1,0:T(8,128)} async-done(((f32[4,128,128]{2,1,0:T(8,128)}), f32[4,128,128]{2,1,0:T(8,128)}) %all-reduce.7.cloned.1.call-update) | async-done | bytes 262160 | tf_op jit(solution)/shard_map/psum | solution.py:11
  126.6 0.0 all-gather.3.cloned.1.call-update
  126.6 0.0 all-reduce.9.cloned.1.call-start
  126.7 0.1 broadcast_and_fusion
  126.7 1.1 copy.17
  127.8 28.3 %all-gather.3.cloned.1.call-done = f32[4,1024,128]{2,1,0:T(8,128)} async-done(((f32[4,128,128]{2,1,0:T(8,128)}), f32[4,1024,128]{2,1,0:T(8,128)}) %all-gather.3.cloned.1.call-update) | async-done | bytes 2097168 | tf_op jit(solution)/shard_map/all_gather | solution.py:34
  156.1 0.0 copy-done
  156.1 3.8 %select_select_fusion.1 = f32[4,128,8,128]{1,3,2,0:T(8,128)S(1)} fusion(f32[4,128,8,128]{1,3,2,0:T(8,128)} %copy-done, f32[4,128,128]{1,2,0:T(8,128)S(1)} %copy.17, pred[8]{0:T(512)(128)(4,1)S(1)} %get-tuple-element.13, pred[4,8]{1,0:T(4,128)(4,1)S(1)} %broadcast_and_fusion, f32[8,4,128,128]{3,2,1,0:T(8,128)} %bitcast.62, s32[]{:T(128)S(6)} %select_n.79, ...), kind=kOutput, calls=%fused_computation.1 | convolution fusion | flops 806879232 | bytes 5242924 | tf_op jit(solution)/shard_map/rib,cjb->ricj/dot_general | solution.py:40
  159.9 0.6 fusion.6
  160.5 0.0 all-reduce.9.cloned.1.call-update
  160.6 0.2 all-reduce.11.cloned.1.call-start
  160.8 0.1 copy.22
  161.0 52.2 %all-reduce.9.cloned.1.call-done = f32[128,128]{0,1:T(8,128)} async-done(((f32[128,128]{0,1:T(8,128)}), f32[128,128]{0,1:T(8,128)}) %all-reduce.9.cloned.1.call-update) | async-done | bytes 65552 | tf_op jit(solution)/shard_map/psum | solution.py:11
  213.2 0.9 copy.21
  214.1 0.9 fusion.9
  215.0 11.7 %cholesky.55 = f32[128,128]{1,0:T(8,128)S(1)} custom-call(f32[128,128]{1,0:T(8,128)S(1)} %fusion.9), custom_call_target="Cholesky" | custom-call | tf_op jit(solution)/shard_map/jit(cholesky)/cholesky | solution.py:18
  226.7 0.6 compare_reduce_fusion
  227.4 0.7 select_bitcast_fusion
  228.0 9.8 %custom-call.7 = f32[1,128,128]{1,2,0:T(8,128)S(1)} custom-call(f32[1,128,128]{2,1,0:T(8,128)S(1)} %get-tuple-element.6), custom_call_target="InvertDiagBlocksLowerTriangular" | custom-call | tf_op jit(solution)/shard_map/jit(_solve_triangular)/triangular_solve | solution.py:20
  237.8 0.4 convolution_bitcast_fusion
  238.3 0.1 copy.23
  238.4 0.8 select_select_fusion.2
  239.2 0.0 all-reduce.11.cloned.1.call-update
  239.2 0.0 all-gather.5.cloned.1.call-start
  239.3 34.8 %all-reduce.11.cloned.1.call-done = f32[4,128,128]{2,1,0:T(8,128)} async-done(((f32[4,128,128]{2,1,0:T(8,128)}), f32[4,128,128]{2,1,0:T(8,128)}) %all-reduce.11.cloned.1.call-update) | async-done | bytes 262160 | tf_op jit(solution)/shard_map/psum | solution.py:11
  274.1 0.0 all-gather.5.cloned.1.call-update
  274.1 0.1 broadcast_and_fusion.1
  274.2 1.1 copy.24
  275.3 28.2 %all-gather.5.cloned.1.call-done = f32[4,1024,128]{2,1,0:T(8,128)} async-done(((f32[4,128,128]{2,1,0:T(8,128)}), f32[4,1024,128]{2,1,0:T(8,128)}) %all-gather.5.cloned.1.call-update) | async-done | bytes 2097168 | tf_op jit(solution)/shard_map/all_gather | solution.py:34
  303.5 4.4 %select_select_fusion = f32[4,128,8,128]{1,3,2,0:T(8,128)} fusion(f32[4,128,8,128]{1,3,2,0:T(8,128)S(1)} %select_select_fusion.1, f32[4,128,128]{1,2,0:T(8,128)S(1)} %copy.24, pred[8]{0:T(512)(128)(4,1)S(1)} %get-tuple-element.15, pred[4,8]{1,0:T(4,128)(4,1)S(1)} %broadcast_and_fusion.1, f32[8,4,128,128]{3,2,1,0:T(8,128)} %bitcast.63, s32[]{:T(128)S(6)} %select_n.79, ...), kind=kOutput, calls=%fused_computation | convolution fusion | flops 806879232 | bytes 5242924 | tf_op jit(solution)/shard_map/rib,cjb->ricj/dot_general | solution.py:40
  307.9 2.9 copy.26
  (11 shorter events, 0.1 us)
Async XLA Ops:
  6.5 59.1 %all-reduce.5.cloned.1.call-start = ((), (), s32[]{:S(2)}) async-start(), calls=%async_computation | async-start | bytes 131072 | tf_op jit(solution)/shard_map/psum | solution.py:11
  6.5 83.8 %slice-start = ((f32[4,128,8,128]{3,2,1,0:T(8,128)}), f32[4,128,1,128]{3,2,1,0:T(1,128)S(1)}, s32[]{:S(2)}) async-start(f32[4,128,8,128]{3,2,1,0:T(8,128)} %param.4), calls=%async_computation.6 | async-start | bytes 524288 | tf_op jit(solution)/shard_map/slice | solution.py:62
  8.5 147.6 %copy-start = (f32[4,128,8,128]{1,3,2,0:T(8,128)}, f32[4,128,8,128]{1,3,2,0:T(8,128)S(1)}, u32[]{:S(2)}) copy-start(f32[4,128,8,128]{1,3,2,0:T(8,128)S(1)} %copy.14) | copy-start | bytes 6291460
  9.3 117.3 %all-reduce.7.cloned.1.call-start = ((), (), s32[]{:S(2)}) async-start(), calls=%async_computation.1 | async-start | bytes 524288 | tf_op jit(solution)/shard_map/psum | solution.py:11
  91.7 64.4 %all-gather.3.cloned.1.call-start = ((), (), s32[]{:S(2)}) async-start(), calls=%async_computation.2 | async-start | bytes 2359296 | tf_op jit(solution)/shard_map/all_gather | solution.py:34
  126.6 86.6 %all-reduce.9.cloned.1.call-start = ((), (), s32[]{:S(2)}) async-start(), calls=%async_computation.3 | async-start | bytes 131072 | tf_op jit(solution)/shard_map/psum | solution.py:11
  160.6 113.5 %all-reduce.11.cloned.1.call-start = ((), (), s32[]{:S(2)}) async-start(), calls=%async_computation.4 | async-start | bytes 524288 | tf_op jit(solution)/shard_map/psum | solution.py:11
  239.2 64.3 %all-gather.5.cloned.1.call-start = ((), (), s32[]{:S(2)}) async-start(), calls=%async_computation.5 | async-start | bytes 2359296 | tf_op jit(solution)/shard_map/all_gather | solution.py:34
Sparse Core Ops, SparseCore 0:
  10.4 55.1 all-reduce.4
  91.8 34.6 all-reduce.6
  128.5 27.6 all-gather.2
  160.7 52.4 all-reduce.8
  239.4 34.6 all-reduce.10
  275.8 27.6 all-gather.4
where the time goes:
time: 318 us
  waiting for transfers between devices  235 us (74%)
  other arithmetic  50.6 us (16%)
  between operations  13.7 us (4%)
  local copies, waits for them, and re-layouts  9.29 us (3%)
  matrix products  8.95 us (3%)
    psum x4, waiting for transfers between devices, from_root(): return lax.psum(kept, axis)  178 us
    all_gather x2, waiting for transfers between devices, mirror(): whole = lax.all_gather(rows_part, 'row', axis=1, tiled=True)  56.5 us
    another operation x6, other arithmetic, solve_panel(): factor = jnp.linalg.cholesky(diagonal)  24.8 us
    another operation x4, other arithmetic, solve_panel(): solved = jax.scipy.linalg.solve_triangular(factor, stacked.T, lower=True).T  20.9 us
    dot_general x2, matrix products, trailing(): jnp.einsum('rib,cjb->ricj', row_panel, col_panel, precision=lax.Precision...  8.13 us
  transfers between devices with their start and end apart: 6, of which 6 were waited for; matrix products, arithmetic and copies ran while one was open for 1% of the time, Pallas kernels for 0%

commit v1 on v0

v1 whole, which is shorter than its diff:
```python
import jax
import jax.numpy as jnp
from jax import lax
from jax.sharding import PartitionSpec as P

EXACT = lax.Precision.HIGHEST


def along_col(value, pairs):
    return lax.ppermute(value, "col", pairs)


def spread_col(own, grid_col, n_col):
    even = (grid_col % 2) == 0
    held = own
    reach = 2
    while reach < n_col:
        moved = along_col(held, [(c, c + reach) for c in range(reach) if c + reach < n_col])
        held = jnp.where(grid_col < reach, held, moved)
        reach *= 2
    other = along_col(held, [(c, c ^ 1) for c in range(n_col)])
    return jnp.where(even, held, other), jnp.where(even, other, held)


def spread_row(own, grid_row, n_row, bits):
    holders = [0, 1]
    held = own
    for bit in bits:
        step = 1 << bit
        moved = lax.ppermute(held, "row", [(r, r + step) for r in holders])
        is_new = jnp.zeros((), bool)
        for r in holders:
            is_new = is_new | (grid_row == r + step)
        held = jnp.where(is_new, moved, held)
        holders = holders + [r + step for r in holders]
    return held


def swap_cores(held, grid_row, n_row):
    other = lax.ppermute(held, "row", [(r, r ^ 1) for r in range(n_row)])
    first = (grid_row % 2) == 0
    return jnp.where(first, held, other), jnp.where(first, other, held)


def inverse(factor):
    breadth = factor.shape[0]
    return jax.scipy.linalg.solve_triangular(factor, jnp.eye(breadth, dtype=factor.dtype), lower=True)


def dot(a, b):
    return jnp.dot(a, b, precision=EXACT)


def shards(kernel):
    grid_row = lax.axis_index("row")
    grid_col = lax.axis_index("col")
    n_row = lax.axis_size("row")
    n_col = lax.axis_size("col")
    local_rows, breadth, local_cols, _ = kernel.shape
    bits = list(range(1, n_row.bit_length() - 1))

    column = kernel[:, :, 0, :]
    near, far = spread_col(column[0], grid_col, n_col)
    pair = spread_row(jnp.stack([near, far]), grid_row, n_row, bits)
    top, bottom = swap_cores(pair, grid_row, n_row)
    a00, a10, a11 = top[0], bottom[0], bottom[1]
    rows0, rows1 = spread_col(column, grid_col, n_col)
    half = local_cols // 2
    left = spread_row(kernel[0, :, :half], grid_row, n_row, bits)
    right = spread_row(kernel[0, :, half:], grid_row, n_row, bits[::-1])
    left0, left1 = swap_cores(left, grid_row, n_row)
    right0, right1 = swap_cores(right, grid_row, n_row)
    top0 = jnp.concatenate([left0, right0], axis=1).reshape(breadth, local_cols * breadth)
    top1 = jnp.concatenate([left1, right1], axis=1).reshape(breadth, local_cols * breadth)

    f0 = jnp.linalg.cholesky(a00)
    w0 = inverse(f0)
    l10 = dot(a10, w0.T)
    f1 = jnp.linalg.cholesky(a11 - dot(l10, l10.T))
    w1 = inverse(f1)

    col0 = dot(w0, top0)
    col1 = dot(w1, top1 - dot(l10, col0))
    flat = local_rows * breadth
    row0 = dot(rows0.reshape(flat, breadth), w0.T)
    row1 = dot(rows1.reshape(flat, breadth) - dot(row0, l10.T), w1.T)
    update = dot(row0, col0) + dot(row1, col1)
    matrix = kernel - update.reshape(kernel.shape)

    global_rows = jnp.arange(local_rows, dtype=jnp.int32) * n_row + grid_row
    global_cols = jnp.arange(local_cols, dtype=jnp.int32) * n_col + grid_col
    gr = global_rows[:, None, None]
    row0 = row0.reshape(local_rows, breadth, breadth)
    row1 = row1.reshape(local_rows, breadth, breadth)
    row0 = jnp.where(gr == 0, f0[None], row0)
    row1 = jnp.where(gr == 0, 0.0, jnp.where(gr == 1, f1[None], row1))
    gr = gr[..., None]
    gc = global_cols[None, None, :, None]
    matrix = jnp.where((gr <= 1) & (gc > gr), 0.0, matrix)
    matrix = jnp.where(gc == 0, row0[:, :, None, :], matrix)
    matrix = jnp.where(gc == 1, row1[:, :, None, :], matrix)
    return matrix


def solution(mesh):
    in_specs = (P(None, "row", None, "col"),)
    out_specs = P(None, "row", None, "col")
    return jax.shard_map(shards, mesh=mesh, in_specs=in_specs, out_specs=out_specs, check_vma=False)
```

time: 318 us -> 99.8 us (0.31)
  waiting for transfers between devices: 235 us -> 6.58 us
  starting transfers between devices: 0.39 us -> 23.3 us
  between operations: 13.7 us -> 0.5 us
  other arithmetic: 50.6 us -> 54.2 us
  local copies, waits for them, and re-layouts: 9.29 us -> 5.69 us
    psum x4 -> x0, waiting for transfers between devices: 178 us -> none  [from_root(): return lax.psum(kept, axis)]
    all_gather x2 -> x0, waiting for transfers between devices: 56.5 us -> none  [mirror(): whole = lax.all_gather(rows_part, 'row', axis=1, tiled=True)]
    ppermute x0 -> x13, starting transfers between devices: none -> 23.3 us  [the longest x6 12.6 us: spread_row(): moved = lax.ppermute(held, 'row', [(r, r + step) for r in holders])]
    ppermute x0 -> x13, waiting for transfers between devices: none -> 6.58 us  [the longest x4 4.27 us: along_col(): return lax.ppermute(value, 'col', pairs)]
    psum x4 -> x0, local copies, waits for them, and re-layouts: 4.01 us -> none  [from_root(): return lax.psum(kept, axis)]
    another operation x10 -> x12, other arithmetic: 45.8 us -> 47.7 us  [the longest x4 22.1 us: inverse(): jax.scipy.linalg.solve_triangular(factor, jnp.eye(breadth, dtype=factor.d...]
    dot_general x2 -> x10, matrix products: 8.13 us -> 7.22 us  [dot(): return jnp.dot(a, b, precision=EXACT)]
  transfers between devices with their start and end apart: 6 -> 13, of which waited for: 6 -> 3; matrix products, arithmetic and copies ran while one was open for 1% -> 58% of each run, Pallas kernels for 0% -> 0%
where the time goes in v1:
time: 99.8 us; the launch traced here: 98.9 us
  other arithmetic  54.2 us (54%)
  starting transfers between devices  23.3 us (23%)
  matrix products  8.63 us (9%)
  waiting for transfers between devices  6.58 us (7%)
  local copies, waits for them, and re-layouts  5.69 us (6%)
    another operation x4, other arithmetic, inverse(): jax.scipy.linalg.solve_triangular(factor, jnp.eye(breadth, dtype=factor.d...  22.1 us
    another operation x3, other arithmetic, shards(): f0 = jnp.linalg.cholesky(a00)  13.2 us
    ppermute x6, starting transfers between devices, spread_row(): moved = lax.ppermute(held, 'row', [(r, r + step) for r in holders])  12.6 us
    another operation x3, other arithmetic, shards(): f1 = jnp.linalg.cholesky(a11 - dot(l10, l10.T))  12.4 us
    ppermute x4, starting transfers between devices, along_col(): return lax.ppermute(value, 'col', pairs)  9.99 us
    dot_general x10, matrix products, dot(): return jnp.dot(a, b, precision=EXACT)  7.22 us
    ppermute x4, waiting for transfers between devices, along_col(): return lax.ppermute(value, 'col', pairs)  4.27 us
    squeeze x1, local copies, waits for them, and re-layouts, shards(): left = spread_row(kernel[0, :, :half], grid_row, n_row, bits)  2.14 us
  transfers between devices with their start and end apart: 13, of which 3 were waited for; matrix products, arithmetic and copies ran while one was open for 58% of the time, Pallas kernels for 0%

profile of v1, /device:TPU:0, one launch (start us, length us, event | category | flops | bytes accessed | tf_op | source)
XLA Modules:
  0.0 98.9 jit_solution(15847630750775753966)
XLA Ops:
  0.0 2.1 %slice_bitcast_fusion.1 = (f32[128,4,128]{2,1,0:T(4,128)S(1)}, f32[128,4,128]{2,1,0:T(4,128)}) fusion(f32[4,128,8,128]{3,2,1,0:T(8,128)} %param.4), kind=kLoop, calls=%fused_computation.13 | loop fusion | bytes 1048576 | tf_op jit(solution)/shard_map/squeeze | solution.py:69
  2.1 4.9 %collective-permute-start.10 = (f32[128,4,128]{2,1,0:T(4,128)}, f32[128,4,128]{2,1,0:T(4,128)S(1)}, u32[]{:S(2)}, u32[]{:S(2)}) collective-permute-start(f32[128,4,128]{2,1,0:T(4,128)} %get-tuple-element.14), channel_id=1, source_target_pairs={{0,16},{4,20},{1,17},{5,21},{2,18},{6,22},{3,19},{7,23}} | collective-permute-start | bytes 786440 | tf_op jit(solution)/shard_map/ppermute | solution.py:30
  7.0 2.0 %collective-permute-start.7 = (f32[128,4,128]{2,1,0:T(4,128)S(1)}, f32[128,4,128]{2,1,0:T(4,128)}, u32[]{:S(2)}, u32[]{:S(2)}) collective-permute-start(f32[128,4,128]{2,1,0:T(4,128)S(1)} %get-tuple-element.13), channel_id=1, source_target_pairs={{0,8},{4,12},{1,9},{5,13},{2,10},{6,14},{3,11},{7,15}} | collective-permute-start | bytes 786440 | tf_op jit(solution)/shard_map/ppermute | solution.py:30
  9.0 1.1 %slice.31 = f32[1,128,1,128]{3,2,1,0:T(1,128)S(1)} slice(f32[4,128,8,128]{3,2,1,0:T(8,128)} %param.4), slice={[0:1], [0:128], [0:1], [0:128]} | slice | bytes 131072 | tf_op jit(solution)/shard_map/slice | solution.py:63
  10.2 4.5 %collective-permute-start = (f32[128,128]{0,1:T(8,128)S(1)}, f32[128,128]{0,1:T(8,128)S(1)}, u32[]{:S(2)}, u32[]{:S(2)}) collective-permute-start(f32[128,128]{0,1:T(8,128)S(1)} %bitcast.115), channel_id=1, source_target_pairs={{0,2},{1,3},{4,6},{5,7},{8,10},{9,11},{12,14},{13,15},{16,18},{17,... | collective-permute-start | bytes 196616 | tf_op jit(solution)/shard_map/ppermute | solution.py:10
  14.7 1.7 %slice.35 = f32[4,128,1,128]{3,2,1,0:T(1,128)S(1)} slice(f32[4,128,8,128]{3,2,1,0:T(8,128)} %param.4), slice={[0:4], [0:128], [0:1], [0:128]} | slice | bytes 524288 | tf_op jit(solution)/shard_map/slice | solution.py:62
  16.4 1.3 %collective-permute-start.5 = (f32[4,128,128]{2,1,0:T(8,128)S(1)}, f32[4,128,128]{2,1,0:T(8,128)S(1)}, u32[]{:S(2)}, u32[]{:S(2)}) collective-permute-start(f32[4,128,128]{2,1,0:T(8,128)S(1)} %bitcast.104), channel_id=1, source_target_pairs={{0,2},{1,3},{4,6},{5,7},{8,10},{9,11},{12,14},{13,15},{16,18},{17,... | collective-permute-start | bytes 786440 | tf_op jit(solution)/shard_map/ppermute | solution.py:10
  18.0 1.6 %collective-permute-start.1 = (f32[128,128]{0,1:T(8,128)S(1)}, f32[128,128]{0,1:T(8,128)S(1)}, u32[]{:S(2)}, u32[]{:S(2)}) collective-permute-start(f32[128,128]{0,1:T(8,128)S(1)} %broadcast_select_fusion.15), channel_id=1, source_target_pairs={{0,1},{1,0},{2,3},{3,2},{4,5},{5,4},{6,7},{7,6},{8,9},{9,8},{10,11... | collective-permute-start | bytes 196616 | tf_op jit(solution)/shard_map/ppermute | solution.py:10
  19.6 0.6 broadcast_compare_fusion.3
  20.2 4.3 %collective-permute-done.1 = f32[128,128]{0,1:T(8,128)S(1)} collective-permute-done((f32[128,128]{0,1:T(8,128)S(1)}, f32[128,128]{0,1:T(8,128)S(1)}, u32[]{:S(2)}, u32[]{:S(2)}) %collective-permute-start.1) | collective-permute-done | bytes 65568 | tf_op jit(solution)/shard_map/ppermute | solution.py:10
  24.5 1.3 %collective-permute-start.2 = (f32[2,128,128]{1,2,0:T(8,128)S(1)}, f32[2,128,128]{1,2,0:T(8,128)S(1)}, u32[]{:S(2)}, u32[]{:S(2)}) collective-permute-start(f32[2,128,128]{1,2,0:T(8,128)S(1)} %pad_maximum_fusion.2), channel_id=1, source_target_pairs={{0,8},{4,12},{1,9},{5,13},{2,10},{6,14},{3,11},{7,15}} | collective-permute-start | bytes 393224 | tf_op jit(solution)/shard_map/ppermute | solution.py:30
  25.8 0.1 broadcast_select_fusion.3
  26.0 1.3 %collective-permute-start.8 = (f32[128,4,128]{2,1,0:T(4,128)S(1)}, f32[128,4,128]{2,1,0:T(4,128)S(1)}, u32[]{:S(2)}, u32[]{:S(2)}) collective-permute-start(f32[128,4,128]{2,1,0:T(4,128)S(1)} %get-tuple-element.11), channel_id=1, source_target_pairs={{0,16},{4,20},{8,24},{12,28},{1,17},{5,21},{9,25},{13,29},{2,18},{... | collective-permute-start | bytes 786440 | tf_op jit(solution)/shard_map/ppermute | solution.py:30
  27.3 1.8 %collective-permute-start.11 = (f32[128,4,128]{2,1,0:T(4,128)S(1)}, f32[128,4,128]{2,1,0:T(4,128)S(1)}, u32[]{:S(2)}, u32[]{:S(2)}) collective-permute-start(f32[128,4,128]{2,1,0:T(4,128)S(1)} %get-tuple-element.12), channel_id=1, source_target_pairs={{0,8},{4,12},{16,24},{20,28},{1,9},{5,13},{17,25},{21,29},{2,10},{... | collective-permute-start | bytes 786440 | tf_op jit(solution)/shard_map/ppermute | solution.py:30
  29.1 1.3 %collective-permute-start.3 = (f32[2,128,128]{1,2,0:T(8,128)S(1)}, f32[2,128,128]{1,2,0:T(8,128)S(1)}, u32[]{:S(2)}, u32[]{:S(2)}) collective-permute-start(f32[2,128,128]{1,2,0:T(8,128)S(1)} %broadcast_select_fusion.12), channel_id=1, source_target_pairs={{0,16},{4,20},{8,24},{12,28},{1,17},{5,21},{9,25},{13,29},{2,18},{... | collective-permute-start | bytes 393224 | tf_op jit(solution)/shard_map/ppermute | solution.py:30
  30.5 2.5 %collective-permute-start.6 = (f32[4,128,128]{2,1,0:T(8,128)S(1)}, f32[4,128,128]{2,1,0:T(8,128)S(1)}, u32[]{:S(2)}, u32[]{:S(2)}) collective-permute-start(f32[4,128,128]{2,1,0:T(8,128)S(1)} %broadcast_select_fusion.9), channel_id=1, source_target_pairs={{0,1},{1,0},{2,3},{3,2},{4,5},{5,4},{6,7},{7,6},{8,9},{9,8},{10,11... | collective-permute-start | bytes 786440 | tf_op jit(solution)/shard_map/ppermute | solution.py:10
  33.0 1.7 %collective-permute-done.3 = f32[2,128,128]{1,2,0:T(8,128)S(1)} collective-permute-done((f32[2,128,128]{1,2,0:T(8,128)S(1)}, f32[2,128,128]{1,2,0:T(8,128)S(1)}, u32[]{:S(2)}, u32[]{:S(2)}) %collective-permute-start.3) | collective-permute-done | bytes 131104 | tf_op jit(solution)/shard_map/ppermute | solution.py:30
  34.9 0.5 collective-permute-start.9
  35.5 0.1 collective-permute-start.12
  35.6 0.6 collective-permute-done.4
  36.3 0.6 fusion.12
  36.9 12.5 %cholesky.44 = f32[128,128]{1,0:T(8,128)S(1)} custom-call(f32[128,128]{1,0:T(8,128)} %fusion.12), custom_call_target="Cholesky" | custom-call | tf_op jit(solution)/shard_map/jit(cholesky)/cholesky | solution.py:76
  49.5 0.6 compare_reduce_fusion.1
  50.1 1.2 %fusion.20 = (f32[1,128,128]{2,1,0:T(8,128)S(1)}, f32[128,128]{1,0:T(8,128)}) fusion(f32[128,128]{1,0:T(8,128)S(1)} %cholesky.44, pred[]{:T(512)} %compare_reduce_fusion.1), kind=kLoop, calls=%fused_computation.52 | loop fusion | flops 65536 | bytes 196609 | tf_op jit(solution)/shard_map/jit(_solve_triangular)/triangular_solve | solution.py:47
  51.3 9.8 %custom-call.6 = f32[1,128,128]{1,2,0:T(8,128)S(1)} custom-call(f32[1,128,128]{2,1,0:T(8,128)S(1)} %get-tuple-element.9), custom_call_target="InvertDiagBlocksLowerTriangular" | custom-call | tf_op jit(solution)/shard_map/jit(_solve_triangular)/triangular_solve | solution.py:47
  61.1 0.3 fusion.8
  61.4 0.3 fusion.10
  61.7 0.3 fusion.11
  62.1 11.7 %cholesky.55 = f32[128,128]{1,0:T(8,128)S(1)} custom-call(f32[128,128]{1,0:T(8,128)S(1)} %fusion.14), custom_call_target="Cholesky" | custom-call | tf_op jit(solution)/shard_map/jit(cholesky)/cholesky | solution.py:79
  73.9 0.6 compare_reduce_fusion
  74.5 0.6 select_bitcast_fusion
  75.1 10.6 %custom-call.7 = f32[1,128,128]{1,2,0:T(8,128)} custom-call(f32[1,128,128]{2,1,0:T(8,128)S(1)} %get-tuple-element.6), custom_call_target="InvertDiagBlocksLowerTriangular" | custom-call | tf_op jit(solution)/shard_map/jit(_solve_triangular)/triangular_solve | solution.py:47
  85.6 1.1 %fusion.6 = f32[128,128]{1,0:T(8,128)S(1)} fusion(f32[1,128,128]{1,2,0:T(8,128)} %custom-call.7), kind=kOutput, calls=%fused_computation.28 | convolution fusion | flops 25198592 | bytes 131072 | tf_op jit(solution)/shard_map/jit(_solve_triangular)/triangular_solve | solution.py:47
  86.8 0.4 fusion.23
  87.2 0.4 bitcast_subtract_fusion.1
  87.6 0.4 fusion.24
  88.0 0.8 select_select_fusion
  88.8 1.0 %broadcast_select_fusion.6 = (f32[64,8,128]{2,1,0:T(8,128)S(1)}, f32[64,8,128]{2,1,0:T(8,128)S(1)}) fusion(f32[64,8,128]{2,1,0:T(8,128)} %bitcast.95, f32[64,8,128]{2,1,0:T(8,128)S(1)} %broadcast_select_fusion.4, pred[]{:T(512)S(6)} %eq.87), kind=kLoop, calls=%fused_computation.22 | loop fusion | flops 131072 | bytes 1048577 | tf_op jit(solution)/shard_map/jit(_where)/select_n | solution.py:42
  89.8 1.0 %broadcast_select_fusion.5 = (f32[64,8,128]{2,1,0:T(8,128)S(1)}, f32[64,8,128]{2,1,0:T(8,128)S(1)}) fusion(f32[64,8,128]{2,1,0:T(8,128)} %bitcast.88, f32[64,8,128]{2,1,0:T(8,128)S(1)} %broadcast_select_fusion.2, pred[]{:T(512)S(6)} %eq.87), kind=kLoop, calls=%fused_computation.21 | loop fusion | flops 131072 | bytes 1048577 | tf_op jit(solution)/shard_map/jit(_where)/select_n | solution.py:42
  90.8 0.1 pad_maximum_fusion
  90.9 0.7 fusion.3
  91.6 1.8 %fusion.25 = f32[512,1024]{1,0:T(8,128)S(1)} fusion(f32[512,128]{1,0:T(8,128)S(1)} %fusion.23, f32[128,1024]{1,0:T(8,128)S(1)} %fusion.3), kind=kOutput, calls=%fused_computation.72 | convolution fusion | flops 805306368 | bytes 2883584 | tf_op jit(solution)/shard_map/dot_general | solution.py:51
  93.4 0.1 pad_maximum_fusion.1
  93.5 0.7 convolution_subtract_fusion
  94.2 0.6 fusion.26
  94.7 1.8 %add_bitcast_fusion = f32[64,8,8,128]{3,1,2,0:T(8,128)S(1)} fusion(f32[512,1024]{1,0:T(8,128)S(1)} %fusion.25, f32[512,128]{1,0:T(8,128)S(1)} %fusion.24, f32[128,1024]{1,0:T(8,128)S(1)} %fusion.26), kind=kOutput, calls=%fused_computation.4 | convolution fusion | flops 805830656 | bytes 4980736 | tf_op jit(solution)/shard_map/dot_general | solution.py:51
  96.6 0.5 copy.10
  97.1 1.8 %fusion.2 = f32[4,128,8,128]{3,2,1,0:T(8,128)} fusion(f32[4,128,8,128]{3,2,1,0:T(8,128)S(1)} %copy-done, f32[4,128,128]{2,1,0:T(8,128)S(1)} %get-tuple-element.24, f32[4,128,128]{2,1,0:T(8,128)S(1)} %get-tuple-element.23, pred[8]{0:T(512)(128)(4,1)S(1)} %get-tuple-element.25, pred[8]{0:T(512)(128)(4,1)S(1)} %get-tuple-element.26, ...), kind=kLoop, calls=%fused_computation.3 | loop fusion | flops 2097152 | bytes 6815792 | tf_op jit(solution)/shard_map/jit(_where)/select_n | solution.py:101
  (37 shorter events, 0.8 us)
Async XLA Ops:
  0.0 25.8 %copy-start = (f32[4,128,8,128]{3,2,1,0:T(8,128)S(1)}, f32[4,128,8,128]{3,2,1,0:T(8,128)}, u32[]{:S(2)}) copy-start(f32[4,128,8,128]{3,2,1,0:T(8,128)} %param.4) | copy-start | bytes 6291460
  2.1 23.7 %collective-permute-start.10 = (f32[128,4,128]{2,1,0:T(4,128)}, f32[128,4,128]{2,1,0:T(4,128)S(1)}, u32[]{:S(2)}, u32[]{:S(2)}) collective-permute-start(f32[128,4,128]{2,1,0:T(4,128)} %get-tuple-element.14), channel_id=1, source_target_pairs={{0,16},{4,20},{1,17},{5,21},{2,18},{6,22},{3,19},{7,23}} | collective-permute-start | bytes 786440 | tf_op jit(solution)/shard_map/ppermute | solution.py:30
  7.0 18.8 %collective-permute-start.7 = (f32[128,4,128]{2,1,0:T(4,128)S(1)}, f32[128,4,128]{2,1,0:T(4,128)}, u32[]{:S(2)}, u32[]{:S(2)}) collective-permute-start(f32[128,4,128]{2,1,0:T(4,128)S(1)} %get-tuple-element.13), channel_id=1, source_target_pairs={{0,8},{4,12},{1,9},{5,13},{2,10},{6,14},{3,11},{7,15}} | collective-permute-start | bytes 786440 | tf_op jit(solution)/shard_map/ppermute | solution.py:30
  10.2 7.7 %collective-permute-start = (f32[128,128]{0,1:T(8,128)S(1)}, f32[128,128]{0,1:T(8,128)S(1)}, u32[]{:S(2)}, u32[]{:S(2)}) collective-permute-start(f32[128,128]{0,1:T(8,128)S(1)} %bitcast.115), channel_id=1, source_target_pairs={{0,2},{1,3},{4,6},{5,7},{8,10},{9,11},{12,14},{13,15},{16,18},{17,... | collective-permute-start | bytes 196616 | tf_op jit(solution)/shard_map/ppermute | solution.py:10
  16.4 14.0 %collective-permute-start.5 = (f32[4,128,128]{2,1,0:T(8,128)S(1)}, f32[4,128,128]{2,1,0:T(8,128)S(1)}, u32[]{:S(2)}, u32[]{:S(2)}) collective-permute-start(f32[4,128,128]{2,1,0:T(8,128)S(1)} %bitcast.104), channel_id=1, source_target_pairs={{0,2},{1,3},{4,6},{5,7},{8,10},{9,11},{12,14},{13,15},{16,18},{17,... | collective-permute-start | bytes 786440 | tf_op jit(solution)/shard_map/ppermute | solution.py:10
  18.0 6.5 %collective-permute-start.1 = (f32[128,128]{0,1:T(8,128)S(1)}, f32[128,128]{0,1:T(8,128)S(1)}, u32[]{:S(2)}, u32[]{:S(2)}) collective-permute-start(f32[128,128]{0,1:T(8,128)S(1)} %broadcast_select_fusion.15), channel_id=1, source_target_pairs={{0,1},{1,0},{2,3},{3,2},{4,5},{5,4},{6,7},{7,6},{8,9},{9,8},{10,11... | collective-permute-start | bytes 196616 | tf_op jit(solution)/shard_map/ppermute | solution.py:10
  24.5 4.6 %collective-permute-start.2 = (f32[2,128,128]{1,2,0:T(8,128)S(1)}, f32[2,128,128]{1,2,0:T(8,128)S(1)}, u32[]{:S(2)}, u32[]{:S(2)}) collective-permute-start(f32[2,128,128]{1,2,0:T(8,128)S(1)} %pad_maximum_fusion.2), channel_id=1, source_target_pairs={{0,8},{4,12},{1,9},{5,13},{2,10},{6,14},{3,11},{7,15}} | collective-permute-start | bytes 393224 | tf_op jit(solution)/shard_map/ppermute | solution.py:30
  26.0 8.9 %collective-permute-start.8 = (f32[128,4,128]{2,1,0:T(4,128)S(1)}, f32[128,4,128]{2,1,0:T(4,128)S(1)}, u32[]{:S(2)}, u32[]{:S(2)}) collective-permute-start(f32[128,4,128]{2,1,0:T(4,128)S(1)} %get-tuple-element.11), channel_id=1, source_target_pairs={{0,16},{4,20},{8,24},{12,28},{1,17},{5,21},{9,25},{13,29},{2,18},{... | collective-permute-start | bytes 786440 | tf_op jit(solution)/shard_map/ppermute | solution.py:30
  27.3 8.1 %collective-permute-start.11 = (f32[128,4,128]{2,1,0:T(4,128)S(1)}, f32[128,4,128]{2,1,0:T(4,128)S(1)}, u32[]{:S(2)}, u32[]{:S(2)}) collective-permute-start(f32[128,4,128]{2,1,0:T(4,128)S(1)} %get-tuple-element.12), channel_id=1, source_target_pairs={{0,8},{4,12},{16,24},{20,28},{1,9},{5,13},{17,25},{21,29},{2,10},{... | collective-permute-start | bytes 786440 | tf_op jit(solution)/shard_map/ppermute | solution.py:30
  29.1 5.6 %collective-permute-start.3 = (f32[2,128,128]{1,2,0:T(8,128)S(1)}, f32[2,128,128]{1,2,0:T(8,128)S(1)}, u32[]{:S(2)}, u32[]{:S(2)}) collective-permute-start(f32[2,128,128]{1,2,0:T(8,128)S(1)} %broadcast_select_fusion.12), channel_id=1, source_target_pairs={{0,16},{4,20},{8,24},{12,28},{1,17},{5,21},{9,25},{13,29},{2,18},{... | collective-permute-start | bytes 393224 | tf_op jit(solution)/shard_map/ppermute | solution.py:30
  30.5 56.3 %collective-permute-start.6 = (f32[4,128,128]{2,1,0:T(8,128)S(1)}, f32[4,128,128]{2,1,0:T(8,128)S(1)}, u32[]{:S(2)}, u32[]{:S(2)}) collective-permute-start(f32[4,128,128]{2,1,0:T(8,128)S(1)} %broadcast_select_fusion.9), channel_id=1, source_target_pairs={{0,1},{1,0},{2,3},{3,2},{4,5},{5,4},{6,7},{7,6},{8,9},{9,8},{10,11... | collective-permute-start | bytes 786440 | tf_op jit(solution)/shard_map/ppermute | solution.py:10
  34.7 1.4 %collective-permute-start.4 = (f32[2,128,128]{1,2,0:T(8,128)S(1)}, f32[2,128,128]{1,2,0:T(8,128)S(1)}, u32[]{:S(2)}, u32[]{:S(2)}) collective-permute-start(f32[2,128,128]{1,2,0:T(8,128)S(1)} %broadcast_select_fusion.13), channel_id=1, source_target_pairs={{0,4},{4,0},{8,12},{12,8},{16,20},{20,16},{24,28},{28,24},{1,5},{5... | collective-permute-start | bytes 393224 | tf_op jit(solution)/shard_map/ppermute | solution.py:40
  34.9 53.9 %collective-permute-start.9 = (f32[128,4,128]{2,1,0:T(4,128)S(1)}, f32[128,4,128]{2,1,0:T(4,128)}, u32[]{:S(2)}, u32[]{:S(2)}) collective-permute-start(f32[128,4,128]{2,1,0:T(4,128)S(1)} %bitcast.107), channel_id=1, source_target_pairs={{0,4},{4,0},{8,12},{12,8},{16,20},{20,16},{24,28},{28,24},{1,5},{5... | collective-permute-start | bytes 786440 | tf_op jit(solution)/shard_map/ppermute | solution.py:40
  35.5 54.3 %collective-permute-start.12 = (f32[128,4,128]{2,1,0:T(4,128)S(1)}, f32[128,4,128]{2,1,0:T(4,128)}, u32[]{:S(2)}, u32[]{:S(2)}) collective-permute-start(f32[128,4,128]{2,1,0:T(4,128)S(1)} %bitcast.108), channel_id=1, source_target_pairs={{0,4},{4,0},{8,12},{12,8},{16,20},{20,16},{24,28},{28,24},{1,5},{5... | collective-permute-start | bytes 786440 | tf_op jit(solution)/shard_map/ppermute | solution.py:40
  61.4 26.6 %copy-start.1 = (f32[128,128]{1,0:T(8,128)S(1)}, f32[128,128]{1,0:T(8,128)}, u32[]{:S(2)}) copy-start(f32[128,128]{1,0:T(8,128)} %get-tuple-element.10) | copy-start | bytes 196612

commit v2 on v1

v2 whole, which is shorter than its diff:
```python
import jax
import jax.numpy as jnp
from jax import lax
from jax.experimental import pallas as pl
from jax.experimental.pallas import tpu as pltpu
from jax.sharding import PartitionSpec as P

EXACT = lax.Precision.HIGHEST
SUB = 8
VMEM = pl.BlockSpec(memory_space=pltpu.VMEM)
SMEM = pl.BlockSpec(memory_space=pltpu.SMEM)


def dot(a, b):
    return lax.dot_general(a, b, (((1,), (0,)), ((), ())), precision=EXACT, preferred_element_type=jnp.float32)


def dot_t(a, b):
    return lax.dot_general(a, b, (((1,), (1,)), ((), ())), precision=EXACT, preferred_element_type=jnp.float32)


def inverse_of(p):
    r = pl.reciprocal(p, approx=True)
    r = r * (2.0 - p * r)
    return r * (2.0 - p * r)


def eliminate(s, sym, aug):
    n = s.shape[0]
    groups = n // SUB
    sub = lax.broadcasted_iota(jnp.int32, (SUB, n), 0)
    lane = lax.broadcasted_iota(jnp.int32, (SUB, n), 1)
    sym[...] = s.reshape(groups, SUB, n)
    rows = lax.broadcasted_iota(jnp.int32, (n, n), 0)
    cols = lax.broadcasted_iota(jnp.int32, (n, n), 1)
    aug[...] = jnp.where(rows == cols, 1.0, 0.0).reshape(groups, SUB, n)
    for g in range(groups):
        start = g * SUB
        left = groups - g
        rest = sym[g:]
        top = sym[g]
        top_aug = aug[g]
        spread = [jnp.broadcast_to(rest[:, :, start + j:start + j + 1], (left, SUB, n)) for j in range(SUB)]
        scaled = []
        scaled_aug = []
        roots = jnp.zeros((SUB, n), jnp.float32)
        for k in range(SUB):
            pivot = jnp.broadcast_to(spread[k][0, k:k + 1, :], (SUB, n))
            recip = inverse_of(pivot)
            roots = jnp.where(sub == k, pivot, roots)
            for j in range(k + 1, SUB):
                factor = jnp.broadcast_to(spread[k][0, j:j + 1, :], (SUB, n)) * recip
                spread[j] = spread[j] - spread[k] * factor[None]
            row = jnp.broadcast_to(top[k:k + 1, :], (SUB, n)) * recip
            row_aug = jnp.broadcast_to(top_aug[k:k + 1, :], (SUB, n)) * recip
            scaled.append(row)
            scaled_aug.append(row_aug)
            if k + 1 < SUB:
                below = jnp.where(sub > k, spread[k][0], 0.0)
                top = top - below * row
                top_aug = top_aug - below * row_aug
        root = lax.rsqrt(roots)
        sym[g] = jnp.where(lane >= start + sub, top * root, 0.0)
        aug[g] = top_aug * root
        if left > 1:
            low = rest[1:]
            low_aug = aug[g + 1:]
            for k in range(SUB):
                low = low - spread[k][1:] * scaled[k][None]
                low_aug = low_aug - spread[k][1:] * scaled_aug[k][None]
            sym[g + 1:] = low
            aug[g + 1:] = low_aug
    upper = sym[...].reshape(n, n)
    return upper.T, aug[...].reshape(n, n)


def first_factor_kernel(a_ref, f_ref, w_ref, sym, aug):
    f_ref[...], w_ref[...] = eliminate(a_ref[...], sym, aug)


def second_factor_kernel(odd_ref, low_ref, a_ref, w0_ref, f_ref, w_ref, mixed_ref, sym, aug):
    n = a_ref.shape[0]
    w0 = w0_ref[...]
    cross = dot_t(low_ref[...], w0)
    f1, w1 = eliminate(a_ref[...] - dot_t(cross, cross), sym, aug)
    f_ref[...] = f1
    w10 = -dot(w1, dot(cross, w0))
    zero = jnp.zeros((n, n), jnp.float32)
    w_ref[:n, :n] = w0
    w_ref[:n, n:] = zero
    w_ref[n:, :n] = w10
    w_ref[n:, n:] = w1
    odd = odd_ref[0] == 1
    mixed_ref[:n, :n] = jnp.where(odd, zero, w0)
    mixed_ref[:n, n:] = jnp.where(odd, w0, zero)
    mixed_ref[n:, :n] = jnp.where(odd, w1, w10)
    mixed_ref[n:, n:] = jnp.where(odd, w10, w1)


def cost(flops, nbytes):
    return pl.CostEstimate(flops=flops, bytes_accessed=nbytes, transcendentals=0)


def first_factor(a):
    n = a.shape[0]
    square = jax.ShapeDtypeStruct((n, n), jnp.float32)
    scratch = [pltpu.VMEM((n // SUB, SUB, n), jnp.float32)] * 2
    return pl.pallas_call(
        first_factor_kernel,
        out_shape=[square, square],
        in_specs=[VMEM],
        out_specs=[VMEM, VMEM],
        scratch_shapes=scratch,
        name="first_factor",
    )(a)


def second_factor(odd, low, a, w0):
    n = a.shape[0]
    square = jax.ShapeDtypeStruct((n, n), jnp.float32)
    double = jax.ShapeDtypeStruct((2 * n, 2 * n), jnp.float32)
    scratch = [pltpu.VMEM((n // SUB, SUB, n), jnp.float32)] * 2
    return pl.pallas_call(
        second_factor_kernel,
        out_shape=[square, double, double],
        in_specs=[SMEM, VMEM, VMEM, VMEM],
        out_specs=[VMEM, VMEM, VMEM],
        scratch_shapes=scratch,
        name="second_factor",
    )(odd, low, a, w0)


def settle_kernel(place_ref, f0_ref, f1_ref, w_ref, mixed_ref, rows0_ref, rows1_ref, ha_ref, hb_ref, oa_ref, ob_ref,
                  matrix_ref, out_ref, panel):
    grid_row = place_ref[0]
    grid_col = place_ref[1]
    step = pl.program_id(0)
    n = f0_ref.shape[0]
    blocks = matrix_ref.shape[0]
    local_cols = matrix_ref.shape[2]

    @pl.when(step == 0)
    def _():
        mixed = mixed_ref[...]
        for j in range(local_cols):
            stacked = jnp.concatenate([ha_ref[:, j, :], hb_ref[:, j, :], oa_ref[:, j, :], ob_ref[:, j, :]], axis=0)
            panel[:, j * n:(j + 1) * n] = dot(mixed, stacked)

    rows = jnp.concatenate(
        [rows0_ref[...].reshape(blocks * n, n), rows1_ref[...].reshape(blocks * n, n)], axis=1)
    solved = dot_t(rows, w_ref[...])
    for j in range(0, local_cols, 2):
        update = dot(solved, panel[:, j * n:(j + 2) * n])
        for b in range(2):
            part = update[:, b * n:(b + 1) * n].reshape(blocks, n, n)
            out_ref[:, :, j + b, :] = matrix_ref[:, :, j + b, :] - part

    @pl.when(grid_col == 0)
    def _():
        out_ref[:, :, 0, :] = solved[:, :n].reshape(blocks, n, n)

    @pl.when(grid_col == 1)
    def _():
        out_ref[:, :, 0, :] = solved[:, n:].reshape(blocks, n, n)

    @pl.when((step == 0) & (grid_row <= 1))
    def _():
        keep = solved[:n, :n]
        out_ref[0] = jnp.zeros(out_ref.shape[1:], jnp.float32)

        @pl.when((grid_row == 0) & (grid_col == 0))
        def _():
            out_ref[0, :, 0, :] = f0_ref[...]

        @pl.when((grid_row == 1) & (grid_col == 0))
        def _():
            out_ref[0, :, 0, :] = keep

        @pl.when((grid_row == 1) & (grid_col == 1))
        def _():
            out_ref[0, :, 0, :] = f1_ref[...]


def settle(place, f0, f1, w, mixed, rows0, rows1, ha, hb, oa, ob, matrix):
    local_rows, n, local_cols, _ = matrix.shape
    per = 2
    strip = pl.BlockSpec((per, n, n), lambda s: (s, 0, 0))
    slab = pl.BlockSpec((per, n, local_cols, n), lambda s: (s, 0, 0, 0))
    return pl.pallas_call(
        settle_kernel,
        grid=(local_rows // per,),
        out_shape=jax.ShapeDtypeStruct(matrix.shape, jnp.float32),
        in_specs=[SMEM] + [VMEM] * 4 + [strip] * 2 + [VMEM] * 4 + [slab],
        out_specs=slab,
        scratch_shapes=[pltpu.VMEM((2 * n, local_cols * n), jnp.float32)],
        compiler_params=pltpu.CompilerParams(vmem_limit_bytes=40 * 1024 * 1024),
        name="settle",
    )(place, f0, f1, w, mixed, rows0, rows1, ha, hb, oa, ob, matrix)


def spread_col(own, grid_col, n_col):
    even = (grid_col % 2) == 0
    held = own
    reach = 2
    while reach < n_col:
        moved = lax.ppermute(held, "col", [(c, c + reach) for c in range(reach) if c + reach < n_col])
        held = jnp.where(grid_col < reach, held, moved)
        reach *= 2
    other = lax.ppermute(held, "col", [(c, c ^ 1) for c in range(n_col)])
    return jnp.where(even, held, other), jnp.where(even, other, held)


def spread_row(own, grid_row, bits, holders=(0, 1)):
    holders = list(holders)
    held = own
    for bit in bits:
        step = 1 << bit
        moved = lax.ppermute(held, "row", [(r, r + step) for r in holders])
        held = jnp.where(((grid_row >> bit) & 1) == 1, moved, held)
        holders = holders + [r + step for r in holders]
    return held


def swap_cores(held, n_row):
    return lax.ppermute(held, "row", [(r, r ^ 1) for r in range(n_row)])


def shards(kernel):
    grid_row = lax.axis_index("row")
    grid_col = lax.axis_index("col")
    n_row = lax.axis_size("row")
    n_col = lax.axis_size("col")
    local_rows, n, local_cols, _ = kernel.shape
    bits = list(range(1, n_row.bit_length() - 1))
    odd = grid_row % 2

    def flat(r, c):
        return r * n_col + c

    block = kernel[0, :, 0, :]
    here0 = block
    here1 = block
    for shift in range(1, n_col):
        pairs = [(flat(0, 0), flat(0, shift)), (flat(1, 0), flat(1, shift))]
        pairs.append((flat(1, 1), flat(1, 0 if shift == 1 else shift ^ 1)))
        moved = lax.ppermute(block, ("row", "col"), pairs)
        here0 = jnp.where(grid_col == shift, moved, here0)
        here1 = jnp.where(grid_col == (0 if shift == 1 else shift ^ 1), moved, here1)
    here0 = spread_row(here0, grid_row, bits)
    here1 = spread_row(here1, grid_row, bits, (1,))
    swapped = swap_cores(here0, n_row)
    a00 = jnp.where(odd == 0, here0, swapped)
    a10 = jnp.where(odd == 0, swapped, here0)
    a11 = jnp.where(odd == 0, lax.ppermute(here1, "row", [(r + 1, r) for r in range(0, n_row, 2)]), here1)

    rows0, rows1 = spread_col(kernel[:, :, 0, :], grid_col, n_col)
    half = n // 2
    ha = spread_row(kernel[0, :half], grid_row, bits)
    hb = spread_row(kernel[0, half:], grid_row, bits[::-1])
    oa = swap_cores(ha, n_row)
    ob = swap_cores(hb, n_row)

    f0, w0 = first_factor(a00)
    f1, w, mixed = second_factor(odd[None], a10, a11, w0)
    place = jnp.stack([grid_row, grid_col])
    return settle(place, f0, f1, w, mixed, rows0, rows1, ha, hb, oa, ob, kernel)


def solution(mesh):
    in_specs = (P(None, "row", None, "col"),)
    out_specs = P(None, "row", None, "col")
    return jax.shard_map(shards, mesh=mesh, in_specs=in_specs, out_specs=out_specs, check_vma=False)
```

time: 99.8 us -> 74.1 us (0.74)
  other arithmetic: 54.2 us -> 2.64 us
  Pallas kernels: 0 us -> 23 us
  matrix products: 8.63 us -> 0 us
  starting transfers between devices: 23.3 us -> 28.7 us
  waiting for transfers between devices: 6.58 us -> 10.4 us
  local copies, waits for them, and re-layouts: 5.69 us -> 8.3 us
    another operation x12 -> x1, other arithmetic: 47.7 us -> 0.08 us  [shards(): place = jnp.stack([grid_row, grid_col])]
    pallas_call x0 -> x3, Pallas kernels: none -> 23 us  [the longest x1 8.67 us: settle(): pl.pallas_call(settle_kernel, grid=(local_rows // per,), out_shape=jax.Sh...]
    ppermute x6 -> x8, waiting for transfers between devices: 1.69 us -> 10.4 us  [spread_row(): moved = lax.ppermute(held, 'row', [(r, r + step) for r in holders])]
    dot_general x10 -> x0, matrix products: 7.22 us -> none  [dot(): return jnp.dot(a, b, precision=EXACT)]
    ppermute x7 -> x9, waiting for transfers between devices: 4.88 us -> 0.02 us  [the longest x3 0.01 us: swap_cores(): return lax.ppermute(held, 'row', [(r, r ^ 1) for r in range(n_row)])]
    select_n x10, other arithmetic: 4.82 us -> 1.52 us  [the longest x1 0.66 us: shards(): a10 = jnp.where(odd == 0, swapped, here0)]
    unnamed x6 -> x10, local copies, waits for them, and re-layouts: 0.57 us -> 3.58 us
    ppermute x7 -> x9, starting transfers between devices: 10.7 us -> 13.6 us  [the longest x3 8.29 us: shards(): moved = lax.ppermute(block, ('row', 'col'), pairs)]
  transfers between devices with their start and end apart: 13 -> 17, of which waited for: 3 -> 3; matrix products, arithmetic and copies ran while one was open for 58% -> 8% of each run, Pallas kernels for 0% -> 20%
where the time goes in v2:
time: 74.1 us; the launch traced here: 73.3 us
  starting transfers between devices  28.7 us (39%)
  Pallas kernels  23 us (31%)
  waiting for transfers between devices  10.4 us (14%)
  local copies, waits for them, and re-layouts  8.3 us (11%)
  other arithmetic  2.64 us (4%)
    ppermute x8, starting transfers between devices, spread_row(): moved = lax.ppermute(held, 'row', [(r, r + step) for r in holders])  15.1 us
    ppermute x8, waiting for transfers between devices, spread_row(): moved = lax.ppermute(held, 'row', [(r, r + step) for r in holders])  10.4 us
    pallas_call x1, Pallas kernels, settle(): pl.pallas_call(settle_kernel, grid=(local_rows // per,), out_shape=jax.Sh...  8.67 us
    ppermute x3, starting transfers between devices, shards(): moved = lax.ppermute(block, ('row', 'col'), pairs)  8.29 us
    pallas_call x1, Pallas kernels, second_factor(): pl.pallas_call(second_factor_kernel, out_shape=[square, double, double],...  7.66 us
    pallas_call x1, Pallas kernels, first_factor(): pl.pallas_call(first_factor_kernel, out_shape=[square, square], in_specs=...  6.65 us
    unnamed x10, local copies, waits for them, and re-layouts  3.58 us
    ppermute x1, starting transfers between devices, spread_col(): lax.ppermute(held, 'col', [(c, c + reach) for c in range(reach) if c + re...  2.01 us
  transfers between devices with their start and end apart: 17, of which 3 were waited for; matrix products, arithmetic and copies ran while one was open for 8% of the time, Pallas kernels for 20%

profile of v2, /device:TPU:0, one launch (start us, length us, event | category | flops | bytes accessed | tf_op | source)
XLA Modules:
  0.0 73.3 jit_solution(6452412387320371798)
XLA Ops:
  0.0 1.2 %slice.12 = f32[1,128,1,128]{3,2,1,0:T(1,128)S(1)} slice(f32[4,128,8,128]{3,2,1,0:T(8,128)} %matrix_ref.1), slice={[0:1], [0:128], [0:1], [0:128]} | slice | bytes 131072 | tf_op jit(solution)/shard_map/slice | solution.py:240
  1.2 4.9 %collective-permute-start.2 = (f32[128,128]{1,0:T(8,128)S(1)}, f32[128,128]{1,0:T(8,128)S(1)}, u32[]{:S(2)}, u32[]{:S(2)}) collective-permute-start(f32[128,128]{1,0:T(8,128)S(1)} %bitcast.19), channel_id=1, source_target_pairs={{0,1},{4,5},{5,4}} | collective-permute-start | bytes 196616 | tf_op jit(solution)/shard_map/ppermute | solution.py:246
  6.2 1.7 %collective-permute-start.1 = (f32[128,128]{1,0:T(8,128)S(1)}, f32[128,128]{1,0:T(8,128)S(1)}, u32[]{:S(2)}, u32[]{:S(2)}) collective-permute-start(f32[128,128]{1,0:T(8,128)S(1)} %bitcast.20), channel_id=1, source_target_pairs={{0,2},{4,6},{5,7}} | collective-permute-start | bytes 196616 | tf_op jit(solution)/shard_map/ppermute | solution.py:246
  7.9 1.7 %collective-permute-start = (f32[128,128]{1,0:T(8,128)S(1)}, f32[128,128]{1,0:T(8,128)S(1)}, u32[]{:S(2)}, u32[]{:S(2)}) collective-permute-start(f32[128,128]{1,0:T(8,128)S(1)} %bitcast.21), channel_id=1, source_target_pairs={{0,3},{4,7},{5,6}} | collective-permute-start | bytes 196616 | tf_op jit(solution)/shard_map/ppermute | solution.py:246
  9.5 1.7 %slice.13 = f32[4,128,1,128]{3,2,1,0:T(1,128)S(1)} slice(f32[4,128,8,128]{3,2,1,0:T(8,128)} %matrix_ref.1), slice={[0:4], [0:128], [0:1], [0:128]} | slice | bytes 524288 | tf_op jit(solution)/shard_map/slice | solution.py:256
  11.3 2.0 %collective-permute-start.9 = (f32[4,128,128]{2,1,0:T(8,128)S(1)}, f32[4,128,128]{2,1,0:T(8,128)}, u32[]{:S(2)}, u32[]{:S(2)}) collective-permute-start(f32[4,128,128]{2,1,0:T(8,128)S(1)} %bitcast.17), channel_id=1, source_target_pairs={{0,2},{1,3},{4,6},{5,7},{8,10},{9,11},{12,14},{13,15},{16,18},{17,... | collective-permute-start | bytes 786440 | tf_op jit(solution)/shard_map/ppermute | solution.py:206
  13.3 1.8 %slice_bitcast_fusion = (f32[64,8,128]{2,1,0:T(8,128)}, f32[64,8,128]{2,1,0:T(8,128)S(1)}) fusion(f32[4,128,8,128]{3,2,1,0:T(8,128)} %matrix_ref.1), kind=kLoop, calls=%fused_computation | loop fusion | bytes 1048576 | tf_op jit(solution)/shard_map/squeeze | solution.py:259
  15.1 1.8 %collective-permute-start.13 = (f32[64,8,128]{2,1,0:T(8,128)}, f32[64,8,128]{2,1,0:T(8,128)S(1)}, u32[]{:S(2)}, u32[]{:S(2)}) collective-permute-start(f32[64,8,128]{2,1,0:T(8,128)} %get-tuple-element.17), channel_id=1, source_target_pairs={{0,16},{4,20},{1,17},{5,21},{2,18},{6,22},{3,19},{7,23}} | collective-permute-start | bytes 786440 | tf_op jit(solution)/shard_map/ppermute | solution.py:218
  16.9 0.0 collective-permute-done.2
  16.9 1.3 %collective-permute-start.11 = (f32[64,8,128]{2,1,0:T(8,128)S(1)}, f32[64,8,128]{2,1,0:T(8,128)S(1)}, u32[]{:S(2)}, u32[]{:S(2)}) collective-permute-start(f32[64,8,128]{2,1,0:T(8,128)S(1)} %get-tuple-element.18), channel_id=1, source_target_pairs={{0,8},{4,12},{1,9},{5,13},{2,10},{6,14},{3,11},{7,15}} | collective-permute-start | bytes 786440 | tf_op jit(solution)/shard_map/ppermute | solution.py:218
  18.2 0.0 collective-permute-done.1
  18.2 0.0 collective-permute-done
  18.3 0.7 collective-permute-start.6
  18.9 0.1 pad_add_fusion.place_ref
  19.0 1.3 %collective-permute-start.3 = (f32[128,128]{1,0:T(8,128)S(1)}, f32[128,128]{1,0:T(8,128)S(1)}, u32[]{:S(2)}, u32[]{:S(2)}) collective-permute-start(f32[128,128]{1,0:T(8,128)S(1)} %get-tuple-element.22), channel_id=1, source_target_pairs={{0,8},{4,12},{1,9},{5,13},{2,10},{6,14},{3,11},{7,15}} | collective-permute-start | bytes 196616 | tf_op jit(solution)/shard_map/ppermute | solution.py:218
  20.3 0.0 collective-permute-done.6
  20.3 0.7 collective-permute-start.7
  21.0 5.0 %collective-permute-done.3 = f32[128,128]{1,0:T(8,128)S(1)} collective-permute-done((f32[128,128]{1,0:T(8,128)S(1)}, f32[128,128]{1,0:T(8,128)S(1)}, u32[]{:S(2)}, u32[]{:S(2)}) %collective-permute-start.3) | collective-permute-done | bytes 65568 | tf_op jit(solution)/shard_map/ppermute | solution.py:218
  26.0 1.3 %collective-permute-start.4 = (f32[128,128]{1,0:T(8,128)S(1)}, f32[128,128]{1,0:T(8,128)S(1)}, u32[]{:S(2)}, u32[]{:S(2)}) collective-permute-start(f32[128,128]{1,0:T(8,128)S(1)} %broadcast_select_fusion.8), channel_id=1, source_target_pairs={{0,16},{4,20},{8,24},{12,28},{1,17},{5,21},{9,25},{13,29},{2,18},{... | collective-permute-start | bytes 196616 | tf_op jit(solution)/shard_map/ppermute | solution.py:218
  27.3 0.0 collective-permute-done.7
  27.3 1.3 %collective-permute-start.8 = (f32[128,128]{1,0:T(8,128)S(1)}, f32[128,128]{1,0:T(8,128)S(1)}, u32[]{:S(2)}, u32[]{:S(2)}) collective-permute-start(f32[128,128]{1,0:T(8,128)S(1)} %broadcast_select_fusion.9), channel_id=1, source_target_pairs={{4,0},{12,8},{20,16},{28,24},{5,1},{13,9},{21,17},{29,25},{6,2},{1... | collective-permute-start | bytes 196616 | tf_op jit(solution)/shard_map/ppermute | solution.py:254
  28.6 0.6 collective-permute-done.4
  29.2 0.7 collective-permute-start.5
  29.8 0.0 collective-permute-done.13
  29.8 0.0 collective-permute-done.11
  29.9 0.1 broadcast_select_fusion.2
  30.0 4.4 %collective-permute-start.14 = (f32[64,8,128]{2,1,0:T(8,128)S(1)}, f32[64,8,128]{2,1,0:T(8,128)S(1)}, u32[]{:S(2)}, u32[]{:S(2)}) collective-permute-start(f32[64,8,128]{2,1,0:T(8,128)S(1)} %get-tuple-element.15), channel_id=1, source_target_pairs={{0,8},{4,12},{16,24},{20,28},{1,9},{5,13},{17,25},{21,29},{2,10},{... | collective-permute-start | bytes 786440 | tf_op jit(solution)/shard_map/ppermute | solution.py:218
  34.4 0.0 collective-permute-done.9
  34.4 1.2 %collective-permute-start.10 = (f32[4,128,128]{2,1,0:T(8,128)S(1)}, f32[4,128,128]{2,1,0:T(8,128)}, u32[]{:S(2)}, u32[]{:S(2)}) collective-permute-start(f32[4,128,128]{2,1,0:T(8,128)S(1)} %broadcast_select_fusion.4), channel_id=1, source_target_pairs={{0,1},{1,0},{2,3},{3,2},{4,5},{5,4},{6,7},{7,6},{8,9},{9,8},{10,11... | collective-permute-start | bytes 786440 | tf_op jit(solution)/shard_map/ppermute | solution.py:209
  35.6 3.7 %collective-permute-start.12 = (f32[64,8,128]{2,1,0:T(8,128)S(1)}, f32[64,8,128]{2,1,0:T(8,128)S(1)}, u32[]{:S(2)}, u32[]{:S(2)}) collective-permute-start(f32[64,8,128]{2,1,0:T(8,128)S(1)} %get-tuple-element.16), channel_id=1, source_target_pairs={{0,16},{4,20},{8,24},{12,28},{1,17},{5,21},{9,25},{13,29},{2,18},{... | collective-permute-start | bytes 786440 | tf_op jit(solution)/shard_map/ppermute | solution.py:218
  39.4 0.0 collective-permute-done.5
  39.4 0.7 broadcast_select_fusion.12
  40.0 0.0 collective-permute-done.14
  40.1 0.1 collective-permute-start.16
  40.2 4.8 %collective-permute-done.12 = f32[64,8,128]{2,1,0:T(8,128)S(1)} collective-permute-done((f32[64,8,128]{2,1,0:T(8,128)S(1)}, f32[64,8,128]{2,1,0:T(8,128)S(1)}, u32[]{:S(2)}, u32[]{:S(2)}) %collective-permute-start.12) | collective-permute-done | bytes 262176 | tf_op jit(solution)/shard_map/ppermute | solution.py:218
  45.0 0.1 collective-permute-start.15
  45.1 0.0 collective-permute-done.8
  45.1 0.6 broadcast_select_fusion.11.a_ref
  45.7 6.6 %first_factor.1 = (f32[128,128]{1,0:T(8,128)}, f32[128,128]{1,0:T(8,128)}) custom-call(f32[128,128]{1,0:T(8,128)} %get-tuple-element.24.a_ref), custom_call_target="tpu_custom_call" | custom-call | tf_op jit(solution)/shard_map/first_factor/pallas_call | solution.py:108
  52.4 7.7 %second_factor.1 = (f32[128,128]{1,0:T(8,128)}, f32[256,256]{1,0:T(8,128)}, f32[256,256]{1,0:T(8,128)}) custom-call(s32[1]{0:T(128)} %bitcast.3.odd_ref, f32[128,128]{1,0:T(8,128)} %get-tuple-element.23.low_ref, f32[128,128]{1,0:T(8,128)} %broadcast_select_fusion.11.a_ref, f32[128,128]{1,0:T(8,128)} %get-tuple-element.11.w0_ref), custom_call_target="tpu_custom_call" | custom-call | tf_op jit(solution)/shard_map/second_factor/pallas_call | solution.py:123
  60.1 1.0 %broadcast_select_fusion.5 = (f32[4,128,128]{2,1,0:T(8,128)S(1)}, f32[4,128,128]{2,1,0:T(8,128)S(1)}) fusion(f32[4,128,128]{2,1,0:T(8,128)} %collective-permute-done.10, f32[4,128,128]{2,1,0:T(8,128)S(1)} %broadcast_select_fusion.4, pred[]{:T(512)S(6)} %eq.44), kind=kLoop, calls=%fused_computation.7 | loop fusion | flops 131072 | bytes 1048577 | tf_op jit(solution)/shard_map/jit(_where)/select_n | solution.py:210
  61.1 0.0 collective-permute-done.16.ob_ref
  61.1 0.0 copy-start.1
  61.1 0.9 %copy-done.1 = f32[256,256]{1,0:T(8,128)S(1)} copy-done((f32[256,256]{1,0:T(8,128)S(1)}, f32[256,256]{1,0:T(8,128)}, u32[]{:S(2)}) %copy-start.1) | copy-done | bytes 262168
  62.0 0.9 %copy-done.2 = f32[256,256]{1,0:T(8,128)S(1)} copy-done((f32[256,256]{1,0:T(8,128)S(1)}, f32[256,256]{1,0:T(8,128)}, u32[]{:S(2)}) %copy-start.2) | copy-done | bytes 262168
  63.0 0.8 %copy-done.3 = f32[128,128]{1,0:T(8,128)S(1)} copy-done((f32[128,128]{1,0:T(8,128)S(1)}, f32[128,128]{1,0:T(8,128)}, u32[]{:S(2)}) %copy-start.3) | copy-done | bytes 65560
  63.8 0.8 %copy-done.4 = f32[128,128]{1,0:T(8,128)S(1)} copy-done((f32[128,128]{1,0:T(8,128)S(1)}, f32[128,128]{1,0:T(8,128)}, u32[]{:S(2)}) %copy-start.4) | copy-done | bytes 65560
  64.7 8.7 %settle.1 = f32[4,128,8,128]{3,2,1,0:T(8,128)} custom-call(s32[2]{0:T(128)S(1)} %pad_add_fusion.place_ref, f32[128,128]{1,0:T(8,128)S(1)} %copy-done.3, f32[128,128]{1,0:T(8,128)S(1)} %copy-done.4, f32[256,256]{1,0:T(8,128)S(1)} %copy-done.1, f32[256,256]{1,0:T(8,128)S(1)} %copy-done.2, f32[4,128,128]{2,1,0:T(8,128)S(1)} %get-tuple-element.20.rows0_ref, ...), custom_call_target="tpu_custom_call" | custom-call | tf_op jit(solution)/shard_map/settle/pallas_call | solution.py:189
  (15 shorter events, 0.2 us)
Async XLA Ops:
  0.0 29.8 %copy-start = (f32[4,128,8,128]{3,2,1,0:T(8,128)S(1)}, f32[4,128,8,128]{3,2,1,0:T(8,128)}, u32[]{:S(2)}) copy-start(f32[4,128,8,128]{3,2,1,0:T(8,128)} %matrix_ref.1) | copy-start | bytes 6291460
  1.2 15.7 %collective-permute-start.2 = (f32[128,128]{1,0:T(8,128)S(1)}, f32[128,128]{1,0:T(8,128)S(1)}, u32[]{:S(2)}, u32[]{:S(2)}) collective-permute-start(f32[128,128]{1,0:T(8,128)S(1)} %bitcast.19), channel_id=1, source_target_pairs={{0,1},{4,5},{5,4}} | collective-permute-start | bytes 196616 | tf_op jit(solution)/shard_map/ppermute | solution.py:246
  6.2 12.0 %collective-permute-start.1 = (f32[128,128]{1,0:T(8,128)S(1)}, f32[128,128]{1,0:T(8,128)S(1)}, u32[]{:S(2)}, u32[]{:S(2)}) collective-permute-start(f32[128,128]{1,0:T(8,128)S(1)} %bitcast.20), channel_id=1, source_target_pairs={{0,2},{4,6},{5,7}} | collective-permute-start | bytes 196616 | tf_op jit(solution)/shard_map/ppermute | solution.py:246
  7.9 10.4 %collective-permute-start = (f32[128,128]{1,0:T(8,128)S(1)}, f32[128,128]{1,0:T(8,128)S(1)}, u32[]{:S(2)}, u32[]{:S(2)}) collective-permute-start(f32[128,128]{1,0:T(8,128)S(1)} %bitcast.21), channel_id=1, source_target_pairs={{0,3},{4,7},{5,6}} | collective-permute-start | bytes 196616 | tf_op jit(solution)/shard_map/ppermute | solution.py:246
  11.3 23.1 %collective-permute-start.9 = (f32[4,128,128]{2,1,0:T(8,128)S(1)}, f32[4,128,128]{2,1,0:T(8,128)}, u32[]{:S(2)}, u32[]{:S(2)}) collective-permute-start(f32[4,128,128]{2,1,0:T(8,128)S(1)} %bitcast.17), channel_id=1, source_target_pairs={{0,2},{1,3},{4,6},{5,7},{8,10},{9,11},{12,14},{13,15},{16,18},{17,... | collective-permute-start | bytes 786440 | tf_op jit(solution)/shard_map/ppermute | solution.py:206
  15.1 14.8 %collective-permute-start.13 = (f32[64,8,128]{2,1,0:T(8,128)}, f32[64,8,128]{2,1,0:T(8,128)S(1)}, u32[]{:S(2)}, u32[]{:S(2)}) collective-permute-start(f32[64,8,128]{2,1,0:T(8,128)} %get-tuple-element.17), channel_id=1, source_target_pairs={{0,16},{4,20},{1,17},{5,21},{2,18},{6,22},{3,19},{7,23}} | collective-permute-start | bytes 786440 | tf_op jit(solution)/shard_map/ppermute | solution.py:218
  16.9 13.0 %collective-permute-start.11 = (f32[64,8,128]{2,1,0:T(8,128)S(1)}, f32[64,8,128]{2,1,0:T(8,128)S(1)}, u32[]{:S(2)}, u32[]{:S(2)}) collective-permute-start(f32[64,8,128]{2,1,0:T(8,128)S(1)} %get-tuple-element.18), channel_id=1, source_target_pairs={{0,8},{4,12},{1,9},{5,13},{2,10},{6,14},{3,11},{7,15}} | collective-permute-start | bytes 786440 | tf_op jit(solution)/shard_map/ppermute | solution.py:218
  18.3 2.0 %collective-permute-start.6 = (f32[128,128]{1,0:T(8,128)S(1)}, f32[128,128]{1,0:T(8,128)S(1)}, u32[]{:S(2)}, u32[]{:S(2)}) collective-permute-start(f32[128,128]{1,0:T(8,128)S(1)} %get-tuple-element.21), channel_id=1, source_target_pairs={{4,12},{5,13},{6,14},{7,15}} | collective-permute-start | bytes 196616 | tf_op jit(solution)/shard_map/ppermute | solution.py:218
  19.0 7.0 %collective-permute-start.3 = (f32[128,128]{1,0:T(8,128)S(1)}, f32[128,128]{1,0:T(8,128)S(1)}, u32[]{:S(2)}, u32[]{:S(2)}) collective-permute-start(f32[128,128]{1,0:T(8,128)S(1)} %get-tuple-element.22), channel_id=1, source_target_pairs={{0,8},{4,12},{1,9},{5,13},{2,10},{6,14},{3,11},{7,15}} | collective-permute-start | bytes 196616 | tf_op jit(solution)/shard_map/ppermute | solution.py:218
  20.3 7.0 %collective-permute-start.7 = (f32[128,128]{1,0:T(8,128)S(1)}, f32[128,128]{1,0:T(8,128)S(1)}, u32[]{:S(2)}, u32[]{:S(2)}) collective-permute-start(f32[128,128]{1,0:T(8,128)S(1)} %broadcast_select_fusion.7), channel_id=1, source_target_pairs={{4,20},{12,28},{5,21},{13,29},{6,22},{14,30},{7,23},{15,31}} | collective-permute-start | bytes 196616 | tf_op jit(solution)/shard_map/ppermute | solution.py:218
  26.0 3.2 %collective-permute-start.4 = (f32[128,128]{1,0:T(8,128)S(1)}, f32[128,128]{1,0:T(8,128)S(1)}, u32[]{:S(2)}, u32[]{:S(2)}) collective-permute-start(f32[128,128]{1,0:T(8,128)S(1)} %broadcast_select_fusion.8), channel_id=1, source_target_pairs={{0,16},{4,20},{8,24},{12,28},{1,17},{5,21},{9,25},{13,29},{2,18},{... | collective-permute-start | bytes 196616 | tf_op jit(solution)/shard_map/ppermute | solution.py:218
  27.3 17.8 %collective-permute-start.8 = (f32[128,128]{1,0:T(8,128)S(1)}, f32[128,128]{1,0:T(8,128)S(1)}, u32[]{:S(2)}, u32[]{:S(2)}) collective-permute-start(f32[128,128]{1,0:T(8,128)S(1)} %broadcast_select_fusion.9), channel_id=1, source_target_pairs={{4,0},{12,8},{20,16},{28,24},{5,1},{13,9},{21,17},{29,25},{6,2},{1... | collective-permute-start | bytes 196616 | tf_op jit(solution)/shard_map/ppermute | solution.py:254
  29.2 10.2 %collective-permute-start.5 = (f32[128,128]{1,0:T(8,128)S(1)}, f32[128,128]{1,0:T(8,128)S(1)}, u32[]{:S(2)}, u32[]{:S(2)}) collective-permute-start(f32[128,128]{1,0:T(8,128)S(1)} %broadcast_select_fusion.10), channel_id=1, source_target_pairs={{0,4},{4,0},{8,12},{12,8},{16,20},{20,16},{24,28},{28,24},{1,5},{5... | collective-permute-start | bytes 196616 | tf_op jit(solution)/shard_map/ppermute | solution.py:225
  30.0 10.1 %collective-permute-start.14 = (f32[64,8,128]{2,1,0:T(8,128)S(1)}, f32[64,8,128]{2,1,0:T(8,128)S(1)}, u32[]{:S(2)}, u32[]{:S(2)}) collective-permute-start(f32[64,8,128]{2,1,0:T(8,128)S(1)} %get-tuple-element.15), channel_id=1, source_target_pairs={{0,8},{4,12},{16,24},{20,28},{1,9},{5,13},{17,25},{21,29},{2,10},{... | collective-permute-start | bytes 786440 | tf_op jit(solution)/shard_map/ppermute | solution.py:218
  34.4 25.6 %collective-permute-start.10 = (f32[4,128,128]{2,1,0:T(8,128)S(1)}, f32[4,128,128]{2,1,0:T(8,128)}, u32[]{:S(2)}, u32[]{:S(2)}) collective-permute-start(f32[4,128,128]{2,1,0:T(8,128)S(1)} %broadcast_select_fusion.4), channel_id=1, source_target_pairs={{0,1},{1,0},{2,3},{3,2},{4,5},{5,4},{6,7},{7,6},{8,9},{9,8},{10,11... | collective-permute-start | bytes 786440 | tf_op jit(solution)/shard_map/ppermute | solution.py:209
  35.6 9.3 %collective-permute-start.12 = (f32[64,8,128]{2,1,0:T(8,128)S(1)}, f32[64,8,128]{2,1,0:T(8,128)S(1)}, u32[]{:S(2)}, u32[]{:S(2)}) collective-permute-start(f32[64,8,128]{2,1,0:T(8,128)S(1)} %get-tuple-element.16), channel_id=1, source_target_pairs={{0,16},{4,20},{8,24},{12,28},{1,17},{5,21},{9,25},{13,29},{2,18},{... | collective-permute-start | bytes 786440 | tf_op jit(solution)/shard_map/ppermute | solution.py:218
  40.1 20.9 %collective-permute-start.16 = (f32[64,8,128]{2,1,0:T(8,128)S(1)}, f32[64,8,128]{2,1,0:T(8,128)S(1)}, u32[]{:S(2)}, u32[]{:S(2)}) collective-permute-start(f32[64,8,128]{2,1,0:T(8,128)S(1)} %broadcast_select_fusion.hb_ref), channel_id=1, source_target_pairs={{0,4},{4,0},{8,12},{12,8},{16,20},{20,16},{24,28},{28,24},{1,5},{5... | collective-permute-start | bytes 786440 | tf_op jit(solution)/shard_map/ppermute | solution.py:225
  45.0 16.1 %collective-permute-start.15 = (f32[64,8,128]{2,1,0:T(8,128)S(1)}, f32[64,8,128]{2,1,0:T(8,128)S(1)}, u32[]{:S(2)}, u32[]{:S(2)}) collective-permute-start(f32[64,8,128]{2,1,0:T(8,128)S(1)} %broadcast_select_fusion.3.ha_ref), channel_id=1, source_target_pairs={{0,4},{4,0},{8,12},{12,8},{16,20},{20,16},{24,28},{28,24},{1,5},{5... | collective-permute-start | bytes 786440 | tf_op jit(solution)/shard_map/ppermute | solution.py:225
  61.1 1.0 %copy-start.1 = (f32[256,256]{1,0:T(8,128)S(1)}, f32[256,256]{1,0:T(8,128)}, u32[]{:S(2)}) copy-start(f32[256,256]{1,0:T(8,128)} %get-tuple-element.13.w_ref) | copy-start | bytes 786436
  62.0 0.9 %copy-start.2 = (f32[256,256]{1,0:T(8,128)S(1)}, f32[256,256]{1,0:T(8,128)}, u32[]{:S(2)}) copy-start(f32[256,256]{1,0:T(8,128)} %get-tuple-element.14.mixed_ref) | copy-start | bytes 786436
  63.0 0.8 %copy-start.3 = (f32[128,128]{1,0:T(8,128)S(1)}, f32[128,128]{1,0:T(8,128)}, u32[]{:S(2)}) copy-start(f32[128,128]{1,0:T(8,128)} %get-tuple-element.10.f0_ref) | copy-start | bytes 196612
  63.8 0.8 %copy-start.4 = (f32[128,128]{1,0:T(8,128)S(1)}, f32[128,128]{1,0:T(8,128)}, u32[]{:S(2)}) copy-start(f32[128,128]{1,0:T(8,128)} %get-tuple-element.12.f1_ref) | copy-start | bytes 196612

commit v3 on v0

v3 whole, which is shorter than its diff:
```python
import jax
import jax.numpy as jnp
from jax import lax
from jax.experimental import pallas as pl
from jax.experimental.pallas import tpu as pltpu
from jax.sharding import PartitionSpec as P

EXACT = lax.Precision.HIGHEST
SUB = 8
MIB = 1024 * 1024
VMEM = pl.BlockSpec(memory_space=pltpu.VMEM)
HBM = pl.BlockSpec(memory_space=pltpu.HBM)


def dot(a, b):
    return lax.dot_general(a, b, (((1,), (0,)), ((), ())), precision=EXACT, preferred_element_type=jnp.float32)


def dot_t(a, b):
    return lax.dot_general(a, b, (((1,), (1,)), ((), ())), precision=EXACT, preferred_element_type=jnp.float32)


def inverse_of(p):
    r = pl.reciprocal(p, approx=True)
    r = r * (2.0 - p * r)
    return r * (2.0 - p * r)


def eliminate(s, sym, aug):
    n = s.shape[0]
    groups = n // SUB
    sub = lax.broadcasted_iota(jnp.int32, (SUB, n), 0)
    lane = lax.broadcasted_iota(jnp.int32, (SUB, n), 1)
    sym[...] = s.reshape(groups, SUB, n)
    rows = lax.broadcasted_iota(jnp.int32, (n, n), 0)
    cols = lax.broadcasted_iota(jnp.int32, (n, n), 1)
    aug[...] = jnp.where(rows == cols, 1.0, 0.0).reshape(groups, SUB, n)
    for g in range(groups):
        start = g * SUB
        left = groups - g
        rest = sym[g:]
        top = sym[g]
        top_aug = aug[g]
        spread = [jnp.broadcast_to(rest[:, :, start + j:start + j + 1], (left, SUB, n)) for j in range(SUB)]
        scaled = []
        scaled_aug = []
        roots = jnp.zeros((SUB, n), jnp.float32)
        for k in range(SUB):
            pivot = jnp.broadcast_to(spread[k][0, k:k + 1, :], (SUB, n))
            recip = inverse_of(pivot)
            roots = jnp.where(sub == k, pivot, roots)
            for j in range(k + 1, SUB):
                factor = jnp.broadcast_to(spread[k][0, j:j + 1, :], (SUB, n)) * recip
                spread[j] = spread[j] - spread[k] * factor[None]
            row = jnp.broadcast_to(top[k:k + 1, :], (SUB, n)) * recip
            row_aug = jnp.broadcast_to(top_aug[k:k + 1, :], (SUB, n)) * recip
            scaled.append(row)
            scaled_aug.append(row_aug)
            if k + 1 < SUB:
                below = jnp.where(sub > k, spread[k][0], 0.0)
                top = top - below * row
                top_aug = top_aug - below * row_aug
        root = lax.rsqrt(roots)
        sym[g] = jnp.where(lane >= start + sub, top * root, 0.0)
        aug[g] = top_aug * root
        if left > 1:
            low = rest[1:]
            low_aug = aug[g + 1:]
            for k in range(SUB):
                low = low - spread[k][1:] * scaled[k][None]
                low_aug = low_aug - spread[k][1:] * scaled_aug[k][None]
            sym[g + 1:] = low
            aug[g + 1:] = low_aug
    upper = sym[...].reshape(n, n)
    return upper.T, aug[...].reshape(n, n)


def joined(mine_ref, other_ref, odd):
    mine, other = mine_ref[...], other_ref[...]
    return jnp.concatenate([jnp.where(odd, other, mine), jnp.where(odd, mine, other)], axis=0)


def is_odd_row():
    return lax.rem(lax.axis_index("row"), 2) == 1


def estimate(flops, nbytes):
    return pl.CostEstimate(flops=flops, bytes_accessed=nbytes, transcendentals=0)


def corner_kernel(matrix_ref, own_ref, send_ref, sems):
    half = own_ref.shape[0]
    odd = lax.rem(lax.axis_index("row"), 2)
    own = pltpu.make_async_copy(matrix_ref.at[0, pl.ds(odd * half, half), 0, :], own_ref, sems.at[0])
    send = pltpu.make_async_copy(matrix_ref.at[0, pl.ds((1 - odd) * half, half), 0, :], send_ref, sems.at[1])
    send.start()
    own.start()
    send.wait()
    own.wait()


def corner_halves(matrix):
    n = matrix.shape[1]
    half = jax.ShapeDtypeStruct((n // 2, n), jnp.float32)
    return pl.pallas_call(
        corner_kernel,
        out_shape=[half, half],
        in_specs=[HBM],
        out_specs=[VMEM, VMEM],
        scratch_shapes=[pltpu.SemaphoreType.DMA((2,))],
        compiler_params=pltpu.CompilerParams(vmem_limit_bytes=2 * MIB),
        cost_estimate=estimate(0, 3 * MIB),
        name="corner_halves",
    )(matrix)


def panels_kernel(matrix_ref, column_ref, upper_ref, lower_ref, sems):
    local_cols, half, _ = upper_ref.shape
    copies = [pltpu.make_async_copy(matrix_ref.at[:, :, 0, :], column_ref, sems.at[0])]
    for j in range(local_cols):
        copies.append(pltpu.make_async_copy(matrix_ref.at[0, pl.ds(0, half), j, :], upper_ref.at[j], sems.at[1 + j]))
        copies.append(pltpu.make_async_copy(
            matrix_ref.at[0, pl.ds(half, half), j, :], lower_ref.at[j], sems.at[1 + local_cols + j]))
    for copy in copies:
        copy.start()
    for copy in copies:
        copy.wait()


def panels(matrix):
    local_rows, n, local_cols, _ = matrix.shape
    strip = jax.ShapeDtypeStruct((local_cols, n // 2, n), jnp.float32)
    return pl.pallas_call(
        panels_kernel,
        out_shape=[jax.ShapeDtypeStruct((local_rows, n, n), jnp.float32), strip, strip],
        in_specs=[HBM],
        out_specs=[VMEM] * 3,
        scratch_shapes=[pltpu.SemaphoreType.DMA((1 + 2 * local_cols,))],
        compiler_params=pltpu.CompilerParams(vmem_limit_bytes=4 * MIB),
        cost_estimate=estimate(0, 4 * MIB),
        name="panels",
    )(matrix)


def first_factor_kernel(mine_ref, other_ref, f_ref, w_ref, sym, aug):
    f_ref[...], w_ref[...] = eliminate(joined(mine_ref, other_ref, is_odd_row()), sym, aug)


def first_factor(mine, other):
    n = mine.shape[1]
    square = jax.ShapeDtypeStruct((n, n), jnp.float32)
    return pl.pallas_call(
        first_factor_kernel,
        out_shape=[square, square],
        in_specs=[VMEM, VMEM],
        out_specs=[VMEM, VMEM],
        scratch_shapes=[pltpu.VMEM((n // SUB, SUB, n), jnp.float32)] * 2,
        compiler_params=pltpu.CompilerParams(vmem_limit_bytes=4 * MIB),
        cost_estimate=estimate(8 * 10**9, 2 * MIB),
        name="first_factor",
    )(mine, other)


def second_factor_kernel(low_mine_ref, low_other_ref, mine_ref, other_ref, w0_ref, matrix_ref, f_ref, w_ref, mixed_ref,
                         blocks_ref, sym, aug, sems):
    n = w0_ref.shape[0]
    local_cols = matrix_ref.shape[2]
    copies = [pltpu.make_async_copy(matrix_ref.at[:, :, j, :], blocks_ref.at[j], sems.at[j]) for j in range(local_cols)]
    for copy in copies:
        copy.start()
    odd = is_odd_row()
    w0 = w0_ref[...]
    cross = dot_t(joined(low_mine_ref, low_other_ref, odd), w0)
    f1, w1 = eliminate(joined(mine_ref, other_ref, odd) - dot_t(cross, cross), sym, aug)
    f_ref[...] = f1
    w10 = -dot(w1, dot(cross, w0))
    zero = jnp.zeros((n, n), jnp.float32)
    w_ref[:n, :n] = w0
    w_ref[:n, n:] = zero
    w_ref[n:, :n] = w10
    w_ref[n:, n:] = w1
    mixed_ref[:n, :n] = jnp.where(odd, zero, w0)
    mixed_ref[:n, n:] = jnp.where(odd, w0, zero)
    mixed_ref[n:, :n] = jnp.where(odd, w1, w10)
    mixed_ref[n:, n:] = jnp.where(odd, w10, w1)
    for copy in copies:
        copy.wait()


def second_factor(low_mine, low_other, mine, other, w0, matrix):
    local_rows, n, local_cols, _ = matrix.shape
    square = jax.ShapeDtypeStruct((n, n), jnp.float32)
    double = jax.ShapeDtypeStruct((2 * n, 2 * n), jnp.float32)
    blocks = jax.ShapeDtypeStruct((local_cols, local_rows, n, n), jnp.float32)
    return pl.pallas_call(
        second_factor_kernel,
        out_shape=[square, double, double, blocks],
        in_specs=[VMEM] * 5 + [HBM],
        out_specs=[VMEM] * 4,
        scratch_shapes=[pltpu.VMEM((n // SUB, SUB, n), jnp.float32)] * 2 + [pltpu.SemaphoreType.DMA((local_cols,))],
        compiler_params=pltpu.CompilerParams(vmem_limit_bytes=12 * MIB),
        cost_estimate=estimate(8 * 10**9, 4 * MIB),
        name="second_factor",
    )(low_mine, low_other, mine, other, w0, matrix)


def settle_kernel(f0_ref, f1_ref, w_ref, mixed_ref, rows_ref, rows_other_ref, ha_ref, hb_ref, oa_ref, ob_ref, blocks_ref,
                  out_ref, result, sems):
    grid_row = lax.axis_index("row")
    grid_col = lax.axis_index("col")
    n = f0_ref.shape[0]
    local_cols, local_rows, _, _ = blocks_ref.shape
    flat = local_rows * n
    own = rows_ref[...].reshape(flat, n)
    other = rows_other_ref[...].reshape(flat, n)
    swapped = lax.rem(grid_col, 2) == 1
    rows = jnp.concatenate([jnp.where(swapped, other, own), jnp.where(swapped, own, other)], axis=1)
    solved = dot_t(rows, w_ref[...])
    mixed = mixed_ref[...]
    copies = []
    for j in range(0, local_cols, 2):
        pair = (j, j + 1)
        stacked = jnp.concatenate(
            [jnp.concatenate([ha_ref[b], hb_ref[b], oa_ref[b], ob_ref[b]], axis=0) for b in pair], axis=1)
        update = dot(solved, dot(mixed, stacked))
        for b in pair:
            part = update[:, (b - j) * n:(b - j + 1) * n].reshape(local_rows, n, n)
            result[b] = blocks_ref[b] - part
        if j == 0:
            @pl.when(grid_col == 0)
            def _():
                result[0] = solved[:, :n].reshape(local_rows, n, n)

            @pl.when(grid_col == 1)
            def _():
                result[0] = solved[:, n:].reshape(local_rows, n, n)

        @pl.when(grid_row <= 1)
        def _():
            for b in pair:
                if b > 0:
                    result[b, 0] = jnp.zeros((n, n), jnp.float32)
            if j == 0:
                @pl.when(grid_col > grid_row)
                def _():
                    result[0, 0] = jnp.zeros((n, n), jnp.float32)

                @pl.when((grid_row == 0) & (grid_col == 0))
                def _():
                    result[0, 0] = f0_ref[...]

                @pl.when((grid_row == 1) & (grid_col == 1))
                def _():
                    result[0, 0] = f1_ref[...]
        for b in pair:
            copy = pltpu.make_async_copy(result.at[b], out_ref.at[:, :, b, :], sems.at[b])
            copy.start()
            copies.append(copy)
    for copy in copies:
        copy.wait()


def settle(f0, f1, w, mixed, rows, rows_other, ha, hb, oa, ob, blocks):
    local_cols, local_rows, n, _ = blocks.shape
    return pl.pallas_call(
        settle_kernel,
        out_shape=jax.ShapeDtypeStruct((local_rows, n, local_cols, n), jnp.float32),
        in_specs=[VMEM] * 11,
        out_specs=HBM,
        scratch_shapes=[pltpu.VMEM(blocks.shape, jnp.float32), pltpu.SemaphoreType.DMA((local_cols,))],
        compiler_params=pltpu.CompilerParams(vmem_limit_bytes=32 * MIB),
        cost_estimate=estimate(4 * 10**9, 6 * MIB),
        name="settle",
    )(f0, f1, w, mixed, rows, rows_other, ha, hb, oa, ob, blocks)


def exchange(value, axis, mask, size):
    return lax.ppermute(value, axis, [(i, i ^ mask) for i in range(size)])


def bit_set(index, bit):
    return ((index >> bit) & 1) == 1


def spread(own, axis, index, size, bits):
    held = own
    for bit in bits:
        held = jnp.where(bit_set(index, bit), exchange(held, axis, 1 << bit, size), held)
    return held


def spread_pairs(own, axis, index, size, bits):
    held = own
    for at in range(0, len(bits) - 1, 2):
        low, high = bits[at], bits[at + 1]
        from_low = exchange(held, axis, 1 << low, size)
        from_high = exchange(held, axis, 1 << high, size)
        from_both = exchange(held, axis, (1 << low) | (1 << high), size)
        has_low, has_high = bit_set(index, low), bit_set(index, high)
        held = jnp.where(has_low & has_high, from_both, jnp.where(has_low, from_low, jnp.where(has_high, from_high, held)))
    if len(bits) % 2:
        held = spread(held, axis, index, size, bits[-1:])
    return held


def shards(kernel):
    grid_row = lax.axis_index("row")
    grid_col = lax.axis_index("col")
    n_row = lax.axis_size("row")
    n_col = lax.axis_size("col")
    row_bits = list(range(1, n_row.bit_length() - 1))
    col_bits = list(range(1, n_col.bit_length() - 1))
    odd = (grid_row % 2) == 1
    right = (grid_col % 2) == 1

    own, send = corner_halves(kernel)
    got = exchange(send, "row", 1, n_row)
    diag = jnp.where(odd != right, got, own)
    low = jnp.where(odd, own, got)
    diag = spread_pairs(diag, "row", grid_row, n_row, row_bits)
    low = spread_pairs(low, "row", grid_row, n_row, row_bits)
    column, upper, lower = panels(kernel)

    diag = spread(diag, "col", grid_col, n_col, col_bits)
    diag_other = exchange(diag, "col", 1, n_col)
    first = jnp.where(right, diag_other, diag)
    second = jnp.where(right, diag, diag_other)
    first_far = exchange(first, "row", 1, n_row)
    low = spread(low, "col", grid_col, n_col, col_bits + [0])
    second_far = exchange(second, "row", 1, n_row)
    low_far = exchange(low, "row", 1, n_row)

    ha = spread(upper, "row", grid_row, n_row, row_bits)
    hb = spread(lower, "row", grid_row, n_row, row_bits[::-1])
    rows = spread(column, "col", grid_col, n_col, col_bits)

    f0, w0 = first_factor(first, first_far)
    oa = exchange(ha, "row", 1, n_row)
    ob = exchange(hb, "row", 1, n_row)
    rows_other = exchange(rows, "col", 1, n_col)
    f1, w, mixed, blocks = second_factor(low, low_far, second, second_far, w0, kernel)
    return settle(f0, f1, w, mixed, rows, rows_other, ha, hb, oa, ob, blocks)


def solution(mesh):
    in_specs = (P(None, "row", None, "col"),)
    out_specs = P(None, "row", None, "col")
    return jax.shard_map(shards, mesh=mesh, in_specs=in_specs, out_specs=out_specs, check_vma=False)
```

time: 318 us -> 60.7 us (0.19)
  waiting for transfers between devices: 235 us -> 13.2 us
  other arithmetic: 50.6 us -> 0.2 us
  starting transfers between devices: 0.39 us -> 24.6 us
  Pallas kernels: 0 us -> 20.5 us
  between operations: 13.7 us -> 0.33 us
  matrix products: 8.95 us -> 0 us
  local copies, waits for them, and re-layouts: 9.29 us -> 1.59 us
    psum x4 -> x0, waiting for transfers between devices: 178 us -> none  [from_root(): return lax.psum(kept, axis)]
    all_gather x2 -> x0, waiting for transfers between devices: 56.5 us -> none  [mirror(): whole = lax.all_gather(rows_part, 'row', axis=1, tiled=True)]
    another operation x10 -> x0, other arithmetic: 45.8 us -> none  [the longest x6 24.8 us: solve_panel(): factor = jnp.linalg.cholesky(diagonal)]
    ppermute x0 -> x22, starting transfers between devices: none -> 24.6 us  [exchange(): return lax.ppermute(value, axis, [(i, i ^ mask) for i in range(size)])]
    pallas_call x0 -> x5, Pallas kernels: none -> 20.5 us  [the longest x1 7.5 us: second_factor(): pl.pallas_call(second_factor_kernel, out_shape=[square, double, double, b...]
    ppermute x0 -> x22, waiting for transfers between devices: none -> 13.2 us  [exchange(): return lax.ppermute(value, axis, [(i, i ^ mask) for i in range(size)])]
    dot_general x2 -> x0, matrix products: 8.13 us -> none  [trailing(): jnp.einsum('rib,cjb->ricj', row_panel, col_panel, precision=lax.Precision...]
    psum x4 -> x0, local copies, waits for them, and re-layouts: 4.01 us -> none  [from_root(): return lax.psum(kept, axis)]
  transfers between devices with their start and end apart: 6 -> 22, of which waited for: 6 -> 9; matrix products, arithmetic and copies ran while one was open for 1% -> 0% of each run, Pallas kernels for 0% -> 22%
where the time goes in v3:
time: 60.7 us; the launch traced here: 60.5 us
  starting transfers between devices  24.6 us (41%)
  Pallas kernels  20.5 us (34%)
  waiting for transfers between devices  13.2 us (22%)
  local copies, waits for them, and re-layouts  1.59 us (3%)
    ppermute x22, starting transfers between devices, exchange(): return lax.ppermute(value, axis, [(i, i ^ mask) for i in range(size)])  24.6 us
    ppermute x22, waiting for transfers between devices, exchange(): return lax.ppermute(value, axis, [(i, i ^ mask) for i in range(size)])  13.2 us
    pallas_call x1, Pallas kernels, second_factor(): pl.pallas_call(second_factor_kernel, out_shape=[square, double, double, b...  7.5 us
    pallas_call x1, Pallas kernels, settle(): pl.pallas_call(settle_kernel, out_shape=jax.ShapeDtypeStruct((local_rows,...  7.07 us
    pallas_call x1, Pallas kernels, first_factor(): pl.pallas_call(first_factor_kernel, out_shape=[square, square], in_specs=...  5.17 us
    unnamed x4, local copies, waits for them, and re-layouts  1.59 us
  transfers between devices with their start and end apart: 22, of which 9 were waited for; matrix products, arithmetic and copies ran while one was open for 0% of the time, Pallas kernels for 22%

profile of v3, /device:TPU:0, one launch (start us, length us, event | category | flops | bytes accessed | tf_op | source)
XLA Modules:
  0.0 60.5 jit_solution(15375357930889445067)
XLA Ops:
  0.0 1.6 %copy-done = f32[4,128,8,128]{3,2,1,0:T(8,128)S(1)} copy-done((f32[4,128,8,128]{3,2,1,0:T(8,128)S(1)}, f32[4,128,8,128]{3,2,1,0:T(8,128)}, u32[]{:S(2)}) %copy-start) | copy-done | bytes 2097176
  1.6 0.1 corner_halves.1
  1.7 0.5 collective-permute-start
  2.2 0.9 %collective-permute-done = f32[64,128]{1,0:T(8,128)S(1)} collective-permute-done((f32[64,128]{1,0:T(8,128)S(1)}, f32[64,128]{1,0:T(8,128)S(1)}, u32[]{:S(2)}, u32[]{:S(2)}) %collective-permute-start) | collective-permute-done | bytes 32800 | tf_op jit(solution)/shard_map/ppermute | solution.py:278
  3.1 2.9 %collective-permute-start.3 = (f32[64,128]{1,0:T(8,128)S(1)}, f32[64,128]{1,0:T(8,128)S(1)}, u32[]{:S(2)}, u32[]{:S(2)}) collective-permute-start(f32[64,128]{1,0:T(8,128)S(1)} %get-tuple-element.30), channel_id=1, source_target_pairs={{0,16},{4,20},{8,24},{12,28},{16,0},{20,4},{24,8},{28,12},{1,17},{... | collective-permute-start | bytes 98312 | tf_op jit(solution)/shard_map/ppermute | solution.py:278
  6.0 1.5 %collective-permute-start.2 = (f32[64,128]{1,0:T(8,128)S(1)}, f32[64,128]{1,0:T(8,128)S(1)}, u32[]{:S(2)}, u32[]{:S(2)}) collective-permute-start(f32[64,128]{1,0:T(8,128)S(1)} %get-tuple-element.30), channel_id=1, source_target_pairs={{0,8},{4,12},{8,0},{12,4},{16,24},{20,28},{24,16},{28,20},{1,9},{5... | collective-permute-start | bytes 98312 | tf_op jit(solution)/shard_map/ppermute | solution.py:278
  7.5 0.0 collective-permute-start.1
  7.5 0.7 %panels.1 = (f32[4,128,128]{2,1,0:T(8,128)S(1)}, f32[8,64,128]{2,1,0:T(8,128)S(1)}, f32[8,64,128]{2,1,0:T(8,128)S(1)}) custom-call(f32[4,128,8,128]{3,2,1,0:T(8,128)S(1)} %copy-done.1), custom_call_target="tpu_custom_call" | custom-call | bytes 4194304 | tf_op jit(solution)/shard_map/panels/pallas_call | solution.py:133
  8.3 3.1 %collective-permute-start.14 = (f32[4,128,128]{2,1,0:T(8,128)S(1)}, f32[4,128,128]{2,1,0:T(8,128)S(1)}, u32[]{:S(2)}, u32[]{:S(2)}) collective-permute-start(f32[4,128,128]{2,1,0:T(8,128)S(1)} %get-tuple-element.23), channel_id=1, source_target_pairs={{0,2},{1,3},{2,0},{3,1},{4,6},{5,7},{6,4},{7,5},{8,10},{9,11},{10,... | collective-permute-start | bytes 786440 | tf_op jit(solution)/shard_map/ppermute | solution.py:278
  11.4 1.5 %collective-permute-start.16 = (f32[8,64,128]{2,1,0:T(8,128)S(1)}, f32[8,64,128]{2,1,0:T(8,128)S(1)}, u32[]{:S(2)}, u32[]{:S(2)}) collective-permute-start(f32[8,64,128]{2,1,0:T(8,128)S(1)} %get-tuple-element.24), channel_id=1, source_target_pairs={{0,8},{4,12},{8,0},{12,4},{16,24},{20,28},{24,16},{28,20},{1,9},{5... | collective-permute-start | bytes 786440 | tf_op jit(solution)/shard_map/ppermute | solution.py:278
  12.8 0.0 collective-permute-done.3
  12.8 1.5 %collective-permute-start.9 = (f32[64,128]{1,0:T(8,128)S(1)}, f32[64,128]{1,0:T(8,128)S(1)}, u32[]{:S(2)}, u32[]{:S(2)}) collective-permute-start(f32[64,128]{1,0:T(8,128)S(1)} %get-tuple-element.29), channel_id=1, source_target_pairs={{0,16},{4,20},{8,24},{12,28},{16,0},{20,4},{24,8},{28,12},{1,17},{... | collective-permute-start | bytes 98312 | tf_op jit(solution)/shard_map/ppermute | solution.py:278
  14.4 0.0 collective-permute-done.2
  14.4 0.5 collective-permute-start.8
  14.9 0.0 collective-permute-done.1
  14.9 1.4 %collective-permute-start.7 = (f32[64,128]{1,0:T(8,128)S(1)}, f32[64,128]{1,0:T(8,128)S(1)}, u32[]{:S(2)}, u32[]{:S(2)}) collective-permute-start(f32[64,128]{1,0:T(8,128)S(1)} %get-tuple-element.29), channel_id=1, source_target_pairs={{0,24},{4,28},{8,16},{12,20},{16,8},{20,12},{24,0},{28,4},{1,25},{... | collective-permute-start | bytes 98312 | tf_op jit(solution)/shard_map/ppermute | solution.py:278
  16.4 0.4 collective-permute-done.9
  16.8 1.5 %collective-permute-start.18 = (f32[8,64,128]{2,1,0:T(8,128)S(1)}, f32[8,64,128]{2,1,0:T(8,128)S(1)}, u32[]{:S(2)}, u32[]{:S(2)}) collective-permute-start(f32[8,64,128]{2,1,0:T(8,128)S(1)} %get-tuple-element.25), channel_id=1, source_target_pairs={{0,16},{4,20},{8,24},{12,28},{16,0},{20,4},{24,8},{28,12},{1,17},{... | collective-permute-start | bytes 786440 | tf_op jit(solution)/shard_map/ppermute | solution.py:278
  18.3 1.3 %collective-permute-done.8 = f32[64,128]{1,0:T(8,128)S(1)} collective-permute-done((f32[64,128]{1,0:T(8,128)S(1)}, f32[64,128]{1,0:T(8,128)S(1)}, u32[]{:S(2)}, u32[]{:S(2)}) %collective-permute-start.8) | collective-permute-done | bytes 32800 | tf_op jit(solution)/shard_map/ppermute | solution.py:278
  19.6 0.7 %collective-permute-start.4 = (f32[64,128]{1,0:T(8,128)S(1)}, f32[64,128]{1,0:T(8,128)S(1)}, u32[]{:S(2)}, u32[]{:S(2)}) collective-permute-start(f32[64,128]{1,0:T(8,128)S(1)} %select_select_fusion.1), channel_id=1, source_target_pairs={{0,2},{1,3},{2,0},{3,1},{4,6},{5,7},{6,4},{7,5},{8,10},{9,11},{10,... | collective-permute-start | bytes 98312 | tf_op jit(solution)/shard_map/ppermute | solution.py:278
  20.3 0.7 %collective-permute-done.7 = f32[64,128]{1,0:T(8,128)S(1)} collective-permute-done((f32[64,128]{1,0:T(8,128)S(1)}, f32[64,128]{1,0:T(8,128)S(1)}, u32[]{:S(2)}, u32[]{:S(2)}) %collective-permute-start.7) | collective-permute-done | bytes 32800 | tf_op jit(solution)/shard_map/ppermute | solution.py:278
  21.0 1.6 %collective-permute-start.10 = (f32[64,128]{1,0:T(8,128)S(1)}, f32[64,128]{1,0:T(8,128)S(1)}, u32[]{:S(2)}, u32[]{:S(2)}) collective-permute-start(f32[64,128]{1,0:T(8,128)S(1)} %select_select_fusion), channel_id=1, source_target_pairs={{0,2},{1,3},{2,0},{3,1},{4,6},{5,7},{6,4},{7,5},{8,10},{9,11},{10,... | collective-permute-start | bytes 98312 | tf_op jit(solution)/shard_map/ppermute | solution.py:278
  22.6 1.9 %collective-permute-done.4 = f32[64,128]{1,0:T(8,128)S(1)} collective-permute-done((f32[64,128]{1,0:T(8,128)S(1)}, f32[64,128]{1,0:T(8,128)S(1)}, u32[]{:S(2)}, u32[]{:S(2)}) %collective-permute-start.4) | collective-permute-done | bytes 32800 | tf_op jit(solution)/shard_map/ppermute | solution.py:278
  24.5 1.5 %collective-permute-start.5 = (f32[64,128]{1,0:T(8,128)S(1)}, f32[64,128]{1,0:T(8,128)S(1)}, u32[]{:S(2)}, u32[]{:S(2)}) collective-permute-start(f32[64,128]{1,0:T(8,128)S(1)} %broadcast_select_fusion.9), channel_id=1, source_target_pairs={{0,1},{1,0},{2,3},{3,2},{4,5},{5,4},{6,7},{7,6},{8,9},{9,8},{10,11... | collective-permute-start | bytes 98312 | tf_op jit(solution)/shard_map/ppermute | solution.py:278
  26.0 0.0 collective-permute-done.10
  26.0 1.5 %collective-permute-start.11 = (f32[64,128]{1,0:T(8,128)S(1)}, f32[64,128]{1,0:T(8,128)S(1)}, u32[]{:S(2)}, u32[]{:S(2)}) collective-permute-start(f32[64,128]{1,0:T(8,128)S(1)} %broadcast_select_fusion.8), channel_id=1, source_target_pairs={{0,1},{1,0},{2,3},{3,2},{4,5},{5,4},{6,7},{7,6},{8,9},{9,8},{10,11... | collective-permute-start | bytes 98312 | tf_op jit(solution)/shard_map/ppermute | solution.py:278
  27.5 0.9 %collective-permute-done.5 = f32[64,128]{1,0:T(8,128)S(1)} collective-permute-done((f32[64,128]{1,0:T(8,128)S(1)}, f32[64,128]{1,0:T(8,128)S(1)}, u32[]{:S(2)}, u32[]{:S(2)}) %collective-permute-start.5) | collective-permute-done | bytes 32800 | tf_op jit(solution)/shard_map/ppermute | solution.py:278
  28.4 0.1 collective-permute-start.6
  28.5 1.5 %collective-permute-done.11 = f32[64,128]{1,0:T(8,128)S(1)} collective-permute-done((f32[64,128]{1,0:T(8,128)S(1)}, f32[64,128]{1,0:T(8,128)S(1)}, u32[]{:S(2)}, u32[]{:S(2)}) %collective-permute-start.11) | collective-permute-done | bytes 32800 | tf_op jit(solution)/shard_map/ppermute | solution.py:278
  30.0 0.0 collective-permute-start.12
  30.0 0.0 collective-permute-done.6.other_ref
  30.0 0.5 collective-permute-start.13
  30.5 5.2 %first_factor.1 = (f32[128,128]{1,0:T(8,128)S(1)}, f32[128,128]{1,0:T(8,128)S(1)}) custom-call(f32[64,128]{1,0:T(8,128)S(1)} %get-tuple-element.28.mine_ref, f32[64,128]{1,0:T(8,128)S(1)} %collective-permute-done.6.other_ref), custom_call_target="tpu_custom_call" | custom-call | flops 8000000000 | bytes 2097152 | tf_op jit(solution)/shard_map/first_factor/pallas_call | solution.py:152
  35.7 0.0 collective-permute-done.16
  35.8 1.7 %collective-permute-start.17 = (f32[8,64,128]{2,1,0:T(8,128)S(1)}, f32[8,64,128]{2,1,0:T(8,128)S(1)}, u32[]{:S(2)}, u32[]{:S(2)}) collective-permute-start(f32[8,64,128]{2,1,0:T(8,128)S(1)} %broadcast_select_fusion.1), channel_id=1, source_target_pairs={{0,16},{4,20},{8,24},{12,28},{16,0},{20,4},{24,8},{28,12},{1,17},{... | collective-permute-start | bytes 786440 | tf_op jit(solution)/shard_map/ppermute | solution.py:278
  37.4 0.0 collective-permute-done.18
  37.5 1.5 %collective-permute-start.19 = (f32[8,64,128]{2,1,0:T(8,128)S(1)}, f32[8,64,128]{2,1,0:T(8,128)S(1)}, u32[]{:S(2)}, u32[]{:S(2)}) collective-permute-start(f32[8,64,128]{2,1,0:T(8,128)S(1)} %broadcast_select_fusion.2), channel_id=1, source_target_pairs={{0,8},{4,12},{8,0},{12,4},{16,24},{20,28},{24,16},{28,20},{1,9},{5... | collective-permute-start | bytes 786440 | tf_op jit(solution)/shard_map/ppermute | solution.py:278
  38.9 0.0 collective-permute-done.14
  39.0 0.9 %collective-permute-start.15 = (f32[4,128,128]{2,1,0:T(8,128)S(1)}, f32[4,128,128]{2,1,0:T(8,128)S(1)}, u32[]{:S(2)}, u32[]{:S(2)}) collective-permute-start(f32[4,128,128]{2,1,0:T(8,128)S(1)} %broadcast_select_fusion.4.rows_ref), channel_id=1, source_target_pairs={{0,1},{1,0},{2,3},{3,2},{4,5},{5,4},{6,7},{7,6},{8,9},{9,8},{10,11... | collective-permute-start | bytes 786440 | tf_op jit(solution)/shard_map/ppermute | solution.py:278
  39.9 4.2 %collective-permute-done.17 = f32[8,64,128]{2,1,0:T(8,128)S(1)} collective-permute-done((f32[8,64,128]{2,1,0:T(8,128)S(1)}, f32[8,64,128]{2,1,0:T(8,128)S(1)}, u32[]{:S(2)}, u32[]{:S(2)}) %collective-permute-start.17) | collective-permute-done | bytes 262176 | tf_op jit(solution)/shard_map/ppermute | solution.py:278
  44.1 0.1 collective-permute-start.20
  44.2 1.3 %collective-permute-done.19 = f32[8,64,128]{2,1,0:T(8,128)S(1)} collective-permute-done((f32[8,64,128]{2,1,0:T(8,128)S(1)}, f32[8,64,128]{2,1,0:T(8,128)S(1)}, u32[]{:S(2)}, u32[]{:S(2)}) %collective-permute-start.19) | collective-permute-done | bytes 262176 | tf_op jit(solution)/shard_map/ppermute | solution.py:278
  45.6 0.1 collective-permute-start.21
  45.7 0.0 collective-permute-done.13.other_ref
  45.7 7.5 %second_factor.1 = (f32[128,128]{1,0:T(8,128)S(1)}, f32[256,256]{1,0:T(8,128)S(1)}, f32[256,256]{1,0:T(8,128)S(1)}, f32[8,4,128,128]{3,2,1,0:T(8,128)S(1)}) custom-call(f32[64,128]{1,0:T(8,128)S(1)} %broadcast_select_fusion.6.low_mine_ref, f32[64,128]{1,0:T(8,128)S(1)} %collective-permute-done.12.low_other_ref, f32[64,128]{1,0:T(8,128)S(1)} %get-tuple-element.27.mine_ref, ...), custom_call_target="tpu_custom_call" | custom-call | flops 8000000000 | bytes 4194304 | tf_op jit(solution)/shard_map/second_factor/pallas_call | solution.py:195
  53.2 0.0 collective-permute-done.20.oa_ref
  53.2 0.0 collective-permute-done.21.ob_ref
  53.2 7.1 %settle.1 = f32[4,128,8,128]{3,2,1,0:T(8,128)} custom-call(f32[128,128]{1,0:T(8,128)S(1)} %get-tuple-element.18.f0_ref, f32[128,128]{1,0:T(8,128)S(1)} %get-tuple-element.20.f1_ref, f32[256,256]{1,0:T(8,128)S(1)} %get-tuple-element.21.w_ref, f32[256,256]{1,0:T(8,128)S(1)} %get-tuple-element.22.mixed_ref, f32[4,128,128]{2,1,0:T(8,128)S(1)} %broadcast_select_fusion.4.rows_ref, ...), custom_call_target="tpu_custom_call" | custom-call | flops 4000000000 | bytes 6291456 | tf_op jit(solution)/shard_map/settle/pallas_call | solution.py:265
  (17 shorter events, 0.2 us)
Async XLA Ops:
  0.0 1.6 %copy-start = (f32[4,128,8,128]{3,2,1,0:T(8,128)S(1)}, f32[4,128,8,128]{3,2,1,0:T(8,128)}, u32[]{:S(2)}) copy-start(f32[4,128,8,128]{3,2,1,0:T(8,128)} %matrix_ref.5) | copy-start | bytes 6291460
  1.6 5.9 %copy-start.1 = (f32[4,128,8,128]{3,2,1,0:T(8,128)S(1)}, f32[4,128,8,128]{3,2,1,0:T(8,128)}, u32[]{:S(2)}) copy-start(f32[4,128,8,128]{3,2,1,0:T(8,128)} %matrix_ref.5) | copy-start | bytes 6291460
  1.7 1.4 %collective-permute-start = (f32[64,128]{1,0:T(8,128)S(1)}, f32[64,128]{1,0:T(8,128)S(1)}, u32[]{:S(2)}, u32[]{:S(2)}) collective-permute-start(f32[64,128]{1,0:T(8,128)S(1)} %get-tuple-element.16), channel_id=1, source_target_pairs={{0,4},{4,0},{8,12},{12,8},{16,20},{20,16},{24,28},{28,24},{1,5},{5... | collective-permute-start | bytes 98312 | tf_op jit(solution)/shard_map/ppermute | solution.py:278
  3.1 9.8 %collective-permute-start.3 = (f32[64,128]{1,0:T(8,128)S(1)}, f32[64,128]{1,0:T(8,128)S(1)}, u32[]{:S(2)}, u32[]{:S(2)}) collective-permute-start(f32[64,128]{1,0:T(8,128)S(1)} %get-tuple-element.30), channel_id=1, source_target_pairs={{0,16},{4,20},{8,24},{12,28},{16,0},{20,4},{24,8},{28,12},{1,17},{... | collective-permute-start | bytes 98312 | tf_op jit(solution)/shard_map/ppermute | solution.py:278
  6.0 8.4 %collective-permute-start.2 = (f32[64,128]{1,0:T(8,128)S(1)}, f32[64,128]{1,0:T(8,128)S(1)}, u32[]{:S(2)}, u32[]{:S(2)}) collective-permute-start(f32[64,128]{1,0:T(8,128)S(1)} %get-tuple-element.30), channel_id=1, source_target_pairs={{0,8},{4,12},{8,0},{12,4},{16,24},{20,28},{24,16},{28,20},{1,9},{5... | collective-permute-start | bytes 98312 | tf_op jit(solution)/shard_map/ppermute | solution.py:278
  7.5 7.4 %collective-permute-start.1 = (f32[64,128]{1,0:T(8,128)S(1)}, f32[64,128]{1,0:T(8,128)}, u32[]{:S(2)}, u32[]{:S(2)}) collective-permute-start(f32[64,128]{1,0:T(8,128)S(1)} %get-tuple-element.30), channel_id=1, source_target_pairs={{0,24},{4,28},{8,16},{12,20},{16,8},{20,12},{24,0},{28,4},{1,25},{... | collective-permute-start | bytes 98312 | tf_op jit(solution)/shard_map/ppermute | solution.py:278
  8.3 30.7 %collective-permute-start.14 = (f32[4,128,128]{2,1,0:T(8,128)S(1)}, f32[4,128,128]{2,1,0:T(8,128)S(1)}, u32[]{:S(2)}, u32[]{:S(2)}) collective-permute-start(f32[4,128,128]{2,1,0:T(8,128)S(1)} %get-tuple-element.23), channel_id=1, source_target_pairs={{0,2},{1,3},{2,0},{3,1},{4,6},{5,7},{6,4},{7,5},{8,10},{9,11},{10,... | collective-permute-start | bytes 786440 | tf_op jit(solution)/shard_map/ppermute | solution.py:278
  11.4 24.4 %collective-permute-start.16 = (f32[8,64,128]{2,1,0:T(8,128)S(1)}, f32[8,64,128]{2,1,0:T(8,128)S(1)}, u32[]{:S(2)}, u32[]{:S(2)}) collective-permute-start(f32[8,64,128]{2,1,0:T(8,128)S(1)} %get-tuple-element.24), channel_id=1, source_target_pairs={{0,8},{4,12},{8,0},{12,4},{16,24},{20,28},{24,16},{28,20},{1,9},{5... | collective-permute-start | bytes 786440 | tf_op jit(solution)/shard_map/ppermute | solution.py:278
  12.8 3.9 %collective-permute-start.9 = (f32[64,128]{1,0:T(8,128)S(1)}, f32[64,128]{1,0:T(8,128)S(1)}, u32[]{:S(2)}, u32[]{:S(2)}) collective-permute-start(f32[64,128]{1,0:T(8,128)S(1)} %get-tuple-element.29), channel_id=1, source_target_pairs={{0,16},{4,20},{8,24},{12,28},{16,0},{20,4},{24,8},{28,12},{1,17},{... | collective-permute-start | bytes 98312 | tf_op jit(solution)/shard_map/ppermute | solution.py:278
  14.4 5.2 %collective-permute-start.8 = (f32[64,128]{1,0:T(8,128)S(1)}, f32[64,128]{1,0:T(8,128)S(1)}, u32[]{:S(2)}, u32[]{:S(2)}) collective-permute-start(f32[64,128]{1,0:T(8,128)S(1)} %get-tuple-element.29), channel_id=1, source_target_pairs={{0,8},{4,12},{8,0},{12,4},{16,24},{20,28},{24,16},{28,20},{1,9},{5... | collective-permute-start | bytes 98312 | tf_op jit(solution)/shard_map/ppermute | solution.py:278
  14.9 6.1 %collective-permute-start.7 = (f32[64,128]{1,0:T(8,128)S(1)}, f32[64,128]{1,0:T(8,128)S(1)}, u32[]{:S(2)}, u32[]{:S(2)}) collective-permute-start(f32[64,128]{1,0:T(8,128)S(1)} %get-tuple-element.29), channel_id=1, source_target_pairs={{0,24},{4,28},{8,16},{12,20},{16,8},{20,12},{24,0},{28,4},{1,25},{... | collective-permute-start | bytes 98312 | tf_op jit(solution)/shard_map/ppermute | solution.py:278
  16.8 20.7 %collective-permute-start.18 = (f32[8,64,128]{2,1,0:T(8,128)S(1)}, f32[8,64,128]{2,1,0:T(8,128)S(1)}, u32[]{:S(2)}, u32[]{:S(2)}) collective-permute-start(f32[8,64,128]{2,1,0:T(8,128)S(1)} %get-tuple-element.25), channel_id=1, source_target_pairs={{0,16},{4,20},{8,24},{12,28},{16,0},{20,4},{24,8},{28,12},{1,17},{... | collective-permute-start | bytes 786440 | tf_op jit(solution)/shard_map/ppermute | solution.py:278
  19.6 4.9 %collective-permute-start.4 = (f32[64,128]{1,0:T(8,128)S(1)}, f32[64,128]{1,0:T(8,128)S(1)}, u32[]{:S(2)}, u32[]{:S(2)}) collective-permute-start(f32[64,128]{1,0:T(8,128)S(1)} %select_select_fusion.1), channel_id=1, source_target_pairs={{0,2},{1,3},{2,0},{3,1},{4,6},{5,7},{6,4},{7,5},{8,10},{9,11},{10,... | collective-permute-start | bytes 98312 | tf_op jit(solution)/shard_map/ppermute | solution.py:278
  21.0 5.0 %collective-permute-start.10 = (f32[64,128]{1,0:T(8,128)S(1)}, f32[64,128]{1,0:T(8,128)S(1)}, u32[]{:S(2)}, u32[]{:S(2)}) collective-permute-start(f32[64,128]{1,0:T(8,128)S(1)} %select_select_fusion), channel_id=1, source_target_pairs={{0,2},{1,3},{2,0},{3,1},{4,6},{5,7},{6,4},{7,5},{8,10},{9,11},{10,... | collective-permute-start | bytes 98312 | tf_op jit(solution)/shard_map/ppermute | solution.py:278
  24.5 3.9 %collective-permute-start.5 = (f32[64,128]{1,0:T(8,128)S(1)}, f32[64,128]{1,0:T(8,128)S(1)}, u32[]{:S(2)}, u32[]{:S(2)}) collective-permute-start(f32[64,128]{1,0:T(8,128)S(1)} %broadcast_select_fusion.9), channel_id=1, source_target_pairs={{0,1},{1,0},{2,3},{3,2},{4,5},{5,4},{6,7},{7,6},{8,9},{9,8},{10,11... | collective-permute-start | bytes 98312 | tf_op jit(solution)/shard_map/ppermute | solution.py:278
  26.0 4.0 %collective-permute-start.11 = (f32[64,128]{1,0:T(8,128)S(1)}, f32[64,128]{1,0:T(8,128)S(1)}, u32[]{:S(2)}, u32[]{:S(2)}) collective-permute-start(f32[64,128]{1,0:T(8,128)S(1)} %broadcast_select_fusion.8), channel_id=1, source_target_pairs={{0,1},{1,0},{2,3},{3,2},{4,5},{5,4},{6,7},{7,6},{8,9},{9,8},{10,11... | collective-permute-start | bytes 98312 | tf_op jit(solution)/shard_map/ppermute | solution.py:278
  28.4 1.6 %collective-permute-start.6 = (f32[64,128]{1,0:T(8,128)S(1)}, f32[64,128]{1,0:T(8,128)S(1)}, u32[]{:S(2)}, u32[]{:S(2)}) collective-permute-start(f32[64,128]{1,0:T(8,128)S(1)} %get-tuple-element.28.mine_ref), channel_id=1, source_target_pairs={{0,4},{4,0},{8,12},{12,8},{16,20},{20,16},{24,28},{28,24},{1,5},{5... | collective-permute-start | bytes 98312 | tf_op jit(solution)/shard_map/ppermute | solution.py:278
  30.0 15.7 %collective-permute-start.12 = (f32[64,128]{1,0:T(8,128)S(1)}, f32[64,128]{1,0:T(8,128)S(1)}, u32[]{:S(2)}, u32[]{:S(2)}) collective-permute-start(f32[64,128]{1,0:T(8,128)S(1)} %broadcast_select_fusion.6.low_mine_ref), channel_id=1, source_target_pairs={{0,4},{4,0},{8,12},{12,8},{16,20},{20,16},{24,28},{28,24},{1,5},{5... | collective-permute-start | bytes 98312 | tf_op jit(solution)/shard_map/ppermute | solution.py:278
  30.0 15.7 %collective-permute-start.13 = (f32[64,128]{1,0:T(8,128)S(1)}, f32[64,128]{1,0:T(8,128)S(1)}, u32[]{:S(2)}, u32[]{:S(2)}) collective-permute-start(f32[64,128]{1,0:T(8,128)S(1)} %get-tuple-element.27.mine_ref), channel_id=1, source_target_pairs={{0,4},{4,0},{8,12},{12,8},{16,20},{20,16},{24,28},{28,24},{1,5},{5... | collective-permute-start | bytes 98312 | tf_op jit(solution)/shard_map/ppermute | solution.py:278
  35.8 8.4 %collective-permute-start.17 = (f32[8,64,128]{2,1,0:T(8,128)S(1)}, f32[8,64,128]{2,1,0:T(8,128)S(1)}, u32[]{:S(2)}, u32[]{:S(2)}) collective-permute-start(f32[8,64,128]{2,1,0:T(8,128)S(1)} %broadcast_select_fusion.1), channel_id=1, source_target_pairs={{0,16},{4,20},{8,24},{12,28},{16,0},{20,4},{24,8},{28,12},{1,17},{... | collective-permute-start | bytes 786440 | tf_op jit(solution)/shard_map/ppermute | solution.py:278
  37.5 8.1 %collective-permute-start.19 = (f32[8,64,128]{2,1,0:T(8,128)S(1)}, f32[8,64,128]{2,1,0:T(8,128)S(1)}, u32[]{:S(2)}, u32[]{:S(2)}) collective-permute-start(f32[8,64,128]{2,1,0:T(8,128)S(1)} %broadcast_select_fusion.2), channel_id=1, source_target_pairs={{0,8},{4,12},{8,0},{12,4},{16,24},{20,28},{24,16},{28,20},{1,9},{5... | collective-permute-start | bytes 786440 | tf_op jit(solution)/shard_map/ppermute | solution.py:278
  39.0 14.2 %collective-permute-start.15 = (f32[4,128,128]{2,1,0:T(8,128)S(1)}, f32[4,128,128]{2,1,0:T(8,128)S(1)}, u32[]{:S(2)}, u32[]{:S(2)}) collective-permute-start(f32[4,128,128]{2,1,0:T(8,128)S(1)} %broadcast_select_fusion.4.rows_ref), channel_id=1, source_target_pairs={{0,1},{1,0},{2,3},{3,2},{4,5},{5,4},{6,7},{7,6},{8,9},{9,8},{10,11... | collective-permute-start | bytes 786440 | tf_op jit(solution)/shard_map/ppermute | solution.py:278
  44.1 9.1 %collective-permute-start.20 = (f32[8,64,128]{2,1,0:T(8,128)S(1)}, f32[8,64,128]{2,1,0:T(8,128)S(1)}, u32[]{:S(2)}, u32[]{:S(2)}) collective-permute-start(f32[8,64,128]{2,1,0:T(8,128)S(1)} %broadcast_select_fusion.3.ha_ref), channel_id=1, source_target_pairs={{0,4},{4,0},{8,12},{12,8},{16,20},{20,16},{24,28},{28,24},{1,5},{5... | collective-permute-start | bytes 786440 | tf_op jit(solution)/shard_map/ppermute | solution.py:278
  45.6 7.6 %collective-permute-start.21 = (f32[8,64,128]{2,1,0:T(8,128)S(1)}, f32[8,64,128]{2,1,0:T(8,128)S(1)}, u32[]{:S(2)}, u32[]{:S(2)}) collective-permute-start(f32[8,64,128]{2,1,0:T(8,128)S(1)} %broadcast_select_fusion.hb_ref), channel_id=1, source_target_pairs={{0,4},{4,0},{8,12},{12,8},{16,20},{20,16},{24,28},{28,24},{1,5},{5... | collective-permute-start | bytes 786440 | tf_op jit(solution)/shard_map/ppermute | solution.py:278

commit v4 on v3

--- a/solution.py
+++ b/solution.py
@@ -75,43 +75,12 @@
     return upper.T, aug[...].reshape(n, n)
 
 
-def joined(mine_ref, other_ref, odd):
-    mine, other = mine_ref[...], other_ref[...]
-    return jnp.concatenate([jnp.where(odd, other, mine), jnp.where(odd, mine, other)], axis=0)
-
-
 def is_odd_row():
     return lax.rem(lax.axis_index("row"), 2) == 1
 
 
 def estimate(flops, nbytes):
     return pl.CostEstimate(flops=flops, bytes_accessed=nbytes, transcendentals=0)
-
-
-def corner_kernel(matrix_ref, own_ref, send_ref, sems):
-    half = own_ref.shape[0]
-    odd = lax.rem(lax.axis_index("row"), 2)
-    own = pltpu.make_async_copy(matrix_ref.at[0, pl.ds(odd * half, half), 0, :], own_ref, sems.at[0])
-    send = pltpu.make_async_copy(matrix_ref.at[0, pl.ds((1 - odd) * half, half), 0, :], send_ref, sems.at[1])
-    send.start()
-    own.start()
-    send.wait()
-    own.wait()
-
-
-def corner_halves(matrix):
-    n = matrix.shape[1]
-    half = jax.ShapeDtypeStruct((n // 2, n), jnp.float32)
-    return pl.pallas_call(
-        corner_kernel,
-        out_shape=[half, half],
-        in_specs=[HBM],
-        out_specs=[VMEM, VMEM],
-        scratch_shapes=[pltpu.SemaphoreType.DMA((2,))],
-        compiler_params=pltpu.CompilerParams(vmem_limit_bytes=2 * MIB),
-        cost_estimate=estimate(0, 3 * MIB),
-        name="corner_halves",
-    )(matrix)
 
 
 def panels_kernel(matrix_ref, column_ref, upper_ref, lower_ref, sems):
@@ -142,26 +111,26 @@
     )(matrix)
 
 
-def first_factor_kernel(mine_ref, other_ref, f_ref, w_ref, sym, aug):
-    f_ref[...], w_ref[...] = eliminate(joined(mine_ref, other_ref, is_odd_row()), sym, aug)
-
-
-def first_factor(mine, other):
-    n = mine.shape[1]
+def first_factor_kernel(a_ref, f_ref, w_ref, sym, aug):
+    f_ref[...], w_ref[...] = eliminate(a_ref[...], sym, aug)
+
+
+def first_factor(a):
+    n = a.shape[1]
     square = jax.ShapeDtypeStruct((n, n), jnp.float32)
     return pl.pallas_call(
         first_factor_kernel,
         out_shape=[square, square],
-        in_specs=[VMEM, VMEM],
+        in_specs=[VMEM],
         out_specs=[VMEM, VMEM],
         scratch_shapes=[pltpu.VMEM((n // SUB, SUB, n), jnp.float32)] * 2,
         compiler_params=pltpu.CompilerParams(vmem_limit_bytes=4 * MIB),
         cost_estimate=estimate(8 * 10**9, 2 * MIB),
         name="first_factor",
-    )(mine, other)
-
-
-def second_factor_kernel(low_mine_ref, low_other_ref, mine_ref, other_ref, w0_ref, matrix_ref, f_ref, w_ref, mixed_ref,
+    )(a)
+
+
+def second_factor_kernel(low_ref, a_ref, w0_ref, matrix_ref, f_ref, w_ref, mixed_ref,
                          blocks_ref, sym, aug, sems):
     n = w0_ref.shape[0]
     local_cols = matrix_ref.shape[2]
@@ -170,8 +139,8 @@
         copy.start()
     odd = is_odd_row()
     w0 = w0_ref[...]
-    cross = dot_t(joined(low_mine_ref, low_other_ref, odd), w0)
-    f1, w1 = eliminate(joined(mine_ref, other_ref, odd) - dot_t(cross, cross), sym, aug)
+    cross = dot_t(low_ref[...], w0)
+    f1, w1 = eliminate(a_ref[...] - dot_t(cross, cross), sym, aug)
     f_ref[...] = f1
     w10 = -dot(w1, dot(cross, w0))
     zero = jnp.zeros((n, n), jnp.float32)
@@ -187,7 +156,7 @@
         copy.wait()
 
 
-def second_factor(low_mine, low_other, mine, other, w0, matrix):
+def second_factor(low, a, w0, matrix):
     local_rows, n, local_cols, _ = matrix.shape
     square = jax.ShapeDtypeStruct((n, n), jnp.float32)
     double = jax.ShapeDtypeStruct((2 * n, 2 * n), jnp.float32)
@@ -195,13 +164,13 @@
     return pl.pallas_call(
         second_factor_kernel,
         out_shape=[square, double, double, blocks],
-        in_specs=[VMEM] * 5 + [HBM],
+        in_specs=[VMEM] * 3 + [HBM],
         out_specs=[VMEM] * 4,
         scratch_shapes=[pltpu.VMEM((n // SUB, SUB, n), jnp.float32)] * 2 + [pltpu.SemaphoreType.DMA((local_cols,))],
         compiler_params=pltpu.CompilerParams(vmem_limit_bytes=12 * MIB),
         cost_estimate=estimate(8 * 10**9, 4 * MIB),
         name="second_factor",
-    )(low_mine, low_other, mine, other, w0, matrix)
+    )(low, a, w0, matrix)
 
 
 def settle_kernel(f0_ref, f1_ref, w_ref, mixed_ref, rows_ref, rows_other_ref, ha_ref, hb_ref, oa_ref, ob_ref, blocks_ref,
@@ -289,18 +258,15 @@
     return held
 
 
-def spread_pairs(own, axis, index, size, bits):
-    held = own
-    for at in range(0, len(bits) - 1, 2):
-        low, high = bits[at], bits[at + 1]
-        from_low = exchange(held, axis, 1 << low, size)
-        from_high = exchange(held, axis, 1 << high, size)
-        from_both = exchange(held, axis, (1 << low) | (1 << high), size)
-        has_low, has_high = bit_set(index, low), bit_set(index, high)
-        held = jnp.where(has_low & has_high, from_both, jnp.where(has_low, from_low, jnp.where(has_high, from_high, held)))
-    if len(bits) % 2:
-        held = spread(held, axis, index, size, bits[-1:])
-    return held
+def corner(block, n_row, n_col):
+    devices = n_row * n_col
+    n = block.shape[0]
+    width = min(n, n * n // devices)
+    slices = block.reshape(devices, n * n // devices // width, width)
+    came = lax.all_to_all(slices, ("row", "col"), 0, 0)
+    mine = jnp.stack([came[0], came[n_col], came[n_col + 1]])
+    every = lax.all_to_all(jnp.broadcast_to(mine[None], (devices,) + mine.shape), ("row", "col"), 0, 0)
+    return [every[:, b].reshape(n, n) for b in range(3)]
 
 
 def shards(kernel):
@@ -310,35 +276,19 @@
     n_col = lax.axis_size("col")
     row_bits = list(range(1, n_row.bit_length() - 1))
     col_bits = list(range(1, n_col.bit_length() - 1))
-    odd = (grid_row % 2) == 1
-    right = (grid_col % 2) == 1
-
-    own, send = corner_halves(kernel)
-    got = exchange(send, "row", 1, n_row)
-    diag = jnp.where(odd != right, got, own)
-    low = jnp.where(odd, own, got)
-    diag = spread_pairs(diag, "row", grid_row, n_row, row_bits)
-    low = spread_pairs(low, "row", grid_row, n_row, row_bits)
+
+    a00, a10, a11 = corner(kernel[0, :, 0, :], n_row, n_col)
+
     column, upper, lower = panels(kernel)
-
-    diag = spread(diag, "col", grid_col, n_col, col_bits)
-    diag_other = exchange(diag, "col", 1, n_col)
-    first = jnp.where(right, diag_other, diag)
-    second = jnp.where(right, diag, diag_other)
-    first_far = exchange(first, "row", 1, n_row)
-    low = spread(low, "col", grid_col, n_col, col_bits + [0])
-    second_far = exchange(second, "row", 1, n_row)
-    low_far = exchange(low, "row", 1, n_row)
-
     ha = spread(upper, "row", grid_row, n_row, row_bits)
     hb = spread(lower, "row", grid_row, n_row, row_bits[::-1])
     rows = spread(column, "col", grid_col, n_col, col_bits)
-
-    f0, w0 = first_factor(first, first_far)
     oa = exchange(ha, "row", 1, n_row)
     ob = exchange(hb, "row", 1, n_row)
     rows_other = exchange(rows, "col", 1, n_col)
-    f1, w, mixed, blocks = second_factor(low, low_far, second, second_far, w0, kernel)
+
+    f0, w0 = first_factor(a00)
+    f1, w, mixed, blocks = second_factor(a10, a11, w0, kernel)
     return settle(f0, f1, w, mixed, rows, rows_other, ha, hb, oa, ob, blocks)
 
 

time: 60.7 us -> 57.8 us (0.952)
  starting transfers between devices: 24.6 us -> 22 us
  waiting for transfers between devices: 13.2 us -> 10.6 us
  local copies, waits for them, and re-layouts: 1.59 us -> 3.88 us
    ppermute x22 -> x8, waiting for transfers between devices: 13.2 us -> 0.02 us  [exchange(): return lax.ppermute(value, axis, [(i, i ^ mask) for i in range(size)])]
    ppermute x22 -> x8, starting transfers between devices: 24.6 us -> 13.8 us  [exchange(): return lax.ppermute(value, axis, [(i, i ^ mask) for i in range(size)])]
    all_to_all x0 -> x2, waiting for transfers between devices: none -> 10.6 us  [the longest x1 7.08 us: corner(): came = lax.all_to_all(slices, ('row', 'col'), 0, 0)]
    all_to_all x0 -> x2, starting transfers between devices: none -> 8.19 us  [the longest x1 4.14 us: corner(): lax.all_to_all(jnp.broadcast_to(mine[None], (devices,) + mine.shape), ('r...]
    slice x0 -> x4, local copies, waits for them, and re-layouts: none -> 1.58 us  [the longest x1 0.92 us: corner(): return [every[:, b].reshape(n, n) for b in range(3)]]
    broadcast_in_dim x0 -> x1, local copies, waits for them, and re-layouts: none -> 0.71 us  [corner(): jnp.broadcast_to(mine[None], (devices,) + mine.shape)]
  transfers between devices with their start and end apart: 22 -> 10, of which waited for: 9 -> 2; matrix products, arithmetic and copies ran while one was open for 0% -> 4% of each run, Pallas kernels for 22% -> 22%
where the time goes in v4:
time: 57.8 us; the launch traced here: 57.4 us
  starting transfers between devices  22 us (38%)
  Pallas kernels  20.5 us (35%)
  waiting for transfers between devices  10.6 us (18%)
  local copies, waits for them, and re-layouts  3.88 us (7%)
    ppermute x8, starting transfers between devices, exchange(): return lax.ppermute(value, axis, [(i, i ^ mask) for i in range(size)])  13.8 us
    pallas_call x1, Pallas kernels, second_factor(): pl.pallas_call(second_factor_kernel, out_shape=[square, double, double, b...  7.49 us
    all_to_all x1, waiting for transfers between devices, corner(): came = lax.all_to_all(slices, ('row', 'col'), 0, 0)  7.08 us
    pallas_call x1, Pallas kernels, settle(): pl.pallas_call(settle_kernel, out_shape=jax.ShapeDtypeStruct((local_rows,...  7.06 us
    pallas_call x1, Pallas kernels, first_factor(): pl.pallas_call(first_factor_kernel, out_shape=[square, square], in_specs=...  5.17 us
    all_to_all x1, starting transfers between devices, corner(): lax.all_to_all(jnp.broadcast_to(mine[None], (devices,) + mine.shape), ('r...  4.14 us
    all_to_all x1, starting transfers between devices, corner(): came = lax.all_to_all(slices, ('row', 'col'), 0, 0)  4.04 us
    all_to_all x1, waiting for transfers between devices, corner(): lax.all_to_all(jnp.broadcast_to(mine[None], (devices,) + mine.shape), ('r...  3.5 us
  transfers between devices with their start and end apart: 10, of which 2 were waited for; matrix products, arithmetic and copies ran while one was open for 4% of the time, Pallas kernels for 22%

profile of v4, /device:TPU:0, one launch (start us, length us, event | category | flops | bytes accessed | tf_op | source)
XLA Modules:
  0.0 57.4 jit_solution(8345093628456859135)
XLA Ops:
  0.0 0.0 copy-start
  0.0 1.6 %copy-done = f32[4,128,8,128]{3,2,1,0:T(8,128)S(1)} copy-done((f32[4,128,8,128]{3,2,1,0:T(8,128)S(1)}, f32[4,128,8,128]{3,2,1,0:T(8,128)}, u32[]{:S(2)}) %copy-start) | copy-done | bytes 2097176
  1.6 0.0 copy-start.1
  1.6 0.7 %panels.1 = (f32[4,128,128]{2,1,0:T(8,128)S(1)}, f32[8,64,128]{2,1,0:T(8,128)S(1)}, f32[8,64,128]{2,1,0:T(8,128)S(1)}) custom-call(f32[4,128,8,128]{3,2,1,0:T(8,128)S(1)} %copy-done), custom_call_target="tpu_custom_call" | custom-call | bytes 4194304 | tf_op jit(solution)/shard_map/panels/pallas_call | solution.py:102
  2.3 4.1 %collective-permute-start = (f32[4,128,128]{2,1,0:T(8,128)S(1)}, f32[4,128,128]{2,1,0:T(8,128)S(1)}, u32[]{:S(2)}, u32[]{:S(2)}) collective-permute-start(f32[4,128,128]{2,1,0:T(8,128)S(1)} %get-tuple-element.19), channel_id=1, source_target_pairs={{0,2},{1,3},{2,0},{3,1},{4,6},{5,7},{6,4},{7,5},{8,10},{9,11},{10,... | collective-permute-start | bytes 786440 | tf_op jit(solution)/shard_map/ppermute | solution.py:247
  6.4 0.0 copy-done.1
  6.4 0.7 %slice.20 = f32[1,128,1,128]{3,2,1,0:T(1,128)} slice(f32[4,128,8,128]{3,2,1,0:T(8,128)S(1)} %copy-done.1), slice={[0:1], [0:128], [0:1], [0:128]} | slice | bytes 131072 | tf_op jit(solution)/shard_map/slice | solution.py:280
  7.1 4.0 %all-to-all-start = ((f32[32,4,128]{2,1,0:T(4,128)}), f32[32,4,128]{2,1,0:T(4,128)S(1)}, u32[]{:S(2)}, u32[]{:S(2)}) async-start(f32[32,4,128]{2,1,0:T(4,128)} %bitcast), calls=%async_computation | async-start | bytes 131072 | tf_op jit(solution)/shard_map/all_to_all | solution.py:266
  11.2 1.8 %collective-permute-start.2 = (f32[8,64,128]{2,1,0:T(8,128)S(1)}, f32[8,64,128]{2,1,0:T(8,128)}, u32[]{:S(2)}, u32[]{:S(2)}) collective-permute-start(f32[8,64,128]{2,1,0:T(8,128)S(1)} %get-tuple-element.20), channel_id=1, source_target_pairs={{0,8},{4,12},{8,0},{12,4},{16,24},{20,28},{24,16},{28,20},{1,9},{5... | collective-permute-start | bytes 786440 | tf_op jit(solution)/shard_map/ppermute | solution.py:247
  13.0 1.5 %collective-permute-start.4 = (f32[8,64,128]{2,1,0:T(8,128)S(1)}, f32[8,64,128]{2,1,0:T(8,128)}, u32[]{:S(2)}, u32[]{:S(2)}) collective-permute-start(f32[8,64,128]{2,1,0:T(8,128)S(1)} %get-tuple-element.21), channel_id=1, source_target_pairs={{0,16},{4,20},{8,24},{12,28},{16,0},{20,4},{24,8},{28,12},{1,17},{... | collective-permute-start | bytes 786440 | tf_op jit(solution)/shard_map/ppermute | solution.py:247
  14.5 7.1 %all-to-all-done = f32[32,4,128]{2,1,0:T(4,128)S(1)} async-done(((f32[32,4,128]{2,1,0:T(4,128)}), f32[32,4,128]{2,1,0:T(4,128)S(1)}, u32[]{:S(2)}, u32[]{:S(2)}) %all-to-all-start) | async-done | bytes 65568 | tf_op jit(solution)/shard_map/all_to_all | solution.py:266
  21.5 0.7 %broadcast_in_dim.2 = f32[32,3,4,128]{3,2,1,0:T(4,128)} broadcast(f32[3,4,128]{2,1,0:T(4,128)S(1)} %pad_maximum_fusion), dimensions={1,2,3} | broadcast | bytes 202752 | tf_op jit(solution)/shard_map/broadcast_in_dim | solution.py:268
  22.3 4.1 %all-to-all-start.1 = ((f32[32,3,4,128]{3,2,1,0:T(4,128)}), f32[32,3,4,128]{3,2,1,0:T(4,128)}, u32[]{:S(2)}, u32[]{:S(2)}) async-start(f32[32,3,4,128]{3,2,1,0:T(4,128)} %broadcast_in_dim.2), calls=%async_computation.1 | async-start | bytes 393216 | tf_op jit(solution)/shard_map/all_to_all | solution.py:268
  26.4 0.0 collective-permute-done
  26.5 1.8 %collective-permute-start.1 = (f32[4,128,128]{2,1,0:T(8,128)S(1)}, f32[4,128,128]{2,1,0:T(8,128)S(1)}, u32[]{:S(2)}, u32[]{:S(2)}) collective-permute-start(f32[4,128,128]{2,1,0:T(8,128)S(1)} %broadcast_select_fusion.4.rows_ref), channel_id=1, source_target_pairs={{0,1},{1,0},{2,3},{3,2},{4,5},{5,4},{6,7},{7,6},{8,9},{9,8},{10,11... | collective-permute-start | bytes 786440 | tf_op jit(solution)/shard_map/ppermute | solution.py:247
  28.2 0.0 collective-permute-done.2
  28.3 1.5 %collective-permute-start.3 = (f32[8,64,128]{2,1,0:T(8,128)S(1)}, f32[8,64,128]{2,1,0:T(8,128)}, u32[]{:S(2)}, u32[]{:S(2)}) collective-permute-start(f32[8,64,128]{2,1,0:T(8,128)S(1)} %broadcast_select_fusion.1), channel_id=1, source_target_pairs={{0,16},{4,20},{8,24},{12,28},{16,0},{20,4},{24,8},{28,12},{1,17},{... | collective-permute-start | bytes 786440 | tf_op jit(solution)/shard_map/ppermute | solution.py:247
  29.8 0.0 collective-permute-done.4
  29.8 2.5 %collective-permute-start.5 = (f32[8,64,128]{2,1,0:T(8,128)S(1)}, f32[8,64,128]{2,1,0:T(8,128)}, u32[]{:S(2)}, u32[]{:S(2)}) collective-permute-start(f32[8,64,128]{2,1,0:T(8,128)S(1)} %broadcast_select_fusion.2), channel_id=1, source_target_pairs={{0,8},{4,12},{8,0},{12,4},{16,24},{20,28},{24,16},{28,20},{1,9},{5... | collective-permute-start | bytes 786440 | tf_op jit(solution)/shard_map/ppermute | solution.py:247
  32.3 3.5 %all-to-all-done.1 = f32[32,3,4,128]{3,2,1,0:T(4,128)} async-done(((f32[32,3,4,128]{3,2,1,0:T(4,128)}), f32[32,3,4,128]{3,2,1,0:T(4,128)}, u32[]{:S(2)}, u32[]{:S(2)}) %all-to-all-start.1) | async-done | bytes 196640 | tf_op jit(solution)/shard_map/all_to_all | solution.py:268
  35.8 0.9 %fusion = (f32[32,1,4,128]{3,2,1,0:T(4,128)S(1)}, f32[32,1,4,128]{3,2,1,0:T(4,128)S(1)}, f32[32,1,4,128]{3,2,1,0:T(4,128)S(1)}) fusion(f32[32,3,4,128]{3,2,1,0:T(4,128)} %all-to-all-done.1), kind=kLoop, calls=%fused_computation.6 | loop fusion | bytes 393216 | tf_op jit(solution)/shard_map/slice | solution.py:269
  36.7 5.2 %first_factor.1 = (f32[128,128]{1,0:T(8,128)S(1)}, f32[128,128]{1,0:T(8,128)S(1)}) custom-call(f32[128,128]{1,0:T(8,128)S(1)} %bitcast.6), custom_call_target="tpu_custom_call" | custom-call | flops 8000000000 | bytes 2097152 | tf_op jit(solution)/shard_map/first_factor/pallas_call | solution.py:121
  41.9 0.0 collective-permute-done.3
  42.0 0.1 collective-permute-start.6
  42.0 0.0 collective-permute-done.5
  42.1 0.5 collective-permute-start.7
  42.7 7.5 %second_factor.1 = (f32[128,128]{1,0:T(8,128)S(1)}, f32[256,256]{1,0:T(8,128)S(1)}, f32[256,256]{1,0:T(8,128)S(1)}, f32[8,4,128,128]{3,2,1,0:T(8,128)S(1)}) custom-call(f32[128,128]{1,0:T(8,128)S(1)} %bitcast.5, f32[128,128]{1,0:T(8,128)S(1)} %bitcast.4, f32[128,128]{1,0:T(8,128)S(1)} %get-tuple-element.15.w0_ref, f32[4,128,8,128]{3,2,1,0:T(8,128)S(1)} %copy-done.1), custom_call_target="tpu_custom_call" | custom-call | flops 8000000000 | bytes 4194304 | tf_op jit(solution)/shard_map/second_factor/pallas_call | solution.py:164
  50.2 0.0 collective-permute-done.1.rows_other_ref
  50.2 0.0 collective-permute-done.6.oa_ref
  50.2 0.0 collective-permute-done.7.ob_ref
  50.2 7.1 %settle.1 = f32[4,128,8,128]{3,2,1,0:T(8,128)} custom-call(f32[128,128]{1,0:T(8,128)S(1)} %get-tuple-element.14.f0_ref, f32[128,128]{1,0:T(8,128)S(1)} %get-tuple-element.16.f1_ref, f32[256,256]{1,0:T(8,128)S(1)} %get-tuple-element.17.w_ref, f32[256,256]{1,0:T(8,128)S(1)} %get-tuple-element.18.mixed_ref, f32[4,128,128]{2,1,0:T(8,128)S(1)} %broadcast_select_fusion.4.rows_ref, ...), custom_call_target="tpu_custom_call" | custom-call | flops 4000000000 | bytes 6291456 | tf_op jit(solution)/shard_map/settle/pallas_call | solution.py:234
  (8 shorter events, 0.2 us)
Async XLA Ops:
  0.0 1.6 %copy-start = (f32[4,128,8,128]{3,2,1,0:T(8,128)S(1)}, f32[4,128,8,128]{3,2,1,0:T(8,128)}, u32[]{:S(2)}) copy-start(f32[4,128,8,128]{3,2,1,0:T(8,128)} %matrix_ref.3) | copy-start | bytes 6291460
  1.6 4.8 %copy-start.1 = (f32[4,128,8,128]{3,2,1,0:T(8,128)S(1)}, f32[4,128,8,128]{3,2,1,0:T(8,128)}, u32[]{:S(2)}) copy-start(f32[4,128,8,128]{3,2,1,0:T(8,128)} %matrix_ref.3) | copy-start | bytes 6291460
  2.3 24.1 %collective-permute-start = (f32[4,128,128]{2,1,0:T(8,128)S(1)}, f32[4,128,128]{2,1,0:T(8,128)S(1)}, u32[]{:S(2)}, u32[]{:S(2)}) collective-permute-start(f32[4,128,128]{2,1,0:T(8,128)S(1)} %get-tuple-element.19), channel_id=1, source_target_pairs={{0,2},{1,3},{2,0},{3,1},{4,6},{5,7},{6,4},{7,5},{8,10},{9,11},{10,... | collective-permute-start | bytes 786440 | tf_op jit(solution)/shard_map/ppermute | solution.py:247
  7.1 14.4 %all-to-all-start = ((f32[32,4,128]{2,1,0:T(4,128)}), f32[32,4,128]{2,1,0:T(4,128)S(1)}, u32[]{:S(2)}, u32[]{:S(2)}) async-start(f32[32,4,128]{2,1,0:T(4,128)} %bitcast), calls=%async_computation | async-start | bytes 131072 | tf_op jit(solution)/shard_map/all_to_all | solution.py:266
  11.2 17.1 %collective-permute-start.2 = (f32[8,64,128]{2,1,0:T(8,128)S(1)}, f32[8,64,128]{2,1,0:T(8,128)}, u32[]{:S(2)}, u32[]{:S(2)}) collective-permute-start(f32[8,64,128]{2,1,0:T(8,128)S(1)} %get-tuple-element.20), channel_id=1, source_target_pairs={{0,8},{4,12},{8,0},{12,4},{16,24},{20,28},{24,16},{28,20},{1,9},{5... | collective-permute-start | bytes 786440 | tf_op jit(solution)/shard_map/ppermute | solution.py:247
  13.0 16.8 %collective-permute-start.4 = (f32[8,64,128]{2,1,0:T(8,128)S(1)}, f32[8,64,128]{2,1,0:T(8,128)}, u32[]{:S(2)}, u32[]{:S(2)}) collective-permute-start(f32[8,64,128]{2,1,0:T(8,128)S(1)} %get-tuple-element.21), channel_id=1, source_target_pairs={{0,16},{4,20},{8,24},{12,28},{16,0},{20,4},{24,8},{28,12},{1,17},{... | collective-permute-start | bytes 786440 | tf_op jit(solution)/shard_map/ppermute | solution.py:247
  22.3 13.6 %all-to-all-start.1 = ((f32[32,3,4,128]{3,2,1,0:T(4,128)}), f32[32,3,4,128]{3,2,1,0:T(4,128)}, u32[]{:S(2)}, u32[]{:S(2)}) async-start(f32[32,3,4,128]{3,2,1,0:T(4,128)} %broadcast_in_dim.2), calls=%async_computation.1 | async-start | bytes 393216 | tf_op jit(solution)/shard_map/all_to_all | solution.py:268
  26.5 23.7 %collective-permute-start.1 = (f32[4,128,128]{2,1,0:T(8,128)S(1)}, f32[4,128,128]{2,1,0:T(8,128)S(1)}, u32[]{:S(2)}, u32[]{:S(2)}) collective-permute-start(f32[4,128,128]{2,1,0:T(8,128)S(1)} %broadcast_select_fusion.4.rows_ref), channel_id=1, source_target_pairs={{0,1},{1,0},{2,3},{3,2},{4,5},{5,4},{6,7},{7,6},{8,9},{9,8},{10,11... | collective-permute-start | bytes 786440 | tf_op jit(solution)/shard_map/ppermute | solution.py:247
  28.3 13.6 %collective-permute-start.3 = (f32[8,64,128]{2,1,0:T(8,128)S(1)}, f32[8,64,128]{2,1,0:T(8,128)}, u32[]{:S(2)}, u32[]{:S(2)}) collective-permute-start(f32[8,64,128]{2,1,0:T(8,128)S(1)} %broadcast_select_fusion.1), channel_id=1, source_target_pairs={{0,16},{4,20},{8,24},{12,28},{16,0},{20,4},{24,8},{28,12},{1,17},{... | collective-permute-start | bytes 786440 | tf_op jit(solution)/shard_map/ppermute | solution.py:247
  29.8 12.2 %collective-permute-start.5 = (f32[8,64,128]{2,1,0:T(8,128)S(1)}, f32[8,64,128]{2,1,0:T(8,128)}, u32[]{:S(2)}, u32[]{:S(2)}) collective-permute-start(f32[8,64,128]{2,1,0:T(8,128)S(1)} %broadcast_select_fusion.2), channel_id=1, source_target_pairs={{0,8},{4,12},{8,0},{12,4},{16,24},{20,28},{24,16},{28,20},{1,9},{5... | collective-permute-start | bytes 786440 | tf_op jit(solution)/shard_map/ppermute | solution.py:247
  42.0 8.2 %collective-permute-start.6 = (f32[8,64,128]{2,1,0:T(8,128)S(1)}, f32[8,64,128]{2,1,0:T(8,128)S(1)}, u32[]{:S(2)}, u32[]{:S(2)}) collective-permute-start(f32[8,64,128]{2,1,0:T(8,128)S(1)} %broadcast_select_fusion.3.ha_ref), channel_id=1, source_target_pairs={{0,4},{4,0},{8,12},{12,8},{16,20},{20,16},{24,28},{28,24},{1,5},{5... | collective-permute-start | bytes 786440 | tf_op jit(solution)/shard_map/ppermute | solution.py:247
  42.1 8.1 %collective-permute-start.7 = (f32[8,64,128]{2,1,0:T(8,128)S(1)}, f32[8,64,128]{2,1,0:T(8,128)S(1)}, u32[]{:S(2)}, u32[]{:S(2)}) collective-permute-start(f32[8,64,128]{2,1,0:T(8,128)S(1)} %broadcast_select_fusion.hb_ref), channel_id=1, source_target_pairs={{0,4},{4,0},{8,12},{12,8},{16,20},{20,16},{24,28},{28,24},{1,5},{5... | collective-permute-start | bytes 786440 | tf_op jit(solution)/shard_map/ppermute | solution.py:247

commit v5 on v4

--- a/solution.py
+++ b/solution.py
@@ -20,10 +20,8 @@
     return lax.dot_general(a, b, (((1,), (1,)), ((), ())), precision=EXACT, preferred_element_type=jnp.float32)
 
 
-def inverse_of(p):
-    r = pl.reciprocal(p, approx=True)
-    r = r * (2.0 - p * r)
-    return r * (2.0 - p * r)
+def full(row):
+    return jnp.broadcast_to(row, (SUB, row.shape[-1]))
 
 
 def eliminate(s, sym, aug):
@@ -42,18 +40,25 @@
         top = sym[g]
         top_aug = aug[g]
         spread = [jnp.broadcast_to(rest[:, :, start + j:start + j + 1], (left, SUB, n)) for j in range(SUB)]
+        unit = {(i, j): full(spread[j][0, i:i + 1, :]) for j in range(SUB) for i in range(j, SUB)}
         scaled = []
         scaled_aug = []
         roots = jnp.zeros((SUB, n), jnp.float32)
         for k in range(SUB):
-            pivot = jnp.broadcast_to(spread[k][0, k:k + 1, :], (SUB, n))
-            recip = inverse_of(pivot)
+            pivot = unit[k, k]
+            guess = pl.reciprocal(pivot, approx=True)
+            rest_of = 2.0 - pivot * guess
+            recip = guess * rest_of
             roots = jnp.where(sub == k, pivot, roots)
             for j in range(k + 1, SUB):
-                factor = jnp.broadcast_to(spread[k][0, j:j + 1, :], (SUB, n)) * recip
+                unit[j, j] = unit[j, j] - (unit[j, k] * unit[j, k] * guess) * rest_of
+                for i in range(j + 1, SUB):
+                    unit[i, j] = unit[i, j] - (unit[i, k] * unit[j, k] * guess) * rest_of
+            for j in range(k + 1, SUB):
+                factor = unit[j, k] * recip
                 spread[j] = spread[j] - spread[k] * factor[None]
-            row = jnp.broadcast_to(top[k:k + 1, :], (SUB, n)) * recip
-            row_aug = jnp.broadcast_to(top_aug[k:k + 1, :], (SUB, n)) * recip
+            row = full(top[k:k + 1, :]) * recip
+            row_aug = full(top_aug[k:k + 1, :]) * recip
             scaled.append(row)
             scaled_aug.append(row_aug)
             if k + 1 < SUB:
@@ -79,8 +84,43 @@
     return lax.rem(lax.axis_index("row"), 2) == 1
 
 
+def parts(x):
+    high = x.astype(jnp.bfloat16)
+    rest = x - high.astype(jnp.float32)
+    middle = rest.astype(jnp.bfloat16)
+    return high, middle, (rest - middle.astype(jnp.float32)).astype(jnp.bfloat16)
+
+
+def dot_parts(a, b, dims=((1,), (0,))):
+    total = None
+    for i, j in ((2, 0), (0, 2), (1, 1), (1, 0), (0, 1), (0, 0)):
+        term = lax.dot_general(a[i], b[j], (dims, ((), ())), preferred_element_type=jnp.float32)
+        total = term if total is None else total + term
+    return total
+
+
 def estimate(flops, nbytes):
     return pl.CostEstimate(flops=flops, bytes_accessed=nbytes, transcendentals=0)
+
+
+def corner_kernel(matrix_ref, block_ref, sem):
+    copy = pltpu.make_async_copy(matrix_ref.at[0, :, 0, :], block_ref, sem)
+    copy.start()
+    copy.wait()
+
+
+def corner_block(matrix):
+    n = matrix.shape[1]
+    return pl.pallas_call(
+        corner_kernel,
+        out_shape=jax.ShapeDtypeStruct((n, n), jnp.float32),
+        in_specs=[HBM],
+        out_specs=VMEM,
+        scratch_shapes=[pltpu.SemaphoreType.DMA(())],
+        compiler_params=pltpu.CompilerParams(vmem_limit_bytes=62 * MIB),
+        cost_estimate=estimate(0, 3 * MIB),
+        name="corner_block",
+    )(matrix)
 
 
 def panels_kernel(matrix_ref, column_ref, upper_ref, lower_ref, sems):
@@ -184,14 +224,15 @@
     other = rows_other_ref[...].reshape(flat, n)
     swapped = lax.rem(grid_col, 2) == 1
     rows = jnp.concatenate([jnp.where(swapped, other, own), jnp.where(swapped, own, other)], axis=1)
-    solved = dot_t(rows, w_ref[...])
-    mixed = mixed_ref[...]
+    solved = dot_parts(parts(rows), parts(w_ref[...]), ((1,), (1,)))
+    left = parts(solved)
+    mixed = parts(mixed_ref[...])
     copies = []
     for j in range(0, local_cols, 2):
         pair = (j, j + 1)
         stacked = jnp.concatenate(
             [jnp.concatenate([ha_ref[b], hb_ref[b], oa_ref[b], ob_ref[b]], axis=0) for b in pair], axis=1)
-        update = dot(solved, dot(mixed, stacked))
+        update = dot_parts(left, parts(dot_parts(mixed, parts(stacked))))
         for b in pair:
             part = update[:, (b - j) * n:(b - j + 1) * n].reshape(local_rows, n, n)
             result[b] = blocks_ref[b] - part
@@ -258,28 +299,27 @@
     return held
 
 
-def corner(block, n_row, n_col):
-    devices = n_row * n_col
-    n = block.shape[0]
-    width = min(n, n * n // devices)
-    slices = block.reshape(devices, n * n // devices // width, width)
-    came = lax.all_to_all(slices, ("row", "col"), 0, 0)
-    mine = jnp.stack([came[0], came[n_col], came[n_col + 1]])
-    every = lax.all_to_all(jnp.broadcast_to(mine[None], (devices,) + mine.shape), ("row", "col"), 0, 0)
-    return [every[:, b].reshape(n, n) for b in range(3)]
-
-
 def shards(kernel):
     grid_row = lax.axis_index("row")
     grid_col = lax.axis_index("col")
     n_row = lax.axis_size("row")
     n_col = lax.axis_size("col")
+    n = kernel.shape[1]
+    half = n // 2
     row_bits = list(range(1, n_row.bit_length() - 1))
     col_bits = list(range(1, n_col.bit_length() - 1))
-
-    a00, a10, a11 = corner(kernel[0, :, 0, :], n_row, n_col)
-
-    column, upper, lower = panels(kernel)
+    odd = (grid_row % 2) == 1
+
+    block = corner_block(kernel)
+    halves = jnp.broadcast_to(block.reshape(1, 2, half, n), (n_row // 2, 2, half, n)).reshape(n_row, half, n)
+    over_row = lax.all_to_all(halves, "row", 0, 0)
+    kernel_then, over_row = lax.optimization_barrier((kernel, over_row))
+    pair = jnp.broadcast_to(over_row[None, :2], (n_col, 2, half, n))
+    over_col = lax.all_to_all(pair, "col", 0, 0)
+    mine = jnp.stack([over_col[0, 0], over_col[0, 1], over_col[1, 1]])
+    other = exchange(mine, "row", 1, n_row)
+
+    column, upper, lower = panels(kernel_then)
     ha = spread(upper, "row", grid_row, n_row, row_bits)
     hb = spread(lower, "row", grid_row, n_row, row_bits[::-1])
     rows = spread(column, "col", grid_col, n_col, col_bits)
@@ -287,8 +327,9 @@
     ob = exchange(hb, "row", 1, n_row)
     rows_other = exchange(rows, "col", 1, n_col)
 
-    f0, w0 = first_factor(a00)
-    f1, w, mixed, blocks = second_factor(a10, a11, w0, kernel)
+    whole = jnp.concatenate([jnp.where(odd, other, mine), jnp.where(odd, mine, other)], axis=1)
+    f0, w0 = first_factor(whole[0])
+    f1, w, mixed, blocks = second_factor(whole[1], whole[2], w0, kernel)
     return settle(f0, f1, w, mixed, rows, rows_other, ha, hb, oa, ob, blocks)
 
 

time: 57.8 us -> 60.2 us (1.042)
  starting transfers between devices: 22 us -> 9.77 us
  blocking collectives: 0 us -> 11.9 us
  waiting for transfers between devices: 10.6 us -> 13 us
  Pallas kernels: 20.5 us -> 21.4 us
  local copies, waits for them, and re-layouts: 3.88 us -> 3.19 us
    ppermute x8 -> x9, waiting for transfers between devices: 0.02 us -> 12 us  [exchange(): return lax.ppermute(value, axis, [(i, i ^ mask) for i in range(size)])]
    all_to_all x0 -> x1, blocking collectives: none -> 11.9 us  [shards(): over_row = lax.all_to_all(halves, 'row', 0, 0)]
    all_to_all x2 -> x1, waiting for transfers between devices: 10.6 us -> 0.95 us  [shards(): over_col = lax.all_to_all(pair, 'col', 0, 0)]
    ppermute x8 -> x9, starting transfers between devices: 13.8 us -> 6.36 us  [exchange(): return lax.ppermute(value, axis, [(i, i ^ mask) for i in range(size)])]
    all_to_all x2 -> x1, starting transfers between devices: 8.19 us -> 3.41 us  [shards(): over_col = lax.all_to_all(pair, 'col', 0, 0)]
    slice x4 -> x1, local copies, waits for them, and re-layouts: 1.58 us -> 0.01 us  [shards(): pair = jnp.broadcast_to(over_row[None, :2], (n_col, 2, half, n))]
    pallas_call x0 -> x1, Pallas kernels: none -> 1.48 us  [corner_block(): pl.pallas_call(corner_kernel, out_shape=jax.ShapeDtypeStruct((n, n), jnp....]
    broadcast_in_dim x1 -> x2, local copies, waits for them, and re-layouts: 0.71 us -> 1.58 us  [the longest x1 0.86 us: shards(): jnp.broadcast_to(block.reshape(1, 2, half, n), (n_row // 2, 2, half, n))]
  transfers between devices with their start and end apart: 10 -> 10, of which waited for: 2 -> 3; matrix products, arithmetic and copies ran while one was open for 4% -> 2% of each run, Pallas kernels for 22% -> 20%
where the time goes in v5:
time: 60.2 us; the launch traced here: 59.8 us
  Pallas kernels  21.4 us (36%)
  waiting for transfers between devices  13 us (22%)
  blocking collectives  11.9 us (20%)
  starting transfers between devices  9.77 us (16%)
  local copies, waits for them, and re-layouts  3.19 us (5%)
    ppermute x9, waiting for transfers between devices, exchange(): return lax.ppermute(value, axis, [(i, i ^ mask) for i in range(size)])  12 us
    all_to_all x1, blocking collectives, shards(): over_row = lax.all_to_all(halves, 'row', 0, 0)  11.9 us
    pallas_call x1, Pallas kernels, second_factor(): pl.pallas_call(second_factor_kernel, out_shape=[square, double, double, b...  7.16 us
    pallas_call x1, Pallas kernels, settle(): pl.pallas_call(settle_kernel, out_shape=jax.ShapeDtypeStruct((local_rows,...  7.07 us
    ppermute x9, starting transfers between devices, exchange(): return lax.ppermute(value, axis, [(i, i ^ mask) for i in range(size)])  6.36 us
    pallas_call x1, Pallas kernels, first_factor(): pl.pallas_call(first_factor_kernel, out_shape=[square, square], in_specs=...  5 us
    all_to_all x1, starting transfers between devices, shards(): over_col = lax.all_to_all(pair, 'col', 0, 0)  3.41 us
    unnamed x4, local copies, waits for them, and re-layouts  1.6 us
  transfers between devices with their start and end apart: 10, of which 3 were waited for; matrix products, arithmetic and copies ran while one was open for 2% of the time, Pallas kernels for 20%

profile of v5, /device:TPU:0, one launch (start us, length us, event | category | flops | bytes accessed | tf_op | source)
XLA Modules:
  0.0 59.8 jit_solution(13531989815634586581)
XLA Ops:
  0.0 1.5 %corner_block.1 = f32[128,128]{1,0:T(8,128)} custom-call(f32[4,128,8,128]{3,2,1,0:T(8,128)} %matrix_ref.4), custom_call_target="tpu_custom_call" | custom-call | bytes 3145728 | tf_op jit(solution)/shard_map/corner_block/pallas_call | solution.py:114
  1.5 0.9 %broadcast_in_dim.14 = f32[4,2,64,128]{3,2,1,0:T(8,128)S(1)} broadcast(f32[2,64,128]{2,1,0:T(8,128)} %bitcast.15), dimensions={1,2,3} | broadcast | bytes 327680 | tf_op jit(solution)/shard_map/broadcast_in_dim | solution.py:314
  2.3 11.9 %all_to_all.10 = f32[8,64,128]{2,1,0:T(8,128)S(1)} all-to-all(f32[8,64,128]{2,1,0:T(8,128)S(1)} %bitcast.14), channel_id=1, replica_groups=mesh['row'=8,'col'=4] {'row'}, dimensions={0} | all-to-all | bytes 524288 | tf_op jit(solution)/shard_map/all_to_all | solution.py:315
  14.3 0.0 copy-start
  14.3 1.6 %copy-done = f32[4,128,8,128]{3,2,1,0:T(8,128)S(1)} copy-done((f32[4,128,8,128]{3,2,1,0:T(8,128)S(1)}, f32[4,128,8,128]{3,2,1,0:T(8,128)}, u32[]{:S(2)}) %copy-start) | copy-done | bytes 2097176
  15.8 0.7 %panels.1 = (f32[4,128,128]{2,1,0:T(8,128)S(1)}, f32[8,64,128]{2,1,0:T(8,128)S(1)}, f32[8,64,128]{2,1,0:T(8,128)S(1)}) custom-call(f32[4,128,8,128]{3,2,1,0:T(8,128)S(1)} %copy-done), custom_call_target="tpu_custom_call" | custom-call | bytes 4194304 | tf_op jit(solution)/shard_map/panels/pallas_call | solution.py:142
  16.6 2.7 %collective-permute-start.1 = (f32[4,128,128]{2,1,0:T(8,128)S(1)}, f32[4,128,128]{2,1,0:T(8,128)S(1)}, u32[]{:S(2)}, u32[]{:S(2)}) collective-permute-start(f32[4,128,128]{2,1,0:T(8,128)S(1)} %get-tuple-element.23), channel_id=1, source_target_pairs={{0,2},{1,3},{2,0},{3,1},{4,6},{5,7},{6,4},{7,5},{8,10},{9,11},{10,... | collective-permute-start | bytes 786440 | tf_op jit(solution)/shard_map/ppermute | solution.py:288
  19.2 0.6 collective-permute-start.3
  19.8 0.7 %broadcast_in_dim.15 = f32[4,2,64,128]{3,2,1,0:T(8,128)} broadcast(f32[2,64,128]{2,1,0:T(8,128)S(1)} %slice.21), dimensions={1,2,3} | broadcast | bytes 327680 | tf_op jit(solution)/shard_map/broadcast_in_dim | solution.py:317
  20.5 3.4 %all-to-all-start.1 = ((f32[4,2,64,128]{3,2,1,0:T(8,128)}), f32[4,2,64,128]{3,2,1,0:T(8,128)S(1)}, u32[]{:S(2)}, u32[]{:S(2)}) async-start(f32[4,2,64,128]{3,2,1,0:T(8,128)} %broadcast_in_dim.15), calls=%async_computation.1 | async-start | bytes 524288 | tf_op jit(solution)/shard_map/all_to_all | solution.py:318
  23.9 0.6 %collective-permute-start.5 = (f32[8,64,128]{2,1,0:T(8,128)S(1)}, f32[8,64,128]{2,1,0:T(8,128)S(1)}, u32[]{:S(2)}, u32[]{:S(2)}) collective-permute-start(f32[8,64,128]{2,1,0:T(8,128)S(1)} %get-tuple-element.25), channel_id=1, source_target_pairs={{0,16},{4,20},{8,24},{12,28},{16,0},{20,4},{24,8},{28,12},{1,17},{... | collective-permute-start | bytes 786440 | tf_op jit(solution)/shard_map/ppermute | solution.py:288
  24.6 10.0 %collective-permute-done.1 = f32[4,128,128]{2,1,0:T(8,128)S(1)} collective-permute-done((f32[4,128,128]{2,1,0:T(8,128)S(1)}, f32[4,128,128]{2,1,0:T(8,128)S(1)}, u32[]{:S(2)}, u32[]{:S(2)}) %collective-permute-start.1) | collective-permute-done | bytes 262176 | tf_op jit(solution)/shard_map/ppermute | solution.py:288
  34.6 0.1 collective-permute-start.2
  34.7 0.0 collective-permute-done.3
  34.7 0.6 %collective-permute-start.4 = (f32[8,64,128]{2,1,0:T(8,128)S(1)}, f32[8,64,128]{2,1,0:T(8,128)S(1)}, u32[]{:S(2)}, u32[]{:S(2)}) collective-permute-start(f32[8,64,128]{2,1,0:T(8,128)S(1)} %broadcast_select_fusion.1), channel_id=1, source_target_pairs={{0,16},{4,20},{8,24},{12,28},{16,0},{20,4},{24,8},{28,12},{1,17},{... | collective-permute-start | bytes 786440 | tf_op jit(solution)/shard_map/ppermute | solution.py:288
  35.4 0.9 %all-to-all-done.1 = f32[4,2,64,128]{3,2,1,0:T(8,128)S(1)} async-done(((f32[4,2,64,128]{3,2,1,0:T(8,128)}), f32[4,2,64,128]{3,2,1,0:T(8,128)S(1)}, u32[]{:S(2)}, u32[]{:S(2)}) %all-to-all-start.1) | async-done | bytes 262176 | tf_op jit(solution)/shard_map/all_to_all | solution.py:318
  36.3 0.1 collective-permute-start
  36.4 0.0 collective-permute-done.5
  36.5 1.4 %collective-permute-start.6 = (f32[8,64,128]{2,1,0:T(8,128)S(1)}, f32[8,64,128]{2,1,0:T(8,128)S(1)}, u32[]{:S(2)}, u32[]{:S(2)}) collective-permute-start(f32[8,64,128]{2,1,0:T(8,128)S(1)} %broadcast_select_fusion.2), channel_id=1, source_target_pairs={{0,8},{4,12},{8,0},{12,4},{16,24},{20,28},{24,16},{28,20},{1,9},{5... | collective-permute-start | bytes 786440 | tf_op jit(solution)/shard_map/ppermute | solution.py:288
  37.9 0.0 collective-permute-done
  37.9 0.0 copy-start.1
  37.9 5.0 %first_factor.1 = (f32[128,128]{1,0:T(8,128)S(1)}, f32[128,128]{1,0:T(8,128)S(1)}) custom-call(f32[128,128]{1,0:T(8,128)S(1)} %get-tuple-element.31.a_ref), custom_call_target="tpu_custom_call" | custom-call | flops 8000000000 | bytes 2097152 | tf_op jit(solution)/shard_map/first_factor/pallas_call | solution.py:161
  42.9 0.0 collective-permute-done.4
  43.0 0.3 collective-permute-start.7
  43.3 2.0 %collective-permute-done.6 = f32[8,64,128]{2,1,0:T(8,128)S(1)} collective-permute-done((f32[8,64,128]{2,1,0:T(8,128)S(1)}, f32[8,64,128]{2,1,0:T(8,128)S(1)}, u32[]{:S(2)}, u32[]{:S(2)}) %collective-permute-start.6) | collective-permute-done | bytes 262176 | tf_op jit(solution)/shard_map/ppermute | solution.py:288
  45.3 0.1 collective-permute-start.8
  45.4 0.0 copy-done.1
  45.4 7.2 %second_factor.1 = (f32[128,128]{1,0:T(8,128)S(1)}, f32[256,256]{1,0:T(8,128)S(1)}, f32[256,256]{1,0:T(8,128)S(1)}, f32[8,4,128,128]{3,2,1,0:T(8,128)S(1)}) custom-call(f32[128,128]{1,0:T(8,128)S(1)} %get-tuple-element.32.low_ref, f32[128,128]{1,0:T(8,128)S(1)} %get-tuple-element.30.a_ref, f32[128,128]{1,0:T(8,128)S(1)} %get-tuple-element.18.w0_ref, ...), custom_call_target="tpu_custom_call" | custom-call | flops 8000000000 | bytes 4194304 | tf_op jit(solution)/shard_map/second_factor/pallas_call | solution.py:204
  52.5 0.0 collective-permute-done.2.rows_other_ref
  52.5 0.0 collective-permute-done.7.oa_ref
  52.5 0.0 collective-permute-done.8.ob_ref
  52.6 7.1 %settle.1 = f32[4,128,8,128]{3,2,1,0:T(8,128)} custom-call(f32[128,128]{1,0:T(8,128)S(1)} %get-tuple-element.17.f0_ref, f32[128,128]{1,0:T(8,128)S(1)} %get-tuple-element.19.f1_ref, f32[256,256]{1,0:T(8,128)S(1)} %get-tuple-element.20.w_ref, f32[256,256]{1,0:T(8,128)S(1)} %get-tuple-element.21.mixed_ref, f32[4,128,128]{2,1,0:T(8,128)S(1)} %broadcast_select_fusion.4.rows_ref, ...), custom_call_target="tpu_custom_call" | custom-call | flops 4000000000 | bytes 6291456 | tf_op jit(solution)/shard_map/settle/pallas_call | solution.py:275
  (10 shorter events, 0.2 us)
Async XLA Ops:
  14.3 1.6 %copy-start = (f32[4,128,8,128]{3,2,1,0:T(8,128)S(1)}, f32[4,128,8,128]{3,2,1,0:T(8,128)}, u32[]{:S(2)}) copy-start(f32[4,128,8,128]{3,2,1,0:T(8,128)} %matrix_ref.4) | copy-start | bytes 6291460
  16.6 18.0 %collective-permute-start.1 = (f32[4,128,128]{2,1,0:T(8,128)S(1)}, f32[4,128,128]{2,1,0:T(8,128)S(1)}, u32[]{:S(2)}, u32[]{:S(2)}) collective-permute-start(f32[4,128,128]{2,1,0:T(8,128)S(1)} %get-tuple-element.23), channel_id=1, source_target_pairs={{0,2},{1,3},{2,0},{3,1},{4,6},{5,7},{6,4},{7,5},{8,10},{9,11},{10,... | collective-permute-start | bytes 786440 | tf_op jit(solution)/shard_map/ppermute | solution.py:288
  19.2 15.5 %collective-permute-start.3 = (f32[8,64,128]{2,1,0:T(8,128)S(1)}, f32[8,64,128]{2,1,0:T(8,128)S(1)}, u32[]{:S(2)}, u32[]{:S(2)}) collective-permute-start(f32[8,64,128]{2,1,0:T(8,128)S(1)} %get-tuple-element.24), channel_id=1, source_target_pairs={{0,8},{4,12},{8,0},{12,4},{16,24},{20,28},{24,16},{28,20},{1,9},{5... | collective-permute-start | bytes 786440 | tf_op jit(solution)/shard_map/ppermute | solution.py:288
  20.5 15.8 %all-to-all-start.1 = ((f32[4,2,64,128]{3,2,1,0:T(8,128)}), f32[4,2,64,128]{3,2,1,0:T(8,128)S(1)}, u32[]{:S(2)}, u32[]{:S(2)}) async-start(f32[4,2,64,128]{3,2,1,0:T(8,128)} %broadcast_in_dim.15), calls=%async_computation.1 | async-start | bytes 524288 | tf_op jit(solution)/shard_map/all_to_all | solution.py:318
  23.9 12.5 %collective-permute-start.5 = (f32[8,64,128]{2,1,0:T(8,128)S(1)}, f32[8,64,128]{2,1,0:T(8,128)S(1)}, u32[]{:S(2)}, u32[]{:S(2)}) collective-permute-start(f32[8,64,128]{2,1,0:T(8,128)S(1)} %get-tuple-element.25), channel_id=1, source_target_pairs={{0,16},{4,20},{8,24},{12,28},{16,0},{20,4},{24,8},{28,12},{1,17},{... | collective-permute-start | bytes 786440 | tf_op jit(solution)/shard_map/ppermute | solution.py:288
  34.6 17.9 %collective-permute-start.2 = (f32[4,128,128]{2,1,0:T(8,128)S(1)}, f32[4,128,128]{2,1,0:T(8,128)S(1)}, u32[]{:S(2)}, u32[]{:S(2)}) collective-permute-start(f32[4,128,128]{2,1,0:T(8,128)S(1)} %broadcast_select_fusion.4.rows_ref), channel_id=1, source_target_pairs={{0,1},{1,0},{2,3},{3,2},{4,5},{5,4},{6,7},{7,6},{8,9},{9,8},{10,11... | collective-permute-start | bytes 786440 | tf_op jit(solution)/shard_map/ppermute | solution.py:288
  34.7 8.2 %collective-permute-start.4 = (f32[8,64,128]{2,1,0:T(8,128)S(1)}, f32[8,64,128]{2,1,0:T(8,128)S(1)}, u32[]{:S(2)}, u32[]{:S(2)}) collective-permute-start(f32[8,64,128]{2,1,0:T(8,128)S(1)} %broadcast_select_fusion.1), channel_id=1, source_target_pairs={{0,16},{4,20},{8,24},{12,28},{16,0},{20,4},{24,8},{28,12},{1,17},{... | collective-permute-start | bytes 786440 | tf_op jit(solution)/shard_map/ppermute | solution.py:288
  36.3 1.5 %collective-permute-start = (f32[3,64,128]{2,1,0:T(8,128)S(1)}, f32[3,64,128]{2,1,0:T(8,128)S(1)}, u32[]{:S(2)}, u32[]{:S(2)}) collective-permute-start(f32[3,64,128]{2,1,0:T(8,128)S(1)} %pad_maximum_fusion), channel_id=1, source_target_pairs={{0,4},{4,0},{8,12},{12,8},{16,20},{20,16},{24,28},{28,24},{1,5},{5... | collective-permute-start | bytes 294920 | tf_op jit(solution)/shard_map/ppermute | solution.py:288
  36.5 8.8 %collective-permute-start.6 = (f32[8,64,128]{2,1,0:T(8,128)S(1)}, f32[8,64,128]{2,1,0:T(8,128)S(1)}, u32[]{:S(2)}, u32[]{:S(2)}) collective-permute-start(f32[8,64,128]{2,1,0:T(8,128)S(1)} %broadcast_select_fusion.2), channel_id=1, source_target_pairs={{0,8},{4,12},{8,0},{12,4},{16,24},{20,28},{24,16},{28,20},{1,9},{5... | collective-permute-start | bytes 786440 | tf_op jit(solution)/shard_map/ppermute | solution.py:288
  37.9 7.4 %copy-start.1 = (f32[4,128,8,128]{3,2,1,0:T(8,128)S(1)}, f32[4,128,8,128]{3,2,1,0:T(8,128)}, u32[]{:S(2)}) copy-start(f32[4,128,8,128]{3,2,1,0:T(8,128)} %matrix_ref.4) | copy-start | bytes 6291460
  43.0 9.5 %collective-permute-start.7 = (f32[8,64,128]{2,1,0:T(8,128)S(1)}, f32[8,64,128]{2,1,0:T(8,128)S(1)}, u32[]{:S(2)}, u32[]{:S(2)}) collective-permute-start(f32[8,64,128]{2,1,0:T(8,128)S(1)} %broadcast_select_fusion.3.ha_ref), channel_id=1, source_target_pairs={{0,4},{4,0},{8,12},{12,8},{16,20},{20,16},{24,28},{28,24},{1,5},{5... | collective-permute-start | bytes 786440 | tf_op jit(solution)/shard_map/ppermute | solution.py:288
  45.3 7.3 %collective-permute-start.8 = (f32[8,64,128]{2,1,0:T(8,128)S(1)}, f32[8,64,128]{2,1,0:T(8,128)S(1)}, u32[]{:S(2)}, u32[]{:S(2)}) collective-permute-start(f32[8,64,128]{2,1,0:T(8,128)S(1)} %broadcast_select_fusion.hb_ref), channel_id=1, source_target_pairs={{0,4},{4,0},{8,12},{12,8},{16,20},{20,16},{24,28},{28,24},{1,5},{5... | collective-permute-start | bytes 786440 | tf_op jit(solution)/shard_map/ppermute | solution.py:288

commit v6 on v5

--- a/solution.py
+++ b/solution.py
@@ -103,23 +103,29 @@
     return pl.CostEstimate(flops=flops, bytes_accessed=nbytes, transcendentals=0)
 
 
-def corner_kernel(matrix_ref, block_ref, sem):
-    copy = pltpu.make_async_copy(matrix_ref.at[0, :, 0, :], block_ref, sem)
-    copy.start()
-    copy.wait()
-
-
-def corner_block(matrix):
+def corner_kernel(matrix_ref, own_ref, send_ref, sems):
+    half = own_ref.shape[0]
+    odd = lax.rem(lax.axis_index("row"), 2)
+    own = pltpu.make_async_copy(matrix_ref.at[0, pl.ds(odd * half, half), 0, :], own_ref, sems.at[0])
+    send = pltpu.make_async_copy(matrix_ref.at[0, pl.ds((1 - odd) * half, half), 0, :], send_ref, sems.at[1])
+    send.start()
+    own.start()
+    send.wait()
+    own.wait()
+
+
+def corner_halves(matrix):
     n = matrix.shape[1]
+    half = jax.ShapeDtypeStruct((n // 2, n), jnp.float32)
     return pl.pallas_call(
         corner_kernel,
-        out_shape=jax.ShapeDtypeStruct((n, n), jnp.float32),
+        out_shape=[half, half],
         in_specs=[HBM],
-        out_specs=VMEM,
-        scratch_shapes=[pltpu.SemaphoreType.DMA(())],
-        compiler_params=pltpu.CompilerParams(vmem_limit_bytes=62 * MIB),
+        out_specs=[VMEM, VMEM],
+        scratch_shapes=[pltpu.SemaphoreType.DMA((2,))],
+        compiler_params=pltpu.CompilerParams(vmem_limit_bytes=2 * MIB),
         cost_estimate=estimate(0, 3 * MIB),
-        name="corner_block",
+        name="corner_halves",
     )(matrix)
 
 
@@ -299,36 +305,47 @@
     return held
 
 
+def after(value, *others):
+    return lax.optimization_barrier((value,) + others)
+
+
 def shards(kernel):
     grid_row = lax.axis_index("row")
     grid_col = lax.axis_index("col")
     n_row = lax.axis_size("row")
     n_col = lax.axis_size("col")
-    n = kernel.shape[1]
-    half = n // 2
     row_bits = list(range(1, n_row.bit_length() - 1))
     col_bits = list(range(1, n_col.bit_length() - 1))
     odd = (grid_row % 2) == 1
-
-    block = corner_block(kernel)
-    halves = jnp.broadcast_to(block.reshape(1, 2, half, n), (n_row // 2, 2, half, n)).reshape(n_row, half, n)
-    over_row = lax.all_to_all(halves, "row", 0, 0)
-    kernel_then, over_row = lax.optimization_barrier((kernel, over_row))
-    pair = jnp.broadcast_to(over_row[None, :2], (n_col, 2, half, n))
-    over_col = lax.all_to_all(pair, "col", 0, 0)
-    mine = jnp.stack([over_col[0, 0], over_col[0, 1], over_col[1, 1]])
+    right = (grid_col % 2) == 1
+
+    own, send = corner_halves(kernel)
+    got = exchange(send, "row", 1, n_row)
+    pair = jnp.stack([jnp.where(odd != right, got, own), jnp.where(odd, own, got)])
+    column, upper, lower = panels(kernel)
+    pair = spread(pair, "row", grid_row, n_row, row_bits)
+    pair, upper, lower = after(pair, upper, lower)
+    pair = spread(pair, "col", grid_col, n_col, col_bits)
+    ha = spread(upper, "row", grid_row, n_row, row_bits[:1])
+    hb = spread(lower, "row", grid_row, n_row, row_bits[:0:-1])
+    pair_far = exchange(pair, "col", 1, n_col)
+    pair_far, column = after(pair_far, column)
+    rows = spread(column, "col", grid_col, n_col, col_bits[:1])
+    mine = jnp.stack([jnp.where(right, pair_far[0], pair[0]), jnp.where(right, pair_far[1], pair[1]),
+                      jnp.where(right, pair[0], pair_far[0])])
     other = exchange(mine, "row", 1, n_row)
-
-    column, upper, lower = panels(kernel_then)
-    ha = spread(upper, "row", grid_row, n_row, row_bits)
-    hb = spread(lower, "row", grid_row, n_row, row_bits[::-1])
-    rows = spread(column, "col", grid_col, n_col, col_bits)
+    mine, other, ha, hb = after(mine, other, ha, hb)
+
+    ha = spread(ha, "row", grid_row, n_row, row_bits[1:])
+    hb = spread(hb, "row", grid_row, n_row, row_bits[:1])
+    whole = jnp.concatenate([jnp.where(odd, other, mine), jnp.where(odd, mine, other)], axis=1)
+    f0, w0 = first_factor(whole[0])
+    w0, rows, ha, hb = after(w0, rows, ha, hb)
+    rows = spread(rows, "col", grid_col, n_col, col_bits[1:])
     oa = exchange(ha, "row", 1, n_row)
     ob = exchange(hb, "row", 1, n_row)
     rows_other = exchange(rows, "col", 1, n_col)
 
-    whole = jnp.concatenate([jnp.where(odd, other, mine), jnp.where(odd, mine, other)], axis=1)
-    f0, w0 = first_factor(whole[0])
     f1, w, mixed, blocks = second_factor(whole[1], whole[2], w0, kernel)
     return settle(f0, f1, w, mixed, rows, rows_other, ha, hb, oa, ob, blocks)
 

time: 60.2 us -> 57.8 us (0.960)
  blocking collectives: 11.9 us -> 0 us
  starting transfers between devices: 9.77 us -> 21.1 us
  local copies, waits for them, and re-layouts: 3.19 us -> 1.59 us
  waiting for transfers between devices: 13 us -> 14.4 us
  Pallas kernels: 21.4 us -> 20 us
    ppermute x9 -> x14, starting transfers between devices: 6.36 us -> 21.1 us  [exchange(): return lax.ppermute(value, axis, [(i, i ^ mask) for i in range(size)])]
    all_to_all x1 -> x0, blocking collectives: 11.9 us -> none  [shards(): over_row = lax.all_to_all(halves, 'row', 0, 0)]
    all_to_all x1 -> x0, starting transfers between devices: 3.41 us -> none  [shards(): over_col = lax.all_to_all(pair, 'col', 0, 0)]
    ppermute x9 -> x14, waiting for transfers between devices: 12 us -> 14.4 us  [exchange(): return lax.ppermute(value, axis, [(i, i ^ mask) for i in range(size)])]
    broadcast_in_dim x2 -> x0, local copies, waits for them, and re-layouts: 1.58 us -> none  [the longest x1 0.86 us: shards(): jnp.broadcast_to(block.reshape(1, 2, half, n), (n_row // 2, 2, half, n))]
    pallas_call x1, Pallas kernels: 1.48 us -> 0.07 us  [corner_halves(): pl.pallas_call(corner_kernel, out_shape=[half, half], in_specs=[HBM], out...]
    all_to_all x1 -> x0, waiting for transfers between devices: 0.95 us -> none  [shards(): over_col = lax.all_to_all(pair, 'col', 0, 0)]
  transfers between devices with their start and end apart: 10 -> 14, of which waited for: 3 -> 7; matrix products, arithmetic and copies ran while one was open for 2% -> 0% of each run, Pallas kernels for 20% -> 23%
where the time goes in v6:
time: 57.8 us; the launch traced here: 57.7 us
  starting transfers between devices  21.1 us (37%)
  Pallas kernels  20 us (35%)
  waiting for transfers between devices  14.4 us (25%)
  local copies, waits for them, and re-layouts  1.59 us (3%)
    ppermute x14, starting transfers between devices, exchange(): return lax.ppermute(value, axis, [(i, i ^ mask) for i in range(size)])  21.1 us
    ppermute x14, waiting for transfers between devices, exchange(): return lax.ppermute(value, axis, [(i, i ^ mask) for i in range(size)])  14.4 us
    pallas_call x1, Pallas kernels, second_factor(): pl.pallas_call(second_factor_kernel, out_shape=[square, double, double, b...  7.33 us
    pallas_call x1, Pallas kernels, settle(): pl.pallas_call(settle_kernel, out_shape=jax.ShapeDtypeStruct((local_rows,...  6.9 us
    pallas_call x1, Pallas kernels, first_factor(): pl.pallas_call(first_factor_kernel, out_shape=[square, square], in_specs=...  5 us
    unnamed x4, local copies, waits for them, and re-layouts  1.59 us
  transfers between devices with their start and end apart: 14, of which 7 were waited for; matrix products, arithmetic and copies ran while one was open for 0% of the time, Pallas kernels for 23%

profile of v6, /device:TPU:0, one launch (start us, length us, event | category | flops | bytes accessed | tf_op | source)
XLA Modules:
  0.0 57.7 jit_solution(5558226991063895115)
XLA Ops:
  0.0 0.0 copy-start
  0.0 1.6 %copy-done = f32[4,128,8,128]{3,2,1,0:T(8,128)S(1)} copy-done((f32[4,128,8,128]{3,2,1,0:T(8,128)S(1)}, f32[4,128,8,128]{3,2,1,0:T(8,128)}, u32[]{:S(2)}) %copy-start) | copy-done | bytes 2097176
  1.6 0.0 copy-start.1
  1.6 0.1 corner_halves.1
  1.7 0.5 collective-permute-start
  2.2 0.9 %collective-permute-done = f32[64,128]{1,0:T(8,128)S(1)} collective-permute-done((f32[64,128]{1,0:T(8,128)S(1)}, f32[64,128]{1,0:T(8,128)S(1)}, u32[]{:S(2)}, u32[]{:S(2)}) %collective-permute-start) | collective-permute-done | bytes 32800 | tf_op jit(solution)/shard_map/ppermute | solution.py:294
  3.1 2.9 %collective-permute-start.1 = (f32[2,64,128]{2,1,0:T(8,128)S(1)}, f32[2,64,128]{2,1,0:T(8,128)S(1)}, u32[]{:S(2)}, u32[]{:S(2)}) collective-permute-start(f32[2,64,128]{2,1,0:T(8,128)S(1)} %pad_maximum_fusion.2), channel_id=1, source_target_pairs={{0,8},{4,12},{8,0},{12,4},{16,24},{20,28},{24,16},{28,20},{1,9},{5... | collective-permute-start | bytes 196616 | tf_op jit(solution)/shard_map/ppermute | solution.py:294
  6.0 2.4 %collective-permute-done.1 = f32[2,64,128]{2,1,0:T(8,128)S(1)} collective-permute-done((f32[2,64,128]{2,1,0:T(8,128)S(1)}, f32[2,64,128]{2,1,0:T(8,128)S(1)}, u32[]{:S(2)}, u32[]{:S(2)}) %collective-permute-start.1) | collective-permute-done | bytes 65568 | tf_op jit(solution)/shard_map/ppermute | solution.py:294
  8.4 1.9 %collective-permute-start.2 = (f32[2,64,128]{2,1,0:T(8,128)S(1)}, f32[2,64,128]{2,1,0:T(8,128)S(1)}, u32[]{:S(2)}, u32[]{:S(2)}) collective-permute-start(f32[2,64,128]{2,1,0:T(8,128)S(1)} %broadcast_select_fusion.7), channel_id=1, source_target_pairs={{0,16},{4,20},{8,24},{12,28},{16,0},{20,4},{24,8},{28,12},{1,17},{... | collective-permute-start | bytes 196616 | tf_op jit(solution)/shard_map/ppermute | solution.py:294
  10.3 0.0 copy-done.1
  10.3 0.7 %panels.1 = (f32[4,128,128]{2,1,0:T(8,128)S(1)}, f32[8,64,128]{2,1,0:T(8,128)S(1)}, f32[8,64,128]{2,1,0:T(8,128)S(1)}) custom-call(f32[4,128,8,128]{3,2,1,0:T(8,128)S(1)} %copy-done.1), custom_call_target="tpu_custom_call" | custom-call | bytes 4194304 | tf_op jit(solution)/shard_map/panels/pallas_call | solution.py:148
  11.1 1.6 %collective-permute-done.2 = f32[2,64,128]{2,1,0:T(8,128)S(1)} collective-permute-done((f32[2,64,128]{2,1,0:T(8,128)S(1)}, f32[2,64,128]{2,1,0:T(8,128)S(1)}, u32[]{:S(2)}, u32[]{:S(2)}) %collective-permute-start.2) | collective-permute-done | bytes 65568 | tf_op jit(solution)/shard_map/ppermute | solution.py:294
  12.7 3.0 %collective-permute-start.3 = (f32[2,64,128]{2,1,0:T(8,128)S(1)}, f32[2,64,128]{2,1,0:T(8,128)S(1)}, u32[]{:S(2)}, u32[]{:S(2)}) collective-permute-start(f32[2,64,128]{2,1,0:T(8,128)S(1)} %broadcast_select_fusion.8), channel_id=1, source_target_pairs={{0,2},{1,3},{2,0},{3,1},{4,6},{5,7},{6,4},{7,5},{8,10},{9,11},{10,... | collective-permute-start | bytes 196616 | tf_op jit(solution)/shard_map/ppermute | solution.py:294
  15.8 2.4 %collective-permute-done.3 = f32[2,64,128]{2,1,0:T(8,128)S(1)} collective-permute-done((f32[2,64,128]{2,1,0:T(8,128)S(1)}, f32[2,64,128]{2,1,0:T(8,128)S(1)}, u32[]{:S(2)}, u32[]{:S(2)}) %collective-permute-start.3) | collective-permute-done | bytes 65568 | tf_op jit(solution)/shard_map/ppermute | solution.py:294
  18.2 1.8 %collective-permute-start.4 = (f32[2,64,128]{2,1,0:T(8,128)S(1)}, f32[2,64,128]{2,1,0:T(8,128)S(1)}, u32[]{:S(2)}, u32[]{:S(2)}) collective-permute-start(f32[2,64,128]{2,1,0:T(8,128)S(1)} %broadcast_select_fusion.9), channel_id=1, source_target_pairs={{0,1},{1,0},{2,3},{3,2},{4,5},{5,4},{6,7},{7,6},{8,9},{9,8},{10,11... | collective-permute-start | bytes 196616 | tf_op jit(solution)/shard_map/ppermute | solution.py:294
  20.0 1.5 %collective-permute-start.6 = (f32[8,64,128]{2,1,0:T(8,128)S(1)}, f32[8,64,128]{2,1,0:T(8,128)S(1)}, u32[]{:S(2)}, u32[]{:S(2)}) collective-permute-start(f32[8,64,128]{2,1,0:T(8,128)S(1)} %get-tuple-element.36), channel_id=1, source_target_pairs={{0,8},{4,12},{8,0},{12,4},{16,24},{20,28},{24,16},{28,20},{1,9},{5... | collective-permute-start | bytes 786440 | tf_op jit(solution)/shard_map/ppermute | solution.py:294
  21.5 1.5 %collective-permute-start.7 = (f32[8,64,128]{2,1,0:T(8,128)S(1)}, f32[8,64,128]{2,1,0:T(8,128)S(1)}, u32[]{:S(2)}, u32[]{:S(2)}) collective-permute-start(f32[8,64,128]{2,1,0:T(8,128)S(1)} %get-tuple-element.37), channel_id=1, source_target_pairs={{0,16},{4,20},{8,24},{12,28},{16,0},{20,4},{24,8},{28,12},{1,17},{... | collective-permute-start | bytes 786440 | tf_op jit(solution)/shard_map/ppermute | solution.py:294
  23.0 0.0 collective-permute-done.4
  23.0 0.1 collective-permute-start.5
  23.1 3.4 %collective-permute-start.8 = (f32[4,128,128]{2,1,0:T(8,128)S(1)}, f32[4,128,128]{2,1,0:T(8,128)S(1)}, u32[]{:S(2)}, u32[]{:S(2)}) collective-permute-start(f32[4,128,128]{2,1,0:T(8,128)S(1)} %get-tuple-element.42), channel_id=1, source_target_pairs={{0,2},{1,3},{2,0},{3,1},{4,6},{5,7},{6,4},{7,5},{8,10},{9,11},{10,... | collective-permute-start | bytes 786440 | tf_op jit(solution)/shard_map/ppermute | solution.py:294
  26.5 0.0 collective-permute-done.6
  26.5 1.3 %collective-permute-done.7 = f32[8,64,128]{2,1,0:T(8,128)S(1)} collective-permute-done((f32[8,64,128]{2,1,0:T(8,128)S(1)}, f32[8,64,128]{2,1,0:T(8,128)S(1)}, u32[]{:S(2)}, u32[]{:S(2)}) %collective-permute-start.7) | collective-permute-done | bytes 262176 | tf_op jit(solution)/shard_map/ppermute | solution.py:294
  27.9 0.0 collective-permute-done.5
  27.9 1.6 %collective-permute-start.9 = (f32[8,64,128]{2,1,0:T(8,128)S(1)}, f32[8,64,128]{2,1,0:T(8,128)S(1)}, u32[]{:S(2)}, u32[]{:S(2)}) collective-permute-start(f32[8,64,128]{2,1,0:T(8,128)S(1)} %broadcast_select_fusion.4), channel_id=1, source_target_pairs={{0,16},{4,20},{8,24},{12,28},{16,0},{20,4},{24,8},{28,12},{1,17},{... | collective-permute-start | bytes 786440 | tf_op jit(solution)/shard_map/ppermute | solution.py:294
  29.5 5.0 %first_factor.1 = (f32[128,128]{1,0:T(8,128)S(1)}, f32[128,128]{1,0:T(8,128)S(1)}) custom-call(f32[128,128]{1,0:T(8,128)S(1)} %get-tuple-element.54.a_ref), custom_call_target="tpu_custom_call" | custom-call | flops 8000000000 | bytes 2097152 | tf_op jit(solution)/shard_map/first_factor/pallas_call | solution.py:167
  34.5 0.6 %collective-permute-start.10 = (f32[8,64,128]{2,1,0:T(8,128)S(1)}, f32[8,64,128]{2,1,0:T(8,128)S(1)}, u32[]{:S(2)}, u32[]{:S(2)}) collective-permute-start(f32[8,64,128]{2,1,0:T(8,128)S(1)} %broadcast_select_fusion.2), channel_id=1, source_target_pairs={{0,8},{4,12},{8,0},{12,4},{16,24},{20,28},{24,16},{28,20},{1,9},{5... | collective-permute-start | bytes 786440 | tf_op jit(solution)/shard_map/ppermute | solution.py:294
  35.1 3.9 %collective-permute-done.8 = f32[4,128,128]{2,1,0:T(8,128)S(1)} collective-permute-done((f32[4,128,128]{2,1,0:T(8,128)S(1)}, f32[4,128,128]{2,1,0:T(8,128)S(1)}, u32[]{:S(2)}, u32[]{:S(2)}) %collective-permute-start.8) | collective-permute-done | bytes 262176 | tf_op jit(solution)/shard_map/ppermute | solution.py:294
  39.0 0.0 collective-permute-done.9
  39.1 1.9 %collective-permute-done.10 = f32[8,64,128]{2,1,0:T(8,128)S(1)} collective-permute-done((f32[8,64,128]{2,1,0:T(8,128)S(1)}, f32[8,64,128]{2,1,0:T(8,128)S(1)}, u32[]{:S(2)}, u32[]{:S(2)}) %collective-permute-start.10) | collective-permute-done | bytes 262176 | tf_op jit(solution)/shard_map/ppermute | solution.py:294
  41.0 1.7 %collective-permute-start.11 = (f32[4,128,128]{2,1,0:T(8,128)S(1)}, f32[4,128,128]{2,1,0:T(8,128)S(1)}, u32[]{:S(2)}, u32[]{:S(2)}) collective-permute-start(f32[4,128,128]{2,1,0:T(8,128)S(1)} %broadcast_select_fusion.rows_ref), channel_id=1, source_target_pairs={{0,1},{1,0},{2,3},{3,2},{4,5},{5,4},{6,7},{7,6},{8,9},{9,8},{10,11... | collective-permute-start | bytes 786440 | tf_op jit(solution)/shard_map/ppermute | solution.py:294
  42.7 0.0 collective-permute-start.12
  42.7 0.5 collective-permute-start.13
  43.2 7.3 %second_factor.1 = (f32[128,128]{1,0:T(8,128)S(1)}, f32[256,256]{1,0:T(8,128)S(1)}, f32[256,256]{1,0:T(8,128)S(1)}, f32[8,4,128,128]{3,2,1,0:T(8,128)S(1)}) custom-call(f32[128,128]{1,0:T(8,128)S(1)} %get-tuple-element.55.low_ref, f32[128,128]{1,0:T(8,128)S(1)} %get-tuple-element.53.a_ref, f32[128,128]{1,0:T(8,128)S(1)} %get-tuple-element.45.w0_ref, ...), custom_call_target="tpu_custom_call" | custom-call | flops 8000000000 | bytes 4194304 | tf_op jit(solution)/shard_map/second_factor/pallas_call | solution.py:210
  50.6 0.0 collective-permute-done.11.rows_other_ref
  50.6 0.0 collective-permute-done.12.oa_ref
  50.6 0.0 collective-permute-done.13.ob_ref
  50.6 6.9 %settle.1 = f32[4,128,8,128]{3,2,1,0:T(8,128)} custom-call(f32[128,128]{1,0:T(8,128)S(1)} %get-tuple-element.40.f0_ref, f32[128,128]{1,0:T(8,128)S(1)} %get-tuple-element.46.f1_ref, f32[256,256]{1,0:T(8,128)S(1)} %get-tuple-element.47.w_ref, f32[256,256]{1,0:T(8,128)S(1)} %get-tuple-element.48.mixed_ref, f32[4,128,128]{2,1,0:T(8,128)S(1)} %broadcast_select_fusion.rows_ref, ...), custom_call_target="tpu_custom_call" | custom-call | flops 4000000000 | bytes 6291456 | tf_op jit(solution)/shard_map/settle/pallas_call | solution.py:281
  (14 shorter events, 0.3 us)
Async XLA Ops:
  0.0 1.6 %copy-start = (f32[4,128,8,128]{3,2,1,0:T(8,128)S(1)}, f32[4,128,8,128]{3,2,1,0:T(8,128)}, u32[]{:S(2)}) copy-start(f32[4,128,8,128]{3,2,1,0:T(8,128)} %matrix_ref.5) | copy-start | bytes 6291460
  1.6 8.8 %copy-start.1 = (f32[4,128,8,128]{3,2,1,0:T(8,128)S(1)}, f32[4,128,8,128]{3,2,1,0:T(8,128)}, u32[]{:S(2)}) copy-start(f32[4,128,8,128]{3,2,1,0:T(8,128)} %matrix_ref.5) | copy-start | bytes 6291460
  1.7 1.4 %collective-permute-start = (f32[64,128]{1,0:T(8,128)S(1)}, f32[64,128]{1,0:T(8,128)S(1)}, u32[]{:S(2)}, u32[]{:S(2)}) collective-permute-start(f32[64,128]{1,0:T(8,128)S(1)} %get-tuple-element.29), channel_id=1, source_target_pairs={{0,4},{4,0},{8,12},{12,8},{16,20},{20,16},{24,28},{28,24},{1,5},{5... | collective-permute-start | bytes 98312 | tf_op jit(solution)/shard_map/ppermute | solution.py:294
  3.1 5.3 %collective-permute-start.1 = (f32[2,64,128]{2,1,0:T(8,128)S(1)}, f32[2,64,128]{2,1,0:T(8,128)S(1)}, u32[]{:S(2)}, u32[]{:S(2)}) collective-permute-start(f32[2,64,128]{2,1,0:T(8,128)S(1)} %pad_maximum_fusion.2), channel_id=1, source_target_pairs={{0,8},{4,12},{8,0},{12,4},{16,24},{20,28},{24,16},{28,20},{1,9},{5... | collective-permute-start | bytes 196616 | tf_op jit(solution)/shard_map/ppermute | solution.py:294
  8.4 4.3 %collective-permute-start.2 = (f32[2,64,128]{2,1,0:T(8,128)S(1)}, f32[2,64,128]{2,1,0:T(8,128)S(1)}, u32[]{:S(2)}, u32[]{:S(2)}) collective-permute-start(f32[2,64,128]{2,1,0:T(8,128)S(1)} %broadcast_select_fusion.7), channel_id=1, source_target_pairs={{0,16},{4,20},{8,24},{12,28},{16,0},{20,4},{24,8},{28,12},{1,17},{... | collective-permute-start | bytes 196616 | tf_op jit(solution)/shard_map/ppermute | solution.py:294
  12.7 5.4 %collective-permute-start.3 = (f32[2,64,128]{2,1,0:T(8,128)S(1)}, f32[2,64,128]{2,1,0:T(8,128)S(1)}, u32[]{:S(2)}, u32[]{:S(2)}) collective-permute-start(f32[2,64,128]{2,1,0:T(8,128)S(1)} %broadcast_select_fusion.8), channel_id=1, source_target_pairs={{0,2},{1,3},{2,0},{3,1},{4,6},{5,7},{6,4},{7,5},{8,10},{9,11},{10,... | collective-permute-start | bytes 196616 | tf_op jit(solution)/shard_map/ppermute | solution.py:294
  18.2 4.8 %collective-permute-start.4 = (f32[2,64,128]{2,1,0:T(8,128)S(1)}, f32[2,64,128]{2,1,0:T(8,128)S(1)}, u32[]{:S(2)}, u32[]{:S(2)}) collective-permute-start(f32[2,64,128]{2,1,0:T(8,128)S(1)} %broadcast_select_fusion.9), channel_id=1, source_target_pairs={{0,1},{1,0},{2,3},{3,2},{4,5},{5,4},{6,7},{7,6},{8,9},{9,8},{10,11... | collective-permute-start | bytes 196616 | tf_op jit(solution)/shard_map/ppermute | solution.py:294
  20.0 6.5 %collective-permute-start.6 = (f32[8,64,128]{2,1,0:T(8,128)S(1)}, f32[8,64,128]{2,1,0:T(8,128)S(1)}, u32[]{:S(2)}, u32[]{:S(2)}) collective-permute-start(f32[8,64,128]{2,1,0:T(8,128)S(1)} %get-tuple-element.36), channel_id=1, source_target_pairs={{0,8},{4,12},{8,0},{12,4},{16,24},{20,28},{24,16},{28,20},{1,9},{5... | collective-permute-start | bytes 786440 | tf_op jit(solution)/shard_map/ppermute | solution.py:294
  21.5 6.4 %collective-permute-start.7 = (f32[8,64,128]{2,1,0:T(8,128)S(1)}, f32[8,64,128]{2,1,0:T(8,128)S(1)}, u32[]{:S(2)}, u32[]{:S(2)}) collective-permute-start(f32[8,64,128]{2,1,0:T(8,128)S(1)} %get-tuple-element.37), channel_id=1, source_target_pairs={{0,16},{4,20},{8,24},{12,28},{16,0},{20,4},{24,8},{28,12},{1,17},{... | collective-permute-start | bytes 786440 | tf_op jit(solution)/shard_map/ppermute | solution.py:294
  23.0 4.9 %collective-permute-start.5 = (f32[3,64,128]{2,1,0:T(8,128)S(1)}, f32[3,64,128]{2,1,0:T(8,128)S(1)}, u32[]{:S(2)}, u32[]{:S(2)}) collective-permute-start(f32[3,64,128]{2,1,0:T(8,128)S(1)} %pad_maximum_fusion), channel_id=1, source_target_pairs={{0,4},{4,0},{8,12},{12,8},{16,20},{20,16},{24,28},{28,24},{1,5},{5... | collective-permute-start | bytes 294920 | tf_op jit(solution)/shard_map/ppermute | solution.py:294
  23.1 15.9 %collective-permute-start.8 = (f32[4,128,128]{2,1,0:T(8,128)S(1)}, f32[4,128,128]{2,1,0:T(8,128)S(1)}, u32[]{:S(2)}, u32[]{:S(2)}) collective-permute-start(f32[4,128,128]{2,1,0:T(8,128)S(1)} %get-tuple-element.42), channel_id=1, source_target_pairs={{0,2},{1,3},{2,0},{3,1},{4,6},{5,7},{6,4},{7,5},{8,10},{9,11},{10,... | collective-permute-start | bytes 786440 | tf_op jit(solution)/shard_map/ppermute | solution.py:294
  27.9 11.1 %collective-permute-start.9 = (f32[8,64,128]{2,1,0:T(8,128)S(1)}, f32[8,64,128]{2,1,0:T(8,128)S(1)}, u32[]{:S(2)}, u32[]{:S(2)}) collective-permute-start(f32[8,64,128]{2,1,0:T(8,128)S(1)} %broadcast_select_fusion.4), channel_id=1, source_target_pairs={{0,16},{4,20},{8,24},{12,28},{16,0},{20,4},{24,8},{28,12},{1,17},{... | collective-permute-start | bytes 786440 | tf_op jit(solution)/shard_map/ppermute | solution.py:294
  34.5 6.4 %collective-permute-start.10 = (f32[8,64,128]{2,1,0:T(8,128)S(1)}, f32[8,64,128]{2,1,0:T(8,128)S(1)}, u32[]{:S(2)}, u32[]{:S(2)}) collective-permute-start(f32[8,64,128]{2,1,0:T(8,128)S(1)} %broadcast_select_fusion.2), channel_id=1, source_target_pairs={{0,8},{4,12},{8,0},{12,4},{16,24},{20,28},{24,16},{28,20},{1,9},{5... | collective-permute-start | bytes 786440 | tf_op jit(solution)/shard_map/ppermute | solution.py:294
  41.0 9.6 %collective-permute-start.11 = (f32[4,128,128]{2,1,0:T(8,128)S(1)}, f32[4,128,128]{2,1,0:T(8,128)S(1)}, u32[]{:S(2)}, u32[]{:S(2)}) collective-permute-start(f32[4,128,128]{2,1,0:T(8,128)S(1)} %broadcast_select_fusion.rows_ref), channel_id=1, source_target_pairs={{0,1},{1,0},{2,3},{3,2},{4,5},{5,4},{6,7},{7,6},{8,9},{9,8},{10,11... | collective-permute-start | bytes 786440 | tf_op jit(solution)/shard_map/ppermute | solution.py:294
  42.7 7.9 %collective-permute-start.12 = (f32[8,64,128]{2,1,0:T(8,128)S(1)}, f32[8,64,128]{2,1,0:T(8,128)S(1)}, u32[]{:S(2)}, u32[]{:S(2)}) collective-permute-start(f32[8,64,128]{2,1,0:T(8,128)S(1)} %broadcast_select_fusion.1.ha_ref), channel_id=1, source_target_pairs={{0,4},{4,0},{8,12},{12,8},{16,20},{20,16},{24,28},{28,24},{1,5},{5... | collective-permute-start | bytes 786440 | tf_op jit(solution)/shard_map/ppermute | solution.py:294
  42.7 7.9 %collective-permute-start.13 = (f32[8,64,128]{2,1,0:T(8,128)S(1)}, f32[8,64,128]{2,1,0:T(8,128)S(1)}, u32[]{:S(2)}, u32[]{:S(2)}) collective-permute-start(f32[8,64,128]{2,1,0:T(8,128)S(1)} %broadcast_select_fusion.3.hb_ref), channel_id=1, source_target_pairs={{0,4},{4,0},{8,12},{12,8},{16,20},{20,16},{24,28},{28,24},{1,5},{5... | collective-permute-start | bytes 786440 | tf_op jit(solution)/shard_map/ppermute | solution.py:294

commit v7 on v6

--- a/solution.py
+++ b/solution.py
@@ -80,10 +80,6 @@
     return upper.T, aug[...].reshape(n, n)
 
 
-def is_odd_row():
-    return lax.rem(lax.axis_index("row"), 2) == 1
-
-
 def parts(x):
     high = x.astype(jnp.bfloat16)
     rest = x - high.astype(jnp.float32)
@@ -176,14 +172,13 @@
     )(a)
 
 
-def second_factor_kernel(low_ref, a_ref, w0_ref, matrix_ref, f_ref, w_ref, mixed_ref,
+def second_factor_kernel(low_ref, a_ref, w0_ref, matrix_ref, f_ref, w_ref,
                          blocks_ref, sym, aug, sems):
     n = w0_ref.shape[0]
     local_cols = matrix_ref.shape[2]
     copies = [pltpu.make_async_copy(matrix_ref.at[:, :, j, :], blocks_ref.at[j], sems.at[j]) for j in range(local_cols)]
     for copy in copies:
         copy.start()
-    odd = is_odd_row()
     w0 = w0_ref[...]
     cross = dot_t(low_ref[...], w0)
     f1, w1 = eliminate(a_ref[...] - dot_t(cross, cross), sym, aug)
@@ -194,10 +189,6 @@
     w_ref[:n, n:] = zero
     w_ref[n:, :n] = w10
     w_ref[n:, n:] = w1
-    mixed_ref[:n, :n] = jnp.where(odd, zero, w0)
-    mixed_ref[:n, n:] = jnp.where(odd, w0, zero)
-    mixed_ref[n:, :n] = jnp.where(odd, w1, w10)
-    mixed_ref[n:, n:] = jnp.where(odd, w10, w1)
     for copy in copies:
         copy.wait()
 
@@ -209,9 +200,9 @@
     blocks = jax.ShapeDtypeStruct((local_cols, local_rows, n, n), jnp.float32)
     return pl.pallas_call(
         second_factor_kernel,
-        out_shape=[square, double, double, blocks],
+        out_shape=[square, double, blocks],
         in_specs=[VMEM] * 3 + [HBM],
-        out_specs=[VMEM] * 4,
+        out_specs=[VMEM] * 3,
         scratch_shapes=[pltpu.VMEM((n // SUB, SUB, n), jnp.float32)] * 2 + [pltpu.SemaphoreType.DMA((local_cols,))],
         compiler_params=pltpu.CompilerParams(vmem_limit_bytes=12 * MIB),
         cost_estimate=estimate(8 * 10**9, 4 * MIB),
@@ -219,26 +210,22 @@
     )(low, a, w0, matrix)
 
 
-def settle_kernel(f0_ref, f1_ref, w_ref, mixed_ref, rows_ref, rows_other_ref, ha_ref, hb_ref, oa_ref, ob_ref, blocks_ref,
-                  out_ref, result, sems):
+def settle_kernel(f0_ref, f1_ref, w_ref, rows_ref, tops_ref, blocks_ref, out_ref, result, sems):
     grid_row = lax.axis_index("row")
     grid_col = lax.axis_index("col")
     n = f0_ref.shape[0]
     local_cols, local_rows, _, _ = blocks_ref.shape
     flat = local_rows * n
-    own = rows_ref[...].reshape(flat, n)
-    other = rows_other_ref[...].reshape(flat, n)
-    swapped = lax.rem(grid_col, 2) == 1
-    rows = jnp.concatenate([jnp.where(swapped, other, own), jnp.where(swapped, own, other)], axis=1)
-    solved = dot_parts(parts(rows), parts(w_ref[...]), ((1,), (1,)))
+    w = parts(w_ref[...])
+    rows = jnp.concatenate([rows_ref[0].reshape(flat, n), rows_ref[1].reshape(flat, n)], axis=1)
+    solved = dot_parts(parts(rows), w, ((1,), (1,)))
     left = parts(solved)
-    mixed = parts(mixed_ref[...])
     copies = []
     for j in range(0, local_cols, 2):
         pair = (j, j + 1)
         stacked = jnp.concatenate(
-            [jnp.concatenate([ha_ref[b], hb_ref[b], oa_ref[b], ob_ref[b]], axis=0) for b in pair], axis=1)
-        update = dot_parts(left, parts(dot_parts(mixed, parts(stacked))))
+            [jnp.concatenate([tops_ref[0, 0, b], tops_ref[0, 1, b], tops_ref[1, 0, b], tops_ref[1, 1, b]], axis=0) for b in pair], axis=1)
+        update = dot_parts(left, parts(dot_parts(w, parts(stacked))))
         for b in pair:
             part = update[:, (b - j) * n:(b - j + 1) * n].reshape(local_rows, n, n)
             result[b] = blocks_ref[b] - part
@@ -276,22 +263,33 @@
         copy.wait()
 
 
-def settle(f0, f1, w, mixed, rows, rows_other, ha, hb, oa, ob, blocks):
+def settle(f0, f1, w, rows, tops, blocks):
     local_cols, local_rows, n, _ = blocks.shape
     return pl.pallas_call(
         settle_kernel,
         out_shape=jax.ShapeDtypeStruct((local_rows, n, local_cols, n), jnp.float32),
-        in_specs=[VMEM] * 11,
+        in_specs=[VMEM] * 6,
         out_specs=HBM,
         scratch_shapes=[pltpu.VMEM(blocks.shape, jnp.float32), pltpu.SemaphoreType.DMA((local_cols,))],
         compiler_params=pltpu.CompilerParams(vmem_limit_bytes=32 * MIB),
         cost_estimate=estimate(4 * 10**9, 6 * MIB),
         name="settle",
-    )(f0, f1, w, mixed, rows, rows_other, ha, hb, oa, ob, blocks)
+    )(f0, f1, w, rows, tops, blocks)
 
 
 def exchange(value, axis, mask, size):
     return lax.ppermute(value, axis, [(i, i ^ mask) for i in range(size)])
+
+
+def gathered(value, axis, mask, size):
+    groups = [[i, i ^ mask] for i in range(size) if not i & mask]
+    return lax.all_gather(value, axis, axis_index_groups=groups)
+
+
+def spread_gathered(own, axis, size, bits):
+    for bit in bits:
+        own = gathered(own, axis, 1 << bit, size)[0]
+    return own
 
 
 def bit_set(index, bit):
@@ -320,34 +318,25 @@
     right = (grid_col % 2) == 1
 
     own, send = corner_halves(kernel)
+    column, upper, lower = panels(kernel)
+    ha = spread_gathered(upper, "row", n_row, row_bits)
+    hb = spread_gathered(lower, "row", n_row, row_bits[::-1])
+    rows = lax.all_gather(column, "col")
     got = exchange(send, "row", 1, n_row)
     pair = jnp.stack([jnp.where(odd != right, got, own), jnp.where(odd, own, got)])
-    column, upper, lower = panels(kernel)
     pair = spread(pair, "row", grid_row, n_row, row_bits)
-    pair, upper, lower = after(pair, upper, lower)
     pair = spread(pair, "col", grid_col, n_col, col_bits)
-    ha = spread(upper, "row", grid_row, n_row, row_bits[:1])
-    hb = spread(lower, "row", grid_row, n_row, row_bits[:0:-1])
     pair_far = exchange(pair, "col", 1, n_col)
-    pair_far, column = after(pair_far, column)
-    rows = spread(column, "col", grid_col, n_col, col_bits[:1])
     mine = jnp.stack([jnp.where(right, pair_far[0], pair[0]), jnp.where(right, pair_far[1], pair[1]),
                       jnp.where(right, pair[0], pair_far[0])])
     other = exchange(mine, "row", 1, n_row)
-    mine, other, ha, hb = after(mine, other, ha, hb)
-
-    ha = spread(ha, "row", grid_row, n_row, row_bits[1:])
-    hb = spread(hb, "row", grid_row, n_row, row_bits[:1])
+
     whole = jnp.concatenate([jnp.where(odd, other, mine), jnp.where(odd, mine, other)], axis=1)
     f0, w0 = first_factor(whole[0])
-    w0, rows, ha, hb = after(w0, rows, ha, hb)
-    rows = spread(rows, "col", grid_col, n_col, col_bits[1:])
-    oa = exchange(ha, "row", 1, n_row)
-    ob = exchange(hb, "row", 1, n_row)
-    rows_other = exchange(rows, "col", 1, n_col)
-
-    f1, w, mixed, blocks = second_factor(whole[1], whole[2], w0, kernel)
-    return settle(f0, f1, w, mixed, rows, rows_other, ha, hb, oa, ob, blocks)
+    w0, ha, hb = after(w0, ha, hb)
+    tops = gathered(jnp.stack([ha, hb]), "row", 1, n_row)
+    f1, w, blocks = second_factor(whole[1], whole[2], w0, kernel)
+    return settle(f0, f1, w, rows, tops, blocks)
 
 
 def solution(mesh):

time: 57.8 us -> 114 us (1.97)
  blocking collectives: 0 us -> 31 us
  waiting for transfers between devices: 14.4 us -> 30.2 us
  between operations: 0.3 us -> 13.6 us
  starting transfers between devices: 21.1 us -> 10 us
  local copies, waits for them, and re-layouts: 1.59 us -> 7.01 us
    all_gather x0 -> x4, blocking collectives: none -> 31 us  [gathered(): return lax.all_gather(value, axis, axis_index_groups=groups)]
    all_gather x0 -> x2, waiting for transfers between devices: none -> 27.9 us  [the longest x1 27.9 us: shards(): rows = lax.all_gather(column, 'col')]
    ppermute x14 -> x6, waiting for transfers between devices: 14.4 us -> 1.8 us  [exchange(): return lax.ppermute(value, axis, [(i, i ^ mask) for i in range(size)])]
    ppermute x14 -> x6, starting transfers between devices: 21.1 us -> 9.79 us  [exchange(): return lax.ppermute(value, axis, [(i, i ^ mask) for i in range(size)])]
    unnamed x4 -> x14, local copies, waits for them, and re-layouts: 1.59 us -> 6.95 us
  transfers between devices with their start and end apart: 14 -> 8, of which waited for: 7 -> 3; matrix products, arithmetic and copies ran while one was open for 0% -> 0% of each run, Pallas kernels for 23% -> 8%
where the time goes in v7:
time: 114 us; the launch traced here: 113 us
  blocking collectives  31 us (27%)
  waiting for transfers between devices  30.2 us (26%)
  Pallas kernels  20.6 us (18%)
  between operations  13.6 us (12%)
  starting transfers between devices  10 us (9%)
  local copies, waits for them, and re-layouts  7.01 us (6%)
    all_gather x4, blocking collectives, gathered(): return lax.all_gather(value, axis, axis_index_groups=groups)  31 us
    all_gather x1, waiting for transfers between devices, shards(): rows = lax.all_gather(column, 'col')  27.9 us
    ppermute x6, starting transfers between devices, exchange(): return lax.ppermute(value, axis, [(i, i ^ mask) for i in range(size)])  9.79 us
    pallas_call x1, Pallas kernels, second_factor(): pl.pallas_call(second_factor_kernel, out_shape=[square, double, blocks],...  7.18 us
    unnamed x14, local copies, waits for them, and re-layouts  6.95 us
    pallas_call x1, Pallas kernels, settle(): pl.pallas_call(settle_kernel, out_shape=jax.ShapeDtypeStruct((local_rows,...  6.9 us
    pallas_call x1, Pallas kernels, first_factor(): pl.pallas_call(first_factor_kernel, out_shape=[square, square], in_specs=...  5 us
  transfers between devices with their start and end apart: 8, of which 3 were waited for; matrix products, arithmetic and copies ran while one was open for 0% of the time, Pallas kernels for 8%

profile of v7, /device:TPU:0, one launch (start us, length us, event | category | flops | bytes accessed | tf_op | source)
XLA Modules:
  0.0 113.4 jit_solution(6663429165960148889)
XLA Ops:
  6.5 0.0 all-gather.11.cloned.1.call-start
  6.5 0.0 copy-start
  6.5 1.6 %copy-done = f32[4,128,8,128]{3,2,1,0:T(8,128)S(1)} copy-done((f32[4,128,8,128]{3,2,1,0:T(8,128)S(1)}, f32[4,128,8,128]{3,2,1,0:T(8,128)}, u32[]{:S(2)}) %copy-start) | copy-done | bytes 2097176
  8.1 0.0 copy-start.1
  8.1 0.1 corner_halves.1
  8.2 0.5 collective-permute-start
  8.7 0.9 collective-permute-done
  9.6 2.9 %collective-permute-start.1 = (f32[2,64,128]{2,1,0:T(8,128)S(1)}, f32[2,64,128]{2,1,0:T(8,128)S(1)}, u32[]{:S(2)}, u32[]{:S(2)}) collective-permute-start(f32[2,64,128]{2,1,0:T(8,128)S(1)} %pad_maximum_fusion.3), channel_id=1, source_target_pairs={{0,8},{4,12},{8,0},{12,4},{16,24},{20,28},{24,16},{28,20},{1,9},{5... | collective-permute-start | bytes 196616 | tf_op jit(solution)/shard_map/ppermute | solution.py:281
  12.5 0.0 copy-done.1
  12.5 1.5 %panels.1 = (f32[4,128,128]{2,1,0:T(8,128)}, f32[8,64,128]{2,1,0:T(8,128)S(1)}, f32[8,64,128]{2,1,0:T(8,128)S(1)}) custom-call(f32[4,128,8,128]{3,2,1,0:T(8,128)S(1)} %copy-done.1), custom_call_target="tpu_custom_call" | custom-call | bytes 4194304 | tf_op jit(solution)/shard_map/panels/pallas_call | solution.py:144
  14.0 0.9 collective-permute-done.1
  14.9 1.9 %collective-permute-start.2 = (f32[2,64,128]{2,1,0:T(8,128)S(1)}, f32[2,64,128]{2,1,0:T(8,128)S(1)}, u32[]{:S(2)}, u32[]{:S(2)}) collective-permute-start(f32[2,64,128]{2,1,0:T(8,128)S(1)} %broadcast_select_fusion.2), channel_id=1, source_target_pairs={{0,16},{4,20},{8,24},{12,28},{16,0},{20,4},{24,8},{28,12},{1,17},{... | collective-permute-start | bytes 196616 | tf_op jit(solution)/shard_map/ppermute | solution.py:281
  16.9 7.6 %all-gather = f32[16,64,128]{2,1,0:T(8,128)S(1)} all-gather(f32[8,64,128]{2,1,0:T(8,128)S(1)} %get-tuple-element.22), channel_id=2, replica_groups={{0,8},{4,12},{16,24},{20,28},{1,9},{5,13},{17,25},{21,29},{2,10},{6,14}..., dimensions={0}, use_global_device_ids=true | all-gather | bytes 786432 | tf_op jit(solution)/shard_map/all_gather | solution.py:286
  24.5 0.0 collective-permute-done.2
  24.5 2.7 %collective-permute-start.3 = (f32[2,64,128]{2,1,0:T(8,128)S(1)}, f32[2,64,128]{2,1,0:T(8,128)S(1)}, u32[]{:S(2)}, u32[]{:S(2)}) collective-permute-start(f32[2,64,128]{2,1,0:T(8,128)S(1)} %broadcast_select_fusion.3), channel_id=1, source_target_pairs={{0,2},{1,3},{2,0},{3,1},{4,6},{5,7},{6,4},{7,5},{8,10},{9,11},{10,... | collective-permute-start | bytes 196616 | tf_op jit(solution)/shard_map/ppermute | solution.py:281
  27.2 7.0 %all-gather.4 = f32[16,64,128]{2,1,0:T(8,128)S(1)} all-gather(f32[8,64,128]{2,1,0:T(8,128)S(1)} %slice.58), channel_id=6, replica_groups={{0,16},{4,20},{8,24},{12,28},{1,17},{5,21},{9,25},{13,29},{2,18},{6,22}..., dimensions={0}, use_global_device_ids=true | all-gather | bytes 786432 | tf_op jit(solution)/shard_map/all_gather | solution.py:286
  34.2 0.0 copy-start.6
  34.2 0.0 collective-permute-done.3
  34.2 1.7 %collective-permute-start.4 = (f32[2,64,128]{2,1,0:T(8,128)S(1)}, f32[2,64,128]{2,1,0:T(8,128)S(1)}, u32[]{:S(2)}, u32[]{:S(2)}) collective-permute-start(f32[2,64,128]{2,1,0:T(8,128)S(1)} %broadcast_select_fusion.4), channel_id=1, source_target_pairs={{0,1},{1,0},{2,3},{3,2},{4,5},{5,4},{6,7},{7,6},{8,9},{9,8},{10,11... | collective-permute-start | bytes 196616 | tf_op jit(solution)/shard_map/ppermute | solution.py:281
  35.9 7.0 %all-gather.1 = f32[16,64,128]{2,1,0:T(8,128)S(1)} all-gather(f32[8,64,128]{2,1,0:T(8,128)S(1)} %get-tuple-element.23), channel_id=3, replica_groups={{0,16},{4,20},{8,24},{12,28},{1,17},{5,21},{9,25},{13,29},{2,18},{6,22}..., dimensions={0}, use_global_device_ids=true | all-gather | bytes 786432 | tf_op jit(solution)/shard_map/all_gather | solution.py:286
  43.0 0.0 collective-permute-done.4
  43.0 0.1 collective-permute-start.5
  43.1 9.4 %all-gather.5 = f32[16,64,128]{2,1,0:T(8,128)S(1)} all-gather(f32[8,64,128]{2,1,0:T(8,128)S(1)} %slice.60), channel_id=7, replica_groups={{0,8},{4,12},{16,24},{20,28},{1,9},{5,13},{17,25},{21,29},{2,10},{6,14}..., dimensions={0}, use_global_device_ids=true | all-gather | bytes 786432 | tf_op jit(solution)/shard_map/all_gather | solution.py:286
  52.5 0.0 collective-permute-done.5
  52.6 0.0 copy-done.6
  52.6 0.0 slice-start
  52.6 5.0 %first_factor.1 = (f32[128,128]{1,0:T(8,128)S(1)}, f32[128,128]{1,0:T(8,128)S(1)}) custom-call(f32[128,128]{1,0:T(8,128)S(1)} %get-tuple-element.32.a_ref), custom_call_target="tpu_custom_call" | custom-call | flops 8000000000 | bytes 2097152 | tf_op jit(solution)/shard_map/first_factor/pallas_call | solution.py:163
  57.6 0.0 slice-done
  57.6 0.9 pad_maximum_fusion
  58.5 0.0 all-gather.11.cloned.1.call-update
  58.5 0.2 all-gather.9.cloned.1.call-start
  58.7 0.5 all-gather.9.cloned.1.call-update
  59.2 7.2 %second_factor.1 = (f32[128,128]{1,0:T(8,128)S(1)}, f32[256,256]{1,0:T(8,128)S(1)}, f32[8,4,128,128]{3,2,1,0:T(8,128)S(1)}) custom-call(f32[128,128]{1,0:T(8,128)S(1)} %get-tuple-element.33.low_ref, f32[128,128]{1,0:T(8,128)S(1)} %get-tuple-element.31.a_ref, f32[128,128]{1,0:T(8,128)S(1)} %get-tuple-element.24.w0_ref, f32[4,128,8,128]{3,2,1,0:T(8,128)S(1)} %copy-done.1), custom_call_target="tpu_custom_call" | custom-call | flops 8000000000 | bytes 4194304 | tf_op jit(solution)/shard_map/second_factor/pallas_call | solution.py:201
  66.4 0.0 copy-start.4
  66.4 1.3 %copy-done.4 = f32[8,4,128,128]{3,2,1,0:T(8,128)} copy-done((f32[8,4,128,128]{3,2,1,0:T(8,128)}, f32[8,4,128,128]{3,2,1,0:T(8,128)S(1)}, u32[]{:S(2)}) %copy-start.4) | copy-done | bytes 2097176
  67.8 0.0 all-gather.11.cloned.1.call-done
  67.8 27.9 %all-gather.9.cloned.1.call-done = f32[16,128,128]{2,1,0:T(8,128)} async-done(((f32[4,128,128]{2,1,0:T(8,128)}), f32[16,128,128]{2,1,0:T(8,128)}) %all-gather.9.cloned.1.call-update) | async-done | bytes 1048592 | tf_op jit(solution)/shard_map/all_gather | solution.py:324
  95.6 0.0 copy-start.2
  95.6 1.2 %copy-done.2 = f32[4,8,64,128]{3,2,1,0:T(8,128)S(1)} copy-done((f32[4,8,64,128]{3,2,1,0:T(8,128)S(1)}, f32[4,8,64,128]{3,2,1,0:T(8,128)}, u32[]{:S(2)}) %copy-start.2) | copy-done | bytes 1048600
  96.9 0.0 copy-start.3
  96.9 1.2 %copy-done.3 = f32[16,128,128]{2,1,0:T(8,128)S(1)} copy-done((f32[16,128,128]{2,1,0:T(8,128)S(1)}, f32[16,128,128]{2,1,0:T(8,128)}, u32[]{:S(2)}) %copy-start.3) | copy-done | bytes 1048600
  98.1 0.0 copy-start.5
  98.1 1.6 %copy-done.5 = f32[8,4,128,128]{3,2,1,0:T(8,128)S(1)} copy-done((f32[8,4,128,128]{3,2,1,0:T(8,128)S(1)}, f32[8,4,128,128]{3,2,1,0:T(8,128)}, u32[]{:S(2)}) %copy-start.5) | copy-done | bytes 2097176
  99.7 6.9 %settle.1 = f32[4,128,8,128]{3,2,1,0:T(8,128)} custom-call(f32[128,128]{1,0:T(8,128)S(1)} %get-tuple-element.20.f0_ref, f32[128,128]{1,0:T(8,128)S(1)} %get-tuple-element.25.f1_ref, f32[256,256]{1,0:T(8,128)S(1)} %get-tuple-element.26.w_ref, f32[4,4,128,128]{3,2,1,0:T(8,128)S(1)} %bitcast.15, f32[2,2,8,64,128]{4,3,2,1,0:T(8,128)S(1)} %bitcast.14, ...), custom_call_target="tpu_custom_call" | custom-call | flops 4000000000 | bytes 6291456 | tf_op jit(solution)/shard_map/settle/pallas_call | solution.py:268
  (12 shorter events, 0.2 us)
Async XLA Ops:
  6.5 61.2 %all-gather.11.cloned.1.call-start = ((), (), s32[]{:S(2)}) async-start(), calls=%async_computation.1 | async-start | bytes 1572864 | tf_op jit(solution)/shard_map/all_gather | solution.py:286
  6.5 1.6 %copy-start = (f32[4,128,8,128]{3,2,1,0:T(8,128)S(1)}, f32[4,128,8,128]{3,2,1,0:T(8,128)}, u32[]{:S(2)}) copy-start(f32[4,128,8,128]{3,2,1,0:T(8,128)} %matrix_ref.5) | copy-start | bytes 6291460
  8.1 4.4 %copy-start.1 = (f32[4,128,8,128]{3,2,1,0:T(8,128)S(1)}, f32[4,128,8,128]{3,2,1,0:T(8,128)}, u32[]{:S(2)}) copy-start(f32[4,128,8,128]{3,2,1,0:T(8,128)} %matrix_ref.5) | copy-start | bytes 6291460
  8.2 1.4 %collective-permute-start = (f32[64,128]{1,0:T(8,128)S(1)}, f32[64,128]{1,0:T(8,128)S(1)}, u32[]{:S(2)}, u32[]{:S(2)}) collective-permute-start(f32[64,128]{1,0:T(8,128)S(1)} %get-tuple-element.18), channel_id=1, source_target_pairs={{0,4},{4,0},{8,12},{12,8},{16,20},{20,16},{24,28},{28,24},{1,5},{5... | collective-permute-start | bytes 98312 | tf_op jit(solution)/shard_map/ppermute | solution.py:281
  9.6 5.3 %collective-permute-start.1 = (f32[2,64,128]{2,1,0:T(8,128)S(1)}, f32[2,64,128]{2,1,0:T(8,128)S(1)}, u32[]{:S(2)}, u32[]{:S(2)}) collective-permute-start(f32[2,64,128]{2,1,0:T(8,128)S(1)} %pad_maximum_fusion.3), channel_id=1, source_target_pairs={{0,8},{4,12},{8,0},{12,4},{16,24},{20,28},{24,16},{28,20},{1,9},{5... | collective-permute-start | bytes 196616 | tf_op jit(solution)/shard_map/ppermute | solution.py:281
  14.9 9.6 %collective-permute-start.2 = (f32[2,64,128]{2,1,0:T(8,128)S(1)}, f32[2,64,128]{2,1,0:T(8,128)S(1)}, u32[]{:S(2)}, u32[]{:S(2)}) collective-permute-start(f32[2,64,128]{2,1,0:T(8,128)S(1)} %broadcast_select_fusion.2), channel_id=1, source_target_pairs={{0,16},{4,20},{8,24},{12,28},{16,0},{20,4},{24,8},{28,12},{1,17},{... | collective-permute-start | bytes 196616 | tf_op jit(solution)/shard_map/ppermute | solution.py:281
  24.5 9.7 %collective-permute-start.3 = (f32[2,64,128]{2,1,0:T(8,128)S(1)}, f32[2,64,128]{2,1,0:T(8,128)S(1)}, u32[]{:S(2)}, u32[]{:S(2)}) collective-permute-start(f32[2,64,128]{2,1,0:T(8,128)S(1)} %broadcast_select_fusion.3), channel_id=1, source_target_pairs={{0,2},{1,3},{2,0},{3,1},{4,6},{5,7},{6,4},{7,5},{8,10},{9,11},{10,... | collective-permute-start | bytes 196616 | tf_op jit(solution)/shard_map/ppermute | solution.py:281
  34.2 18.4 %copy-start.6 = (f32[16,64,128]{2,1,0:T(8,128)}, f32[16,64,128]{2,1,0:T(8,128)S(1)}, u32[]{:S(2)}) copy-start(f32[16,64,128]{2,1,0:T(8,128)S(1)} %all-gather.4) | copy-start | bytes 1572868
  34.2 8.8 %collective-permute-start.4 = (f32[2,64,128]{2,1,0:T(8,128)S(1)}, f32[2,64,128]{2,1,0:T(8,128)S(1)}, u32[]{:S(2)}, u32[]{:S(2)}) collective-permute-start(f32[2,64,128]{2,1,0:T(8,128)S(1)} %broadcast_select_fusion.4), channel_id=1, source_target_pairs={{0,1},{1,0},{2,3},{3,2},{4,5},{5,4},{6,7},{7,6},{8,9},{9,8},{10,11... | collective-permute-start | bytes 196616 | tf_op jit(solution)/shard_map/ppermute | solution.py:281
  43.0 9.5 %collective-permute-start.5 = (f32[3,64,128]{2,1,0:T(8,128)S(1)}, f32[3,64,128]{2,1,0:T(8,128)S(1)}, u32[]{:S(2)}, u32[]{:S(2)}) collective-permute-start(f32[3,64,128]{2,1,0:T(8,128)S(1)} %pad_maximum_fusion.1), channel_id=1, source_target_pairs={{0,4},{4,0},{8,12},{12,8},{16,20},{20,16},{24,28},{28,24},{1,5},{5... | collective-permute-start | bytes 294920 | tf_op jit(solution)/shard_map/ppermute | solution.py:281
  52.6 5.0 %slice-start = ((f32[16,64,128]{2,1,0:T(8,128)}), f32[8,64,128]{2,1,0:T(8,128)S(1)}, s32[]{:S(2)}) async-start(f32[16,64,128]{2,1,0:T(8,128)} %copy-done.6), calls=%async_computation.2 | async-start | bytes 524288 | tf_op jit(solution)/shard_map/slice | solution.py:291
  58.5 37.1 %all-gather.9.cloned.1.call-start = ((), (), s32[]{:S(2)}) async-start(), calls=%async_computation | async-start | bytes 1310720 | tf_op jit(solution)/shard_map/all_gather | solution.py:324
  66.4 1.3 %copy-start.4 = (f32[8,4,128,128]{3,2,1,0:T(8,128)}, f32[8,4,128,128]{3,2,1,0:T(8,128)S(1)}, u32[]{:S(2)}) copy-start(f32[8,4,128,128]{3,2,1,0:T(8,128)S(1)} %get-tuple-element.30.blocks_ref) | copy-start | bytes 6291460
  95.6 1.2 %copy-start.2 = (f32[4,8,64,128]{3,2,1,0:T(8,128)S(1)}, f32[4,8,64,128]{3,2,1,0:T(8,128)}, u32[]{:S(2)}) copy-start(f32[4,8,64,128]{3,2,1,0:T(8,128)} %all-gather.11.cloned.1.call-done) | copy-start | bytes 3145732
  96.9 1.2 %copy-start.3 = (f32[16,128,128]{2,1,0:T(8,128)S(1)}, f32[16,128,128]{2,1,0:T(8,128)}, u32[]{:S(2)}) copy-start(f32[16,128,128]{2,1,0:T(8,128)} %all-gather.9.cloned.1.call-done) | copy-start | bytes 3145732
  98.1 1.6 %copy-start.5 = (f32[8,4,128,128]{3,2,1,0:T(8,128)S(1)}, f32[8,4,128,128]{3,2,1,0:T(8,128)}, u32[]{:S(2)}) copy-start(f32[8,4,128,128]{3,2,1,0:T(8,128)} %copy-done.4) | copy-start | bytes 6291460
Sparse Core Ops, SparseCore 0:
  58.6 6.3 all-gather.10
  66.5 29.0 all-gather.8

commit v8 on v5

--- a/solution.py
+++ b/solution.py
@@ -91,12 +91,10 @@
     return high, middle, (rest - middle.astype(jnp.float32)).astype(jnp.bfloat16)
 
 
-def dot_parts(a, b, dims=((1,), (0,))):
-    total = None
-    for i, j in ((2, 0), (0, 2), (1, 1), (1, 0), (0, 1), (0, 0)):
-        term = lax.dot_general(a[i], b[j], (dims, ((), ())), preferred_element_type=jnp.float32)
-        total = term if total is None else total + term
-    return total
+def dot_parts(a, b):
+    lhs = jnp.concatenate([a[2], a[0], a[1], a[1], a[0], a[0]], axis=1)
+    rhs = jnp.concatenate([b[0], b[2], b[1], b[0], b[1], b[0]], axis=0)
+    return jnp.dot(lhs, rhs, preferred_element_type=jnp.float32)
 
 
 def estimate(flops, nbytes):
@@ -117,7 +115,7 @@
         in_specs=[HBM],
         out_specs=VMEM,
         scratch_shapes=[pltpu.SemaphoreType.DMA(())],
-        compiler_params=pltpu.CompilerParams(vmem_limit_bytes=62 * MIB),
+        compiler_params=pltpu.CompilerParams(vmem_limit_bytes=2 * MIB),
         cost_estimate=estimate(0, 3 * MIB),
         name="corner_block",
     )(matrix)
@@ -224,7 +222,7 @@
     other = rows_other_ref[...].reshape(flat, n)
     swapped = lax.rem(grid_col, 2) == 1
     rows = jnp.concatenate([jnp.where(swapped, other, own), jnp.where(swapped, own, other)], axis=1)
-    solved = dot_parts(parts(rows), parts(w_ref[...]), ((1,), (1,)))
+    solved = dot_parts(parts(rows), parts(w_ref[...].T))
     left = parts(solved)
     mixed = parts(mixed_ref[...])
     copies = []
@@ -299,37 +297,46 @@
     return held
 
 
+def after(value, *others):
+    return lax.optimization_barrier((value,) + others)
+
+
 def shards(kernel):
     grid_row = lax.axis_index("row")
     grid_col = lax.axis_index("col")
     n_row = lax.axis_size("row")
     n_col = lax.axis_size("col")
-    n = kernel.shape[1]
-    half = n // 2
     row_bits = list(range(1, n_row.bit_length() - 1))
     col_bits = list(range(1, n_col.bit_length() - 1))
     odd = (grid_row % 2) == 1
+    right = (grid_col % 2) == 1
 
     block = corner_block(kernel)
-    halves = jnp.broadcast_to(block.reshape(1, 2, half, n), (n_row // 2, 2, half, n)).reshape(n_row, half, n)
-    over_row = lax.all_to_all(halves, "row", 0, 0)
-    kernel_then, over_row = lax.optimization_barrier((kernel, over_row))
-    pair = jnp.broadcast_to(over_row[None, :2], (n_col, 2, half, n))
-    over_col = lax.all_to_all(pair, "col", 0, 0)
-    mine = jnp.stack([over_col[0, 0], over_col[0, 1], over_col[1, 1]])
+    column, upper, lower = panels(kernel)
+    block = spread(block, "row", grid_row, n_row, row_bits[:1])
+    block, upper, lower = after(block, upper, lower)
+    block = spread(block, "row", grid_row, n_row, row_bits[1:])
+    ha = spread(upper, "row", grid_row, n_row, row_bits[:1])
+    hb = spread(lower, "row", grid_row, n_row, row_bits[:0:-1])
+    rows = spread(column, "col", grid_col, n_col, col_bits)
+    block = spread(block, "col", grid_col, n_col, col_bits)
+    block, ha, hb = after(block, ha, hb)
+    across = exchange(block, "col", 1, n_col)
+    ha = spread(ha, "row", grid_row, n_row, row_bits[1:])
+    hb = spread(hb, "row", grid_row, n_row, row_bits[:1])
+    mine = jnp.stack([jnp.where(right, across, block), jnp.where(right, block, across)])
+    mine, rows = after(mine, rows)
     other = exchange(mine, "row", 1, n_row)
-
-    column, upper, lower = panels(kernel_then)
-    ha = spread(upper, "row", grid_row, n_row, row_bits)
-    hb = spread(lower, "row", grid_row, n_row, row_bits[::-1])
-    rows = spread(column, "col", grid_col, n_col, col_bits)
+    rows_other = exchange(rows, "col", 1, n_col)
+
+    a00 = jnp.where(odd, other[0], mine[0])
+    a10 = jnp.where(odd, mine[0], other[0])
+    a11 = jnp.where(odd, mine[1], other[1])
+    f0, w0 = first_factor(a00)
+    w0, ha, hb = after(w0, ha, hb)
     oa = exchange(ha, "row", 1, n_row)
     ob = exchange(hb, "row", 1, n_row)
-    rows_other = exchange(rows, "col", 1, n_col)
-
-    whole = jnp.concatenate([jnp.where(odd, other, mine), jnp.where(odd, mine, other)], axis=1)
-    f0, w0 = first_factor(whole[0])
-    f1, w, mixed, blocks = second_factor(whole[1], whole[2], w0, kernel)
+    f1, w, mixed, blocks = second_factor(a10, a11, w0, kernel)
     return settle(f0, f1, w, mixed, rows, rows_other, ha, hb, oa, ob, blocks)
 
 

time: 60.2 us -> 55.4 us (0.920)
  blocking collectives: 11.9 us -> 0 us
  starting transfers between devices: 9.77 us -> 17.1 us
  waiting for transfers between devices: 13 us -> 15.5 us
  local copies, waits for them, and re-layouts: 3.19 us -> 1.59 us
  Pallas kernels: 21.4 us -> 20.5 us
    all_to_all x1 -> x0, blocking collectives: 11.9 us -> none  [shards(): over_row = lax.all_to_all(halves, 'row', 0, 0)]
    ppermute x9 -> x13, starting transfers between devices: 6.36 us -> 17.1 us  [exchange(): return lax.ppermute(value, axis, [(i, i ^ mask) for i in range(size)])]
    ppermute x9 -> x13, waiting for transfers between devices: 12 us -> 15.5 us  [exchange(): return lax.ppermute(value, axis, [(i, i ^ mask) for i in range(size)])]
    all_to_all x1 -> x0, starting transfers between devices: 3.41 us -> none  [shards(): over_col = lax.all_to_all(pair, 'col', 0, 0)]
    broadcast_in_dim x2 -> x0, local copies, waits for them, and re-layouts: 1.58 us -> none  [the longest x1 0.86 us: shards(): jnp.broadcast_to(block.reshape(1, 2, half, n), (n_row // 2, 2, half, n))]
    pallas_call x1, Pallas kernels: 1.48 us -> 0.06 us  [corner_block(): pl.pallas_call(corner_kernel, out_shape=jax.ShapeDtypeStruct((n, n), jnp....]
    all_to_all x1 -> x0, waiting for transfers between devices: 0.95 us -> none  [shards(): over_col = lax.all_to_all(pair, 'col', 0, 0)]
  transfers between devices with their start and end apart: 10 -> 13, of which waited for: 3 -> 8; matrix products, arithmetic and copies ran while one was open for 2% -> 0% of each run, Pallas kernels for 20% -> 24%
where the time goes in v8:
time: 55.4 us; the launch traced here: 55.2 us
  Pallas kernels  20.5 us (37%)
  starting transfers between devices  17.1 us (31%)
  waiting for transfers between devices  15.5 us (28%)
  local copies, waits for them, and re-layouts  1.59 us (3%)
    ppermute x13, starting transfers between devices, exchange(): return lax.ppermute(value, axis, [(i, i ^ mask) for i in range(size)])  17.1 us
    ppermute x13, waiting for transfers between devices, exchange(): return lax.ppermute(value, axis, [(i, i ^ mask) for i in range(size)])  15.5 us
    pallas_call x1, Pallas kernels, settle(): pl.pallas_call(settle_kernel, out_shape=jax.ShapeDtypeStruct((local_rows,...  7.37 us
    pallas_call x1, Pallas kernels, second_factor(): pl.pallas_call(second_factor_kernel, out_shape=[square, double, double, b...  7.31 us
    pallas_call x1, Pallas kernels, first_factor(): pl.pallas_call(first_factor_kernel, out_shape=[square, square], in_specs=...  5 us
    unnamed x4, local copies, waits for them, and re-layouts  1.59 us
  transfers between devices with their start and end apart: 13, of which 8 were waited for; matrix products, arithmetic and copies ran while one was open for 0% of the time, Pallas kernels for 24%

profile of v8, /device:TPU:0, one launch (start us, length us, event | category | flops | bytes accessed | tf_op | source)
XLA Modules:
  0.0 55.2 jit_solution(7784842128799279862)
XLA Ops:
  0.0 0.0 copy-start
  0.0 1.6 %copy-done = f32[4,128,8,128]{3,2,1,0:T(8,128)S(1)} copy-done((f32[4,128,8,128]{3,2,1,0:T(8,128)S(1)}, f32[4,128,8,128]{3,2,1,0:T(8,128)}, u32[]{:S(2)}) %copy-start) | copy-done | bytes 2097176
  1.6 0.0 copy-start.1
  1.6 0.1 corner_block.1
  1.7 3.0 %collective-permute-start = (f32[128,128]{1,0:T(8,128)S(1)}, f32[128,128]{1,0:T(8,128)S(1)}, u32[]{:S(2)}, u32[]{:S(2)}) collective-permute-start(f32[128,128]{1,0:T(8,128)S(1)} %corner_block.1), channel_id=1, source_target_pairs={{0,8},{4,12},{8,0},{12,4},{16,24},{20,28},{24,16},{28,20},{1,9},{5... | collective-permute-start | bytes 196616 | tf_op jit(solution)/shard_map/ppermute | solution.py:286
  4.7 0.0 copy-done.1
  4.7 0.7 %panels.1 = (f32[4,128,128]{2,1,0:T(8,128)S(1)}, f32[8,64,128]{2,1,0:T(8,128)S(1)}, f32[8,64,128]{2,1,0:T(8,128)S(1)}) custom-call(f32[4,128,8,128]{3,2,1,0:T(8,128)S(1)} %copy-done.1), custom_call_target="tpu_custom_call" | custom-call | bytes 4194304 | tf_op jit(solution)/shard_map/panels/pallas_call | solution.py:140
  5.4 1.5 %collective-permute-done = f32[128,128]{1,0:T(8,128)S(1)} collective-permute-done((f32[128,128]{1,0:T(8,128)S(1)}, f32[128,128]{1,0:T(8,128)S(1)}, u32[]{:S(2)}, u32[]{:S(2)}) %collective-permute-start) | collective-permute-done | bytes 65568 | tf_op jit(solution)/shard_map/ppermute | solution.py:286
  6.9 2.1 %collective-permute-start.1 = (f32[128,128]{1,0:T(8,128)S(1)}, f32[128,128]{1,0:T(8,128)S(1)}, u32[]{:S(2)}, u32[]{:S(2)}) collective-permute-start(f32[128,128]{1,0:T(8,128)S(1)} %broadcast_select_fusion.5), channel_id=1, source_target_pairs={{0,16},{4,20},{8,24},{12,28},{16,0},{20,4},{24,8},{28,12},{1,17},{... | collective-permute-start | bytes 196616 | tf_op jit(solution)/shard_map/ppermute | solution.py:286
  9.0 2.2 %collective-permute-done.1 = f32[128,128]{1,0:T(8,128)S(1)} collective-permute-done((f32[128,128]{1,0:T(8,128)S(1)}, f32[128,128]{1,0:T(8,128)S(1)}, u32[]{:S(2)}, u32[]{:S(2)}) %collective-permute-start.1) | collective-permute-done | bytes 65568 | tf_op jit(solution)/shard_map/ppermute | solution.py:286
  11.3 3.2 %collective-permute-start.2 = (f32[128,128]{1,0:T(8,128)S(1)}, f32[128,128]{1,0:T(8,128)S(1)}, u32[]{:S(2)}, u32[]{:S(2)}) collective-permute-start(f32[128,128]{1,0:T(8,128)S(1)} %broadcast_select_fusion.6), channel_id=1, source_target_pairs={{0,2},{1,3},{2,0},{3,1},{4,6},{5,7},{6,4},{7,5},{8,10},{9,11},{10,... | collective-permute-start | bytes 196616 | tf_op jit(solution)/shard_map/ppermute | solution.py:286
  14.4 1.5 %collective-permute-start.3 = (f32[8,64,128]{2,1,0:T(8,128)S(1)}, f32[8,64,128]{2,1,0:T(8,128)}, u32[]{:S(2)}, u32[]{:S(2)}) collective-permute-start(f32[8,64,128]{2,1,0:T(8,128)S(1)} %get-tuple-element.28), channel_id=1, source_target_pairs={{0,8},{4,12},{8,0},{12,4},{16,24},{20,28},{24,16},{28,20},{1,9},{5... | collective-permute-start | bytes 786440 | tf_op jit(solution)/shard_map/ppermute | solution.py:286
  15.9 0.3 collective-permute-start.6
  16.3 1.5 %collective-permute-start.4 = (f32[8,64,128]{2,1,0:T(8,128)S(1)}, f32[8,64,128]{2,1,0:T(8,128)S(1)}, u32[]{:S(2)}, u32[]{:S(2)}) collective-permute-start(f32[8,64,128]{2,1,0:T(8,128)S(1)} %get-tuple-element.29), channel_id=1, source_target_pairs={{0,16},{4,20},{8,24},{12,28},{16,0},{20,4},{24,8},{28,12},{1,17},{... | collective-permute-start | bytes 786440 | tf_op jit(solution)/shard_map/ppermute | solution.py:286
  17.8 0.0 collective-permute-done.2
  17.8 3.1 %collective-permute-done.3 = f32[8,64,128]{2,1,0:T(8,128)} collective-permute-done((f32[8,64,128]{2,1,0:T(8,128)S(1)}, f32[8,64,128]{2,1,0:T(8,128)}, u32[]{:S(2)}, u32[]{:S(2)}) %collective-permute-start.3) | collective-permute-done | bytes 262176 | tf_op jit(solution)/shard_map/ppermute | solution.py:286
  21.0 1.7 %collective-permute-done.4 = f32[8,64,128]{2,1,0:T(8,128)S(1)} collective-permute-done((f32[8,64,128]{2,1,0:T(8,128)S(1)}, f32[8,64,128]{2,1,0:T(8,128)S(1)}, u32[]{:S(2)}, u32[]{:S(2)}) %collective-permute-start.4) | collective-permute-done | bytes 262176 | tf_op jit(solution)/shard_map/ppermute | solution.py:286
  22.7 1.6 %collective-permute-start.5 = (f32[128,128]{1,0:T(8,128)S(1)}, f32[128,128]{1,0:T(8,128)S(1)}, u32[]{:S(2)}, u32[]{:S(2)}) collective-permute-start(f32[128,128]{1,0:T(8,128)S(1)} %broadcast_select_fusion.7), channel_id=1, source_target_pairs={{0,1},{1,0},{2,3},{3,2},{4,5},{5,4},{6,7},{7,6},{8,9},{9,8},{10,11... | collective-permute-start | bytes 196616 | tf_op jit(solution)/shard_map/ppermute | solution.py:286
  24.3 4.5 %collective-permute-done.6 = f32[4,128,128]{2,1,0:T(8,128)} collective-permute-done((f32[4,128,128]{2,1,0:T(8,128)S(1)}, f32[4,128,128]{2,1,0:T(8,128)}, u32[]{:S(2)}, u32[]{:S(2)}) %collective-permute-start.6) | collective-permute-done | bytes 262176 | tf_op jit(solution)/shard_map/ppermute | solution.py:286
  28.9 0.5 collective-permute-done.5
  29.4 0.1 collective-permute-start.7
  29.5 1.9 %collective-permute-start.8 = (f32[8,64,128]{2,1,0:T(8,128)S(1)}, f32[8,64,128]{2,1,0:T(8,128)S(1)}, u32[]{:S(2)}, u32[]{:S(2)}) collective-permute-start(f32[8,64,128]{2,1,0:T(8,128)S(1)} %broadcast_select_fusion.4), channel_id=1, source_target_pairs={{0,16},{4,20},{8,24},{12,28},{16,0},{20,4},{24,8},{28,12},{1,17},{... | collective-permute-start | bytes 786440 | tf_op jit(solution)/shard_map/ppermute | solution.py:286
  31.4 1.3 %collective-permute-start.9 = (f32[8,64,128]{2,1,0:T(8,128)S(1)}, f32[8,64,128]{2,1,0:T(8,128)S(1)}, u32[]{:S(2)}, u32[]{:S(2)}) collective-permute-start(f32[8,64,128]{2,1,0:T(8,128)S(1)} %broadcast_select_fusion.2), channel_id=1, source_target_pairs={{0,8},{4,12},{8,0},{12,4},{16,24},{20,28},{24,16},{28,20},{1,9},{5... | collective-permute-start | bytes 786440 | tf_op jit(solution)/shard_map/ppermute | solution.py:286
  32.7 0.0 collective-permute-start.10
  32.7 0.0 collective-permute-done.7
  32.7 5.0 %first_factor.1 = (f32[128,128]{1,0:T(8,128)S(1)}, f32[128,128]{1,0:T(8,128)S(1)}) custom-call(f32[128,128]{1,0:T(8,128)S(1)} %get-tuple-element.47.a_ref), custom_call_target="tpu_custom_call" | custom-call | flops 8000000000 | bytes 2097152 | tf_op jit(solution)/shard_map/first_factor/pallas_call | solution.py:159
  37.7 0.5 collective-permute-done.8
  38.3 1.4 %collective-permute-done.9 = f32[8,64,128]{2,1,0:T(8,128)S(1)} collective-permute-done((f32[8,64,128]{2,1,0:T(8,128)S(1)}, f32[8,64,128]{2,1,0:T(8,128)S(1)}, u32[]{:S(2)}, u32[]{:S(2)}) %collective-permute-start.9) | collective-permute-done | bytes 262176 | tf_op jit(solution)/shard_map/ppermute | solution.py:286
  39.8 0.1 collective-permute-start.11
  39.9 0.5 collective-permute-start.12
  40.3 7.3 %second_factor.1 = (f32[128,128]{1,0:T(8,128)S(1)}, f32[256,256]{1,0:T(8,128)S(1)}, f32[256,256]{1,0:T(8,128)S(1)}, f32[8,4,128,128]{3,2,1,0:T(8,128)S(1)}) custom-call(f32[128,128]{1,0:T(8,128)S(1)} %get-tuple-element.46.low_ref, f32[128,128]{1,0:T(8,128)S(1)} %get-tuple-element.45.a_ref, f32[128,128]{1,0:T(8,128)S(1)} %get-tuple-element.37.w0_ref, ...), custom_call_target="tpu_custom_call" | custom-call | flops 8000000000 | bytes 4194304 | tf_op jit(solution)/shard_map/second_factor/pallas_call | solution.py:202
  47.7 0.0 collective-permute-done.10.rows_other_ref
  47.7 0.0 collective-permute-done.11.oa_ref
  47.7 0.0 collective-permute-done.12.ob_ref
  47.7 7.4 %settle.1 = f32[4,128,8,128]{3,2,1,0:T(8,128)} custom-call(f32[128,128]{1,0:T(8,128)S(1)} %get-tuple-element.33.f0_ref, f32[128,128]{1,0:T(8,128)S(1)} %get-tuple-element.38.f1_ref, f32[256,256]{1,0:T(8,128)S(1)} %get-tuple-element.39.w_ref, f32[256,256]{1,0:T(8,128)S(1)} %get-tuple-element.40.mixed_ref, f32[4,128,128]{2,1,0:T(8,128)S(1)} %broadcast_select_fusion.rows_ref, ...), custom_call_target="tpu_custom_call" | custom-call | flops 4000000000 | bytes 6291456 | tf_op jit(solution)/shard_map/settle/pallas_call | solution.py:273
  (11 shorter events, 0.2 us)
Async XLA Ops:
  0.0 1.6 %copy-start = (f32[4,128,8,128]{3,2,1,0:T(8,128)S(1)}, f32[4,128,8,128]{3,2,1,0:T(8,128)}, u32[]{:S(2)}) copy-start(f32[4,128,8,128]{3,2,1,0:T(8,128)} %matrix_ref.5) | copy-start | bytes 6291460
  1.6 3.1 %copy-start.1 = (f32[4,128,8,128]{3,2,1,0:T(8,128)S(1)}, f32[4,128,8,128]{3,2,1,0:T(8,128)}, u32[]{:S(2)}) copy-start(f32[4,128,8,128]{3,2,1,0:T(8,128)} %matrix_ref.5) | copy-start | bytes 6291460
  1.7 5.2 %collective-permute-start = (f32[128,128]{1,0:T(8,128)S(1)}, f32[128,128]{1,0:T(8,128)S(1)}, u32[]{:S(2)}, u32[]{:S(2)}) collective-permute-start(f32[128,128]{1,0:T(8,128)S(1)} %corner_block.1), channel_id=1, source_target_pairs={{0,8},{4,12},{8,0},{12,4},{16,24},{20,28},{24,16},{28,20},{1,9},{5... | collective-permute-start | bytes 196616 | tf_op jit(solution)/shard_map/ppermute | solution.py:286
  6.9 4.4 %collective-permute-start.1 = (f32[128,128]{1,0:T(8,128)S(1)}, f32[128,128]{1,0:T(8,128)S(1)}, u32[]{:S(2)}, u32[]{:S(2)}) collective-permute-start(f32[128,128]{1,0:T(8,128)S(1)} %broadcast_select_fusion.5), channel_id=1, source_target_pairs={{0,16},{4,20},{8,24},{12,28},{16,0},{20,4},{24,8},{28,12},{1,17},{... | collective-permute-start | bytes 196616 | tf_op jit(solution)/shard_map/ppermute | solution.py:286
  11.3 6.5 %collective-permute-start.2 = (f32[128,128]{1,0:T(8,128)S(1)}, f32[128,128]{1,0:T(8,128)S(1)}, u32[]{:S(2)}, u32[]{:S(2)}) collective-permute-start(f32[128,128]{1,0:T(8,128)S(1)} %broadcast_select_fusion.6), channel_id=1, source_target_pairs={{0,2},{1,3},{2,0},{3,1},{4,6},{5,7},{6,4},{7,5},{8,10},{9,11},{10,... | collective-permute-start | bytes 196616 | tf_op jit(solution)/shard_map/ppermute | solution.py:286
  14.4 6.5 %collective-permute-start.3 = (f32[8,64,128]{2,1,0:T(8,128)S(1)}, f32[8,64,128]{2,1,0:T(8,128)}, u32[]{:S(2)}, u32[]{:S(2)}) collective-permute-start(f32[8,64,128]{2,1,0:T(8,128)S(1)} %get-tuple-element.28), channel_id=1, source_target_pairs={{0,8},{4,12},{8,0},{12,4},{16,24},{20,28},{24,16},{28,20},{1,9},{5... | collective-permute-start | bytes 786440 | tf_op jit(solution)/shard_map/ppermute | solution.py:286
  15.9 12.9 %collective-permute-start.6 = (f32[4,128,128]{2,1,0:T(8,128)S(1)}, f32[4,128,128]{2,1,0:T(8,128)}, u32[]{:S(2)}, u32[]{:S(2)}) collective-permute-start(f32[4,128,128]{2,1,0:T(8,128)S(1)} %get-tuple-element.31), channel_id=1, source_target_pairs={{0,2},{1,3},{2,0},{3,1},{4,6},{5,7},{6,4},{7,5},{8,10},{9,11},{10,... | collective-permute-start | bytes 786440 | tf_op jit(solution)/shard_map/ppermute | solution.py:286
  16.3 6.4 %collective-permute-start.4 = (f32[8,64,128]{2,1,0:T(8,128)S(1)}, f32[8,64,128]{2,1,0:T(8,128)S(1)}, u32[]{:S(2)}, u32[]{:S(2)}) collective-permute-start(f32[8,64,128]{2,1,0:T(8,128)S(1)} %get-tuple-element.29), channel_id=1, source_target_pairs={{0,16},{4,20},{8,24},{12,28},{16,0},{20,4},{24,8},{28,12},{1,17},{... | collective-permute-start | bytes 786440 | tf_op jit(solution)/shard_map/ppermute | solution.py:286
  22.7 6.6 %collective-permute-start.5 = (f32[128,128]{1,0:T(8,128)S(1)}, f32[128,128]{1,0:T(8,128)S(1)}, u32[]{:S(2)}, u32[]{:S(2)}) collective-permute-start(f32[128,128]{1,0:T(8,128)S(1)} %broadcast_select_fusion.7), channel_id=1, source_target_pairs={{0,1},{1,0},{2,3},{3,2},{4,5},{5,4},{6,7},{7,6},{8,9},{9,8},{10,11... | collective-permute-start | bytes 196616 | tf_op jit(solution)/shard_map/ppermute | solution.py:286
  29.4 3.3 %collective-permute-start.7 = (f32[2,128,128]{2,1,0:T(8,128)S(1)}, f32[2,128,128]{2,1,0:T(8,128)S(1)}, u32[]{:S(2)}, u32[]{:S(2)}) collective-permute-start(f32[2,128,128]{2,1,0:T(8,128)S(1)} %pad_maximum_fusion), channel_id=1, source_target_pairs={{0,4},{4,0},{8,12},{12,8},{16,20},{20,16},{24,28},{28,24},{1,5},{5... | collective-permute-start | bytes 393224 | tf_op jit(solution)/shard_map/ppermute | solution.py:286
  29.5 8.8 %collective-permute-start.8 = (f32[8,64,128]{2,1,0:T(8,128)S(1)}, f32[8,64,128]{2,1,0:T(8,128)S(1)}, u32[]{:S(2)}, u32[]{:S(2)}) collective-permute-start(f32[8,64,128]{2,1,0:T(8,128)S(1)} %broadcast_select_fusion.4), channel_id=1, source_target_pairs={{0,16},{4,20},{8,24},{12,28},{16,0},{20,4},{24,8},{28,12},{1,17},{... | collective-permute-start | bytes 786440 | tf_op jit(solution)/shard_map/ppermute | solution.py:286
  31.4 8.4 %collective-permute-start.9 = (f32[8,64,128]{2,1,0:T(8,128)S(1)}, f32[8,64,128]{2,1,0:T(8,128)S(1)}, u32[]{:S(2)}, u32[]{:S(2)}) collective-permute-start(f32[8,64,128]{2,1,0:T(8,128)S(1)} %broadcast_select_fusion.2), channel_id=1, source_target_pairs={{0,8},{4,12},{8,0},{12,4},{16,24},{20,28},{24,16},{28,20},{1,9},{5... | collective-permute-start | bytes 786440 | tf_op jit(solution)/shard_map/ppermute | solution.py:286
  32.7 15.0 %collective-permute-start.10 = (f32[4,128,128]{2,1,0:T(8,128)S(1)}, f32[4,128,128]{2,1,0:T(8,128)S(1)}, u32[]{:S(2)}, u32[]{:S(2)}) collective-permute-start(f32[4,128,128]{2,1,0:T(8,128)S(1)} %broadcast_select_fusion.rows_ref), channel_id=1, source_target_pairs={{0,1},{1,0},{2,3},{3,2},{4,5},{5,4},{6,7},{7,6},{8,9},{9,8},{10,11... | collective-permute-start | bytes 786440 | tf_op jit(solution)/shard_map/ppermute | solution.py:286
  39.8 7.9 %collective-permute-start.11 = (f32[8,64,128]{2,1,0:T(8,128)S(1)}, f32[8,64,128]{2,1,0:T(8,128)S(1)}, u32[]{:S(2)}, u32[]{:S(2)}) collective-permute-start(f32[8,64,128]{2,1,0:T(8,128)S(1)} %broadcast_select_fusion.1.ha_ref), channel_id=1, source_target_pairs={{0,4},{4,0},{8,12},{12,8},{16,20},{20,16},{24,28},{28,24},{1,5},{5... | collective-permute-start | bytes 786440 | tf_op jit(solution)/shard_map/ppermute | solution.py:286
  39.9 7.8 %collective-permute-start.12 = (f32[8,64,128]{2,1,0:T(8,128)S(1)}, f32[8,64,128]{2,1,0:T(8,128)S(1)}, u32[]{:S(2)}, u32[]{:S(2)}) collective-permute-start(f32[8,64,128]{2,1,0:T(8,128)S(1)} %broadcast_select_fusion.3.hb_ref), channel_id=1, source_target_pairs={{0,4},{4,0},{8,12},{12,8},{16,20},{20,16},{24,28},{28,24},{1,5},{5... | collective-permute-start | bytes 786440 | tf_op jit(solution)/shard_map/ppermute | solution.py:286

commit v9 on v8

--- a/solution.py
+++ b/solution.py
@@ -91,10 +91,12 @@
     return high, middle, (rest - middle.astype(jnp.float32)).astype(jnp.bfloat16)
 
 
-def dot_parts(a, b):
-    lhs = jnp.concatenate([a[2], a[0], a[1], a[1], a[0], a[0]], axis=1)
-    rhs = jnp.concatenate([b[0], b[2], b[1], b[0], b[1], b[0]], axis=0)
-    return jnp.dot(lhs, rhs, preferred_element_type=jnp.float32)
+def dot_parts(a, b, dims=((1,), (0,))):
+    total = None
+    for i, j in ((2, 0), (0, 2), (1, 1), (1, 0), (0, 1), (0, 0)):
+        term = lax.dot_general(a[i], b[j], (dims, ((), ())), preferred_element_type=jnp.float32)
+        total = term if total is None else total + term
+    return total
 
 
 def estimate(flops, nbytes):
@@ -222,7 +224,7 @@
     other = rows_other_ref[...].reshape(flat, n)
     swapped = lax.rem(grid_col, 2) == 1
     rows = jnp.concatenate([jnp.where(swapped, other, own), jnp.where(swapped, own, other)], axis=1)
-    solved = dot_parts(parts(rows), parts(w_ref[...].T))
+    solved = dot_parts(parts(rows), parts(w_ref[...]), ((1,), (1,)))
     left = parts(solved)
     mixed = parts(mixed_ref[...])
     copies = []
@@ -320,23 +322,22 @@
     hb = spread(lower, "row", grid_row, n_row, row_bits[:0:-1])
     rows = spread(column, "col", grid_col, n_col, col_bits)
     block = spread(block, "col", grid_col, n_col, col_bits)
-    block, ha, hb = after(block, ha, hb)
     across = exchange(block, "col", 1, n_col)
-    ha = spread(ha, "row", grid_row, n_row, row_bits[1:])
-    hb = spread(hb, "row", grid_row, n_row, row_bits[:1])
     mine = jnp.stack([jnp.where(right, across, block), jnp.where(right, block, across)])
-    mine, rows = after(mine, rows)
     other = exchange(mine, "row", 1, n_row)
-    rows_other = exchange(rows, "col", 1, n_col)
 
     a00 = jnp.where(odd, other[0], mine[0])
     a10 = jnp.where(odd, mine[0], other[0])
     a11 = jnp.where(odd, mine[1], other[1])
     f0, w0 = first_factor(a00)
-    w0, ha, hb = after(w0, ha, hb)
+    w0, rows, ha, hb = after(w0, rows, ha, hb)
+    ha = spread(ha, "row", grid_row, n_row, row_bits[1:])
+    hb = spread(hb, "row", grid_row, n_row, row_bits[:1])
+    rows_other = exchange(rows, "col", 1, n_col)
+    f1, w, mixed, blocks = second_factor(a10, a11, w0, kernel)
+    w, ha, hb = after(w, ha, hb)
     oa = exchange(ha, "row", 1, n_row)
     ob = exchange(hb, "row", 1, n_row)
-    f1, w, mixed, blocks = second_factor(a10, a11, w0, kernel)
     return settle(f0, f1, w, mixed, rows, rows_other, ha, hb, oa, ob, blocks)
 
 

time: 55.4 us -> 54.9 us (level)
  starting transfers between devices: 17.1 us -> 20.2 us
  waiting for transfers between devices: 15.5 us -> 12.5 us
    ppermute x13, waiting for transfers between devices: 15.5 us -> 12.5 us  [exchange(): return lax.ppermute(value, axis, [(i, i ^ mask) for i in range(size)])]
    ppermute x13, starting transfers between devices: 17.1 us -> 20.2 us  [exchange(): return lax.ppermute(value, axis, [(i, i ^ mask) for i in range(size)])]
  transfers between devices with their start and end apart: 13 -> 13, of which waited for: 8 -> 6; matrix products, arithmetic and copies ran while one was open for 0% -> 0% of each run, Pallas kernels for 24% -> 15%
where the time goes in v9:
time: 54.9 us; the launch traced here: 54.8 us
  starting transfers between devices  20.2 us (37%)
  Pallas kernels  20 us (36%)
  waiting for transfers between devices  12.5 us (23%)
  local copies, waits for them, and re-layouts  1.59 us (3%)
    ppermute x13, starting transfers between devices, exchange(): return lax.ppermute(value, axis, [(i, i ^ mask) for i in range(size)])  20.2 us
    ppermute x13, waiting for transfers between devices, exchange(): return lax.ppermute(value, axis, [(i, i ^ mask) for i in range(size)])  12.5 us
    pallas_call x1, Pallas kernels, second_factor(): pl.pallas_call(second_factor_kernel, out_shape=[square, double, double, b...  7.33 us
    pallas_call x1, Pallas kernels, settle(): pl.pallas_call(settle_kernel, out_shape=jax.ShapeDtypeStruct((local_rows,...  6.9 us
    pallas_call x1, Pallas kernels, first_factor(): pl.pallas_call(first_factor_kernel, out_shape=[square, square], in_specs=...  5 us
    unnamed x4, local copies, waits for them, and re-layouts  1.59 us
  transfers between devices with their start and end apart: 13, of which 6 were waited for; matrix products, arithmetic and copies ran while one was open for 0% of the time, Pallas kernels for 15%

profile of v9, /device:TPU:0, one launch (start us, length us, event | category | flops | bytes accessed | tf_op | source)
XLA Modules:
  0.0 54.8 jit_solution(4855674785289076826)
XLA Ops:
  0.0 0.0 copy-start
  0.0 1.6 %copy-done = f32[4,128,8,128]{3,2,1,0:T(8,128)S(1)} copy-done((f32[4,128,8,128]{3,2,1,0:T(8,128)S(1)}, f32[4,128,8,128]{3,2,1,0:T(8,128)}, u32[]{:S(2)}) %copy-start) | copy-done | bytes 2097176
  1.6 0.0 copy-start.1
  1.6 0.1 corner_block.1
  1.7 3.0 %collective-permute-start = (f32[128,128]{1,0:T(8,128)S(1)}, f32[128,128]{1,0:T(8,128)S(1)}, u32[]{:S(2)}, u32[]{:S(2)}) collective-permute-start(f32[128,128]{1,0:T(8,128)S(1)} %corner_block.1), channel_id=1, source_target_pairs={{0,8},{4,12},{8,0},{12,4},{16,24},{20,28},{24,16},{28,20},{1,9},{5... | collective-permute-start | bytes 196616 | tf_op jit(solution)/shard_map/ppermute | solution.py:288
  4.7 0.0 copy-done.1
  4.7 0.7 %panels.1 = (f32[4,128,128]{2,1,0:T(8,128)S(1)}, f32[8,64,128]{2,1,0:T(8,128)S(1)}, f32[8,64,128]{2,1,0:T(8,128)S(1)}) custom-call(f32[4,128,8,128]{3,2,1,0:T(8,128)S(1)} %copy-done.1), custom_call_target="tpu_custom_call" | custom-call | bytes 4194304 | tf_op jit(solution)/shard_map/panels/pallas_call | solution.py:142
  5.4 1.5 %collective-permute-done = f32[128,128]{1,0:T(8,128)S(1)} collective-permute-done((f32[128,128]{1,0:T(8,128)S(1)}, f32[128,128]{1,0:T(8,128)S(1)}, u32[]{:S(2)}, u32[]{:S(2)}) %collective-permute-start) | collective-permute-done | bytes 65568 | tf_op jit(solution)/shard_map/ppermute | solution.py:288
  6.9 2.1 %collective-permute-start.1 = (f32[128,128]{1,0:T(8,128)S(1)}, f32[128,128]{1,0:T(8,128)S(1)}, u32[]{:S(2)}, u32[]{:S(2)}) collective-permute-start(f32[128,128]{1,0:T(8,128)S(1)} %broadcast_select_fusion.5), channel_id=1, source_target_pairs={{0,16},{4,20},{8,24},{12,28},{16,0},{20,4},{24,8},{28,12},{1,17},{... | collective-permute-start | bytes 196616 | tf_op jit(solution)/shard_map/ppermute | solution.py:288
  9.0 2.2 %collective-permute-done.1 = f32[128,128]{1,0:T(8,128)S(1)} collective-permute-done((f32[128,128]{1,0:T(8,128)S(1)}, f32[128,128]{1,0:T(8,128)S(1)}, u32[]{:S(2)}, u32[]{:S(2)}) %collective-permute-start.1) | collective-permute-done | bytes 65568 | tf_op jit(solution)/shard_map/ppermute | solution.py:288
  11.3 3.2 %collective-permute-start.2 = (f32[128,128]{1,0:T(8,128)S(1)}, f32[128,128]{1,0:T(8,128)S(1)}, u32[]{:S(2)}, u32[]{:S(2)}) collective-permute-start(f32[128,128]{1,0:T(8,128)S(1)} %broadcast_select_fusion.6), channel_id=1, source_target_pairs={{0,2},{1,3},{2,0},{3,1},{4,6},{5,7},{6,4},{7,5},{8,10},{9,11},{10,... | collective-permute-start | bytes 196616 | tf_op jit(solution)/shard_map/ppermute | solution.py:288
  14.4 2.3 %collective-permute-done.2 = f32[128,128]{1,0:T(8,128)S(1)} collective-permute-done((f32[128,128]{1,0:T(8,128)S(1)}, f32[128,128]{1,0:T(8,128)S(1)}, u32[]{:S(2)}, u32[]{:S(2)}) %collective-permute-start.2) | collective-permute-done | bytes 65568 | tf_op jit(solution)/shard_map/ppermute | solution.py:288
  16.8 1.9 %collective-permute-start.3 = (f32[128,128]{1,0:T(8,128)S(1)}, f32[128,128]{1,0:T(8,128)S(1)}, u32[]{:S(2)}, u32[]{:S(2)}) collective-permute-start(f32[128,128]{1,0:T(8,128)S(1)} %broadcast_select_fusion.7), channel_id=1, source_target_pairs={{0,1},{1,0},{2,3},{3,2},{4,5},{5,4},{6,7},{7,6},{8,9},{9,8},{10,11... | collective-permute-start | bytes 196616 | tf_op jit(solution)/shard_map/ppermute | solution.py:288
  18.7 3.3 %collective-permute-start.5 = (f32[4,128,128]{2,1,0:T(8,128)S(1)}, f32[4,128,128]{2,1,0:T(8,128)S(1)}, u32[]{:S(2)}, u32[]{:S(2)}) collective-permute-start(f32[4,128,128]{2,1,0:T(8,128)S(1)} %get-tuple-element.29), channel_id=1, source_target_pairs={{0,2},{1,3},{2,0},{3,1},{4,6},{5,7},{6,4},{7,5},{8,10},{9,11},{10,... | collective-permute-start | bytes 786440 | tf_op jit(solution)/shard_map/ppermute | solution.py:288
  21.9 1.5 %collective-permute-start.6 = (f32[8,64,128]{2,1,0:T(8,128)S(1)}, f32[8,64,128]{2,1,0:T(8,128)S(1)}, u32[]{:S(2)}, u32[]{:S(2)}) collective-permute-start(f32[8,64,128]{2,1,0:T(8,128)S(1)} %get-tuple-element.30), channel_id=1, source_target_pairs={{0,8},{4,12},{8,0},{12,4},{16,24},{20,28},{24,16},{28,20},{1,9},{5... | collective-permute-start | bytes 786440 | tf_op jit(solution)/shard_map/ppermute | solution.py:288
  23.4 1.5 %collective-permute-start.7 = (f32[8,64,128]{2,1,0:T(8,128)S(1)}, f32[8,64,128]{2,1,0:T(8,128)S(1)}, u32[]{:S(2)}, u32[]{:S(2)}) collective-permute-start(f32[8,64,128]{2,1,0:T(8,128)S(1)} %get-tuple-element.31), channel_id=1, source_target_pairs={{0,16},{4,20},{8,24},{12,28},{16,0},{20,4},{24,8},{28,12},{1,17},{... | collective-permute-start | bytes 786440 | tf_op jit(solution)/shard_map/ppermute | solution.py:288
  24.9 0.0 collective-permute-done.3
  25.0 0.1 collective-permute-start.4
  25.1 5.0 %collective-permute-done.5 = f32[4,128,128]{2,1,0:T(8,128)S(1)} collective-permute-done((f32[4,128,128]{2,1,0:T(8,128)S(1)}, f32[4,128,128]{2,1,0:T(8,128)S(1)}, u32[]{:S(2)}, u32[]{:S(2)}) %collective-permute-start.5) | collective-permute-done | bytes 262176 | tf_op jit(solution)/shard_map/ppermute | solution.py:288
  30.1 0.0 collective-permute-done.6
  30.1 0.0 collective-permute-done.7
  30.2 0.0 collective-permute-done.4
  30.2 5.0 %first_factor.1 = (f32[128,128]{1,0:T(8,128)S(1)}, f32[128,128]{1,0:T(8,128)S(1)}) custom-call(f32[128,128]{1,0:T(8,128)S(1)} %get-tuple-element.44.a_ref), custom_call_target="tpu_custom_call" | custom-call | flops 8000000000 | bytes 2097152 | tf_op jit(solution)/shard_map/first_factor/pallas_call | solution.py:161
  35.2 1.6 %collective-permute-start.8 = (f32[8,64,128]{2,1,0:T(8,128)S(1)}, f32[8,64,128]{2,1,0:T(8,128)S(1)}, u32[]{:S(2)}, u32[]{:S(2)}) collective-permute-start(f32[8,64,128]{2,1,0:T(8,128)S(1)} %broadcast_select_fusion.3), channel_id=1, source_target_pairs={{0,16},{4,20},{8,24},{12,28},{16,0},{20,4},{24,8},{28,12},{1,17},{... | collective-permute-start | bytes 786440 | tf_op jit(solution)/shard_map/ppermute | solution.py:288
  36.8 1.5 %collective-permute-start.9 = (f32[8,64,128]{2,1,0:T(8,128)S(1)}, f32[8,64,128]{2,1,0:T(8,128)S(1)}, u32[]{:S(2)}, u32[]{:S(2)}) collective-permute-start(f32[8,64,128]{2,1,0:T(8,128)S(1)} %broadcast_select_fusion.1), channel_id=1, source_target_pairs={{0,8},{4,12},{8,0},{12,4},{16,24},{20,28},{24,16},{28,20},{1,9},{5... | collective-permute-start | bytes 786440 | tf_op jit(solution)/shard_map/ppermute | solution.py:288
  38.3 0.0 collective-permute-start.10
  38.3 7.3 %second_factor.1 = (f32[128,128]{1,0:T(8,128)S(1)}, f32[256,256]{1,0:T(8,128)S(1)}, f32[256,256]{1,0:T(8,128)S(1)}, f32[8,4,128,128]{3,2,1,0:T(8,128)S(1)}) custom-call(f32[128,128]{1,0:T(8,128)S(1)} %get-tuple-element.43.low_ref, f32[128,128]{1,0:T(8,128)S(1)} %get-tuple-element.45.a_ref, f32[128,128]{1,0:T(8,128)S(1)} %get-tuple-element.32.w0_ref, ...), custom_call_target="tpu_custom_call" | custom-call | flops 8000000000 | bytes 4194304 | tf_op jit(solution)/shard_map/second_factor/pallas_call | solution.py:204
  45.6 0.0 collective-permute-done.8
  45.7 0.0 collective-permute-done.9
  45.7 0.1 collective-permute-start.11
  45.8 0.5 collective-permute-start.12
  46.3 0.0 collective-permute-done.10.rows_other_ref
  46.3 1.0 %collective-permute-done.11.oa_ref = f32[8,64,128]{2,1,0:T(8,128)S(1)} collective-permute-done((f32[8,64,128]{2,1,0:T(8,128)S(1)}, f32[8,64,128]{2,1,0:T(8,128)S(1)}, u32[]{:S(2)}, u32[]{:S(2)}) %collective-permute-start.11) | collective-permute-done | bytes 262176 | tf_op jit(solution)/shard_map/ppermute | solution.py:288
  47.3 0.4 collective-permute-done.12.ob_ref
  47.7 6.9 %settle.1 = f32[4,128,8,128]{3,2,1,0:T(8,128)} custom-call(f32[128,128]{1,0:T(8,128)S(1)} %get-tuple-element.27.f0_ref, f32[128,128]{1,0:T(8,128)S(1)} %get-tuple-element.33.f1_ref, f32[256,256]{1,0:T(8,128)S(1)} %get-tuple-element.37.w_ref, f32[256,256]{1,0:T(8,128)S(1)} %get-tuple-element.38.mixed_ref, f32[4,128,128]{2,1,0:T(8,128)S(1)} %broadcast_select_fusion.4.rows_ref, ...), custom_call_target="tpu_custom_call" | custom-call | flops 4000000000 | bytes 6291456 | tf_op jit(solution)/shard_map/settle/pallas_call | solution.py:275
  (11 shorter events, 0.2 us)
Async XLA Ops:
  0.0 1.6 %copy-start = (f32[4,128,8,128]{3,2,1,0:T(8,128)S(1)}, f32[4,128,8,128]{3,2,1,0:T(8,128)}, u32[]{:S(2)}) copy-start(f32[4,128,8,128]{3,2,1,0:T(8,128)} %matrix_ref.5) | copy-start | bytes 6291460
  1.6 3.1 %copy-start.1 = (f32[4,128,8,128]{3,2,1,0:T(8,128)S(1)}, f32[4,128,8,128]{3,2,1,0:T(8,128)}, u32[]{:S(2)}) copy-start(f32[4,128,8,128]{3,2,1,0:T(8,128)} %matrix_ref.5) | copy-start | bytes 6291460
  1.7 5.2 %collective-permute-start = (f32[128,128]{1,0:T(8,128)S(1)}, f32[128,128]{1,0:T(8,128)S(1)}, u32[]{:S(2)}, u32[]{:S(2)}) collective-permute-start(f32[128,128]{1,0:T(8,128)S(1)} %corner_block.1), channel_id=1, source_target_pairs={{0,8},{4,12},{8,0},{12,4},{16,24},{20,28},{24,16},{28,20},{1,9},{5... | collective-permute-start | bytes 196616 | tf_op jit(solution)/shard_map/ppermute | solution.py:288
  6.9 4.4 %collective-permute-start.1 = (f32[128,128]{1,0:T(8,128)S(1)}, f32[128,128]{1,0:T(8,128)S(1)}, u32[]{:S(2)}, u32[]{:S(2)}) collective-permute-start(f32[128,128]{1,0:T(8,128)S(1)} %broadcast_select_fusion.5), channel_id=1, source_target_pairs={{0,16},{4,20},{8,24},{12,28},{16,0},{20,4},{24,8},{28,12},{1,17},{... | collective-permute-start | bytes 196616 | tf_op jit(solution)/shard_map/ppermute | solution.py:288
  11.3 5.5 %collective-permute-start.2 = (f32[128,128]{1,0:T(8,128)S(1)}, f32[128,128]{1,0:T(8,128)S(1)}, u32[]{:S(2)}, u32[]{:S(2)}) collective-permute-start(f32[128,128]{1,0:T(8,128)S(1)} %broadcast_select_fusion.6), channel_id=1, source_target_pairs={{0,2},{1,3},{2,0},{3,1},{4,6},{5,7},{6,4},{7,5},{8,10},{9,11},{10,... | collective-permute-start | bytes 196616 | tf_op jit(solution)/shard_map/ppermute | solution.py:288
  16.8 8.2 %collective-permute-start.3 = (f32[128,128]{1,0:T(8,128)S(1)}, f32[128,128]{1,0:T(8,128)S(1)}, u32[]{:S(2)}, u32[]{:S(2)}) collective-permute-start(f32[128,128]{1,0:T(8,128)S(1)} %broadcast_select_fusion.7), channel_id=1, source_target_pairs={{0,1},{1,0},{2,3},{3,2},{4,5},{5,4},{6,7},{7,6},{8,9},{9,8},{10,11... | collective-permute-start | bytes 196616 | tf_op jit(solution)/shard_map/ppermute | solution.py:288
  18.7 11.4 %collective-permute-start.5 = (f32[4,128,128]{2,1,0:T(8,128)S(1)}, f32[4,128,128]{2,1,0:T(8,128)S(1)}, u32[]{:S(2)}, u32[]{:S(2)}) collective-permute-start(f32[4,128,128]{2,1,0:T(8,128)S(1)} %get-tuple-element.29), channel_id=1, source_target_pairs={{0,2},{1,3},{2,0},{3,1},{4,6},{5,7},{6,4},{7,5},{8,10},{9,11},{10,... | collective-permute-start | bytes 786440 | tf_op jit(solution)/shard_map/ppermute | solution.py:288
  21.9 8.1 %collective-permute-start.6 = (f32[8,64,128]{2,1,0:T(8,128)S(1)}, f32[8,64,128]{2,1,0:T(8,128)S(1)}, u32[]{:S(2)}, u32[]{:S(2)}) collective-permute-start(f32[8,64,128]{2,1,0:T(8,128)S(1)} %get-tuple-element.30), channel_id=1, source_target_pairs={{0,8},{4,12},{8,0},{12,4},{16,24},{20,28},{24,16},{28,20},{1,9},{5... | collective-permute-start | bytes 786440 | tf_op jit(solution)/shard_map/ppermute | solution.py:288
  23.4 6.7 %collective-permute-start.7 = (f32[8,64,128]{2,1,0:T(8,128)S(1)}, f32[8,64,128]{2,1,0:T(8,128)S(1)}, u32[]{:S(2)}, u32[]{:S(2)}) collective-permute-start(f32[8,64,128]{2,1,0:T(8,128)S(1)} %get-tuple-element.31), channel_id=1, source_target_pairs={{0,16},{4,20},{8,24},{12,28},{16,0},{20,4},{24,8},{28,12},{1,17},{... | collective-permute-start | bytes 786440 | tf_op jit(solution)/shard_map/ppermute | solution.py:288
  25.0 5.2 %collective-permute-start.4 = (f32[2,128,128]{2,1,0:T(8,128)S(1)}, f32[2,128,128]{2,1,0:T(8,128)S(1)}, u32[]{:S(2)}, u32[]{:S(2)}) collective-permute-start(f32[2,128,128]{2,1,0:T(8,128)S(1)} %pad_maximum_fusion), channel_id=1, source_target_pairs={{0,4},{4,0},{8,12},{12,8},{16,20},{20,16},{24,28},{28,24},{1,5},{5... | collective-permute-start | bytes 393224 | tf_op jit(solution)/shard_map/ppermute | solution.py:288
  35.2 10.4 %collective-permute-start.8 = (f32[8,64,128]{2,1,0:T(8,128)S(1)}, f32[8,64,128]{2,1,0:T(8,128)S(1)}, u32[]{:S(2)}, u32[]{:S(2)}) collective-permute-start(f32[8,64,128]{2,1,0:T(8,128)S(1)} %broadcast_select_fusion.3), channel_id=1, source_target_pairs={{0,16},{4,20},{8,24},{12,28},{16,0},{20,4},{24,8},{28,12},{1,17},{... | collective-permute-start | bytes 786440 | tf_op jit(solution)/shard_map/ppermute | solution.py:288
  36.8 8.9 %collective-permute-start.9 = (f32[8,64,128]{2,1,0:T(8,128)S(1)}, f32[8,64,128]{2,1,0:T(8,128)S(1)}, u32[]{:S(2)}, u32[]{:S(2)}) collective-permute-start(f32[8,64,128]{2,1,0:T(8,128)S(1)} %broadcast_select_fusion.1), channel_id=1, source_target_pairs={{0,8},{4,12},{8,0},{12,4},{16,24},{20,28},{24,16},{28,20},{1,9},{5... | collective-permute-start | bytes 786440 | tf_op jit(solution)/shard_map/ppermute | solution.py:288
  38.3 8.0 %collective-permute-start.10 = (f32[4,128,128]{2,1,0:T(8,128)S(1)}, f32[4,128,128]{2,1,0:T(8,128)S(1)}, u32[]{:S(2)}, u32[]{:S(2)}) collective-permute-start(f32[4,128,128]{2,1,0:T(8,128)S(1)} %broadcast_select_fusion.4.rows_ref), channel_id=1, source_target_pairs={{0,1},{1,0},{2,3},{3,2},{4,5},{5,4},{6,7},{7,6},{8,9},{9,8},{10,11... | collective-permute-start | bytes 786440 | tf_op jit(solution)/shard_map/ppermute | solution.py:288
  45.7 1.6 %collective-permute-start.11 = (f32[8,64,128]{2,1,0:T(8,128)S(1)}, f32[8,64,128]{2,1,0:T(8,128)S(1)}, u32[]{:S(2)}, u32[]{:S(2)}) collective-permute-start(f32[8,64,128]{2,1,0:T(8,128)S(1)} %broadcast_select_fusion.ha_ref), channel_id=1, source_target_pairs={{0,4},{4,0},{8,12},{12,8},{16,20},{20,16},{24,28},{28,24},{1,5},{5... | collective-permute-start | bytes 786440 | tf_op jit(solution)/shard_map/ppermute | solution.py:288
  45.8 1.9 %collective-permute-start.12 = (f32[8,64,128]{2,1,0:T(8,128)S(1)}, f32[8,64,128]{2,1,0:T(8,128)S(1)}, u32[]{:S(2)}, u32[]{:S(2)}) collective-permute-start(f32[8,64,128]{2,1,0:T(8,128)S(1)} %broadcast_select_fusion.2.hb_ref), channel_id=1, source_target_pairs={{0,4},{4,0},{8,12},{12,8},{16,20},{20,16},{24,28},{28,24},{1,5},{5... | collective-permute-start | bytes 786440 | tf_op jit(solution)/shard_map/ppermute | solution.py:288

commit v10 on v9

--- a/solution.py
+++ b/solution.py
@@ -318,9 +318,6 @@
     block = spread(block, "row", grid_row, n_row, row_bits[:1])
     block, upper, lower = after(block, upper, lower)
     block = spread(block, "row", grid_row, n_row, row_bits[1:])
-    ha = spread(upper, "row", grid_row, n_row, row_bits[:1])
-    hb = spread(lower, "row", grid_row, n_row, row_bits[:0:-1])
-    rows = spread(column, "col", grid_col, n_col, col_bits)
     block = spread(block, "col", grid_col, n_col, col_bits)
     across = exchange(block, "col", 1, n_col)
     mine = jnp.stack([jnp.where(right, across, block), jnp.where(right, block, across)])
@@ -330,9 +327,10 @@
     a10 = jnp.where(odd, mine[0], other[0])
     a11 = jnp.where(odd, mine[1], other[1])
     f0, w0 = first_factor(a00)
-    w0, rows, ha, hb = after(w0, rows, ha, hb)
-    ha = spread(ha, "row", grid_row, n_row, row_bits[1:])
-    hb = spread(hb, "row", grid_row, n_row, row_bits[:1])
+    w0, row_then, col_then = after(w0, grid_row, grid_col)
+    ha = spread(upper, "row", row_then, n_row, row_bits)
+    hb = spread(lower, "row", row_then, n_row, row_bits[::-1])
+    rows = spread(column, "col", col_then, n_col, col_bits)
     rows_other = exchange(rows, "col", 1, n_col)
     f1, w, mixed, blocks = second_factor(a10, a11, w0, kernel)
     w, ha, hb = after(w, ha, hb)

time: 54.9 us -> 55.8 us (1.016)
  starting transfers between devices: 20.2 us -> 23.1 us
  waiting for transfers between devices: 12.5 us -> 10.3 us
    ppermute x13, starting transfers between devices: 20.2 us -> 23.1 us  [exchange(): return lax.ppermute(value, axis, [(i, i ^ mask) for i in range(size)])]
    ppermute x13, waiting for transfers between devices: 12.5 us -> 10.3 us  [exchange(): return lax.ppermute(value, axis, [(i, i ^ mask) for i in range(size)])]
  transfers between devices with their start and end apart: 13 -> 13, of which waited for: 6 -> 7; matrix products, arithmetic and copies ran while one was open for 0% -> 0% of each run, Pallas kernels for 15% -> 23%
where the time goes in v10:
time: 55.8 us; the launch traced here: 55.6 us
  starting transfers between devices  23.1 us (41%)
  Pallas kernels  20 us (36%)
  waiting for transfers between devices  10.3 us (18%)
  local copies, waits for them, and re-layouts  1.59 us (3%)
    ppermute x13, starting transfers between devices, exchange(): return lax.ppermute(value, axis, [(i, i ^ mask) for i in range(size)])  23.1 us
    ppermute x13, waiting for transfers between devices, exchange(): return lax.ppermute(value, axis, [(i, i ^ mask) for i in range(size)])  10.3 us
    pallas_call x1, Pallas kernels, second_factor(): pl.pallas_call(second_factor_kernel, out_shape=[square, double, double, b...  7.33 us
    pallas_call x1, Pallas kernels, settle(): pl.pallas_call(settle_kernel, out_shape=jax.ShapeDtypeStruct((local_rows,...  6.89 us
    pallas_call x1, Pallas kernels, first_factor(): pl.pallas_call(first_factor_kernel, out_shape=[square, square], in_specs=...  5 us
    unnamed x4, local copies, waits for them, and re-layouts  1.59 us
  transfers between devices with their start and end apart: 13, of which 7 were waited for; matrix products, arithmetic and copies ran while one was open for 0% of the time, Pallas kernels for 23%

profile of v10, /device:TPU:0, one launch (start us, length us, event | category | flops | bytes accessed | tf_op | source)
XLA Modules:
  0.0 55.6 jit_solution(14142624388799646344)
XLA Ops:
  0.0 0.0 copy-start
  0.0 1.6 %copy-done = f32[4,128,8,128]{3,2,1,0:T(8,128)S(1)} copy-done((f32[4,128,8,128]{3,2,1,0:T(8,128)S(1)}, f32[4,128,8,128]{3,2,1,0:T(8,128)}, u32[]{:S(2)}) %copy-start) | copy-done | bytes 2097176
  1.6 0.0 copy-start.1
  1.6 0.1 corner_block.1
  1.7 3.0 %collective-permute-start = (f32[128,128]{1,0:T(8,128)S(1)}, f32[128,128]{1,0:T(8,128)S(1)}, u32[]{:S(2)}, u32[]{:S(2)}) collective-permute-start(f32[128,128]{1,0:T(8,128)S(1)} %corner_block.1), channel_id=1, source_target_pairs={{0,8},{4,12},{8,0},{12,4},{16,24},{20,28},{24,16},{28,20},{1,9},{5... | collective-permute-start | bytes 196616 | tf_op jit(solution)/shard_map/ppermute | solution.py:288
  4.7 0.0 copy-done.1
  4.7 0.7 %panels.1 = (f32[4,128,128]{2,1,0:T(8,128)S(1)}, f32[8,64,128]{2,1,0:T(8,128)S(1)}, f32[8,64,128]{2,1,0:T(8,128)S(1)}) custom-call(f32[4,128,8,128]{3,2,1,0:T(8,128)S(1)} %copy-done.1), custom_call_target="tpu_custom_call" | custom-call | bytes 4194304 | tf_op jit(solution)/shard_map/panels/pallas_call | solution.py:142
  5.4 1.5 %collective-permute-done = f32[128,128]{1,0:T(8,128)S(1)} collective-permute-done((f32[128,128]{1,0:T(8,128)S(1)}, f32[128,128]{1,0:T(8,128)S(1)}, u32[]{:S(2)}, u32[]{:S(2)}) %collective-permute-start) | collective-permute-done | bytes 65568 | tf_op jit(solution)/shard_map/ppermute | solution.py:288
  6.9 2.1 %collective-permute-start.1 = (f32[128,128]{1,0:T(8,128)S(1)}, f32[128,128]{1,0:T(8,128)S(1)}, u32[]{:S(2)}, u32[]{:S(2)}) collective-permute-start(f32[128,128]{1,0:T(8,128)S(1)} %broadcast_select_fusion.5), channel_id=1, source_target_pairs={{0,16},{4,20},{8,24},{12,28},{16,0},{20,4},{24,8},{28,12},{1,17},{... | collective-permute-start | bytes 196616 | tf_op jit(solution)/shard_map/ppermute | solution.py:288
  9.0 2.2 %collective-permute-done.1 = f32[128,128]{1,0:T(8,128)S(1)} collective-permute-done((f32[128,128]{1,0:T(8,128)S(1)}, f32[128,128]{1,0:T(8,128)S(1)}, u32[]{:S(2)}, u32[]{:S(2)}) %collective-permute-start.1) | collective-permute-done | bytes 65568 | tf_op jit(solution)/shard_map/ppermute | solution.py:288
  11.3 3.2 %collective-permute-start.2 = (f32[128,128]{1,0:T(8,128)S(1)}, f32[128,128]{1,0:T(8,128)S(1)}, u32[]{:S(2)}, u32[]{:S(2)}) collective-permute-start(f32[128,128]{1,0:T(8,128)S(1)} %broadcast_select_fusion.6), channel_id=1, source_target_pairs={{0,2},{1,3},{2,0},{3,1},{4,6},{5,7},{6,4},{7,5},{8,10},{9,11},{10,... | collective-permute-start | bytes 196616 | tf_op jit(solution)/shard_map/ppermute | solution.py:288
  14.4 2.3 %collective-permute-done.2 = f32[128,128]{1,0:T(8,128)S(1)} collective-permute-done((f32[128,128]{1,0:T(8,128)S(1)}, f32[128,128]{1,0:T(8,128)S(1)}, u32[]{:S(2)}, u32[]{:S(2)}) %collective-permute-start.2) | collective-permute-done | bytes 65568 | tf_op jit(solution)/shard_map/ppermute | solution.py:288
  16.8 1.9 %collective-permute-start.3 = (f32[128,128]{1,0:T(8,128)S(1)}, f32[128,128]{1,0:T(8,128)S(1)}, u32[]{:S(2)}, u32[]{:S(2)}) collective-permute-start(f32[128,128]{1,0:T(8,128)S(1)} %broadcast_select_fusion.7), channel_id=1, source_target_pairs={{0,1},{1,0},{2,3},{3,2},{4,5},{5,4},{6,7},{7,6},{8,9},{9,8},{10,11... | collective-permute-start | bytes 196616 | tf_op jit(solution)/shard_map/ppermute | solution.py:288
  18.7 2.4 %collective-permute-done.3 = f32[128,128]{1,0:T(8,128)S(1)} collective-permute-done((f32[128,128]{1,0:T(8,128)S(1)}, f32[128,128]{1,0:T(8,128)S(1)}, u32[]{:S(2)}, u32[]{:S(2)}) %collective-permute-start.3) | collective-permute-done | bytes 65568 | tf_op jit(solution)/shard_map/ppermute | solution.py:288
  21.1 0.1 collective-permute-start.4
  21.2 3.5 %collective-permute-start.9 = (f32[4,128,128]{2,1,0:T(8,128)S(1)}, f32[4,128,128]{2,1,0:T(8,128)}, u32[]{:S(2)}, u32[]{:S(2)}) collective-permute-start(f32[4,128,128]{2,1,0:T(8,128)S(1)} %get-tuple-element.37), channel_id=1, source_target_pairs={{0,2},{1,3},{2,0},{3,1},{4,6},{5,7},{6,4},{7,5},{8,10},{9,11},{10,... | collective-permute-start | bytes 786440 | tf_op jit(solution)/shard_map/ppermute | solution.py:288
  24.7 1.5 %collective-permute-start.5 = (f32[8,64,128]{2,1,0:T(8,128)S(1)}, f32[8,64,128]{2,1,0:T(8,128)}, u32[]{:S(2)}, u32[]{:S(2)}) collective-permute-start(f32[8,64,128]{2,1,0:T(8,128)S(1)} %get-tuple-element.32), channel_id=1, source_target_pairs={{0,8},{4,12},{8,0},{12,4},{16,24},{20,28},{24,16},{28,20},{1,9},{5... | collective-permute-start | bytes 786440 | tf_op jit(solution)/shard_map/ppermute | solution.py:288
  26.2 1.5 %collective-permute-start.7 = (f32[8,64,128]{2,1,0:T(8,128)S(1)}, f32[8,64,128]{2,1,0:T(8,128)}, u32[]{:S(2)}, u32[]{:S(2)}) collective-permute-start(f32[8,64,128]{2,1,0:T(8,128)S(1)} %get-tuple-element.33), channel_id=1, source_target_pairs={{0,16},{4,20},{8,24},{12,28},{16,0},{20,4},{24,8},{28,12},{1,17},{... | collective-permute-start | bytes 786440 | tf_op jit(solution)/shard_map/ppermute | solution.py:288
  27.7 0.0 collective-permute-done.4
  27.7 5.0 %first_factor.1 = (f32[128,128]{1,0:T(8,128)S(1)}, f32[128,128]{1,0:T(8,128)S(1)}) custom-call(f32[128,128]{1,0:T(8,128)S(1)} %get-tuple-element.42.a_ref), custom_call_target="tpu_custom_call" | custom-call | flops 8000000000 | bytes 2097152 | tf_op jit(solution)/shard_map/first_factor/pallas_call | solution.py:161
  32.7 0.4 collective-permute-done.5
  33.2 1.6 %collective-permute-start.6 = (f32[8,64,128]{2,1,0:T(8,128)S(1)}, f32[8,64,128]{2,1,0:T(8,128)S(1)}, u32[]{:S(2)}, u32[]{:S(2)}) collective-permute-start(f32[8,64,128]{2,1,0:T(8,128)S(1)} %broadcast_select_fusion.2), channel_id=1, source_target_pairs={{0,16},{4,20},{8,24},{12,28},{16,0},{20,4},{24,8},{28,12},{1,17},{... | collective-permute-start | bytes 786440 | tf_op jit(solution)/shard_map/ppermute | solution.py:288
  34.8 0.0 collective-permute-done.7
  34.8 2.5 %collective-permute-start.8 = (f32[8,64,128]{2,1,0:T(8,128)S(1)}, f32[8,64,128]{2,1,0:T(8,128)S(1)}, u32[]{:S(2)}, u32[]{:S(2)}) collective-permute-start(f32[8,64,128]{2,1,0:T(8,128)S(1)} %broadcast_select_fusion.3), channel_id=1, source_target_pairs={{0,8},{4,12},{8,0},{12,4},{16,24},{20,28},{24,16},{28,20},{1,9},{5... | collective-permute-start | bytes 786440 | tf_op jit(solution)/shard_map/ppermute | solution.py:288
  37.3 0.0 collective-permute-done.9
  37.4 1.8 %collective-permute-start.10 = (f32[4,128,128]{2,1,0:T(8,128)S(1)}, f32[4,128,128]{2,1,0:T(8,128)S(1)}, u32[]{:S(2)}, u32[]{:S(2)}) collective-permute-start(f32[4,128,128]{2,1,0:T(8,128)S(1)} %broadcast_select_fusion.rows_ref), channel_id=1, source_target_pairs={{0,1},{1,0},{2,3},{3,2},{4,5},{5,4},{6,7},{7,6},{8,9},{9,8},{10,11... | collective-permute-start | bytes 786440 | tf_op jit(solution)/shard_map/ppermute | solution.py:288
  39.1 7.3 %second_factor.1 = (f32[128,128]{1,0:T(8,128)S(1)}, f32[256,256]{1,0:T(8,128)S(1)}, f32[256,256]{1,0:T(8,128)S(1)}, f32[8,4,128,128]{3,2,1,0:T(8,128)S(1)}) custom-call(f32[128,128]{1,0:T(8,128)S(1)} %get-tuple-element.41.low_ref, f32[128,128]{1,0:T(8,128)S(1)} %get-tuple-element.43.a_ref, f32[128,128]{1,0:T(8,128)S(1)} %get-tuple-element.28.w0_ref, ...), custom_call_target="tpu_custom_call" | custom-call | flops 8000000000 | bytes 4194304 | tf_op jit(solution)/shard_map/second_factor/pallas_call | solution.py:204
  46.5 0.0 collective-permute-done.6
  46.5 0.0 collective-permute-done.8
  46.6 0.1 collective-permute-start.11
  46.7 0.5 collective-permute-start.12
  47.2 0.0 collective-permute-done.10.rows_other_ref
  47.2 1.0 %collective-permute-done.11.oa_ref = f32[8,64,128]{2,1,0:T(8,128)S(1)} collective-permute-done((f32[8,64,128]{2,1,0:T(8,128)S(1)}, f32[8,64,128]{2,1,0:T(8,128)S(1)}, u32[]{:S(2)}, u32[]{:S(2)}) %collective-permute-start.11) | collective-permute-done | bytes 262176 | tf_op jit(solution)/shard_map/ppermute | solution.py:288
  48.2 0.4 collective-permute-done.12.ob_ref
  48.6 6.9 %settle.1 = f32[4,128,8,128]{3,2,1,0:T(8,128)} custom-call(f32[128,128]{1,0:T(8,128)S(1)} %get-tuple-element.26.f0_ref, f32[128,128]{1,0:T(8,128)S(1)} %get-tuple-element.29.f1_ref, f32[256,256]{1,0:T(8,128)S(1)} %get-tuple-element.34.w_ref, f32[256,256]{1,0:T(8,128)S(1)} %get-tuple-element.35.mixed_ref, f32[4,128,128]{2,1,0:T(8,128)S(1)} %broadcast_select_fusion.rows_ref, ...), custom_call_target="tpu_custom_call" | custom-call | flops 4000000000 | bytes 6291456 | tf_op jit(solution)/shard_map/settle/pallas_call | solution.py:275
  (11 shorter events, 0.2 us)
Async XLA Ops:
  0.0 1.6 %copy-start = (f32[4,128,8,128]{3,2,1,0:T(8,128)S(1)}, f32[4,128,8,128]{3,2,1,0:T(8,128)}, u32[]{:S(2)}) copy-start(f32[4,128,8,128]{3,2,1,0:T(8,128)} %matrix_ref.5) | copy-start | bytes 6291460
  1.6 3.1 %copy-start.1 = (f32[4,128,8,128]{3,2,1,0:T(8,128)S(1)}, f32[4,128,8,128]{3,2,1,0:T(8,128)}, u32[]{:S(2)}) copy-start(f32[4,128,8,128]{3,2,1,0:T(8,128)} %matrix_ref.5) | copy-start | bytes 6291460
  1.7 5.2 %collective-permute-start = (f32[128,128]{1,0:T(8,128)S(1)}, f32[128,128]{1,0:T(8,128)S(1)}, u32[]{:S(2)}, u32[]{:S(2)}) collective-permute-start(f32[128,128]{1,0:T(8,128)S(1)} %corner_block.1), channel_id=1, source_target_pairs={{0,8},{4,12},{8,0},{12,4},{16,24},{20,28},{24,16},{28,20},{1,9},{5... | collective-permute-start | bytes 196616 | tf_op jit(solution)/shard_map/ppermute | solution.py:288
  6.9 4.4 %collective-permute-start.1 = (f32[128,128]{1,0:T(8,128)S(1)}, f32[128,128]{1,0:T(8,128)S(1)}, u32[]{:S(2)}, u32[]{:S(2)}) collective-permute-start(f32[128,128]{1,0:T(8,128)S(1)} %broadcast_select_fusion.5), channel_id=1, source_target_pairs={{0,16},{4,20},{8,24},{12,28},{16,0},{20,4},{24,8},{28,12},{1,17},{... | collective-permute-start | bytes 196616 | tf_op jit(solution)/shard_map/ppermute | solution.py:288
  11.3 5.5 %collective-permute-start.2 = (f32[128,128]{1,0:T(8,128)S(1)}, f32[128,128]{1,0:T(8,128)S(1)}, u32[]{:S(2)}, u32[]{:S(2)}) collective-permute-start(f32[128,128]{1,0:T(8,128)S(1)} %broadcast_select_fusion.6), channel_id=1, source_target_pairs={{0,2},{1,3},{2,0},{3,1},{4,6},{5,7},{6,4},{7,5},{8,10},{9,11},{10,... | collective-permute-start | bytes 196616 | tf_op jit(solution)/shard_map/ppermute | solution.py:288
  16.8 4.3 %collective-permute-start.3 = (f32[128,128]{1,0:T(8,128)S(1)}, f32[128,128]{1,0:T(8,128)S(1)}, u32[]{:S(2)}, u32[]{:S(2)}) collective-permute-start(f32[128,128]{1,0:T(8,128)S(1)} %broadcast_select_fusion.7), channel_id=1, source_target_pairs={{0,1},{1,0},{2,3},{3,2},{4,5},{5,4},{6,7},{7,6},{8,9},{9,8},{10,11... | collective-permute-start | bytes 196616 | tf_op jit(solution)/shard_map/ppermute | solution.py:288
  21.1 6.5 %collective-permute-start.4 = (f32[2,128,128]{2,1,0:T(8,128)S(1)}, f32[2,128,128]{2,1,0:T(8,128)S(1)}, u32[]{:S(2)}, u32[]{:S(2)}) collective-permute-start(f32[2,128,128]{2,1,0:T(8,128)S(1)} %pad_maximum_fusion), channel_id=1, source_target_pairs={{0,4},{4,0},{8,12},{12,8},{16,20},{20,16},{24,28},{28,24},{1,5},{5... | collective-permute-start | bytes 393224 | tf_op jit(solution)/shard_map/ppermute | solution.py:288
  21.2 16.1 %collective-permute-start.9 = (f32[4,128,128]{2,1,0:T(8,128)S(1)}, f32[4,128,128]{2,1,0:T(8,128)}, u32[]{:S(2)}, u32[]{:S(2)}) collective-permute-start(f32[4,128,128]{2,1,0:T(8,128)S(1)} %get-tuple-element.37), channel_id=1, source_target_pairs={{0,2},{1,3},{2,0},{3,1},{4,6},{5,7},{6,4},{7,5},{8,10},{9,11},{10,... | collective-permute-start | bytes 786440 | tf_op jit(solution)/shard_map/ppermute | solution.py:288
  24.7 8.5 %collective-permute-start.5 = (f32[8,64,128]{2,1,0:T(8,128)S(1)}, f32[8,64,128]{2,1,0:T(8,128)}, u32[]{:S(2)}, u32[]{:S(2)}) collective-permute-start(f32[8,64,128]{2,1,0:T(8,128)S(1)} %get-tuple-element.32), channel_id=1, source_target_pairs={{0,8},{4,12},{8,0},{12,4},{16,24},{20,28},{24,16},{28,20},{1,9},{5... | collective-permute-start | bytes 786440 | tf_op jit(solution)/shard_map/ppermute | solution.py:288
  26.2 8.6 %collective-permute-start.7 = (f32[8,64,128]{2,1,0:T(8,128)S(1)}, f32[8,64,128]{2,1,0:T(8,128)}, u32[]{:S(2)}, u32[]{:S(2)}) collective-permute-start(f32[8,64,128]{2,1,0:T(8,128)S(1)} %get-tuple-element.33), channel_id=1, source_target_pairs={{0,16},{4,20},{8,24},{12,28},{16,0},{20,4},{24,8},{28,12},{1,17},{... | collective-permute-start | bytes 786440 | tf_op jit(solution)/shard_map/ppermute | solution.py:288
  33.2 13.3 %collective-permute-start.6 = (f32[8,64,128]{2,1,0:T(8,128)S(1)}, f32[8,64,128]{2,1,0:T(8,128)S(1)}, u32[]{:S(2)}, u32[]{:S(2)}) collective-permute-start(f32[8,64,128]{2,1,0:T(8,128)S(1)} %broadcast_select_fusion.2), channel_id=1, source_target_pairs={{0,16},{4,20},{8,24},{12,28},{16,0},{20,4},{24,8},{28,12},{1,17},{... | collective-permute-start | bytes 786440 | tf_op jit(solution)/shard_map/ppermute | solution.py:288
  34.8 11.7 %collective-permute-start.8 = (f32[8,64,128]{2,1,0:T(8,128)S(1)}, f32[8,64,128]{2,1,0:T(8,128)S(1)}, u32[]{:S(2)}, u32[]{:S(2)}) collective-permute-start(f32[8,64,128]{2,1,0:T(8,128)S(1)} %broadcast_select_fusion.3), channel_id=1, source_target_pairs={{0,8},{4,12},{8,0},{12,4},{16,24},{20,28},{24,16},{28,20},{1,9},{5... | collective-permute-start | bytes 786440 | tf_op jit(solution)/shard_map/ppermute | solution.py:288
  37.4 9.8 %collective-permute-start.10 = (f32[4,128,128]{2,1,0:T(8,128)S(1)}, f32[4,128,128]{2,1,0:T(8,128)S(1)}, u32[]{:S(2)}, u32[]{:S(2)}) collective-permute-start(f32[4,128,128]{2,1,0:T(8,128)S(1)} %broadcast_select_fusion.rows_ref), channel_id=1, source_target_pairs={{0,1},{1,0},{2,3},{3,2},{4,5},{5,4},{6,7},{7,6},{8,9},{9,8},{10,11... | collective-permute-start | bytes 786440 | tf_op jit(solution)/shard_map/ppermute | solution.py:288
  46.6 1.6 %collective-permute-start.11 = (f32[8,64,128]{2,1,0:T(8,128)S(1)}, f32[8,64,128]{2,1,0:T(8,128)S(1)}, u32[]{:S(2)}, u32[]{:S(2)}) collective-permute-start(f32[8,64,128]{2,1,0:T(8,128)S(1)} %broadcast_select_fusion.4.ha_ref), channel_id=1, source_target_pairs={{0,4},{4,0},{8,12},{12,8},{16,20},{20,16},{24,28},{28,24},{1,5},{5... | collective-permute-start | bytes 786440 | tf_op jit(solution)/shard_map/ppermute | solution.py:288
  46.7 1.9 %collective-permute-start.12 = (f32[8,64,128]{2,1,0:T(8,128)S(1)}, f32[8,64,128]{2,1,0:T(8,128)S(1)}, u32[]{:S(2)}, u32[]{:S(2)}) collective-permute-start(f32[8,64,128]{2,1,0:T(8,128)S(1)} %broadcast_select_fusion.1.hb_ref), channel_id=1, source_target_pairs={{0,4},{4,0},{8,12},{12,8},{16,20},{20,16},{24,28},{28,24},{1,5},{5... | collective-permute-start | bytes 786440 | tf_op jit(solution)/shard_map/ppermute | solution.py:288

commit v11 on v10

--- a/solution.py
+++ b/solution.py
@@ -299,6 +299,16 @@
     return held
 
 
+def region(run, *values):
+    shapes = jax.eval_shape(run, *values)
+
+    def skip(*_):
+        return jax.tree.map(lambda leaf: jnp.zeros(leaf.shape, leaf.dtype), shapes)
+
+    everywhere = lax.axis_index("row") < lax.axis_size("row")
+    return lax.cond(everywhere, run, skip, *values)
+
+
 def after(value, *others):
     return lax.optimization_barrier((value,) + others)
 
@@ -315,27 +325,54 @@
 
     block = corner_block(kernel)
     column, upper, lower = panels(kernel)
-    block = spread(block, "row", grid_row, n_row, row_bits[:1])
-    block, upper, lower = after(block, upper, lower)
-    block = spread(block, "row", grid_row, n_row, row_bits[1:])
-    block = spread(block, "col", grid_col, n_col, col_bits)
+    first_bit, last_bit = row_bits[0], row_bits[-1]
+    moved = exchange(block, "row", 1 << first_bit, n_row)
+    upper_moved = exchange(upper, "row", 1 << first_bit, n_row)
+    column_moved = exchange(column, "col", 1 << col_bits[0], n_col)
+    block = region(lambda new, old: jnp.where(bit_set(grid_row, first_bit), new, old), moved, block)
+
+    block, lower = after(block, lower)
+    moved = exchange(block, "row", 1 << row_bits[1], n_row)
+    lower_moved = exchange(lower, "row", 1 << last_bit, n_row)
+
+    def along_col(new, old):
+        block = jnp.where(bit_set(grid_row, row_bits[1]), new, old)
+        block = spread(block, "row", grid_row, n_row, row_bits[2:])
+        return spread(block, "col", grid_col, n_col, col_bits)
+
+    moved, block, upper_moved = after(moved, block, upper_moved)
+    block = region(along_col, moved, block)
+
+    block, row_then = after(block, grid_row)
     across = exchange(block, "col", 1, n_col)
-    mine = jnp.stack([jnp.where(right, across, block), jnp.where(right, block, across)])
-    other = exchange(mine, "row", 1, n_row)
-
-    a00 = jnp.where(odd, other[0], mine[0])
-    a10 = jnp.where(odd, mine[0], other[0])
-    a11 = jnp.where(odd, mine[1], other[1])
-    f0, w0 = first_factor(a00)
+    ha = jnp.where(bit_set(row_then, first_bit), upper_moved, upper)
+    hb = jnp.where(bit_set(row_then, last_bit), lower_moved, lower)
+    rows = jnp.where(bit_set(grid_col, col_bits[0]), column_moved, column)
+    across, block, ha, hb, rows = after(across, block, ha, hb, rows)
+    ha_moved = exchange(ha, "row", 1 << row_bits[1], n_row)
+    hb_moved = exchange(hb, "row", 1 << row_bits[-2], n_row)
+
+    def factor(across, block):
+        mine = jnp.stack([jnp.where(right, across, block), jnp.where(right, block, across)])
+        other = exchange(mine, "row", 1, n_row)
+        a00 = jnp.where(odd, other[0], mine[0])
+        a10 = jnp.where(odd, mine[0], other[0])
+        a11 = jnp.where(odd, mine[1], other[1])
+        f0, w0 = first_factor(a00)
+        return a10, a11, f0, w0
+
+    a10, a11, f0, w0 = region(factor, across, block)
+
     w0, row_then, col_then = after(w0, grid_row, grid_col)
-    ha = spread(upper, "row", row_then, n_row, row_bits)
-    hb = spread(lower, "row", row_then, n_row, row_bits[::-1])
-    rows = spread(column, "col", col_then, n_col, col_bits)
+    ha = jnp.where(bit_set(row_then, row_bits[1]), ha_moved, ha)
+    ha = spread(ha, "row", row_then, n_row, row_bits[2:])
+    hb = jnp.where(bit_set(row_then, row_bits[-2]), hb_moved, hb)
+    hb = spread(hb, "row", row_then, n_row, row_bits[:-2][::-1])
+    rows = spread(rows, "col", col_then, n_col, col_bits[1:])
     rows_other = exchange(rows, "col", 1, n_col)
-    f1, w, mixed, blocks = second_factor(a10, a11, w0, kernel)
-    w, ha, hb = after(w, ha, hb)
     oa = exchange(ha, "row", 1, n_row)
     ob = exchange(hb, "row", 1, n_row)
+    f1, w, mixed, blocks = second_factor(a10, a11, w0, kernel)
     return settle(f0, f1, w, mixed, rows, rows_other, ha, hb, oa, ob, blocks)
 
 

time: 55.8 us -> 65.8 us (1.18)
  waiting for transfers between devices: 10.3 us -> 22.9 us
  starting transfers between devices: 23.1 us -> 15 us
  other arithmetic: 0.23 us -> 3.42 us
  Pallas kernels: 20 us -> 22.3 us
    ppermute x13, waiting for transfers between devices: 10.3 us -> 22.9 us  [exchange(): return lax.ppermute(value, axis, [(i, i ^ mask) for i in range(size)])]
    ppermute x13, starting transfers between devices: 23.1 us -> 15 us  [exchange(): return lax.ppermute(value, axis, [(i, i ^ mask) for i in range(size)])]
    select_n x1 -> x8, other arithmetic: 0.02 us -> 1.73 us  [the longest x1 1.57 us: factor(): a00 = jnp.where(odd, other[0], mine[0])]
    another operation x2, other arithmetic: 0.02 us -> 1.67 us  [factor(): jnp.stack([jnp.where(right, across, block), jnp.where(right, block, acros...]
    pallas_call x1, Pallas kernels: 7.33 us -> 8.24 us  [second_factor(): pl.pallas_call(second_factor_kernel, out_shape=[square, double, double, b...]
    pallas_call x1, Pallas kernels: 6.89 us -> 7.73 us  [settle(): pl.pallas_call(settle_kernel, out_shape=jax.ShapeDtypeStruct((local_rows,...]
    unnamed x4 -> x6, local copies, waits for them, and re-layouts: 1.59 us -> 1.6 us
  transfers between devices with their start and end apart: 13 -> 13, of which waited for: 7 -> 4; matrix products, arithmetic and copies ran while one was open for 0% -> 5% of each run, Pallas kernels for 23% -> 21%
where the time goes in v11:
time: 65.8 us; the launch traced here: 65.5 us
  waiting for transfers between devices  22.9 us (35%)
  Pallas kernels  22.3 us (34%)
  starting transfers between devices  15 us (23%)
  other arithmetic  3.42 us (5%)
  local copies, waits for them, and re-layouts  1.6 us (2%)
    ppermute x13, waiting for transfers between devices, exchange(): return lax.ppermute(value, axis, [(i, i ^ mask) for i in range(size)])  22.9 us
    ppermute x13, starting transfers between devices, exchange(): return lax.ppermute(value, axis, [(i, i ^ mask) for i in range(size)])  15 us
    pallas_call x1, Pallas kernels, second_factor(): pl.pallas_call(second_factor_kernel, out_shape=[square, double, double, b...  8.24 us
    pallas_call x1, Pallas kernels, settle(): pl.pallas_call(settle_kernel, out_shape=jax.ShapeDtypeStruct((local_rows,...  7.73 us
    pallas_call x1, Pallas kernels, first_factor(): pl.pallas_call(first_factor_kernel, out_shape=[square, square], in_specs=...  5.54 us
    another operation x2, other arithmetic, factor(): jnp.stack([jnp.where(right, across, block), jnp.where(right, block, acros...  1.67 us
    unnamed x6, local copies, waits for them, and re-layouts  1.6 us
    select_n x1, other arithmetic, factor(): a00 = jnp.where(odd, other[0], mine[0])  1.57 us
  transfers between devices with their start and end apart: 13, of which 4 were waited for; matrix products, arithmetic and copies ran while one was open for 5% of the time, Pallas kernels for 21%

profile of v11, /device:TPU:0, one launch (start us, length us, event | category | flops | bytes accessed | tf_op | source)
XLA Modules:
  0.0 65.5 jit_solution(11225655244584844654)
XLA Ops:
  0.0 0.0 copy-start
  0.0 1.6 %copy-done = f32[4,128,8,128]{3,2,1,0:T(8,128)S(1)} copy-done((f32[4,128,8,128]{3,2,1,0:T(8,128)S(1)}, f32[4,128,8,128]{3,2,1,0:T(8,128)}, u32[]{:S(2)}) %copy-start) | copy-done | bytes 2097176
  1.6 0.7 %panels.1 = (f32[4,128,128]{2,1,0:T(8,128)S(1)}, f32[8,64,128]{2,1,0:T(8,128)S(1)}, f32[8,64,128]{2,1,0:T(8,128)S(1)}) custom-call(f32[4,128,8,128]{3,2,1,0:T(8,128)S(1)} %copy-done), custom_call_target="tpu_custom_call" | custom-call | bytes 4194304 | tf_op jit(solution)/shard_map/panels/pallas_call | solution.py:142
  2.3 3.0 %collective-permute-start.4 = (f32[8,64,128]{2,1,0:T(8,128)S(1)}, f32[8,64,128]{2,1,0:T(8,128)S(1)}, u32[]{:S(2)}, u32[]{:S(2)}) collective-permute-start(f32[8,64,128]{2,1,0:T(8,128)S(1)} %get-tuple-element.123), channel_id=1, source_target_pairs={{0,8},{4,12},{8,0},{12,4},{16,24},{20,28},{24,16},{28,20},{1,9},{5... | collective-permute-start | bytes 786440 | tf_op jit(solution)/shard_map/ppermute | solution.py:288
  5.3 0.1 corner_block.1
  5.4 0.1 collective-permute-start.2
  5.5 7.6 %collective-permute-done.2 = f32[128,128]{1,0:T(8,128)S(1)} collective-permute-done((f32[128,128]{1,0:T(8,128)S(1)}, f32[128,128]{1,0:T(8,128)S(1)}, u32[]{:S(2)}, u32[]{:S(2)}) %collective-permute-start.2) | collective-permute-done | bytes 65568 | tf_op jit(solution)/shard_map/ppermute | solution.py:288
  13.1 1.8 %collective-permute-start.3 = (f32[128,128]{1,0:T(8,128)S(1)}, f32[128,128]{1,0:T(8,128)S(1)}, u32[]{:S(2)}, u32[]{:S(2)}) collective-permute-start(f32[128,128]{1,0:T(8,128)S(1)} %get-tuple-element.159), channel_id=1, source_target_pairs={{0,16},{4,20},{8,24},{12,28},{16,0},{20,4},{24,8},{28,12},{1,17},{... | collective-permute-start | bytes 196616 | tf_op jit(solution)/shard_map/ppermute | solution.py:288
  14.9 2.6 %collective-permute-start.7 = (f32[4,128,128]{2,1,0:T(8,128)S(1)}, f32[4,128,128]{2,1,0:T(8,128)S(1)}, u32[]{:S(2)}, u32[]{:S(2)}) collective-permute-start(f32[4,128,128]{2,1,0:T(8,128)S(1)} %get-tuple-element.130), channel_id=1, source_target_pairs={{0,2},{1,3},{2,0},{3,1},{4,6},{5,7},{6,4},{7,5},{8,10},{9,11},{10,... | collective-permute-start | bytes 786440 | tf_op jit(solution)/shard_map/ppermute | solution.py:288
  17.5 0.5 collective-permute-start.6
  18.0 0.0 collective-permute-done.3
  18.0 0.0 collective-permute-done.4
  18.0 13.1 %conditional.4 = (f32[128,128]{1,0:T(8,128)S(1)}) conditional(s32[]{:T(128)} %convert_element_type.2, () %tuple.33, (s32[]{:T(128)}, s32[]{:T(128)}, f32[128,128]{1,0:T(8,128)S(1)}, f32[128,128]{1,0:T(8,128)S(1)}) %tuple.38), branch_computations={%region_2.3_spmd, %region_3.4_spmd} | conditional | flops 32774 | bytes 655476 | solution.py:309
  18.0 3.0 %collective-permute-start = (f32[128,128]{1,0:T(8,128)S(1)}, f32[128,128]{1,0:T(8,128)S(1)}, u32[]{:S(2)}, u32[]{:S(2)}) collective-permute-start(f32[128,128]{1,0:T(8,128)S(1)} %broadcast_select_fusion.1), channel_id=1, source_target_pairs={{0,2},{1,3},{2,0},{3,1},{4,6},{5,7},{6,4},{7,5},{8,10},{9,11},{10,... | collective-permute-start | bytes 196616 | tf_op jit(solution)/shard_map/cond/branch_1_fun/ppermute | solution.py:288
  21.0 10.1 %collective-permute-done = f32[128,128]{1,0:T(8,128)S(1)} collective-permute-done((f32[128,128]{1,0:T(8,128)S(1)}, f32[128,128]{1,0:T(8,128)S(1)}, u32[]{:S(2)}, u32[]{:S(2)}) %collective-permute-start) | collective-permute-done | bytes 65568 | tf_op jit(solution)/shard_map/cond/branch_1_fun/ppermute | solution.py:288
  31.1 0.7 %collective-permute-start.5 = (f32[128,128]{1,0:T(8,128)S(1)}, f32[128,128]{1,0:T(8,128)S(1)}, u32[]{:S(2)}, u32[]{:S(2)}) collective-permute-start(f32[128,128]{1,0:T(8,128)S(1)} %get-tuple-element.160), channel_id=1, source_target_pairs={{0,1},{1,0},{2,3},{3,2},{4,5},{5,4},{6,7},{7,6},{8,9},{9,8},{10,11... | collective-permute-start | bytes 196616 | tf_op jit(solution)/shard_map/ppermute | solution.py:288
  31.9 0.0 collective-permute-done.7
  32.0 0.0 collective-permute-done.6
  32.0 3.5 %collective-permute-done.5 = f32[128,128]{1,0:T(8,128)S(1)} collective-permute-done((f32[128,128]{1,0:T(8,128)S(1)}, f32[128,128]{1,0:T(8,128)S(1)}, u32[]{:S(2)}, u32[]{:S(2)}) %collective-permute-start.5) | collective-permute-done | bytes 65568 | tf_op jit(solution)/shard_map/ppermute | solution.py:288
  35.5 0.0 copy-start.2
  35.5 0.6 collective-permute-start.9
  36.0 1.4 %collective-permute-start.10 = (f32[8,64,128]{2,1,0:T(8,128)S(1)}, f32[8,64,128]{2,1,0:T(8,128)S(1)}, u32[]{:S(2)}, u32[]{:S(2)}) collective-permute-start(f32[8,64,128]{2,1,0:T(8,128)S(1)} %broadcast_select_fusion.8), channel_id=1, source_target_pairs={{0,8},{4,12},{8,0},{12,4},{16,24},{20,28},{24,16},{28,20},{1,9},{5... | collective-permute-start | bytes 786440 | tf_op jit(solution)/shard_map/ppermute | solution.py:288
  37.5 0.0 copy-done.2
  37.5 0.0 copy-start.1
  37.5 10.5 %conditional.5 = (f32[128,128]{1,0:T(8,128)}, f32[128,128]{1,0:T(8,128)}, f32[128,128]{1,0:T(8,128)}, f32[128,128]{1,0:T(8,128)}) conditional(s32[]{:T(128)} %convert_element_type.2, () %tuple.32, (s32[]{:T(128)}, s32[]{:T(128)}, f32[128,128]{1,0:T(8,128)}, f32[128,128]{1,0:T(8,128)S(1)}) %tuple.52), branch_computations={%region_4.5_spmd, %region_5.6_spmd} | conditional | flops 8000131072 | bytes 3670327 | solution.py:309
  37.5 1.0 %fusion.3 = (f32[1,128,128]{2,1,0:T(8,128)S(1)}, f32[128,128]{1,0:T(8,128)S(1)}) fusion(f32[128,128]{1,0:T(8,128)S(1)} %get-tuple-element.93, f32[128,128]{1,0:T(8,128)} %get-tuple-element.92, pred[]{:T(512)S(6)} %eq.29), kind=kLoop, calls=%fused_computation.11 | loop fusion | flops 32768 | bytes 262145 | tf_op jit(solution)/shard_map/cond/branch_1_fun/stack | solution.py:356
  38.5 0.7 %pad_maximum_fusion = f32[2,128,128]{2,1,0:T(8,128)} fusion(f32[1,128,128]{2,1,0:T(8,128)S(1)} %get-tuple-element.149, f32[1,128,128]{2,1,0:T(8,128)S(1)} %bitcast.13), kind=kLoop, calls=%fused_computation.3 | loop fusion | flops 32768 | bytes 262144 | tf_op jit(solution)/shard_map/cond/branch_1_fun/stack | solution.py:356
  39.1 0.0 collective-permute-start.1
  39.1 1.7 %collective-permute-done.1 = f32[2,128,128]{2,1,0:T(8,128)} collective-permute-done((f32[2,128,128]{2,1,0:T(8,128)}, f32[2,128,128]{2,1,0:T(8,128)}, u32[]{:S(2)}, u32[]{:S(2)}) %collective-permute-start.1) | collective-permute-done | bytes 131104 | tf_op jit(solution)/shard_map/cond/branch_1_fun/ppermute | solution.py:288
  40.8 1.6 %fusion.1 = (f32[128,128]{1,0:T(8,128)S(1)}, f32[128,128]{1,0:T(8,128)}, f32[128,128]{1,0:T(8,128)}) fusion(f32[128,128]{1,0:T(8,128)S(1)} %get-tuple-element.150, f32[2,128,128]{2,1,0:T(8,128)} %collective-permute-done.1, pred[]{:T(512)S(6)} %eq.28, f32[128,128]{1,0:T(8,128)S(1)} %get-tuple-element.93, f32[128,128]{1,0:T(8,128)} %get-tuple-element.92, ...), kind=kLoop, calls=%fused_computation.7 | loop fusion | flops 65536 | bytes 524290 | tf_op jit(solution)/shard_map/cond/branch_1_fun/jit(_where)/select_n | solution.py:358
  42.4 5.5 %first_factor.1 = (f32[128,128]{1,0:T(8,128)}, f32[128,128]{1,0:T(8,128)}) custom-call(f32[128,128]{1,0:T(8,128)S(1)} %get-tuple-element.146.a_ref), custom_call_target="tpu_custom_call" | custom-call | flops 8000000000 | bytes 2097152 | tf_op jit(solution)/shard_map/cond/branch_1_fun/first_factor/pallas_call | solution.py:161
  47.9 0.6 collective-permute-start.8
  48.6 0.0 collective-permute-done.9
  48.6 0.1 collective-permute-start.11
  48.7 0.0 collective-permute-done.10
  48.8 0.5 collective-permute-start.12
  49.3 0.0 copy-done.1
  49.3 8.2 %second_factor.1 = (f32[128,128]{1,0:T(8,128)S(1)}, f32[256,256]{1,0:T(8,128)S(1)}, f32[256,256]{1,0:T(8,128)S(1)}, f32[8,4,128,128]{3,2,1,0:T(8,128)S(1)}) custom-call(f32[128,128]{1,0:T(8,128)} %get-tuple-element.134.low_ref, f32[128,128]{1,0:T(8,128)} %get-tuple-element.135.a_ref, f32[128,128]{1,0:T(8,128)} %get-tuple-element.137.w0_ref, ...), custom_call_target="tpu_custom_call" | custom-call | flops 8000000000 | bytes 4194304 | tf_op jit(solution)/shard_map/second_factor/pallas_call | solution.py:204
  57.6 0.0 collective-permute-done.8.rows_other_ref
  57.6 0.0 collective-permute-done.11.oa_ref
  57.6 0.0 collective-permute-done.12.ob_ref
  57.6 7.7 %settle.1 = f32[4,128,8,128]{3,2,1,0:T(8,128)} custom-call(f32[128,128]{1,0:T(8,128)} %get-tuple-element.133.f0_ref, f32[128,128]{1,0:T(8,128)S(1)} %get-tuple-element.138.f1_ref, f32[256,256]{1,0:T(8,128)S(1)} %get-tuple-element.139.w_ref, f32[256,256]{1,0:T(8,128)S(1)} %get-tuple-element.140.mixed_ref, f32[4,128,128]{2,1,0:T(8,128)S(1)} %broadcast_select_fusion.7.rows_ref, ...), custom_call_target="tpu_custom_call" | custom-call | flops 4000000000 | bytes 6291456 | tf_op jit(solution)/shard_map/settle/pallas_call | solution.py:275
  (9 shorter events, 0.2 us)
Async XLA Ops:
  0.0 1.6 %copy-start = (f32[4,128,8,128]{3,2,1,0:T(8,128)S(1)}, f32[4,128,8,128]{3,2,1,0:T(8,128)}, u32[]{:S(2)}) copy-start(f32[4,128,8,128]{3,2,1,0:T(8,128)} %matrix_ref.5) | copy-start | bytes 6291460
  2.3 15.7 %collective-permute-start.4 = (f32[8,64,128]{2,1,0:T(8,128)S(1)}, f32[8,64,128]{2,1,0:T(8,128)S(1)}, u32[]{:S(2)}, u32[]{:S(2)}) collective-permute-start(f32[8,64,128]{2,1,0:T(8,128)S(1)} %get-tuple-element.123), channel_id=1, source_target_pairs={{0,8},{4,12},{8,0},{12,4},{16,24},{20,28},{24,16},{28,20},{1,9},{5... | collective-permute-start | bytes 786440 | tf_op jit(solution)/shard_map/ppermute | solution.py:288
  5.4 7.6 %collective-permute-start.2 = (f32[128,128]{1,0:T(8,128)S(1)}, f32[128,128]{1,0:T(8,128)S(1)}, u32[]{:S(2)}, u32[]{:S(2)}) collective-permute-start(f32[128,128]{1,0:T(8,128)S(1)} %corner_block.1), channel_id=1, source_target_pairs={{0,8},{4,12},{8,0},{12,4},{16,24},{20,28},{24,16},{28,20},{1,9},{5... | collective-permute-start | bytes 196616 | tf_op jit(solution)/shard_map/ppermute | solution.py:288
  13.1 4.9 %collective-permute-start.3 = (f32[128,128]{1,0:T(8,128)S(1)}, f32[128,128]{1,0:T(8,128)S(1)}, u32[]{:S(2)}, u32[]{:S(2)}) collective-permute-start(f32[128,128]{1,0:T(8,128)S(1)} %get-tuple-element.159), channel_id=1, source_target_pairs={{0,16},{4,20},{8,24},{12,28},{16,0},{20,4},{24,8},{28,12},{1,17},{... | collective-permute-start | bytes 196616 | tf_op jit(solution)/shard_map/ppermute | solution.py:288
  14.9 17.0 %collective-permute-start.7 = (f32[4,128,128]{2,1,0:T(8,128)S(1)}, f32[4,128,128]{2,1,0:T(8,128)S(1)}, u32[]{:S(2)}, u32[]{:S(2)}) collective-permute-start(f32[4,128,128]{2,1,0:T(8,128)S(1)} %get-tuple-element.130), channel_id=1, source_target_pairs={{0,2},{1,3},{2,0},{3,1},{4,6},{5,7},{6,4},{7,5},{8,10},{9,11},{10,... | collective-permute-start | bytes 786440 | tf_op jit(solution)/shard_map/ppermute | solution.py:288
  17.5 14.5 %collective-permute-start.6 = (f32[8,64,128]{2,1,0:T(8,128)S(1)}, f32[8,64,128]{2,1,0:T(8,128)S(1)}, u32[]{:S(2)}, u32[]{:S(2)}) collective-permute-start(f32[8,64,128]{2,1,0:T(8,128)S(1)} %get-tuple-element.129), channel_id=1, source_target_pairs={{0,16},{4,20},{8,24},{12,28},{16,0},{20,4},{24,8},{28,12},{1,17},{... | collective-permute-start | bytes 786440 | tf_op jit(solution)/shard_map/ppermute | solution.py:288
  18.0 13.1 %collective-permute-start = (f32[128,128]{1,0:T(8,128)S(1)}, f32[128,128]{1,0:T(8,128)S(1)}, u32[]{:S(2)}, u32[]{:S(2)}) collective-permute-start(f32[128,128]{1,0:T(8,128)S(1)} %broadcast_select_fusion.1), channel_id=1, source_target_pairs={{0,2},{1,3},{2,0},{3,1},{4,6},{5,7},{6,4},{7,5},{8,10},{9,11},{10,... | collective-permute-start | bytes 196616 | tf_op jit(solution)/shard_map/cond/branch_1_fun/ppermute | solution.py:288
  31.1 4.3 %collective-permute-start.5 = (f32[128,128]{1,0:T(8,128)S(1)}, f32[128,128]{1,0:T(8,128)S(1)}, u32[]{:S(2)}, u32[]{:S(2)}) collective-permute-start(f32[128,128]{1,0:T(8,128)S(1)} %get-tuple-element.160), channel_id=1, source_target_pairs={{0,1},{1,0},{2,3},{3,2},{4,5},{5,4},{6,7},{7,6},{8,9},{9,8},{10,11... | collective-permute-start | bytes 196616 | tf_op jit(solution)/shard_map/ppermute | solution.py:288
  35.5 2.0 %copy-start.2 = (f32[128,128]{1,0:T(8,128)}, f32[128,128]{1,0:T(8,128)S(1)}, u32[]{:S(2)}) copy-start(f32[128,128]{1,0:T(8,128)S(1)} %collective-permute-done.5) | copy-start | bytes 196612
  35.5 13.1 %collective-permute-start.9 = (f32[8,64,128]{2,1,0:T(8,128)S(1)}, f32[8,64,128]{2,1,0:T(8,128)S(1)}, u32[]{:S(2)}, u32[]{:S(2)}) collective-permute-start(f32[8,64,128]{2,1,0:T(8,128)S(1)} %broadcast_select_fusion.9), channel_id=1, source_target_pairs={{0,16},{4,20},{8,24},{12,28},{16,0},{20,4},{24,8},{28,12},{1,17},{... | collective-permute-start | bytes 786440 | tf_op jit(solution)/shard_map/ppermute | solution.py:288
  36.0 12.7 %collective-permute-start.10 = (f32[8,64,128]{2,1,0:T(8,128)S(1)}, f32[8,64,128]{2,1,0:T(8,128)S(1)}, u32[]{:S(2)}, u32[]{:S(2)}) collective-permute-start(f32[8,64,128]{2,1,0:T(8,128)S(1)} %broadcast_select_fusion.8), channel_id=1, source_target_pairs={{0,8},{4,12},{8,0},{12,4},{16,24},{20,28},{24,16},{28,20},{1,9},{5... | collective-permute-start | bytes 786440 | tf_op jit(solution)/shard_map/ppermute | solution.py:288
  37.5 11.8 %copy-start.1 = (f32[4,128,8,128]{3,2,1,0:T(8,128)S(1)}, f32[4,128,8,128]{3,2,1,0:T(8,128)}, u32[]{:S(2)}) copy-start(f32[4,128,8,128]{3,2,1,0:T(8,128)} %matrix_ref.5) | copy-start | bytes 6291460
  39.1 1.7 %collective-permute-start.1 = (f32[2,128,128]{2,1,0:T(8,128)}, f32[2,128,128]{2,1,0:T(8,128)}, u32[]{:S(2)}, u32[]{:S(2)}) collective-permute-start(f32[2,128,128]{2,1,0:T(8,128)} %pad_maximum_fusion), channel_id=1, source_target_pairs={{0,4},{4,0},{8,12},{12,8},{16,20},{20,16},{24,28},{28,24},{1,5},{5... | collective-permute-start | bytes 393224 | tf_op jit(solution)/shard_map/cond/branch_1_fun/ppermute | solution.py:288
  47.9 9.6 %collective-permute-start.8 = (f32[4,128,128]{2,1,0:T(8,128)S(1)}, f32[4,128,128]{2,1,0:T(8,128)S(1)}, u32[]{:S(2)}, u32[]{:S(2)}) collective-permute-start(f32[4,128,128]{2,1,0:T(8,128)S(1)} %broadcast_select_fusion.7.rows_ref), channel_id=1, source_target_pairs={{0,1},{1,0},{2,3},{3,2},{4,5},{5,4},{6,7},{7,6},{8,9},{9,8},{10,11... | collective-permute-start | bytes 786440 | tf_op jit(solution)/shard_map/ppermute | solution.py:288
  48.6 8.9 %collective-permute-start.11 = (f32[8,64,128]{2,1,0:T(8,128)S(1)}, f32[8,64,128]{2,1,0:T(8,128)S(1)}, u32[]{:S(2)}, u32[]{:S(2)}) collective-permute-start(f32[8,64,128]{2,1,0:T(8,128)S(1)} %broadcast_select_fusion.6.ha_ref), channel_id=1, source_target_pairs={{0,4},{4,0},{8,12},{12,8},{16,20},{20,16},{24,28},{28,24},{1,5},{5... | collective-permute-start | bytes 786440 | tf_op jit(solution)/shard_map/ppermute | solution.py:288
  48.8 8.8 %collective-permute-start.12 = (f32[8,64,128]{2,1,0:T(8,128)S(1)}, f32[8,64,128]{2,1,0:T(8,128)S(1)}, u32[]{:S(2)}, u32[]{:S(2)}) collective-permute-start(f32[8,64,128]{2,1,0:T(8,128)S(1)} %broadcast_select_fusion.5.hb_ref), channel_id=1, source_target_pairs={{0,4},{4,0},{8,12},{12,8},{16,20},{20,16},{24,28},{28,24},{1,5},{5... | collective-permute-start | bytes 786440 | tf_op jit(solution)/shard_map/ppermute | solution.py:288

commit v12 on v11

--- a/solution.py
+++ b/solution.py
@@ -326,48 +326,44 @@
     block = corner_block(kernel)
     column, upper, lower = panels(kernel)
     first_bit, last_bit = row_bits[0], row_bits[-1]
+    column_moved = exchange(column, "col", 1 << col_bits[0], n_col)
     moved = exchange(block, "row", 1 << first_bit, n_row)
+    block = region(lambda new, old: jnp.where(bit_set(grid_row, first_bit), new, old), moved, block)
+
+    block, upper, lower = after(block, upper, lower)
+    moved = exchange(block, "row", 1 << row_bits[1], n_row)
     upper_moved = exchange(upper, "row", 1 << first_bit, n_row)
-    column_moved = exchange(column, "col", 1 << col_bits[0], n_col)
-    block = region(lambda new, old: jnp.where(bit_set(grid_row, first_bit), new, old), moved, block)
-
-    block, lower = after(block, lower)
-    moved = exchange(block, "row", 1 << row_bits[1], n_row)
     lower_moved = exchange(lower, "row", 1 << last_bit, n_row)
+    moved, block, column_moved = after(moved, block, column_moved)
 
     def along_col(new, old):
         block = jnp.where(bit_set(grid_row, row_bits[1]), new, old)
         block = spread(block, "row", grid_row, n_row, row_bits[2:])
         return spread(block, "col", grid_col, n_col, col_bits)
 
-    moved, block, upper_moved = after(moved, block, upper_moved)
     block = region(along_col, moved, block)
 
     block, row_then = after(block, grid_row)
-    across = exchange(block, "col", 1, n_col)
     ha = jnp.where(bit_set(row_then, first_bit), upper_moved, upper)
     hb = jnp.where(bit_set(row_then, last_bit), lower_moved, lower)
-    rows = jnp.where(bit_set(grid_col, col_bits[0]), column_moved, column)
-    across, block, ha, hb, rows = after(across, block, ha, hb, rows)
+    block, ha, hb = after(block, ha, hb)
+    across = exchange(block, "col", 1, n_col)
+    mine = jnp.stack([jnp.where(right, across, block), jnp.where(right, block, across)])
+    other = exchange(mine, "row", 1, n_row)
     ha_moved = exchange(ha, "row", 1 << row_bits[1], n_row)
     hb_moved = exchange(hb, "row", 1 << row_bits[-2], n_row)
 
-    def factor(across, block):
-        mine = jnp.stack([jnp.where(right, across, block), jnp.where(right, block, across)])
-        other = exchange(mine, "row", 1, n_row)
-        a00 = jnp.where(odd, other[0], mine[0])
-        a10 = jnp.where(odd, mine[0], other[0])
-        a11 = jnp.where(odd, mine[1], other[1])
-        f0, w0 = first_factor(a00)
-        return a10, a11, f0, w0
-
-    a10, a11, f0, w0 = region(factor, across, block)
+    a00 = jnp.where(odd, other[0], mine[0])
+    a10 = jnp.where(odd, mine[0], other[0])
+    a11 = jnp.where(odd, mine[1], other[1])
+    f0, w0 = first_factor(a00)
 
     w0, row_then, col_then = after(w0, grid_row, grid_col)
     ha = jnp.where(bit_set(row_then, row_bits[1]), ha_moved, ha)
     ha = spread(ha, "row", row_then, n_row, row_bits[2:])
     hb = jnp.where(bit_set(row_then, row_bits[-2]), hb_moved, hb)
     hb = spread(hb, "row", row_then, n_row, row_bits[:-2][::-1])
+    rows = jnp.where(bit_set(col_then, col_bits[0]), column_moved, column)
     rows = spread(rows, "col", col_then, n_col, col_bits[1:])
     rows_other = exchange(rows, "col", 1, n_col)
     oa = exchange(ha, "row", 1, n_row)

time: 65.8 us -> 58.8 us (0.89)
  other arithmetic: 3.42 us -> 0.26 us
  Pallas kernels: 22.3 us -> 20 us
  waiting for transfers between devices: 22.9 us -> 20.9 us
    ppermute x13, waiting for transfers between devices: 22.9 us -> 20.9 us  [exchange(): return lax.ppermute(value, axis, [(i, i ^ mask) for i in range(size)])]
    another operation x2, other arithmetic: 1.67 us -> 0.03 us  [shards(): jnp.stack([jnp.where(right, across, block), jnp.where(right, block, acros...]
    select_n x2, other arithmetic: 1.6 us -> 0.06 us  [the longest x1 0.04 us: shards(): rows = jnp.where(bit_set(col_then, col_bits[0]), column_moved, column)]
    pallas_call x1, Pallas kernels: 8.24 us -> 7.35 us  [second_factor(): pl.pallas_call(second_factor_kernel, out_shape=[square, double, double, b...]
    pallas_call x1, Pallas kernels: 7.73 us -> 6.9 us  [settle(): pl.pallas_call(settle_kernel, out_shape=jax.ShapeDtypeStruct((local_rows,...]
  transfers between devices with their start and end apart: 13 -> 13, of which waited for: 4 -> 6; matrix products, arithmetic and copies ran while one was open for 5% -> 0% of each run, Pallas kernels for 21% -> 22%
where the time goes in v12:
time: 58.8 us; the launch traced here: 58.3 us
  waiting for transfers between devices  20.9 us (36%)
  Pallas kernels  20 us (34%)
  starting transfers between devices  14.5 us (25%)
  local copies, waits for them, and re-layouts  2.25 us (4%)
    ppermute x13, waiting for transfers between devices, exchange(): return lax.ppermute(value, axis, [(i, i ^ mask) for i in range(size)])  20.9 us
    ppermute x13, starting transfers between devices, exchange(): return lax.ppermute(value, axis, [(i, i ^ mask) for i in range(size)])  14.5 us
    pallas_call x1, Pallas kernels, second_factor(): pl.pallas_call(second_factor_kernel, out_shape=[square, double, double, b...  7.35 us
    pallas_call x1, Pallas kernels, settle(): pl.pallas_call(settle_kernel, out_shape=jax.ShapeDtypeStruct((local_rows,...  6.9 us
    pallas_call x1, Pallas kernels, first_factor(): pl.pallas_call(first_factor_kernel, out_shape=[square, square], in_specs=...  5 us
    unnamed x6, local copies, waits for them, and re-layouts  1.6 us
  transfers between devices with their start and end apart: 13, of which 6 were waited for; matrix products, arithmetic and copies ran while one was open for 0% of the time, Pallas kernels for 22%

profile of v12, /device:TPU:0, one launch (start us, length us, event | category | flops | bytes accessed | tf_op | source)
XLA Modules:
  0.0 58.3 jit_solution(9495930193753068520)
XLA Ops:
  0.0 0.0 copy-start
  0.0 1.6 %copy-done = f32[4,128,8,128]{3,2,1,0:T(8,128)S(1)} copy-done((f32[4,128,8,128]{3,2,1,0:T(8,128)S(1)}, f32[4,128,8,128]{3,2,1,0:T(8,128)}, u32[]{:S(2)}) %copy-start) | copy-done | bytes 2097176
  1.6 0.0 copy-start.1
  1.6 0.1 corner_block.1
  1.7 3.0 %collective-permute-start.1 = (f32[128,128]{1,0:T(8,128)S(1)}, f32[128,128]{1,0:T(8,128)S(1)}, u32[]{:S(2)}, u32[]{:S(2)}) collective-permute-start(f32[128,128]{1,0:T(8,128)S(1)} %corner_block.1), channel_id=1, source_target_pairs={{0,8},{4,12},{8,0},{12,4},{16,24},{20,28},{24,16},{28,20},{1,9},{5... | collective-permute-start | bytes 196616 | tf_op jit(solution)/shard_map/ppermute | solution.py:288
  4.7 0.0 copy-done.1
  4.7 0.7 %panels.1 = (f32[4,128,128]{2,1,0:T(8,128)S(1)}, f32[8,64,128]{2,1,0:T(8,128)S(1)}, f32[8,64,128]{2,1,0:T(8,128)S(1)}) custom-call(f32[4,128,8,128]{3,2,1,0:T(8,128)S(1)} %copy-done.1), custom_call_target="tpu_custom_call" | custom-call | bytes 4194304 | tf_op jit(solution)/shard_map/panels/pallas_call | solution.py:142
  5.4 2.7 %collective-permute-start.3 = (f32[4,128,128]{2,1,0:T(8,128)S(1)}, f32[4,128,128]{2,1,0:T(8,128)S(1)}, u32[]{:S(2)}, u32[]{:S(2)}) collective-permute-start(f32[4,128,128]{2,1,0:T(8,128)S(1)} %get-tuple-element.58), channel_id=1, source_target_pairs={{0,2},{1,3},{2,0},{3,1},{4,6},{5,7},{6,4},{7,5},{8,10},{9,11},{10,... | collective-permute-start | bytes 786440 | tf_op jit(solution)/shard_map/ppermute | solution.py:288
  8.1 0.0 collective-permute-done.1
  8.1 1.5 %collective-permute-start.4 = (f32[8,64,128]{2,1,0:T(8,128)S(1)}, f32[8,64,128]{2,1,0:T(8,128)S(1)}, u32[]{:S(2)}, u32[]{:S(2)}) collective-permute-start(f32[8,64,128]{2,1,0:T(8,128)S(1)} %get-tuple-element.63), channel_id=1, source_target_pairs={{0,8},{4,12},{8,0},{12,4},{16,24},{20,28},{24,16},{28,20},{1,9},{5... | collective-permute-start | bytes 786440 | tf_op jit(solution)/shard_map/ppermute | solution.py:288
  9.6 1.5 %collective-permute-start.2 = (f32[128,128]{1,0:T(8,128)S(1)}, f32[128,128]{1,0:T(8,128)S(1)}, u32[]{:S(2)}, u32[]{:S(2)}) collective-permute-start(f32[128,128]{1,0:T(8,128)S(1)} %get-tuple-element.83), channel_id=1, source_target_pairs={{0,16},{4,20},{8,24},{12,28},{16,0},{20,4},{24,8},{28,12},{1,17},{... | collective-permute-start | bytes 196616 | tf_op jit(solution)/shard_map/ppermute | solution.py:288
  11.1 0.5 collective-permute-start.5
  11.6 2.9 %collective-permute-done.2 = f32[128,128]{1,0:T(8,128)S(1)} collective-permute-done((f32[128,128]{1,0:T(8,128)S(1)}, f32[128,128]{1,0:T(8,128)S(1)}, u32[]{:S(2)}, u32[]{:S(2)}) %collective-permute-start.2) | collective-permute-done | bytes 65568 | tf_op jit(solution)/shard_map/ppermute | solution.py:288
  14.5 5.5 %collective-permute-done.3 = f32[4,128,128]{2,1,0:T(8,128)S(1)} collective-permute-done((f32[4,128,128]{2,1,0:T(8,128)S(1)}, f32[4,128,128]{2,1,0:T(8,128)S(1)}, u32[]{:S(2)}, u32[]{:S(2)}) %collective-permute-start.3) | collective-permute-done | bytes 262176 | tf_op jit(solution)/shard_map/ppermute | solution.py:288
  19.9 0.0 copy-start.2
  19.9 7.4 %conditional.3 = (f32[128,128]{1,0:T(8,128)S(1)}) conditional(s32[]{:T(128)} %convert_element_type.4, () %tuple.22, (s32[]{:T(128)}, s32[]{:T(128)}, f32[128,128]{1,0:T(8,128)S(1)}, f32[128,128]{1,0:T(8,128)S(1)}) %tuple.27), branch_computations={%region_2.3_spmd, %region_3.4_spmd} | conditional | flops 32774 | bytes 917648 | solution.py:309
  19.9 0.0 copy-start.3
  20.0 0.6 %copy-done.3 = f32[128,128]{1,0:T(8,128)} copy-done((f32[128,128]{1,0:T(8,128)}, f32[128,128]{1,0:T(8,128)S(1)}, u32[]{:S(2)}) %copy-start.3) | copy-done | bytes 65560 | tf_op jit(solution)/shard_map/cond
  20.6 0.1 collective-permute-start
  20.7 6.6 %collective-permute-done = f32[128,128]{1,0:T(8,128)} collective-permute-done((f32[128,128]{1,0:T(8,128)S(1)}, f32[128,128]{1,0:T(8,128)}, u32[]{:S(2)}, u32[]{:S(2)}) %collective-permute-start) | collective-permute-done | bytes 65568 | tf_op jit(solution)/shard_map/cond/branch_1_fun/ppermute | solution.py:288
  27.3 0.0 copy-done.2
  27.3 0.0 collective-permute-done.4
  27.4 0.0 collective-permute-done.5
  27.4 0.1 collective-permute-start.6
  27.5 4.2 %collective-permute-done.6 = f32[128,128]{1,0:T(8,128)S(1)} collective-permute-done((f32[128,128]{1,0:T(8,128)S(1)}, f32[128,128]{1,0:T(8,128)S(1)}, u32[]{:S(2)}, u32[]{:S(2)}) %collective-permute-start.6) | collective-permute-done | bytes 65568 | tf_op jit(solution)/shard_map/ppermute | solution.py:288
  31.8 0.1 collective-permute-start.7
  31.9 3.4 %collective-permute-start.9 = (f32[8,64,128]{2,1,0:T(8,128)S(1)}, f32[8,64,128]{2,1,0:T(8,128)}, u32[]{:S(2)}, u32[]{:S(2)}) collective-permute-start(f32[8,64,128]{2,1,0:T(8,128)S(1)} %broadcast_select_fusion.7), channel_id=1, source_target_pairs={{0,16},{4,20},{8,24},{12,28},{16,0},{20,4},{24,8},{28,12},{1,17},{... | collective-permute-start | bytes 786440 | tf_op jit(solution)/shard_map/ppermute | solution.py:288
  35.3 1.5 %collective-permute-start.10 = (f32[8,64,128]{2,1,0:T(8,128)S(1)}, f32[8,64,128]{2,1,0:T(8,128)}, u32[]{:S(2)}, u32[]{:S(2)}) collective-permute-start(f32[8,64,128]{2,1,0:T(8,128)S(1)} %broadcast_select_fusion.6), channel_id=1, source_target_pairs={{0,8},{4,12},{8,0},{12,4},{16,24},{20,28},{24,16},{28,20},{1,9},{5... | collective-permute-start | bytes 786440 | tf_op jit(solution)/shard_map/ppermute | solution.py:288
  36.7 0.0 collective-permute-done.7
  36.8 5.0 %first_factor.1 = (f32[128,128]{1,0:T(8,128)S(1)}, f32[128,128]{1,0:T(8,128)S(1)}) custom-call(f32[128,128]{1,0:T(8,128)S(1)} %get-tuple-element.79.a_ref), custom_call_target="tpu_custom_call" | custom-call | flops 8000000000 | bytes 2097152 | tf_op jit(solution)/shard_map/first_factor/pallas_call | solution.py:161
  41.8 0.1 collective-permute-start.8
  41.9 0.3 collective-permute-done.9
  42.3 0.1 collective-permute-start.11
  42.4 1.4 %collective-permute-done.10 = f32[8,64,128]{2,1,0:T(8,128)} collective-permute-done((f32[8,64,128]{2,1,0:T(8,128)S(1)}, f32[8,64,128]{2,1,0:T(8,128)}, u32[]{:S(2)}, u32[]{:S(2)}) %collective-permute-start.10) | collective-permute-done | bytes 262176 | tf_op jit(solution)/shard_map/ppermute | solution.py:288
  43.8 0.1 collective-permute-start.12
  43.8 7.3 %second_factor.1 = (f32[128,128]{1,0:T(8,128)S(1)}, f32[256,256]{1,0:T(8,128)S(1)}, f32[256,256]{1,0:T(8,128)S(1)}, f32[8,4,128,128]{3,2,1,0:T(8,128)S(1)}) custom-call(f32[128,128]{1,0:T(8,128)S(1)} %get-tuple-element.78.low_ref, f32[128,128]{1,0:T(8,128)S(1)} %get-tuple-element.80.a_ref, f32[128,128]{1,0:T(8,128)S(1)} %get-tuple-element.68.w0_ref, ...), custom_call_target="tpu_custom_call" | custom-call | flops 8000000000 | bytes 4194304 | tf_op jit(solution)/shard_map/second_factor/pallas_call | solution.py:204
  51.2 0.0 collective-permute-done.8.rows_other_ref
  51.2 0.0 collective-permute-done.11.oa_ref
  51.2 0.0 collective-permute-done.12.ob_ref
  51.2 6.9 %settle.1 = f32[4,128,8,128]{3,2,1,0:T(8,128)} custom-call(f32[128,128]{1,0:T(8,128)S(1)} %get-tuple-element.66.f0_ref, f32[128,128]{1,0:T(8,128)S(1)} %get-tuple-element.69.f1_ref, f32[256,256]{1,0:T(8,128)S(1)} %get-tuple-element.70.w_ref, f32[256,256]{1,0:T(8,128)S(1)} %get-tuple-element.71.mixed_ref, f32[4,128,128]{2,1,0:T(8,128)S(1)} %broadcast_select_fusion.5.rows_ref, ...), custom_call_target="tpu_custom_call" | custom-call | flops 4000000000 | bytes 6291456 | tf_op jit(solution)/shard_map/settle/pallas_call | solution.py:275
  (12 shorter events, 0.3 us)
Async XLA Ops:
  0.0 1.6 %copy-start = (f32[4,128,8,128]{3,2,1,0:T(8,128)S(1)}, f32[4,128,8,128]{3,2,1,0:T(8,128)}, u32[]{:S(2)}) copy-start(f32[4,128,8,128]{3,2,1,0:T(8,128)} %matrix_ref.5) | copy-start | bytes 6291460
  1.6 3.1 %copy-start.1 = (f32[4,128,8,128]{3,2,1,0:T(8,128)S(1)}, f32[4,128,8,128]{3,2,1,0:T(8,128)}, u32[]{:S(2)}) copy-start(f32[4,128,8,128]{3,2,1,0:T(8,128)} %matrix_ref.5) | copy-start | bytes 6291460
  1.7 6.4 %collective-permute-start.1 = (f32[128,128]{1,0:T(8,128)S(1)}, f32[128,128]{1,0:T(8,128)S(1)}, u32[]{:S(2)}, u32[]{:S(2)}) collective-permute-start(f32[128,128]{1,0:T(8,128)S(1)} %corner_block.1), channel_id=1, source_target_pairs={{0,8},{4,12},{8,0},{12,4},{16,24},{20,28},{24,16},{28,20},{1,9},{5... | collective-permute-start | bytes 196616 | tf_op jit(solution)/shard_map/ppermute | solution.py:288
  5.4 14.5 %collective-permute-start.3 = (f32[4,128,128]{2,1,0:T(8,128)S(1)}, f32[4,128,128]{2,1,0:T(8,128)S(1)}, u32[]{:S(2)}, u32[]{:S(2)}) collective-permute-start(f32[4,128,128]{2,1,0:T(8,128)S(1)} %get-tuple-element.58), channel_id=1, source_target_pairs={{0,2},{1,3},{2,0},{3,1},{4,6},{5,7},{6,4},{7,5},{8,10},{9,11},{10,... | collective-permute-start | bytes 786440 | tf_op jit(solution)/shard_map/ppermute | solution.py:288
  8.1 19.3 %collective-permute-start.4 = (f32[8,64,128]{2,1,0:T(8,128)S(1)}, f32[8,64,128]{2,1,0:T(8,128)S(1)}, u32[]{:S(2)}, u32[]{:S(2)}) collective-permute-start(f32[8,64,128]{2,1,0:T(8,128)S(1)} %get-tuple-element.63), channel_id=1, source_target_pairs={{0,8},{4,12},{8,0},{12,4},{16,24},{20,28},{24,16},{28,20},{1,9},{5... | collective-permute-start | bytes 786440 | tf_op jit(solution)/shard_map/ppermute | solution.py:288
  9.6 4.9 %collective-permute-start.2 = (f32[128,128]{1,0:T(8,128)S(1)}, f32[128,128]{1,0:T(8,128)S(1)}, u32[]{:S(2)}, u32[]{:S(2)}) collective-permute-start(f32[128,128]{1,0:T(8,128)S(1)} %get-tuple-element.83), channel_id=1, source_target_pairs={{0,16},{4,20},{8,24},{12,28},{16,0},{20,4},{24,8},{28,12},{1,17},{... | collective-permute-start | bytes 196616 | tf_op jit(solution)/shard_map/ppermute | solution.py:288
  11.1 16.3 %collective-permute-start.5 = (f32[8,64,128]{2,1,0:T(8,128)S(1)}, f32[8,64,128]{2,1,0:T(8,128)}, u32[]{:S(2)}, u32[]{:S(2)}) collective-permute-start(f32[8,64,128]{2,1,0:T(8,128)S(1)} %get-tuple-element.64), channel_id=1, source_target_pairs={{0,16},{4,20},{8,24},{12,28},{16,0},{20,4},{24,8},{28,12},{1,17},{... | collective-permute-start | bytes 786440 | tf_op jit(solution)/shard_map/ppermute | solution.py:288
  19.9 7.4 %copy-start.2 = (f32[4,128,128]{2,1,0:T(8,128)}, f32[4,128,128]{2,1,0:T(8,128)S(1)}, u32[]{:S(2)}) copy-start(f32[4,128,128]{2,1,0:T(8,128)S(1)} %collective-permute-done.3) | copy-start | bytes 786436
  19.9 0.6 %copy-start.3 = (f32[128,128]{1,0:T(8,128)}, f32[128,128]{1,0:T(8,128)S(1)}, u32[]{:S(2)}) copy-start(f32[128,128]{1,0:T(8,128)S(1)} %get-tuple-element.30) | copy-start | bytes 196612 | tf_op jit(solution)/shard_map/cond
  20.6 6.7 %collective-permute-start = (f32[128,128]{1,0:T(8,128)S(1)}, f32[128,128]{1,0:T(8,128)}, u32[]{:S(2)}, u32[]{:S(2)}) collective-permute-start(f32[128,128]{1,0:T(8,128)S(1)} %broadcast_select_fusion.1), channel_id=1, source_target_pairs={{0,2},{1,3},{2,0},{3,1},{4,6},{5,7},{6,4},{7,5},{8,10},{9,11},{10,... | collective-permute-start | bytes 196616 | tf_op jit(solution)/shard_map/cond/branch_1_fun/ppermute | solution.py:288
  27.4 4.3 %collective-permute-start.6 = (f32[128,128]{1,0:T(8,128)S(1)}, f32[128,128]{1,0:T(8,128)S(1)}, u32[]{:S(2)}, u32[]{:S(2)}) collective-permute-start(f32[128,128]{1,0:T(8,128)S(1)} %get-tuple-element.84), channel_id=1, source_target_pairs={{0,1},{1,0},{2,3},{3,2},{4,5},{5,4},{6,7},{7,6},{8,9},{9,8},{10,11... | collective-permute-start | bytes 196616 | tf_op jit(solution)/shard_map/ppermute | solution.py:288
  31.8 4.9 %collective-permute-start.7 = (f32[2,128,128]{2,1,0:T(8,128)S(1)}, f32[2,128,128]{2,1,0:T(8,128)S(1)}, u32[]{:S(2)}, u32[]{:S(2)}) collective-permute-start(f32[2,128,128]{2,1,0:T(8,128)S(1)} %pad_maximum_fusion), channel_id=1, source_target_pairs={{0,4},{4,0},{8,12},{12,8},{16,20},{20,16},{24,28},{28,24},{1,5},{5... | collective-permute-start | bytes 393224 | tf_op jit(solution)/shard_map/ppermute | solution.py:288
  31.9 10.3 %collective-permute-start.9 = (f32[8,64,128]{2,1,0:T(8,128)S(1)}, f32[8,64,128]{2,1,0:T(8,128)}, u32[]{:S(2)}, u32[]{:S(2)}) collective-permute-start(f32[8,64,128]{2,1,0:T(8,128)S(1)} %broadcast_select_fusion.7), channel_id=1, source_target_pairs={{0,16},{4,20},{8,24},{12,28},{16,0},{20,4},{24,8},{28,12},{1,17},{... | collective-permute-start | bytes 786440 | tf_op jit(solution)/shard_map/ppermute | solution.py:288
  35.3 8.5 %collective-permute-start.10 = (f32[8,64,128]{2,1,0:T(8,128)S(1)}, f32[8,64,128]{2,1,0:T(8,128)}, u32[]{:S(2)}, u32[]{:S(2)}) collective-permute-start(f32[8,64,128]{2,1,0:T(8,128)S(1)} %broadcast_select_fusion.6), channel_id=1, source_target_pairs={{0,8},{4,12},{8,0},{12,4},{16,24},{20,28},{24,16},{28,20},{1,9},{5... | collective-permute-start | bytes 786440 | tf_op jit(solution)/shard_map/ppermute | solution.py:288
  41.8 9.4 %collective-permute-start.8 = (f32[4,128,128]{2,1,0:T(8,128)S(1)}, f32[4,128,128]{2,1,0:T(8,128)S(1)}, u32[]{:S(2)}, u32[]{:S(2)}) collective-permute-start(f32[4,128,128]{2,1,0:T(8,128)S(1)} %broadcast_select_fusion.5.rows_ref), channel_id=1, source_target_pairs={{0,1},{1,0},{2,3},{3,2},{4,5},{5,4},{6,7},{7,6},{8,9},{9,8},{10,11... | collective-permute-start | bytes 786440 | tf_op jit(solution)/shard_map/ppermute | solution.py:288
  42.3 8.9 %collective-permute-start.11 = (f32[8,64,128]{2,1,0:T(8,128)S(1)}, f32[8,64,128]{2,1,0:T(8,128)S(1)}, u32[]{:S(2)}, u32[]{:S(2)}) collective-permute-start(f32[8,64,128]{2,1,0:T(8,128)S(1)} %broadcast_select_fusion.4.ha_ref), channel_id=1, source_target_pairs={{0,4},{4,0},{8,12},{12,8},{16,20},{20,16},{24,28},{28,24},{1,5},{5... | collective-permute-start | bytes 786440 | tf_op jit(solution)/shard_map/ppermute | solution.py:288
  43.8 7.5 %collective-permute-start.12 = (f32[8,64,128]{2,1,0:T(8,128)S(1)}, f32[8,64,128]{2,1,0:T(8,128)S(1)}, u32[]{:S(2)}, u32[]{:S(2)}) collective-permute-start(f32[8,64,128]{2,1,0:T(8,128)S(1)} %broadcast_select_fusion.3.hb_ref), channel_id=1, source_target_pairs={{0,4},{4,0},{8,12},{12,8},{16,20},{20,16},{24,28},{28,24},{1,5},{5... | collective-permute-start | bytes 786440 | tf_op jit(solution)/shard_map/ppermute | solution.py:288

commit v13 on v12

--- a/solution.py
+++ b/solution.py
@@ -326,44 +326,46 @@
     block = corner_block(kernel)
     column, upper, lower = panels(kernel)
     first_bit, last_bit = row_bits[0], row_bits[-1]
-    column_moved = exchange(column, "col", 1 << col_bits[0], n_col)
-    moved = exchange(block, "row", 1 << first_bit, n_row)
-    block = region(lambda new, old: jnp.where(bit_set(grid_row, first_bit), new, old), moved, block)
-
-    block, upper, lower = after(block, upper, lower)
-    moved = exchange(block, "row", 1 << row_bits[1], n_row)
+
+    moved = exchange(block, "col", 1 << col_bits[0], n_col)
     upper_moved = exchange(upper, "row", 1 << first_bit, n_row)
     lower_moved = exchange(lower, "row", 1 << last_bit, n_row)
-    moved, block, column_moved = after(moved, block, column_moved)
 
     def along_col(new, old):
-        block = jnp.where(bit_set(grid_row, row_bits[1]), new, old)
-        block = spread(block, "row", grid_row, n_row, row_bits[2:])
-        return spread(block, "col", grid_col, n_col, col_bits)
+        block = jnp.where(bit_set(grid_col, col_bits[0]), new, old)
+        return spread(block, "col", grid_col, n_col, col_bits[1:])
 
     block = region(along_col, moved, block)
-
-    block, row_then = after(block, grid_row)
-    ha = jnp.where(bit_set(row_then, first_bit), upper_moved, upper)
-    hb = jnp.where(bit_set(row_then, last_bit), lower_moved, lower)
-    block, ha, hb = after(block, ha, hb)
     across = exchange(block, "col", 1, n_col)
-    mine = jnp.stack([jnp.where(right, across, block), jnp.where(right, block, across)])
-    other = exchange(mine, "row", 1, n_row)
+    ha = jnp.where(bit_set(grid_row, first_bit), upper_moved, upper)
+    hb = jnp.where(bit_set(grid_row, last_bit), lower_moved, lower)
+    across, block, ha, hb, column = after(across, block, ha, hb, column)
+
+    pair = jnp.stack([jnp.where(right, across, block), jnp.where(right, block, across)])
+    moved = exchange(pair, "row", 1 << first_bit, n_row)
+    column_moved = exchange(column, "col", 1 << col_bits[0], n_col)
+
+    def over_row(new, old):
+        pair = jnp.where(bit_set(grid_row, first_bit), new, old)
+        pair = spread(pair, "row", grid_row, n_row, row_bits[1:])
+        return pair, exchange(pair, "row", 1, n_row)
+
+    pair, other = region(over_row, moved, pair)
+    pair, ha, hb = after(pair, ha, hb)
     ha_moved = exchange(ha, "row", 1 << row_bits[1], n_row)
     hb_moved = exchange(hb, "row", 1 << row_bits[-2], n_row)
-
-    a00 = jnp.where(odd, other[0], mine[0])
-    a10 = jnp.where(odd, mine[0], other[0])
-    a11 = jnp.where(odd, mine[1], other[1])
+    rows = jnp.where(bit_set(grid_col, col_bits[0]), column_moved, column)
+    pair, other, rows = after(pair, other, rows)
+    a00 = jnp.where(odd, other[0], pair[0])
+    a10 = jnp.where(odd, pair[0], other[0])
+    a11 = jnp.where(odd, pair[1], other[1])
     f0, w0 = first_factor(a00)
 
-    w0, row_then, col_then = after(w0, grid_row, grid_col)
+    w0, rows, row_then, col_then = after(w0, rows, grid_row, grid_col)
     ha = jnp.where(bit_set(row_then, row_bits[1]), ha_moved, ha)
     ha = spread(ha, "row", row_then, n_row, row_bits[2:])
     hb = jnp.where(bit_set(row_then, row_bits[-2]), hb_moved, hb)
     hb = spread(hb, "row", row_then, n_row, row_bits[:-2][::-1])
-    rows = jnp.where(bit_set(col_then, col_bits[0]), column_moved, column)
     rows = spread(rows, "col", col_then, n_col, col_bits[1:])
     rows_other = exchange(rows, "col", 1, n_col)
     oa = exchange(ha, "row", 1, n_row)

time: 58.8 us -> 55.7 us (0.947)
  waiting for transfers between devices: 20.9 us -> 14.2 us
  starting transfers between devices: 14.5 us -> 17.6 us
  other arithmetic: 0.26 us -> 1.82 us
  local copies, waits for them, and re-layouts: 2.25 us -> 1.6 us
    ppermute x13, waiting for transfers between devices: 20.9 us -> 14.2 us  [exchange(): return lax.ppermute(value, axis, [(i, i ^ mask) for i in range(size)])]
    ppermute x13, starting transfers between devices: 14.5 us -> 17.6 us  [exchange(): return lax.ppermute(value, axis, [(i, i ^ mask) for i in range(size)])]
    select_n x6, other arithmetic: 0.15 us -> 1.07 us  [the longest x1 0.96 us: shards(): a11 = jnp.where(odd, pair[1], other[1])]
    select_n x1, other arithmetic: 0.01 us -> 0.67 us  [spread(): jnp.where(bit_set(index, bit), exchange(held, axis, 1 << bit, size), held)]
    cond x2 -> x0, local copies, waits for them, and re-layouts: 0.65 us -> none
    unnamed x6 -> x4, local copies, waits for them, and re-layouts: 1.6 us -> 1.6 us
  transfers between devices with their start and end apart: 13 -> 13, of which waited for: 6 -> 5; matrix products, arithmetic and copies ran while one was open for 0% -> 3% of each run, Pallas kernels for 22% -> 22%
where the time goes in v13:
time: 55.7 us; the launch traced here: 55.5 us
  Pallas kernels  20 us (36%)
  starting transfers between devices  17.6 us (32%)
  waiting for transfers between devices  14.2 us (25%)
  other arithmetic  1.82 us (3%)
  local copies, waits for them, and re-layouts  1.6 us (3%)
    ppermute x13, starting transfers between devices, exchange(): return lax.ppermute(value, axis, [(i, i ^ mask) for i in range(size)])  17.6 us
    ppermute x13, waiting for transfers between devices, exchange(): return lax.ppermute(value, axis, [(i, i ^ mask) for i in range(size)])  14.2 us
    pallas_call x1, Pallas kernels, second_factor(): pl.pallas_call(second_factor_kernel, out_shape=[square, double, double, b...  7.34 us
    pallas_call x1, Pallas kernels, settle(): pl.pallas_call(settle_kernel, out_shape=jax.ShapeDtypeStruct((local_rows,...  6.9 us
    pallas_call x1, Pallas kernels, first_factor(): pl.pallas_call(first_factor_kernel, out_shape=[square, square], in_specs=...  5 us
    unnamed x4, local copies, waits for them, and re-layouts  1.6 us
  transfers between devices with their start and end apart: 13, of which 5 were waited for; matrix products, arithmetic and copies ran while one was open for 3% of the time, Pallas kernels for 22%

profile of v13, /device:TPU:0, one launch (start us, length us, event | category | flops | bytes accessed | tf_op | source)
XLA Modules:
  0.0 55.5 jit_solution(7122095802315239493)
XLA Ops:
  0.0 0.0 copy-start
  0.0 1.6 %copy-done = f32[4,128,8,128]{3,2,1,0:T(8,128)S(1)} copy-done((f32[4,128,8,128]{3,2,1,0:T(8,128)S(1)}, f32[4,128,8,128]{3,2,1,0:T(8,128)}, u32[]{:S(2)}) %copy-start) | copy-done | bytes 2097176
  1.6 0.7 %panels.1 = (f32[4,128,128]{2,1,0:T(8,128)S(1)}, f32[8,64,128]{2,1,0:T(8,128)S(1)}, f32[8,64,128]{2,1,0:T(8,128)S(1)}) custom-call(f32[4,128,8,128]{3,2,1,0:T(8,128)S(1)} %copy-done), custom_call_target="tpu_custom_call" | custom-call | bytes 4194304 | tf_op jit(solution)/shard_map/panels/pallas_call | solution.py:142
  2.3 3.0 %collective-permute-start.4 = (f32[8,64,128]{2,1,0:T(8,128)S(1)}, f32[8,64,128]{2,1,0:T(8,128)S(1)}, u32[]{:S(2)}, u32[]{:S(2)}) collective-permute-start(f32[8,64,128]{2,1,0:T(8,128)S(1)} %get-tuple-element.51), channel_id=1, source_target_pairs={{0,8},{4,12},{8,0},{12,4},{16,24},{20,28},{24,16},{28,20},{1,9},{5... | collective-permute-start | bytes 786440 | tf_op jit(solution)/shard_map/ppermute | solution.py:288
  5.3 0.1 corner_block.1
  5.4 2.7 %collective-permute-start.2 = (f32[128,128]{1,0:T(8,128)S(1)}, f32[128,128]{1,0:T(8,128)S(1)}, u32[]{:S(2)}, u32[]{:S(2)}) collective-permute-start(f32[128,128]{1,0:T(8,128)S(1)} %corner_block.1), channel_id=1, source_target_pairs={{0,2},{1,3},{2,0},{3,1},{4,6},{5,7},{6,4},{7,5},{8,10},{9,11},{10,... | collective-permute-start | bytes 196616 | tf_op jit(solution)/shard_map/ppermute | solution.py:288
  8.1 1.5 %collective-permute-start.5 = (f32[8,64,128]{2,1,0:T(8,128)S(1)}, f32[8,64,128]{2,1,0:T(8,128)S(1)}, u32[]{:S(2)}, u32[]{:S(2)}) collective-permute-start(f32[8,64,128]{2,1,0:T(8,128)S(1)} %get-tuple-element.52), channel_id=1, source_target_pairs={{0,16},{4,20},{8,24},{12,28},{16,0},{20,4},{24,8},{28,12},{1,17},{... | collective-permute-start | bytes 786440 | tf_op jit(solution)/shard_map/ppermute | solution.py:288
  9.6 1.4 %collective-permute-done.2 = f32[128,128]{1,0:T(8,128)S(1)} collective-permute-done((f32[128,128]{1,0:T(8,128)S(1)}, f32[128,128]{1,0:T(8,128)S(1)}, u32[]{:S(2)}, u32[]{:S(2)}) %collective-permute-start.2) | collective-permute-done | bytes 65568 | tf_op jit(solution)/shard_map/ppermute | solution.py:288
  10.9 1.3 %collective-permute-start.3 = (f32[128,128]{1,0:T(8,128)S(1)}, f32[128,128]{1,0:T(8,128)S(1)}, u32[]{:S(2)}, u32[]{:S(2)}) collective-permute-start(f32[128,128]{1,0:T(8,128)S(1)} %get-tuple-element.85), channel_id=1, source_target_pairs={{0,1},{1,0},{2,3},{3,2},{4,5},{5,4},{6,7},{7,6},{8,9},{9,8},{10,11... | collective-permute-start | bytes 196616 | tf_op jit(solution)/shard_map/ppermute | solution.py:288
  12.3 0.0 collective-permute-done.4
  12.3 3.2 %collective-permute-done.5 = f32[8,64,128]{2,1,0:T(8,128)S(1)} collective-permute-done((f32[8,64,128]{2,1,0:T(8,128)S(1)}, f32[8,64,128]{2,1,0:T(8,128)S(1)}, u32[]{:S(2)}, u32[]{:S(2)}) %collective-permute-start.5) | collective-permute-done | bytes 262176 | tf_op jit(solution)/shard_map/ppermute | solution.py:288
  15.6 0.0 collective-permute-done.3
  15.6 2.1 %collective-permute-start.7 = (f32[4,128,128]{2,1,0:T(8,128)S(1)}, f32[4,128,128]{2,1,0:T(8,128)S(1)}, u32[]{:S(2)}, u32[]{:S(2)}) collective-permute-start(f32[4,128,128]{2,1,0:T(8,128)S(1)} %get-tuple-element.61), channel_id=1, source_target_pairs={{0,2},{1,3},{2,0},{3,1},{4,6},{5,7},{6,4},{7,5},{8,10},{9,11},{10,... | collective-permute-start | bytes 786440 | tf_op jit(solution)/shard_map/ppermute | solution.py:288
  17.7 0.6 %collective-permute-start.6 = (f32[2,128,128]{2,1,0:T(8,128)S(1)}, f32[2,128,128]{2,1,0:T(8,128)S(1)}, u32[]{:S(2)}, u32[]{:S(2)}) collective-permute-start(f32[2,128,128]{2,1,0:T(8,128)S(1)} %pad_maximum_fusion), channel_id=1, source_target_pairs={{0,8},{4,12},{8,0},{12,4},{16,24},{20,28},{24,16},{28,20},{1,9},{5... | collective-permute-start | bytes 393224 | tf_op jit(solution)/shard_map/ppermute | solution.py:288
  18.3 4.4 %collective-permute-done.6 = f32[2,128,128]{2,1,0:T(8,128)S(1)} collective-permute-done((f32[2,128,128]{2,1,0:T(8,128)S(1)}, f32[2,128,128]{2,1,0:T(8,128)S(1)}, u32[]{:S(2)}, u32[]{:S(2)}) %collective-permute-start.6) | collective-permute-done | bytes 131104 | tf_op jit(solution)/shard_map/ppermute | solution.py:288
  22.8 7.4 %conditional.3 = (f32[2,128,128]{2,1,0:T(8,128)}, f32[2,128,128]{2,1,0:T(8,128)}) conditional(s32[]{:T(128)} %convert_element_type.4, () %tuple.23, (s32[]{:T(128)}, f32[2,128,128]{2,1,0:T(8,128)S(1)}, f32[2,128,128]{2,1,0:T(8,128)S(1)}) %tuple.27), branch_computations={%region_2.3_spmd, %region_3.4_spmd} | conditional | flops 65542 | bytes 1835172 | solution.py:309
  22.8 1.6 %collective-permute-start = (f32[2,128,128]{2,1,0:T(8,128)S(1)}, f32[2,128,128]{2,1,0:T(8,128)S(1)}, u32[]{:S(2)}, u32[]{:S(2)}) collective-permute-start(f32[2,128,128]{2,1,0:T(8,128)S(1)} %broadcast_select_fusion.1), channel_id=1, source_target_pairs={{0,16},{4,20},{8,24},{12,28},{16,0},{20,4},{24,8},{28,12},{1,17},{... | collective-permute-start | bytes 393224 | tf_op jit(solution)/shard_map/cond/branch_1_fun/ppermute | solution.py:288
  24.4 3.4 %collective-permute-done = f32[2,128,128]{2,1,0:T(8,128)S(1)} collective-permute-done((f32[2,128,128]{2,1,0:T(8,128)S(1)}, f32[2,128,128]{2,1,0:T(8,128)S(1)}, u32[]{:S(2)}, u32[]{:S(2)}) %collective-permute-start) | collective-permute-done | bytes 131104 | tf_op jit(solution)/shard_map/cond/branch_1_fun/ppermute | solution.py:288
  27.8 0.7 %broadcast_select_fusion.2 = f32[2,128,128]{2,1,0:T(8,128)} fusion(f32[2,128,128]{2,1,0:T(8,128)S(1)} %collective-permute-done, f32[2,128,128]{2,1,0:T(8,128)S(1)} %broadcast_select_fusion.1, pred[]{:T(512)S(6)} %eq.24), kind=kLoop, calls=%fused_computation.2 | loop fusion | flops 32768 | bytes 393217 | tf_op jit(solution)/shard_map/cond/branch_1_fun/jit(_where)/select_n | solution.py:298
  28.5 0.0 collective-permute-start.1
  28.5 1.7 %collective-permute-done.1 = f32[2,128,128]{2,1,0:T(8,128)} collective-permute-done((f32[2,128,128]{2,1,0:T(8,128)}, f32[2,128,128]{2,1,0:T(8,128)}, u32[]{:S(2)}, u32[]{:S(2)}) %collective-permute-start.1) | collective-permute-done | bytes 131104 | tf_op jit(solution)/shard_map/cond/branch_1_fun/ppermute | solution.py:288
  30.2 1.5 %collective-permute-start.9 = (f32[8,64,128]{2,1,0:T(8,128)S(1)}, f32[8,64,128]{2,1,0:T(8,128)S(1)}, u32[]{:S(2)}, u32[]{:S(2)}) collective-permute-start(f32[8,64,128]{2,1,0:T(8,128)S(1)} %broadcast_select_fusion.7), channel_id=1, source_target_pairs={{0,16},{4,20},{8,24},{12,28},{16,0},{20,4},{24,8},{28,12},{1,17},{... | collective-permute-start | bytes 786440 | tf_op jit(solution)/shard_map/ppermute | solution.py:288
  31.7 0.5 collective-permute-start.10
  32.2 0.0 collective-permute-done.7
  32.3 1.0 %select_bitcast_fusion = (f32[128,128]{1,0:T(8,128)S(1)}, f32[128,128]{1,0:T(8,128)S(1)}, f32[128,128]{1,0:T(8,128)S(1)}) fusion(f32[2,128,128]{2,1,0:T(8,128)} %get-tuple-element.62, f32[2,128,128]{2,1,0:T(8,128)} %get-tuple-element.63, pred[]{:T(512)S(6)} %eq.33), kind=kLoop, calls=%fused_computation.9 | loop fusion | flops 49152 | bytes 458753 | tf_op jit(solution)/shard_map/jit(_where)/select_n | solution.py:361
  33.2 0.0 copy-start.1
  33.3 5.0 %first_factor.1 = (f32[128,128]{1,0:T(8,128)S(1)}, f32[128,128]{1,0:T(8,128)S(1)}) custom-call(f32[128,128]{1,0:T(8,128)S(1)} %get-tuple-element.78.a_ref), custom_call_target="tpu_custom_call" | custom-call | flops 8000000000 | bytes 2097152 | tf_op jit(solution)/shard_map/first_factor/pallas_call | solution.py:161
  38.3 2.1 %collective-permute-start.8 = (f32[4,128,128]{2,1,0:T(8,128)S(1)}, f32[4,128,128]{2,1,0:T(8,128)S(1)}, u32[]{:S(2)}, u32[]{:S(2)}) collective-permute-start(f32[4,128,128]{2,1,0:T(8,128)S(1)} %broadcast_select_fusion.5.rows_ref), channel_id=1, source_target_pairs={{0,1},{1,0},{2,3},{3,2},{4,5},{5,4},{6,7},{7,6},{8,9},{9,8},{10,11... | collective-permute-start | bytes 786440 | tf_op jit(solution)/shard_map/ppermute | solution.py:288
  40.3 0.0 collective-permute-done.10
  40.4 0.1 collective-permute-start.12
  40.5 0.0 collective-permute-done.9
  40.5 0.5 collective-permute-start.11
  41.1 0.0 copy-done.1
  41.1 7.3 %second_factor.1 = (f32[128,128]{1,0:T(8,128)S(1)}, f32[256,256]{1,0:T(8,128)S(1)}, f32[256,256]{1,0:T(8,128)S(1)}, f32[8,4,128,128]{3,2,1,0:T(8,128)S(1)}) custom-call(f32[128,128]{1,0:T(8,128)S(1)} %get-tuple-element.77.low_ref, f32[128,128]{1,0:T(8,128)S(1)} %get-tuple-element.76.a_ref, f32[128,128]{1,0:T(8,128)S(1)} %get-tuple-element.67.w0_ref, ...), custom_call_target="tpu_custom_call" | custom-call | flops 8000000000 | bytes 4194304 | tf_op jit(solution)/shard_map/second_factor/pallas_call | solution.py:204
  48.4 0.0 collective-permute-done.8.rows_other_ref
  48.4 0.0 collective-permute-done.12.ob_ref
  48.4 0.0 collective-permute-done.11.oa_ref
  48.5 6.9 %settle.1 = f32[4,128,8,128]{3,2,1,0:T(8,128)} custom-call(f32[128,128]{1,0:T(8,128)S(1)} %get-tuple-element.64.f0_ref, f32[128,128]{1,0:T(8,128)S(1)} %get-tuple-element.68.f1_ref, f32[256,256]{1,0:T(8,128)S(1)} %get-tuple-element.69.w_ref, f32[256,256]{1,0:T(8,128)S(1)} %get-tuple-element.70.mixed_ref, f32[4,128,128]{2,1,0:T(8,128)S(1)} %broadcast_select_fusion.5.rows_ref, ...), custom_call_target="tpu_custom_call" | custom-call | flops 4000000000 | bytes 6291456 | tf_op jit(solution)/shard_map/settle/pallas_call | solution.py:275
  (10 shorter events, 0.2 us)
Async XLA Ops:
  0.0 1.6 %copy-start = (f32[4,128,8,128]{3,2,1,0:T(8,128)S(1)}, f32[4,128,8,128]{3,2,1,0:T(8,128)}, u32[]{:S(2)}) copy-start(f32[4,128,8,128]{3,2,1,0:T(8,128)} %matrix_ref.5) | copy-start | bytes 6291460
  2.3 10.0 %collective-permute-start.4 = (f32[8,64,128]{2,1,0:T(8,128)S(1)}, f32[8,64,128]{2,1,0:T(8,128)S(1)}, u32[]{:S(2)}, u32[]{:S(2)}) collective-permute-start(f32[8,64,128]{2,1,0:T(8,128)S(1)} %get-tuple-element.51), channel_id=1, source_target_pairs={{0,8},{4,12},{8,0},{12,4},{16,24},{20,28},{24,16},{28,20},{1,9},{5... | collective-permute-start | bytes 786440 | tf_op jit(solution)/shard_map/ppermute | solution.py:288
  5.4 5.5 %collective-permute-start.2 = (f32[128,128]{1,0:T(8,128)S(1)}, f32[128,128]{1,0:T(8,128)S(1)}, u32[]{:S(2)}, u32[]{:S(2)}) collective-permute-start(f32[128,128]{1,0:T(8,128)S(1)} %corner_block.1), channel_id=1, source_target_pairs={{0,2},{1,3},{2,0},{3,1},{4,6},{5,7},{6,4},{7,5},{8,10},{9,11},{10,... | collective-permute-start | bytes 196616 | tf_op jit(solution)/shard_map/ppermute | solution.py:288
  8.1 7.5 %collective-permute-start.5 = (f32[8,64,128]{2,1,0:T(8,128)S(1)}, f32[8,64,128]{2,1,0:T(8,128)S(1)}, u32[]{:S(2)}, u32[]{:S(2)}) collective-permute-start(f32[8,64,128]{2,1,0:T(8,128)S(1)} %get-tuple-element.52), channel_id=1, source_target_pairs={{0,16},{4,20},{8,24},{12,28},{16,0},{20,4},{24,8},{28,12},{1,17},{... | collective-permute-start | bytes 786440 | tf_op jit(solution)/shard_map/ppermute | solution.py:288
  10.9 4.6 %collective-permute-start.3 = (f32[128,128]{1,0:T(8,128)S(1)}, f32[128,128]{1,0:T(8,128)S(1)}, u32[]{:S(2)}, u32[]{:S(2)}) collective-permute-start(f32[128,128]{1,0:T(8,128)S(1)} %get-tuple-element.85), channel_id=1, source_target_pairs={{0,1},{1,0},{2,3},{3,2},{4,5},{5,4},{6,7},{7,6},{8,9},{9,8},{10,11... | collective-permute-start | bytes 196616 | tf_op jit(solution)/shard_map/ppermute | solution.py:288
  15.6 16.7 %collective-permute-start.7 = (f32[4,128,128]{2,1,0:T(8,128)S(1)}, f32[4,128,128]{2,1,0:T(8,128)S(1)}, u32[]{:S(2)}, u32[]{:S(2)}) collective-permute-start(f32[4,128,128]{2,1,0:T(8,128)S(1)} %get-tuple-element.61), channel_id=1, source_target_pairs={{0,2},{1,3},{2,0},{3,1},{4,6},{5,7},{6,4},{7,5},{8,10},{9,11},{10,... | collective-permute-start | bytes 786440 | tf_op jit(solution)/shard_map/ppermute | solution.py:288
  17.7 5.0 %collective-permute-start.6 = (f32[2,128,128]{2,1,0:T(8,128)S(1)}, f32[2,128,128]{2,1,0:T(8,128)S(1)}, u32[]{:S(2)}, u32[]{:S(2)}) collective-permute-start(f32[2,128,128]{2,1,0:T(8,128)S(1)} %pad_maximum_fusion), channel_id=1, source_target_pairs={{0,8},{4,12},{8,0},{12,4},{16,24},{20,28},{24,16},{28,20},{1,9},{5... | collective-permute-start | bytes 393224 | tf_op jit(solution)/shard_map/ppermute | solution.py:288
  22.8 5.0 %collective-permute-start = (f32[2,128,128]{2,1,0:T(8,128)S(1)}, f32[2,128,128]{2,1,0:T(8,128)S(1)}, u32[]{:S(2)}, u32[]{:S(2)}) collective-permute-start(f32[2,128,128]{2,1,0:T(8,128)S(1)} %broadcast_select_fusion.1), channel_id=1, source_target_pairs={{0,16},{4,20},{8,24},{12,28},{16,0},{20,4},{24,8},{28,12},{1,17},{... | collective-permute-start | bytes 393224 | tf_op jit(solution)/shard_map/cond/branch_1_fun/ppermute | solution.py:288
  28.5 1.7 %collective-permute-start.1 = (f32[2,128,128]{2,1,0:T(8,128)}, f32[2,128,128]{2,1,0:T(8,128)}, u32[]{:S(2)}, u32[]{:S(2)}) collective-permute-start(f32[2,128,128]{2,1,0:T(8,128)} %broadcast_select_fusion.2), channel_id=1, source_target_pairs={{0,4},{4,0},{8,12},{12,8},{16,20},{20,16},{24,28},{28,24},{1,5},{5... | collective-permute-start | bytes 393224 | tf_op jit(solution)/shard_map/cond/branch_1_fun/ppermute | solution.py:288
  30.2 10.3 %collective-permute-start.9 = (f32[8,64,128]{2,1,0:T(8,128)S(1)}, f32[8,64,128]{2,1,0:T(8,128)S(1)}, u32[]{:S(2)}, u32[]{:S(2)}) collective-permute-start(f32[8,64,128]{2,1,0:T(8,128)S(1)} %broadcast_select_fusion.7), channel_id=1, source_target_pairs={{0,16},{4,20},{8,24},{12,28},{16,0},{20,4},{24,8},{28,12},{1,17},{... | collective-permute-start | bytes 786440 | tf_op jit(solution)/shard_map/ppermute | solution.py:288
  31.7 8.6 %collective-permute-start.10 = (f32[8,64,128]{2,1,0:T(8,128)S(1)}, f32[8,64,128]{2,1,0:T(8,128)}, u32[]{:S(2)}, u32[]{:S(2)}) collective-permute-start(f32[8,64,128]{2,1,0:T(8,128)S(1)} %broadcast_select_fusion.6), channel_id=1, source_target_pairs={{0,8},{4,12},{8,0},{12,4},{16,24},{20,28},{24,16},{28,20},{1,9},{5... | collective-permute-start | bytes 786440 | tf_op jit(solution)/shard_map/ppermute | solution.py:288
  33.2 7.8 %copy-start.1 = (f32[4,128,8,128]{3,2,1,0:T(8,128)S(1)}, f32[4,128,8,128]{3,2,1,0:T(8,128)}, u32[]{:S(2)}) copy-start(f32[4,128,8,128]{3,2,1,0:T(8,128)} %matrix_ref.5) | copy-start | bytes 6291460
  38.3 10.2 %collective-permute-start.8 = (f32[4,128,128]{2,1,0:T(8,128)S(1)}, f32[4,128,128]{2,1,0:T(8,128)S(1)}, u32[]{:S(2)}, u32[]{:S(2)}) collective-permute-start(f32[4,128,128]{2,1,0:T(8,128)S(1)} %broadcast_select_fusion.5.rows_ref), channel_id=1, source_target_pairs={{0,1},{1,0},{2,3},{3,2},{4,5},{5,4},{6,7},{7,6},{8,9},{9,8},{10,11... | collective-permute-start | bytes 786440 | tf_op jit(solution)/shard_map/ppermute | solution.py:288
  40.4 8.0 %collective-permute-start.12 = (f32[8,64,128]{2,1,0:T(8,128)S(1)}, f32[8,64,128]{2,1,0:T(8,128)S(1)}, u32[]{:S(2)}, u32[]{:S(2)}) collective-permute-start(f32[8,64,128]{2,1,0:T(8,128)S(1)} %broadcast_select_fusion.3.hb_ref), channel_id=1, source_target_pairs={{0,4},{4,0},{8,12},{12,8},{16,20},{20,16},{24,28},{28,24},{1,5},{5... | collective-permute-start | bytes 786440 | tf_op jit(solution)/shard_map/ppermute | solution.py:288
  40.5 7.9 %collective-permute-start.11 = (f32[8,64,128]{2,1,0:T(8,128)S(1)}, f32[8,64,128]{2,1,0:T(8,128)S(1)}, u32[]{:S(2)}, u32[]{:S(2)}) collective-permute-start(f32[8,64,128]{2,1,0:T(8,128)S(1)} %broadcast_select_fusion.4.ha_ref), channel_id=1, source_target_pairs={{0,4},{4,0},{8,12},{12,8},{16,20},{20,16},{24,28},{28,24},{1,5},{5... | collective-permute-start | bytes 786440 | tf_op jit(solution)/shard_map/ppermute | solution.py:288

commit v14 on v13

--- a/solution.py
+++ b/solution.py
@@ -24,60 +24,54 @@
     return jnp.broadcast_to(row, (SUB, row.shape[-1]))
 
 
-def eliminate(s, sym, aug):
+def eliminate(s, extra, scratch):
     n = s.shape[0]
     groups = n // SUB
     sub = lax.broadcasted_iota(jnp.int32, (SUB, n), 0)
     lane = lax.broadcasted_iota(jnp.int32, (SUB, n), 1)
-    sym[...] = s.reshape(groups, SUB, n)
     rows = lax.broadcasted_iota(jnp.int32, (n, n), 0)
     cols = lax.broadcasted_iota(jnp.int32, (n, n), 1)
-    aug[...] = jnp.where(rows == cols, 1.0, 0.0).reshape(groups, SUB, n)
+    for ref, value in zip(scratch, (s, jnp.where(rows == cols, 1.0, 0.0), extra)):
+        ref[...] = value.reshape(groups, SUB, n)
+    sides = range(len(scratch))
     for g in range(groups):
         start = g * SUB
         left = groups - g
-        rest = sym[g:]
-        top = sym[g]
-        top_aug = aug[g]
+        rest = scratch[0][g:]
         spread = [jnp.broadcast_to(rest[:, :, start + j:start + j + 1], (left, SUB, n)) for j in range(SUB)]
         unit = {(i, j): full(spread[j][0, i:i + 1, :]) for j in range(SUB) for i in range(j, SUB)}
-        scaled = []
-        scaled_aug = []
-        roots = jnp.zeros((SUB, n), jnp.float32)
+        row = [[full(ref[g, k:k + 1, :]) for k in range(SUB)] for ref in scratch]
+        scaled = [[] for _ in sides]
+        tops = [None for _ in sides]
         for k in range(SUB):
             pivot = unit[k, k]
             guess = pl.reciprocal(pivot, approx=True)
             rest_of = 2.0 - pivot * guess
             recip = guess * rest_of
-            roots = jnp.where(sub == k, pivot, roots)
+            root = lax.rsqrt(pivot)
             for j in range(k + 1, SUB):
-                unit[j, j] = unit[j, j] - (unit[j, k] * unit[j, k] * guess) * rest_of
-                for i in range(j + 1, SUB):
+                for i in range(j, SUB):
                     unit[i, j] = unit[i, j] - (unit[i, k] * unit[j, k] * guess) * rest_of
+            factors = {j: unit[j, k] * recip for j in range(k + 1, SUB)}
             for j in range(k + 1, SUB):
-                factor = unit[j, k] * recip
-                spread[j] = spread[j] - spread[k] * factor[None]
-            row = full(top[k:k + 1, :]) * recip
-            row_aug = full(top_aug[k:k + 1, :]) * recip
-            scaled.append(row)
-            scaled_aug.append(row_aug)
-            if k + 1 < SUB:
-                below = jnp.where(sub > k, spread[k][0], 0.0)
-                top = top - below * row
-                top_aug = top_aug - below * row_aug
-        root = lax.rsqrt(roots)
-        sym[g] = jnp.where(lane >= start + sub, top * root, 0.0)
-        aug[g] = top_aug * root
+                spread[j] = spread[j] - spread[k] * factors[j][None]
+            for m in sides:
+                for j in range(k + 1, SUB):
+                    row[m][j] = row[m][j] - row[m][k] * factors[j]
+                scaled[m].append(row[m][k] * recip)
+                final = row[m][k] * root
+                tops[m] = final if k == 0 else jnp.where(sub == k, final, tops[m])
+        scratch[0][g] = jnp.where(lane >= start + sub, tops[0], 0.0)
+        for m in sides[1:]:
+            scratch[m][g] = tops[m]
         if left > 1:
-            low = rest[1:]
-            low_aug = aug[g + 1:]
-            for k in range(SUB):
-                low = low - spread[k][1:] * scaled[k][None]
-                low_aug = low_aug - spread[k][1:] * scaled_aug[k][None]
-            sym[g + 1:] = low
-            aug[g + 1:] = low_aug
-    upper = sym[...].reshape(n, n)
-    return upper.T, aug[...].reshape(n, n)
+            for m in sides:
+                low = scratch[m][g + 1:]
+                for k in range(SUB):
+                    low = low - spread[k][1:] * scaled[m][k][None]
+                scratch[m][g + 1:] = low
+    upper, inverse, product = [ref[...].reshape(n, n) for ref in scratch]
+    return upper.T, inverse, product
 
 
 def is_odd_row():
@@ -151,38 +145,42 @@
     )(matrix)
 
 
-def first_factor_kernel(a_ref, f_ref, w_ref, sym, aug):
-    f_ref[...], w_ref[...] = eliminate(a_ref[...], sym, aug)
-
-
-def first_factor(a):
+def first_factor_kernel(a_ref, side_ref, f_ref, w_ref, cross_ref, *scratch):
+    f_ref[...], w_ref[...], cross_ref[...] = eliminate(a_ref[...], side_ref[...], scratch)
+
+
+def elimination_scratch(n):
+    return [pltpu.VMEM((n // SUB, SUB, n), jnp.float32)] * 3
+
+
+def first_factor(a, side):
     n = a.shape[1]
     square = jax.ShapeDtypeStruct((n, n), jnp.float32)
     return pl.pallas_call(
         first_factor_kernel,
-        out_shape=[square, square],
-        in_specs=[VMEM],
-        out_specs=[VMEM, VMEM],
-        scratch_shapes=[pltpu.VMEM((n // SUB, SUB, n), jnp.float32)] * 2,
+        out_shape=[square] * 3,
+        in_specs=[VMEM] * 2,
+        out_specs=[VMEM] * 3,
+        scratch_shapes=elimination_scratch(n),
         compiler_params=pltpu.CompilerParams(vmem_limit_bytes=4 * MIB),
         cost_estimate=estimate(8 * 10**9, 2 * MIB),
         name="first_factor",
-    )(a)
-
-
-def second_factor_kernel(low_ref, a_ref, w0_ref, matrix_ref, f_ref, w_ref, mixed_ref,
-                         blocks_ref, sym, aug, sems):
+    )(a, side)
+
+
+def second_factor_kernel(a_ref, cross_ref, w0_ref, matrix_ref, f_ref, w_ref, mixed_ref, blocks_ref, *scratch):
     n = w0_ref.shape[0]
     local_cols = matrix_ref.shape[2]
+    sems = scratch[-1]
     copies = [pltpu.make_async_copy(matrix_ref.at[:, :, j, :], blocks_ref.at[j], sems.at[j]) for j in range(local_cols)]
     for copy in copies:
         copy.start()
     odd = is_odd_row()
     w0 = w0_ref[...]
-    cross = dot_t(low_ref[...], w0)
-    f1, w1 = eliminate(a_ref[...] - dot_t(cross, cross), sym, aug)
+    cross = cross_ref[...]
+    both = dot(cross.T, jnp.concatenate([cross, w0], axis=1))
+    f1, w1, w10 = eliminate(a_ref[...] - both[:, :n], -both[:, n:], scratch[:-1])
     f_ref[...] = f1
-    w10 = -dot(w1, dot(cross, w0))
     zero = jnp.zeros((n, n), jnp.float32)
     w_ref[:n, :n] = w0
     w_ref[:n, n:] = zero
@@ -196,7 +194,7 @@
         copy.wait()
 
 
-def second_factor(low, a, w0, matrix):
+def second_factor(a, cross, w0, matrix):
     local_rows, n, local_cols, _ = matrix.shape
     square = jax.ShapeDtypeStruct((n, n), jnp.float32)
     double = jax.ShapeDtypeStruct((2 * n, 2 * n), jnp.float32)
@@ -206,11 +204,11 @@
         out_shape=[square, double, double, blocks],
         in_specs=[VMEM] * 3 + [HBM],
         out_specs=[VMEM] * 4,
-        scratch_shapes=[pltpu.VMEM((n // SUB, SUB, n), jnp.float32)] * 2 + [pltpu.SemaphoreType.DMA((local_cols,))],
+        scratch_shapes=elimination_scratch(n) + [pltpu.SemaphoreType.DMA((local_cols,))],
         compiler_params=pltpu.CompilerParams(vmem_limit_bytes=12 * MIB),
         cost_estimate=estimate(8 * 10**9, 4 * MIB),
         name="second_factor",
-    )(low, a, w0, matrix)
+    )(a, cross, w0, matrix)
 
 
 def settle_kernel(f0_ref, f1_ref, w_ref, mixed_ref, rows_ref, rows_other_ref, ha_ref, hb_ref, oa_ref, ob_ref, blocks_ref,
@@ -324,7 +322,8 @@
     right = (grid_col % 2) == 1
 
     block = corner_block(kernel)
-    column, upper, lower = panels(kernel)
+    block, kernel_then = after(block, kernel)
+    column, upper, lower = panels(kernel_then)
     first_bit, last_bit = row_bits[0], row_bits[-1]
 
     moved = exchange(block, "col", 1 << col_bits[0], n_col)
@@ -342,6 +341,7 @@
     across, block, ha, hb, column = after(across, block, ha, hb, column)
 
     pair = jnp.stack([jnp.where(right, across, block), jnp.where(right, block, across)])
+    pair, column = after(pair, column)
     moved = exchange(pair, "row", 1 << first_bit, n_row)
     column_moved = exchange(column, "col", 1 << col_bits[0], n_col)
 
@@ -357,9 +357,9 @@
     rows = jnp.where(bit_set(grid_col, col_bits[0]), column_moved, column)
     pair, other, rows = after(pair, other, rows)
     a00 = jnp.where(odd, other[0], pair[0])
-    a10 = jnp.where(odd, pair[0], other[0])
+    a01 = jnp.where(odd, other[1], pair[1])
     a11 = jnp.where(odd, pair[1], other[1])
-    f0, w0 = first_factor(a00)
+    f0, w0, cross = first_factor(a00, a01)
 
     w0, rows, row_then, col_then = after(w0, rows, grid_row, grid_col)
     ha = jnp.where(bit_set(row_then, row_bits[1]), ha_moved, ha)
@@ -370,7 +370,7 @@
     rows_other = exchange(rows, "col", 1, n_col)
     oa = exchange(ha, "row", 1, n_row)
     ob = exchange(hb, "row", 1, n_row)
-    f1, w, mixed, blocks = second_factor(a10, a11, w0, kernel)
+    f1, w, mixed, blocks = second_factor(a11, cross, w0, kernel)
     return settle(f0, f1, w, mixed, rows, rows_other, ha, hb, oa, ob, blocks)
 
 

time: 55.7 us -> 57 us (1.023)
  local copies, waits for them, and re-layouts: 1.6 us -> 3.12 us
    unnamed x4, local copies, waits for them, and re-layouts: 1.6 us -> 3.12 us
  transfers between devices with their start and end apart: 13 -> 13, of which waited for: 5 -> 5; matrix products, arithmetic and copies ran while one was open for 3% -> 3% of each run, Pallas kernels for 22% -> 21%
where the time goes in v14:
time: 57 us; the launch traced here: 56.7 us
  Pallas kernels  19.8 us (35%)
  starting transfers between devices  17.4 us (31%)
  waiting for transfers between devices  14.3 us (25%)
  local copies, waits for them, and re-layouts  3.12 us (5%)
  other arithmetic  1.84 us (3%)
    ppermute x13, starting transfers between devices, exchange(): return lax.ppermute(value, axis, [(i, i ^ mask) for i in range(size)])  17.4 us
    ppermute x13, waiting for transfers between devices, exchange(): return lax.ppermute(value, axis, [(i, i ^ mask) for i in range(size)])  14.3 us
    pallas_call x1, Pallas kernels, second_factor(): pl.pallas_call(second_factor_kernel, out_shape=[square, double, double, b...  6.99 us
    pallas_call x1, Pallas kernels, settle(): pl.pallas_call(settle_kernel, out_shape=jax.ShapeDtypeStruct((local_rows,...  6.9 us
    pallas_call x1, Pallas kernels, first_factor(): pl.pallas_call(first_factor_kernel, out_shape=[square] * 3, in_specs=[VME...  5.11 us
    unnamed x4, local copies, waits for them, and re-layouts  3.12 us
  transfers between devices with their start and end apart: 13, of which 5 were waited for; matrix products, arithmetic and copies ran while one was open for 3% of the time, Pallas kernels for 21%

profile of v14, /device:TPU:0, one launch (start us, length us, event | category | flops | bytes accessed | tf_op | source)
XLA Modules:
  0.0 56.7 jit_solution(3892773622846676689)
XLA Ops:
  0.0 0.0 copy-start
  0.0 1.6 %copy-done = f32[4,128,8,128]{3,2,1,0:T(8,128)S(1)} copy-done((f32[4,128,8,128]{3,2,1,0:T(8,128)S(1)}, f32[4,128,8,128]{3,2,1,0:T(8,128)}, u32[]{:S(2)}) %copy-start) | copy-done | bytes 2097176
  1.6 0.0 copy-start.1
  1.6 0.1 corner_block.1
  1.7 1.5 %copy-done.1 = f32[4,128,8,128]{3,2,1,0:T(8,128)S(1)} copy-done((f32[4,128,8,128]{3,2,1,0:T(8,128)S(1)}, f32[4,128,8,128]{3,2,1,0:T(8,128)}, u32[]{:S(2)}) %copy-start.1) | copy-done | bytes 2097176
  3.2 0.7 %panels.1 = (f32[4,128,128]{2,1,0:T(8,128)S(1)}, f32[8,64,128]{2,1,0:T(8,128)S(1)}, f32[8,64,128]{2,1,0:T(8,128)S(1)}) custom-call(f32[4,128,8,128]{3,2,1,0:T(8,128)S(1)} %copy-done.1), custom_call_target="tpu_custom_call" | custom-call | bytes 4194304 | tf_op jit(solution)/shard_map/panels/pallas_call | solution.py:136
  3.9 3.0 %collective-permute-start.4 = (f32[8,64,128]{2,1,0:T(8,128)S(1)}, f32[8,64,128]{2,1,0:T(8,128)S(1)}, u32[]{:S(2)}, u32[]{:S(2)}) collective-permute-start(f32[8,64,128]{2,1,0:T(8,128)S(1)} %get-tuple-element.58), channel_id=1, source_target_pairs={{0,8},{4,12},{8,0},{12,4},{16,24},{20,28},{24,16},{28,20},{1,9},{5... | collective-permute-start | bytes 786440 | tf_op jit(solution)/shard_map/ppermute | solution.py:286
  6.9 2.6 %collective-permute-start.2 = (f32[128,128]{1,0:T(8,128)S(1)}, f32[128,128]{1,0:T(8,128)S(1)}, u32[]{:S(2)}, u32[]{:S(2)}) collective-permute-start(f32[128,128]{1,0:T(8,128)S(1)} %corner_block.1), channel_id=1, source_target_pairs={{0,2},{1,3},{2,0},{3,1},{4,6},{5,7},{6,4},{7,5},{8,10},{9,11},{10,... | collective-permute-start | bytes 196616 | tf_op jit(solution)/shard_map/ppermute | solution.py:286
  9.5 1.5 %collective-permute-start.5 = (f32[8,64,128]{2,1,0:T(8,128)S(1)}, f32[8,64,128]{2,1,0:T(8,128)}, u32[]{:S(2)}, u32[]{:S(2)}) collective-permute-start(f32[8,64,128]{2,1,0:T(8,128)S(1)} %get-tuple-element.59), channel_id=1, source_target_pairs={{0,16},{4,20},{8,24},{12,28},{16,0},{20,4},{24,8},{28,12},{1,17},{... | collective-permute-start | bytes 786440 | tf_op jit(solution)/shard_map/ppermute | solution.py:286
  11.0 1.4 %collective-permute-done.2 = f32[128,128]{1,0:T(8,128)S(1)} collective-permute-done((f32[128,128]{1,0:T(8,128)S(1)}, f32[128,128]{1,0:T(8,128)S(1)}, u32[]{:S(2)}, u32[]{:S(2)}) %collective-permute-start.2) | collective-permute-done | bytes 65568 | tf_op jit(solution)/shard_map/ppermute | solution.py:286
  12.4 1.3 %collective-permute-start.3 = (f32[128,128]{1,0:T(8,128)S(1)}, f32[128,128]{1,0:T(8,128)S(1)}, u32[]{:S(2)}, u32[]{:S(2)}) collective-permute-start(f32[128,128]{1,0:T(8,128)S(1)} %get-tuple-element.95), channel_id=1, source_target_pairs={{0,1},{1,0},{2,3},{3,2},{4,5},{5,4},{6,7},{7,6},{8,9},{9,8},{10,11... | collective-permute-start | bytes 196616 | tf_op jit(solution)/shard_map/ppermute | solution.py:286
  13.7 0.0 collective-permute-done.4
  13.8 3.3 %collective-permute-done.5 = f32[8,64,128]{2,1,0:T(8,128)} collective-permute-done((f32[8,64,128]{2,1,0:T(8,128)S(1)}, f32[8,64,128]{2,1,0:T(8,128)}, u32[]{:S(2)}, u32[]{:S(2)}) %collective-permute-start.5) | collective-permute-done | bytes 262176 | tf_op jit(solution)/shard_map/ppermute | solution.py:286
  17.1 0.0 collective-permute-done.3
  17.2 2.1 %collective-permute-start.7 = (f32[4,128,128]{2,1,0:T(8,128)S(1)}, f32[4,128,128]{2,1,0:T(8,128)S(1)}, u32[]{:S(2)}, u32[]{:S(2)}) collective-permute-start(f32[4,128,128]{2,1,0:T(8,128)S(1)} %get-tuple-element.70), channel_id=1, source_target_pairs={{0,2},{1,3},{2,0},{3,1},{4,6},{5,7},{6,4},{7,5},{8,10},{9,11},{10,... | collective-permute-start | bytes 786440 | tf_op jit(solution)/shard_map/ppermute | solution.py:286
  19.3 0.5 collective-permute-start.6
  19.8 4.4 %collective-permute-done.6 = f32[2,128,128]{2,1,0:T(8,128)S(1)} collective-permute-done((f32[2,128,128]{2,1,0:T(8,128)S(1)}, f32[2,128,128]{2,1,0:T(8,128)S(1)}, u32[]{:S(2)}, u32[]{:S(2)}) %collective-permute-start.6) | collective-permute-done | bytes 131104 | tf_op jit(solution)/shard_map/ppermute | solution.py:286
  24.2 7.4 %conditional.3 = (f32[2,128,128]{2,1,0:T(8,128)}, f32[2,128,128]{2,1,0:T(8,128)}) conditional(s32[]{:T(128)} %convert_element_type.4, () %tuple.25, (s32[]{:T(128)}, f32[2,128,128]{2,1,0:T(8,128)S(1)}, f32[2,128,128]{2,1,0:T(8,128)S(1)}) %tuple.31), branch_computations={%region_2.3_spmd, %region_3.4_spmd} | conditional | flops 65542 | bytes 1835172 | solution.py:307
  24.3 1.6 %collective-permute-start = (f32[2,128,128]{2,1,0:T(8,128)S(1)}, f32[2,128,128]{2,1,0:T(8,128)S(1)}, u32[]{:S(2)}, u32[]{:S(2)}) collective-permute-start(f32[2,128,128]{2,1,0:T(8,128)S(1)} %broadcast_select_fusion.1), channel_id=1, source_target_pairs={{0,16},{4,20},{8,24},{12,28},{16,0},{20,4},{24,8},{28,12},{1,17},{... | collective-permute-start | bytes 393224 | tf_op jit(solution)/shard_map/cond/branch_1_fun/ppermute | solution.py:286
  25.8 3.4 %collective-permute-done = f32[2,128,128]{2,1,0:T(8,128)S(1)} collective-permute-done((f32[2,128,128]{2,1,0:T(8,128)S(1)}, f32[2,128,128]{2,1,0:T(8,128)S(1)}, u32[]{:S(2)}, u32[]{:S(2)}) %collective-permute-start) | collective-permute-done | bytes 131104 | tf_op jit(solution)/shard_map/cond/branch_1_fun/ppermute | solution.py:286
  29.3 0.7 %broadcast_select_fusion.2 = f32[2,128,128]{2,1,0:T(8,128)} fusion(f32[2,128,128]{2,1,0:T(8,128)S(1)} %collective-permute-done, f32[2,128,128]{2,1,0:T(8,128)S(1)} %broadcast_select_fusion.1, pred[]{:T(512)S(6)} %eq.24), kind=kLoop, calls=%fused_computation.2 | loop fusion | flops 32768 | bytes 393217 | tf_op jit(solution)/shard_map/cond/branch_1_fun/jit(_where)/select_n | solution.py:296
  30.0 0.0 collective-permute-start.1
  30.0 1.7 %collective-permute-done.1 = f32[2,128,128]{2,1,0:T(8,128)} collective-permute-done((f32[2,128,128]{2,1,0:T(8,128)}, f32[2,128,128]{2,1,0:T(8,128)}, u32[]{:S(2)}, u32[]{:S(2)}) %collective-permute-start.1) | collective-permute-done | bytes 131104 | tf_op jit(solution)/shard_map/cond/branch_1_fun/ppermute | solution.py:286
  31.7 1.5 %collective-permute-start.9 = (f32[8,64,128]{2,1,0:T(8,128)S(1)}, f32[8,64,128]{2,1,0:T(8,128)}, u32[]{:S(2)}, u32[]{:S(2)}) collective-permute-start(f32[8,64,128]{2,1,0:T(8,128)S(1)} %broadcast_select_fusion.7), channel_id=1, source_target_pairs={{0,16},{4,20},{8,24},{12,28},{16,0},{20,4},{24,8},{28,12},{1,17},{... | collective-permute-start | bytes 786440 | tf_op jit(solution)/shard_map/ppermute | solution.py:286
  33.2 0.5 collective-permute-start.10
  33.7 0.0 collective-permute-done.7
  33.7 1.0 %select_bitcast_fusion = (f32[128,128]{1,0:T(8,128)S(1)}, f32[128,128]{1,0:T(8,128)S(1)}, f32[128,128]{1,0:T(8,128)S(1)}) fusion(f32[2,128,128]{2,1,0:T(8,128)} %get-tuple-element.72, f32[2,128,128]{2,1,0:T(8,128)} %get-tuple-element.71, pred[]{:T(512)S(6)} %eq.33), kind=kLoop, calls=%fused_computation.9 | loop fusion | flops 49152 | bytes 458753 | tf_op jit(solution)/shard_map/jit(_where)/select_n | solution.py:361
  34.7 5.1 %first_factor.1 = (f32[128,128]{1,0:T(8,128)S(1)}, f32[128,128]{1,0:T(8,128)S(1)}, f32[128,128]{1,0:T(8,128)S(1)}) custom-call(f32[128,128]{1,0:T(8,128)S(1)} %get-tuple-element.88.a_ref, f32[128,128]{1,0:T(8,128)S(1)} %get-tuple-element.87.side_ref), custom_call_target="tpu_custom_call" | custom-call | flops 8000000000 | bytes 2097152 | tf_op jit(solution)/shard_map/first_factor/pallas_call | solution.py:159
  39.8 2.1 %collective-permute-start.8 = (f32[4,128,128]{2,1,0:T(8,128)S(1)}, f32[4,128,128]{2,1,0:T(8,128)S(1)}, u32[]{:S(2)}, u32[]{:S(2)}) collective-permute-start(f32[4,128,128]{2,1,0:T(8,128)S(1)} %broadcast_select_fusion.5.rows_ref), channel_id=1, source_target_pairs={{0,1},{1,0},{2,3},{3,2},{4,5},{5,4},{6,7},{7,6},{8,9},{9,8},{10,11... | collective-permute-start | bytes 786440 | tf_op jit(solution)/shard_map/ppermute | solution.py:286
  41.9 0.0 collective-permute-done.10
  41.9 0.1 collective-permute-start.12
  42.0 0.0 collective-permute-done.9
  42.1 0.5 collective-permute-start.11
  42.6 7.0 %second_factor.1 = (f32[128,128]{1,0:T(8,128)S(1)}, f32[256,256]{1,0:T(8,128)S(1)}, f32[256,256]{1,0:T(8,128)S(1)}, f32[8,4,128,128]{3,2,1,0:T(8,128)S(1)}) custom-call(f32[128,128]{1,0:T(8,128)S(1)} %get-tuple-element.86.a_ref, f32[128,128]{1,0:T(8,128)S(1)} %get-tuple-element.74.cross_ref, f32[128,128]{1,0:T(8,128)S(1)} %get-tuple-element.77.w0_ref, ...), custom_call_target="tpu_custom_call" | custom-call | flops 8000000000 | bytes 4194304 | tf_op jit(solution)/shard_map/second_factor/pallas_call | solution.py:202
  49.6 0.0 collective-permute-done.8.rows_other_ref
  49.6 0.0 collective-permute-done.12.ob_ref
  49.6 0.0 collective-permute-done.11.oa_ref
  49.7 6.9 %settle.1 = f32[4,128,8,128]{3,2,1,0:T(8,128)} custom-call(f32[128,128]{1,0:T(8,128)S(1)} %get-tuple-element.73.f0_ref, f32[128,128]{1,0:T(8,128)S(1)} %get-tuple-element.78.f1_ref, f32[256,256]{1,0:T(8,128)S(1)} %get-tuple-element.79.w_ref, f32[256,256]{1,0:T(8,128)S(1)} %get-tuple-element.80.mixed_ref, f32[4,128,128]{2,1,0:T(8,128)S(1)} %broadcast_select_fusion.5.rows_ref, ...), custom_call_target="tpu_custom_call" | custom-call | flops 4000000000 | bytes 6291456 | tf_op jit(solution)/shard_map/settle/pallas_call | solution.py:273
  (10 shorter events, 0.2 us)
Async XLA Ops:
  0.0 1.6 %copy-start = (f32[4,128,8,128]{3,2,1,0:T(8,128)S(1)}, f32[4,128,8,128]{3,2,1,0:T(8,128)}, u32[]{:S(2)}) copy-start(f32[4,128,8,128]{3,2,1,0:T(8,128)} %matrix_ref.4) | copy-start | bytes 6291460
  1.6 1.6 %copy-start.1 = (f32[4,128,8,128]{3,2,1,0:T(8,128)S(1)}, f32[4,128,8,128]{3,2,1,0:T(8,128)}, u32[]{:S(2)}) copy-start(f32[4,128,8,128]{3,2,1,0:T(8,128)} %matrix_ref.4) | copy-start | bytes 6291460
  3.9 9.8 %collective-permute-start.4 = (f32[8,64,128]{2,1,0:T(8,128)S(1)}, f32[8,64,128]{2,1,0:T(8,128)S(1)}, u32[]{:S(2)}, u32[]{:S(2)}) collective-permute-start(f32[8,64,128]{2,1,0:T(8,128)S(1)} %get-tuple-element.58), channel_id=1, source_target_pairs={{0,8},{4,12},{8,0},{12,4},{16,24},{20,28},{24,16},{28,20},{1,9},{5... | collective-permute-start | bytes 786440 | tf_op jit(solution)/shard_map/ppermute | solution.py:286
  6.9 5.5 %collective-permute-start.2 = (f32[128,128]{1,0:T(8,128)S(1)}, f32[128,128]{1,0:T(8,128)S(1)}, u32[]{:S(2)}, u32[]{:S(2)}) collective-permute-start(f32[128,128]{1,0:T(8,128)S(1)} %corner_block.1), channel_id=1, source_target_pairs={{0,2},{1,3},{2,0},{3,1},{4,6},{5,7},{6,4},{7,5},{8,10},{9,11},{10,... | collective-permute-start | bytes 196616 | tf_op jit(solution)/shard_map/ppermute | solution.py:286
  9.5 7.6 %collective-permute-start.5 = (f32[8,64,128]{2,1,0:T(8,128)S(1)}, f32[8,64,128]{2,1,0:T(8,128)}, u32[]{:S(2)}, u32[]{:S(2)}) collective-permute-start(f32[8,64,128]{2,1,0:T(8,128)S(1)} %get-tuple-element.59), channel_id=1, source_target_pairs={{0,16},{4,20},{8,24},{12,28},{16,0},{20,4},{24,8},{28,12},{1,17},{... | collective-permute-start | bytes 786440 | tf_op jit(solution)/shard_map/ppermute | solution.py:286
  12.4 4.7 %collective-permute-start.3 = (f32[128,128]{1,0:T(8,128)S(1)}, f32[128,128]{1,0:T(8,128)S(1)}, u32[]{:S(2)}, u32[]{:S(2)}) collective-permute-start(f32[128,128]{1,0:T(8,128)S(1)} %get-tuple-element.95), channel_id=1, source_target_pairs={{0,1},{1,0},{2,3},{3,2},{4,5},{5,4},{6,7},{7,6},{8,9},{9,8},{10,11... | collective-permute-start | bytes 196616 | tf_op jit(solution)/shard_map/ppermute | solution.py:286
  17.2 16.5 %collective-permute-start.7 = (f32[4,128,128]{2,1,0:T(8,128)S(1)}, f32[4,128,128]{2,1,0:T(8,128)S(1)}, u32[]{:S(2)}, u32[]{:S(2)}) collective-permute-start(f32[4,128,128]{2,1,0:T(8,128)S(1)} %get-tuple-element.70), channel_id=1, source_target_pairs={{0,2},{1,3},{2,0},{3,1},{4,6},{5,7},{6,4},{7,5},{8,10},{9,11},{10,... | collective-permute-start | bytes 786440 | tf_op jit(solution)/shard_map/ppermute | solution.py:286
  19.3 5.0 %collective-permute-start.6 = (f32[2,128,128]{2,1,0:T(8,128)S(1)}, f32[2,128,128]{2,1,0:T(8,128)S(1)}, u32[]{:S(2)}, u32[]{:S(2)}) collective-permute-start(f32[2,128,128]{2,1,0:T(8,128)S(1)} %pad_maximum_fusion), channel_id=1, source_target_pairs={{0,8},{4,12},{8,0},{12,4},{16,24},{20,28},{24,16},{28,20},{1,9},{5... | collective-permute-start | bytes 393224 | tf_op jit(solution)/shard_map/ppermute | solution.py:286
  24.3 5.0 %collective-permute-start = (f32[2,128,128]{2,1,0:T(8,128)S(1)}, f32[2,128,128]{2,1,0:T(8,128)S(1)}, u32[]{:S(2)}, u32[]{:S(2)}) collective-permute-start(f32[2,128,128]{2,1,0:T(8,128)S(1)} %broadcast_select_fusion.1), channel_id=1, source_target_pairs={{0,16},{4,20},{8,24},{12,28},{16,0},{20,4},{24,8},{28,12},{1,17},{... | collective-permute-start | bytes 393224 | tf_op jit(solution)/shard_map/cond/branch_1_fun/ppermute | solution.py:286
  30.0 1.7 %collective-permute-start.1 = (f32[2,128,128]{2,1,0:T(8,128)}, f32[2,128,128]{2,1,0:T(8,128)}, u32[]{:S(2)}, u32[]{:S(2)}) collective-permute-start(f32[2,128,128]{2,1,0:T(8,128)} %broadcast_select_fusion.2), channel_id=1, source_target_pairs={{0,4},{4,0},{8,12},{12,8},{16,20},{20,16},{24,28},{28,24},{1,5},{5... | collective-permute-start | bytes 393224 | tf_op jit(solution)/shard_map/cond/branch_1_fun/ppermute | solution.py:286
  31.7 10.4 %collective-permute-start.9 = (f32[8,64,128]{2,1,0:T(8,128)S(1)}, f32[8,64,128]{2,1,0:T(8,128)}, u32[]{:S(2)}, u32[]{:S(2)}) collective-permute-start(f32[8,64,128]{2,1,0:T(8,128)S(1)} %broadcast_select_fusion.7), channel_id=1, source_target_pairs={{0,16},{4,20},{8,24},{12,28},{16,0},{20,4},{24,8},{28,12},{1,17},{... | collective-permute-start | bytes 786440 | tf_op jit(solution)/shard_map/ppermute | solution.py:286
  33.2 8.7 %collective-permute-start.10 = (f32[8,64,128]{2,1,0:T(8,128)S(1)}, f32[8,64,128]{2,1,0:T(8,128)}, u32[]{:S(2)}, u32[]{:S(2)}) collective-permute-start(f32[8,64,128]{2,1,0:T(8,128)S(1)} %broadcast_select_fusion.6), channel_id=1, source_target_pairs={{0,8},{4,12},{8,0},{12,4},{16,24},{20,28},{24,16},{28,20},{1,9},{5... | collective-permute-start | bytes 786440 | tf_op jit(solution)/shard_map/ppermute | solution.py:286
  39.8 9.8 %collective-permute-start.8 = (f32[4,128,128]{2,1,0:T(8,128)S(1)}, f32[4,128,128]{2,1,0:T(8,128)S(1)}, u32[]{:S(2)}, u32[]{:S(2)}) collective-permute-start(f32[4,128,128]{2,1,0:T(8,128)S(1)} %broadcast_select_fusion.5.rows_ref), channel_id=1, source_target_pairs={{0,1},{1,0},{2,3},{3,2},{4,5},{5,4},{6,7},{7,6},{8,9},{9,8},{10,11... | collective-permute-start | bytes 786440 | tf_op jit(solution)/shard_map/ppermute | solution.py:286
  41.9 7.7 %collective-permute-start.12 = (f32[8,64,128]{2,1,0:T(8,128)S(1)}, f32[8,64,128]{2,1,0:T(8,128)S(1)}, u32[]{:S(2)}, u32[]{:S(2)}) collective-permute-start(f32[8,64,128]{2,1,0:T(8,128)S(1)} %broadcast_select_fusion.3.hb_ref), channel_id=1, source_target_pairs={{0,4},{4,0},{8,12},{12,8},{16,20},{20,16},{24,28},{28,24},{1,5},{5... | collective-permute-start | bytes 786440 | tf_op jit(solution)/shard_map/ppermute | solution.py:286
  42.1 7.6 %collective-permute-start.11 = (f32[8,64,128]{2,1,0:T(8,128)S(1)}, f32[8,64,128]{2,1,0:T(8,128)S(1)}, u32[]{:S(2)}, u32[]{:S(2)}) collective-permute-start(f32[8,64,128]{2,1,0:T(8,128)S(1)} %broadcast_select_fusion.4.ha_ref), channel_id=1, source_target_pairs={{0,4},{4,0},{8,12},{12,8},{16,20},{20,16},{24,28},{28,24},{1,5},{5... | collective-permute-start | bytes 786440 | tf_op jit(solution)/shard_map/ppermute | solution.py:286

commit v15 on v14

--- a/solution.py
+++ b/solution.py
@@ -7,6 +7,7 @@
 
 EXACT = lax.Precision.HIGHEST
 SUB = 8
+PANEL = 4
 MIB = 1024 * 1024
 VMEM = pl.BlockSpec(memory_space=pltpu.VMEM)
 HBM = pl.BlockSpec(memory_space=pltpu.HBM)
@@ -36,8 +37,9 @@
     sides = range(len(scratch))
     for g in range(groups):
         start = g * SUB
-        left = groups - g
-        rest = scratch[0][g:]
+        until = (g // PANEL + 1) * PANEL
+        left = until - g
+        rest = scratch[0][g:until]
         spread = [jnp.broadcast_to(rest[:, :, start + j:start + j + 1], (left, SUB, n)) for j in range(SUB)]
         unit = {(i, j): full(spread[j][0, i:i + 1, :]) for j in range(SUB) for i in range(j, SUB)}
         row = [[full(ref[g, k:k + 1, :]) for k in range(SUB)] for ref in scratch]
@@ -66,10 +68,18 @@
             scratch[m][g] = tops[m]
         if left > 1:
             for m in sides:
-                low = scratch[m][g + 1:]
+                low = scratch[m][g + 1:until]
                 for k in range(SUB):
                     low = low - spread[k][1:] * scaled[m][k][None]
-                scratch[m][g + 1:] = low
+                scratch[m][g + 1:until] = low
+        elif until < groups:
+            done = [ref[until - PANEL:until].reshape(PANEL * SUB, n) for ref in scratch]
+            update = lax.dot_general(
+                done[0], jnp.concatenate(done, axis=1), (((0,), (0,)), ((), ())), precision=EXACT,
+                preferred_element_type=jnp.float32)
+            for m in sides:
+                part = update[until * SUB:, m * n:(m + 1) * n]
+                scratch[m][until:] = scratch[m][until:] - part.reshape(groups - until, SUB, n)
     upper, inverse, product = [ref[...].reshape(n, n) for ref in scratch]
     return upper.T, inverse, product
 
@@ -119,7 +129,7 @@
 
 def panels_kernel(matrix_ref, column_ref, upper_ref, lower_ref, sems):
     local_cols, half, _ = upper_ref.shape
-    copies = [pltpu.make_async_copy(matrix_ref.at[:, :, 0, :], column_ref, sems.at[0])]
+    copies = [pltpu.make_async_copy(matrix_ref.at[pl.ds(1, column_ref.shape[0]), :, 0, :], column_ref, sems.at[0])]
     for j in range(local_cols):
         copies.append(pltpu.make_async_copy(matrix_ref.at[0, pl.ds(0, half), j, :], upper_ref.at[j], sems.at[1 + j]))
         copies.append(pltpu.make_async_copy(
@@ -135,7 +145,7 @@
     strip = jax.ShapeDtypeStruct((local_cols, n // 2, n), jnp.float32)
     return pl.pallas_call(
         panels_kernel,
-        out_shape=[jax.ShapeDtypeStruct((local_rows, n, n), jnp.float32), strip, strip],
+        out_shape=[jax.ShapeDtypeStruct((local_rows - 1, n, n), jnp.float32), strip, strip],
         in_specs=[HBM],
         out_specs=[VMEM] * 3,
         scratch_shapes=[pltpu.SemaphoreType.DMA((1 + 2 * local_cols,))],
@@ -211,17 +221,19 @@
     )(a, cross, w0, matrix)
 
 
-def settle_kernel(f0_ref, f1_ref, w_ref, mixed_ref, rows_ref, rows_other_ref, ha_ref, hb_ref, oa_ref, ob_ref, blocks_ref,
-                  out_ref, result, sems):
+def settle_kernel(f0_ref, f1_ref, w_ref, mixed_ref, first_ref, rows_ref, rows_other_ref, ha_ref, hb_ref, oa_ref, ob_ref,
+                  blocks_ref, out_ref, result, sems):
     grid_row = lax.axis_index("row")
     grid_col = lax.axis_index("col")
     n = f0_ref.shape[0]
     local_cols, local_rows, _, _ = blocks_ref.shape
-    flat = local_rows * n
+    flat = (local_rows - 1) * n
     own = rows_ref[...].reshape(flat, n)
     other = rows_other_ref[...].reshape(flat, n)
     swapped = lax.rem(grid_col, 2) == 1
-    rows = jnp.concatenate([jnp.where(swapped, other, own), jnp.where(swapped, own, other)], axis=1)
+    rows = jnp.concatenate([
+        jnp.concatenate([first_ref[0], jnp.where(swapped, other, own)], axis=0),
+        jnp.concatenate([first_ref[1], jnp.where(swapped, own, other)], axis=0)], axis=1)
     solved = dot_parts(parts(rows), parts(w_ref[...]), ((1,), (1,)))
     left = parts(solved)
     mixed = parts(mixed_ref[...])
@@ -268,18 +280,18 @@
         copy.wait()
 
 
-def settle(f0, f1, w, mixed, rows, rows_other, ha, hb, oa, ob, blocks):
+def settle(f0, f1, w, mixed, first_rows, rows, rows_other, ha, hb, oa, ob, blocks):
     local_cols, local_rows, n, _ = blocks.shape
     return pl.pallas_call(
         settle_kernel,
         out_shape=jax.ShapeDtypeStruct((local_rows, n, local_cols, n), jnp.float32),
-        in_specs=[VMEM] * 11,
+        in_specs=[VMEM] * 12,
         out_specs=HBM,
         scratch_shapes=[pltpu.VMEM(blocks.shape, jnp.float32), pltpu.SemaphoreType.DMA((local_cols,))],
         compiler_params=pltpu.CompilerParams(vmem_limit_bytes=32 * MIB),
         cost_estimate=estimate(4 * 10**9, 6 * MIB),
         name="settle",
-    )(f0, f1, w, mixed, rows, rows_other, ha, hb, oa, ob, blocks)
+    )(f0, f1, w, mixed, first_rows, rows, rows_other, ha, hb, oa, ob, blocks)
 
 
 def exchange(value, axis, mask, size):
@@ -322,8 +334,7 @@
     right = (grid_col % 2) == 1
 
     block = corner_block(kernel)
-    block, kernel_then = after(block, kernel)
-    column, upper, lower = panels(kernel_then)
+    column, upper, lower = panels(kernel)
     first_bit, last_bit = row_bits[0], row_bits[-1]
 
     moved = exchange(block, "col", 1 << col_bits[0], n_col)
@@ -341,21 +352,18 @@
     across, block, ha, hb, column = after(across, block, ha, hb, column)
 
     pair = jnp.stack([jnp.where(right, across, block), jnp.where(right, block, across)])
-    pair, column = after(pair, column)
+    first_rows = pair
     moved = exchange(pair, "row", 1 << first_bit, n_row)
     column_moved = exchange(column, "col", 1 << col_bits[0], n_col)
-
-    def over_row(new, old):
-        pair = jnp.where(bit_set(grid_row, first_bit), new, old)
-        pair = spread(pair, "row", grid_row, n_row, row_bits[1:])
-        return pair, exchange(pair, "row", 1, n_row)
-
-    pair, other = region(over_row, moved, pair)
+    pair = jnp.where(bit_set(grid_row, first_bit), moved, pair)
+    pair = spread(pair, "row", grid_row, n_row, row_bits[1:])
     pair, ha, hb = after(pair, ha, hb)
     ha_moved = exchange(ha, "row", 1 << row_bits[1], n_row)
     hb_moved = exchange(hb, "row", 1 << row_bits[-2], n_row)
     rows = jnp.where(bit_set(grid_col, col_bits[0]), column_moved, column)
-    pair, other, rows = after(pair, other, rows)
+    pair, rows = after(pair, rows)
+    other = exchange(pair, "row", 1, n_row)
+
     a00 = jnp.where(odd, other[0], pair[0])
     a01 = jnp.where(odd, other[1], pair[1])
     a11 = jnp.where(odd, pair[1], other[1])
@@ -371,7 +379,7 @@
     oa = exchange(ha, "row", 1, n_row)
     ob = exchange(hb, "row", 1, n_row)
     f1, w, mixed, blocks = second_factor(a11, cross, w0, kernel)
-    return settle(f0, f1, w, mixed, rows, rows_other, ha, hb, oa, ob, blocks)
+    return settle(f0, f1, w, mixed, first_rows, rows, rows_other, ha, hb, oa, ob, blocks)
 
 
 def solution(mesh):

time: 57 us -> 50.2 us (0.88)
  other arithmetic: 1.84 us -> 0.23 us
  waiting for transfers between devices: 14.3 us -> 12.7 us
  local copies, waits for them, and re-layouts: 3.12 us -> 1.6 us
  starting transfers between devices: 17.4 us -> 16.3 us
  Pallas kernels: 19.8 us -> 19.1 us
    ppermute x13, waiting for transfers between devices: 14.3 us -> 12.7 us  [exchange(): return lax.ppermute(value, axis, [(i, i ^ mask) for i in range(size)])]
    unnamed x4, local copies, waits for them, and re-layouts: 3.12 us -> 1.6 us
    ppermute x13, starting transfers between devices: 17.4 us -> 16.3 us  [exchange(): return lax.ppermute(value, axis, [(i, i ^ mask) for i in range(size)])]
    select_n x1, other arithmetic: 0.96 us -> 0.02 us  [shards(): a11 = jnp.where(odd, pair[1], other[1])]
    select_n x1, other arithmetic: 0.67 us -> 0.02 us  [spread(): jnp.where(bit_set(index, bit), exchange(held, axis, 1 << bit, size), held)]
  transfers between devices with their start and end apart: 13 -> 13, of which waited for: 5 -> 6; matrix products, arithmetic and copies ran while one was open for 3% -> 0% of each run, Pallas kernels for 21% -> 23%
where the time goes in v15:
time: 50.2 us; the launch traced here: 50 us
  Pallas kernels  19.1 us (38%)
  starting transfers between devices  16.3 us (32%)
  waiting for transfers between devices  12.7 us (25%)
  local copies, waits for them, and re-layouts  1.6 us (3%)
    ppermute x13, starting transfers between devices, exchange(): return lax.ppermute(value, axis, [(i, i ^ mask) for i in range(size)])  16.3 us
    ppermute x13, waiting for transfers between devices, exchange(): return lax.ppermute(value, axis, [(i, i ^ mask) for i in range(size)])  12.7 us
    pallas_call x1, Pallas kernels, settle(): pl.pallas_call(settle_kernel, out_shape=jax.ShapeDtypeStruct((local_rows,...  6.9 us
    pallas_call x1, Pallas kernels, second_factor(): pl.pallas_call(second_factor_kernel, out_shape=[square, double, double, b...  6.69 us
    pallas_call x1, Pallas kernels, first_factor(): pl.pallas_call(first_factor_kernel, out_shape=[square] * 3, in_specs=[VME...  4.76 us
    unnamed x4, local copies, waits for them, and re-layouts  1.6 us
  transfers between devices with their start and end apart: 13, of which 6 were waited for; matrix products, arithmetic and copies ran while one was open for 0% of the time, Pallas kernels for 23%

profile of v15, /device:TPU:0, one launch (start us, length us, event | category | flops | bytes accessed | tf_op | source)
XLA Modules:
  0.0 50.0 jit_solution(1029341343334657161)
XLA Ops:
  0.0 0.0 copy-start
  0.0 1.6 %copy-done = f32[4,128,8,128]{3,2,1,0:T(8,128)S(1)} copy-done((f32[4,128,8,128]{3,2,1,0:T(8,128)S(1)}, f32[4,128,8,128]{3,2,1,0:T(8,128)}, u32[]{:S(2)}) %copy-start) | copy-done | bytes 2097176
  1.6 0.7 %panels.1 = (f32[3,128,128]{2,1,0:T(8,128)S(1)}, f32[8,64,128]{2,1,0:T(8,128)S(1)}, f32[8,64,128]{2,1,0:T(8,128)S(1)}) custom-call(f32[4,128,8,128]{3,2,1,0:T(8,128)S(1)} %copy-done), custom_call_target="tpu_custom_call" | custom-call | bytes 4194304 | tf_op jit(solution)/shard_map/panels/pallas_call | solution.py:146
  2.3 3.0 %collective-permute-start.2 = (f32[8,64,128]{2,1,0:T(8,128)S(1)}, f32[8,64,128]{2,1,0:T(8,128)S(1)}, u32[]{:S(2)}, u32[]{:S(2)}) collective-permute-start(f32[8,64,128]{2,1,0:T(8,128)S(1)} %get-tuple-element.40), channel_id=1, source_target_pairs={{0,8},{4,12},{8,0},{12,4},{16,24},{20,28},{24,16},{28,20},{1,9},{5... | collective-permute-start | bytes 786440 | tf_op jit(solution)/shard_map/ppermute | solution.py:298
  5.3 0.1 corner_block.1
  5.4 2.7 %collective-permute-start = (f32[128,128]{1,0:T(8,128)S(1)}, f32[128,128]{1,0:T(8,128)S(1)}, u32[]{:S(2)}, u32[]{:S(2)}) collective-permute-start(f32[128,128]{1,0:T(8,128)S(1)} %corner_block.1), channel_id=1, source_target_pairs={{0,2},{1,3},{2,0},{3,1},{4,6},{5,7},{6,4},{7,5},{8,10},{9,11},{10,... | collective-permute-start | bytes 196616 | tf_op jit(solution)/shard_map/ppermute | solution.py:298
  8.0 1.5 %collective-permute-start.3 = (f32[8,64,128]{2,1,0:T(8,128)S(1)}, f32[8,64,128]{2,1,0:T(8,128)S(1)}, u32[]{:S(2)}, u32[]{:S(2)}) collective-permute-start(f32[8,64,128]{2,1,0:T(8,128)S(1)} %get-tuple-element.41), channel_id=1, source_target_pairs={{0,16},{4,20},{8,24},{12,28},{16,0},{20,4},{24,8},{28,12},{1,17},{... | collective-permute-start | bytes 786440 | tf_op jit(solution)/shard_map/ppermute | solution.py:298
  9.5 1.4 %collective-permute-done = f32[128,128]{1,0:T(8,128)S(1)} collective-permute-done((f32[128,128]{1,0:T(8,128)S(1)}, f32[128,128]{1,0:T(8,128)S(1)}, u32[]{:S(2)}, u32[]{:S(2)}) %collective-permute-start) | collective-permute-done | bytes 65568 | tf_op jit(solution)/shard_map/ppermute | solution.py:298
  10.9 1.3 %collective-permute-start.1 = (f32[128,128]{1,0:T(8,128)S(1)}, f32[128,128]{1,0:T(8,128)S(1)}, u32[]{:S(2)}, u32[]{:S(2)}) collective-permute-start(f32[128,128]{1,0:T(8,128)S(1)} %get-tuple-element.68), channel_id=1, source_target_pairs={{0,1},{1,0},{2,3},{3,2},{4,5},{5,4},{6,7},{7,6},{8,9},{9,8},{10,11... | collective-permute-start | bytes 196616 | tf_op jit(solution)/shard_map/ppermute | solution.py:298
  12.2 0.0 collective-permute-done.2
  12.3 3.2 %collective-permute-done.3 = f32[8,64,128]{2,1,0:T(8,128)S(1)} collective-permute-done((f32[8,64,128]{2,1,0:T(8,128)S(1)}, f32[8,64,128]{2,1,0:T(8,128)S(1)}, u32[]{:S(2)}, u32[]{:S(2)}) %collective-permute-start.3) | collective-permute-done | bytes 262176 | tf_op jit(solution)/shard_map/ppermute | solution.py:298
  15.5 0.0 collective-permute-done.1
  15.6 0.6 %collective-permute-start.4 = (f32[2,128,128]{2,1,0:T(8,128)S(1)}, f32[2,128,128]{2,1,0:T(8,128)S(1)}, u32[]{:S(2)}, u32[]{:S(2)}) collective-permute-start(f32[2,128,128]{2,1,0:T(8,128)S(1)} %pad_maximum_fusion.first_ref), channel_id=1, source_target_pairs={{0,8},{4,12},{8,0},{12,4},{16,24},{20,28},{24,16},{28,20},{1,9},{5... | collective-permute-start | bytes 393224 | tf_op jit(solution)/shard_map/ppermute | solution.py:298
  16.2 2.1 %collective-permute-start.6 = (f32[3,128,128]{2,1,0:T(8,128)S(1)}, f32[3,128,128]{2,1,0:T(8,128)S(1)}, u32[]{:S(2)}, u32[]{:S(2)}) collective-permute-start(f32[3,128,128]{2,1,0:T(8,128)S(1)} %get-tuple-element.48), channel_id=1, source_target_pairs={{0,2},{1,3},{2,0},{3,1},{4,6},{5,7},{6,4},{7,5},{8,10},{9,11},{10,... | collective-permute-start | bytes 589832 | tf_op jit(solution)/shard_map/ppermute | solution.py:298
  18.3 2.3 %collective-permute-done.4 = f32[2,128,128]{2,1,0:T(8,128)S(1)} collective-permute-done((f32[2,128,128]{2,1,0:T(8,128)S(1)}, f32[2,128,128]{2,1,0:T(8,128)S(1)}, u32[]{:S(2)}, u32[]{:S(2)}) %collective-permute-start.4) | collective-permute-done | bytes 131104 | tf_op jit(solution)/shard_map/ppermute | solution.py:298
  20.6 1.6 %collective-permute-start.5 = (f32[2,128,128]{2,1,0:T(8,128)S(1)}, f32[2,128,128]{2,1,0:T(8,128)S(1)}, u32[]{:S(2)}, u32[]{:S(2)}) collective-permute-start(f32[2,128,128]{2,1,0:T(8,128)S(1)} %broadcast_select_fusion.6), channel_id=1, source_target_pairs={{0,16},{4,20},{8,24},{12,28},{16,0},{20,4},{24,8},{28,12},{1,17},{... | collective-permute-start | bytes 393224 | tf_op jit(solution)/shard_map/ppermute | solution.py:298
  22.2 4.0 %collective-permute-done.6 = f32[3,128,128]{2,1,0:T(8,128)S(1)} collective-permute-done((f32[3,128,128]{2,1,0:T(8,128)S(1)}, f32[3,128,128]{2,1,0:T(8,128)S(1)}, u32[]{:S(2)}, u32[]{:S(2)}) %collective-permute-start.6) | collective-permute-done | bytes 196640 | tf_op jit(solution)/shard_map/ppermute | solution.py:298
  26.2 0.0 collective-permute-done.5
  26.2 0.1 collective-permute-start.7
  26.3 1.6 %collective-permute-start.9 = (f32[8,64,128]{2,1,0:T(8,128)S(1)}, f32[8,64,128]{2,1,0:T(8,128)}, u32[]{:S(2)}, u32[]{:S(2)}) collective-permute-start(f32[8,64,128]{2,1,0:T(8,128)S(1)} %broadcast_select_fusion.4), channel_id=1, source_target_pairs={{0,16},{4,20},{8,24},{12,28},{16,0},{20,4},{24,8},{28,12},{1,17},{... | collective-permute-start | bytes 786440 | tf_op jit(solution)/shard_map/ppermute | solution.py:298
  27.9 1.5 %collective-permute-start.10 = (f32[8,64,128]{2,1,0:T(8,128)S(1)}, f32[8,64,128]{2,1,0:T(8,128)S(1)}, u32[]{:S(2)}, u32[]{:S(2)}) collective-permute-start(f32[8,64,128]{2,1,0:T(8,128)S(1)} %broadcast_select_fusion.3), channel_id=1, source_target_pairs={{0,8},{4,12},{8,0},{12,4},{16,24},{20,28},{24,16},{28,20},{1,9},{5... | collective-permute-start | bytes 786440 | tf_op jit(solution)/shard_map/ppermute | solution.py:298
  29.4 0.0 collective-permute-done.7
  29.4 0.0 copy-start.1
  29.4 4.8 %first_factor.1 = (f32[128,128]{1,0:T(8,128)S(1)}, f32[128,128]{1,0:T(8,128)S(1)}, f32[128,128]{1,0:T(8,128)S(1)}) custom-call(f32[128,128]{1,0:T(8,128)S(1)} %get-tuple-element.65.a_ref, f32[128,128]{1,0:T(8,128)S(1)} %get-tuple-element.64.side_ref), custom_call_target="tpu_custom_call" | custom-call | flops 8000000000 | bytes 2097152 | tf_op jit(solution)/shard_map/first_factor/pallas_call | solution.py:169
  34.2 0.1 collective-permute-start.8
  34.3 0.8 %collective-permute-done.9 = f32[8,64,128]{2,1,0:T(8,128)} collective-permute-done((f32[8,64,128]{2,1,0:T(8,128)S(1)}, f32[8,64,128]{2,1,0:T(8,128)}, u32[]{:S(2)}, u32[]{:S(2)}) %collective-permute-start.9) | collective-permute-done | bytes 262176 | tf_op jit(solution)/shard_map/ppermute | solution.py:298
  35.2 0.1 collective-permute-start.11
  35.3 1.0 %collective-permute-done.10 = f32[8,64,128]{2,1,0:T(8,128)S(1)} collective-permute-done((f32[8,64,128]{2,1,0:T(8,128)S(1)}, f32[8,64,128]{2,1,0:T(8,128)S(1)}, u32[]{:S(2)}, u32[]{:S(2)}) %collective-permute-start.10) | collective-permute-done | bytes 262176 | tf_op jit(solution)/shard_map/ppermute | solution.py:298
  36.3 0.1 collective-permute-start.12
  36.4 0.0 copy-done.1
  36.4 6.7 %second_factor.1 = (f32[128,128]{1,0:T(8,128)S(1)}, f32[256,256]{1,0:T(8,128)S(1)}, f32[256,256]{1,0:T(8,128)S(1)}, f32[8,4,128,128]{3,2,1,0:T(8,128)S(1)}) custom-call(f32[128,128]{1,0:T(8,128)S(1)} %get-tuple-element.63.a_ref, f32[128,128]{1,0:T(8,128)S(1)} %get-tuple-element.51.cross_ref, f32[128,128]{1,0:T(8,128)S(1)} %get-tuple-element.54.w0_ref, ...), custom_call_target="tpu_custom_call" | custom-call | flops 8000000000 | bytes 4194304 | tf_op jit(solution)/shard_map/second_factor/pallas_call | solution.py:212
  43.1 0.0 collective-permute-done.8.rows_other_ref
  43.1 0.0 collective-permute-done.11.oa_ref
  43.1 0.0 collective-permute-done.12.ob_ref
  43.1 6.9 %settle.1 = f32[4,128,8,128]{3,2,1,0:T(8,128)} custom-call(f32[128,128]{1,0:T(8,128)S(1)} %get-tuple-element.50.f0_ref, f32[128,128]{1,0:T(8,128)S(1)} %get-tuple-element.55.f1_ref, f32[256,256]{1,0:T(8,128)S(1)} %get-tuple-element.56.w_ref, f32[256,256]{1,0:T(8,128)S(1)} %get-tuple-element.57.mixed_ref, f32[2,128,128]{2,1,0:T(8,128)S(1)} %pad_maximum_fusion.first_ref, ...), custom_call_target="tpu_custom_call" | custom-call | flops 4000000000 | bytes 6291456 | tf_op jit(solution)/shard_map/settle/pallas_call | solution.py:285
  (12 shorter events, 0.2 us)
Async XLA Ops:
  0.0 1.6 %copy-start = (f32[4,128,8,128]{3,2,1,0:T(8,128)S(1)}, f32[4,128,8,128]{3,2,1,0:T(8,128)}, u32[]{:S(2)}) copy-start(f32[4,128,8,128]{3,2,1,0:T(8,128)} %matrix_ref.5) | copy-start | bytes 6291460
  2.3 10.0 %collective-permute-start.2 = (f32[8,64,128]{2,1,0:T(8,128)S(1)}, f32[8,64,128]{2,1,0:T(8,128)S(1)}, u32[]{:S(2)}, u32[]{:S(2)}) collective-permute-start(f32[8,64,128]{2,1,0:T(8,128)S(1)} %get-tuple-element.40), channel_id=1, source_target_pairs={{0,8},{4,12},{8,0},{12,4},{16,24},{20,28},{24,16},{28,20},{1,9},{5... | collective-permute-start | bytes 786440 | tf_op jit(solution)/shard_map/ppermute | solution.py:298
  5.4 5.5 %collective-permute-start = (f32[128,128]{1,0:T(8,128)S(1)}, f32[128,128]{1,0:T(8,128)S(1)}, u32[]{:S(2)}, u32[]{:S(2)}) collective-permute-start(f32[128,128]{1,0:T(8,128)S(1)} %corner_block.1), channel_id=1, source_target_pairs={{0,2},{1,3},{2,0},{3,1},{4,6},{5,7},{6,4},{7,5},{8,10},{9,11},{10,... | collective-permute-start | bytes 196616 | tf_op jit(solution)/shard_map/ppermute | solution.py:298
  8.0 7.5 %collective-permute-start.3 = (f32[8,64,128]{2,1,0:T(8,128)S(1)}, f32[8,64,128]{2,1,0:T(8,128)S(1)}, u32[]{:S(2)}, u32[]{:S(2)}) collective-permute-start(f32[8,64,128]{2,1,0:T(8,128)S(1)} %get-tuple-element.41), channel_id=1, source_target_pairs={{0,16},{4,20},{8,24},{12,28},{16,0},{20,4},{24,8},{28,12},{1,17},{... | collective-permute-start | bytes 786440 | tf_op jit(solution)/shard_map/ppermute | solution.py:298
  10.9 4.6 %collective-permute-start.1 = (f32[128,128]{1,0:T(8,128)S(1)}, f32[128,128]{1,0:T(8,128)S(1)}, u32[]{:S(2)}, u32[]{:S(2)}) collective-permute-start(f32[128,128]{1,0:T(8,128)S(1)} %get-tuple-element.68), channel_id=1, source_target_pairs={{0,1},{1,0},{2,3},{3,2},{4,5},{5,4},{6,7},{7,6},{8,9},{9,8},{10,11... | collective-permute-start | bytes 196616 | tf_op jit(solution)/shard_map/ppermute | solution.py:298
  15.6 5.0 %collective-permute-start.4 = (f32[2,128,128]{2,1,0:T(8,128)S(1)}, f32[2,128,128]{2,1,0:T(8,128)S(1)}, u32[]{:S(2)}, u32[]{:S(2)}) collective-permute-start(f32[2,128,128]{2,1,0:T(8,128)S(1)} %pad_maximum_fusion.first_ref), channel_id=1, source_target_pairs={{0,8},{4,12},{8,0},{12,4},{16,24},{20,28},{24,16},{28,20},{1,9},{5... | collective-permute-start | bytes 393224 | tf_op jit(solution)/shard_map/ppermute | solution.py:298
  16.2 10.0 %collective-permute-start.6 = (f32[3,128,128]{2,1,0:T(8,128)S(1)}, f32[3,128,128]{2,1,0:T(8,128)S(1)}, u32[]{:S(2)}, u32[]{:S(2)}) collective-permute-start(f32[3,128,128]{2,1,0:T(8,128)S(1)} %get-tuple-element.48), channel_id=1, source_target_pairs={{0,2},{1,3},{2,0},{3,1},{4,6},{5,7},{6,4},{7,5},{8,10},{9,11},{10,... | collective-permute-start | bytes 589832 | tf_op jit(solution)/shard_map/ppermute | solution.py:298
  20.6 5.6 %collective-permute-start.5 = (f32[2,128,128]{2,1,0:T(8,128)S(1)}, f32[2,128,128]{2,1,0:T(8,128)S(1)}, u32[]{:S(2)}, u32[]{:S(2)}) collective-permute-start(f32[2,128,128]{2,1,0:T(8,128)S(1)} %broadcast_select_fusion.6), channel_id=1, source_target_pairs={{0,16},{4,20},{8,24},{12,28},{16,0},{20,4},{24,8},{28,12},{1,17},{... | collective-permute-start | bytes 393224 | tf_op jit(solution)/shard_map/ppermute | solution.py:298
  26.2 3.2 %collective-permute-start.7 = (f32[2,128,128]{2,1,0:T(8,128)S(1)}, f32[2,128,128]{2,1,0:T(8,128)S(1)}, u32[]{:S(2)}, u32[]{:S(2)}) collective-permute-start(f32[2,128,128]{2,1,0:T(8,128)S(1)} %broadcast_select_fusion.7), channel_id=1, source_target_pairs={{0,4},{4,0},{8,12},{12,8},{16,20},{20,16},{24,28},{28,24},{1,5},{5... | collective-permute-start | bytes 393224 | tf_op jit(solution)/shard_map/ppermute | solution.py:298
  26.3 8.8 %collective-permute-start.9 = (f32[8,64,128]{2,1,0:T(8,128)S(1)}, f32[8,64,128]{2,1,0:T(8,128)}, u32[]{:S(2)}, u32[]{:S(2)}) collective-permute-start(f32[8,64,128]{2,1,0:T(8,128)S(1)} %broadcast_select_fusion.4), channel_id=1, source_target_pairs={{0,16},{4,20},{8,24},{12,28},{16,0},{20,4},{24,8},{28,12},{1,17},{... | collective-permute-start | bytes 786440 | tf_op jit(solution)/shard_map/ppermute | solution.py:298
  27.9 8.4 %collective-permute-start.10 = (f32[8,64,128]{2,1,0:T(8,128)S(1)}, f32[8,64,128]{2,1,0:T(8,128)S(1)}, u32[]{:S(2)}, u32[]{:S(2)}) collective-permute-start(f32[8,64,128]{2,1,0:T(8,128)S(1)} %broadcast_select_fusion.3), channel_id=1, source_target_pairs={{0,8},{4,12},{8,0},{12,4},{16,24},{20,28},{24,16},{28,20},{1,9},{5... | collective-permute-start | bytes 786440 | tf_op jit(solution)/shard_map/ppermute | solution.py:298
  29.4 7.0 %copy-start.1 = (f32[4,128,8,128]{3,2,1,0:T(8,128)S(1)}, f32[4,128,8,128]{3,2,1,0:T(8,128)}, u32[]{:S(2)}) copy-start(f32[4,128,8,128]{3,2,1,0:T(8,128)} %matrix_ref.5) | copy-start | bytes 6291460
  34.2 8.9 %collective-permute-start.8 = (f32[3,128,128]{2,1,0:T(8,128)S(1)}, f32[3,128,128]{2,1,0:T(8,128)S(1)}, u32[]{:S(2)}, u32[]{:S(2)}) collective-permute-start(f32[3,128,128]{2,1,0:T(8,128)S(1)} %broadcast_select_fusion.5.rows_ref), channel_id=1, source_target_pairs={{0,1},{1,0},{2,3},{3,2},{4,5},{5,4},{6,7},{7,6},{8,9},{9,8},{10,11... | collective-permute-start | bytes 589832 | tf_op jit(solution)/shard_map/ppermute | solution.py:298
  35.2 7.9 %collective-permute-start.11 = (f32[8,64,128]{2,1,0:T(8,128)S(1)}, f32[8,64,128]{2,1,0:T(8,128)S(1)}, u32[]{:S(2)}, u32[]{:S(2)}) collective-permute-start(f32[8,64,128]{2,1,0:T(8,128)S(1)} %broadcast_select_fusion.2.ha_ref), channel_id=1, source_target_pairs={{0,4},{4,0},{8,12},{12,8},{16,20},{20,16},{24,28},{28,24},{1,5},{5... | collective-permute-start | bytes 786440 | tf_op jit(solution)/shard_map/ppermute | solution.py:298
  36.3 6.8 %collective-permute-start.12 = (f32[8,64,128]{2,1,0:T(8,128)S(1)}, f32[8,64,128]{2,1,0:T(8,128)S(1)}, u32[]{:S(2)}, u32[]{:S(2)}) collective-permute-start(f32[8,64,128]{2,1,0:T(8,128)S(1)} %broadcast_select_fusion.1.hb_ref), channel_id=1, source_target_pairs={{0,4},{4,0},{8,12},{12,8},{16,20},{20,16},{24,28},{28,24},{1,5},{5... | collective-permute-start | bytes 786440 | tf_op jit(solution)/shard_map/ppermute | solution.py:298

commit v16 on v15

--- a/solution.py
+++ b/solution.py
@@ -1,3 +1,5 @@
+import functools
+
 import jax
 import jax.numpy as jnp
 from jax import lax
@@ -5,7 +7,6 @@
 from jax.experimental.pallas import tpu as pltpu
 from jax.sharding import PartitionSpec as P
 
-EXACT = lax.Precision.HIGHEST
 SUB = 8
 PANEL = 4
 MIB = 1024 * 1024
@@ -13,12 +14,18 @@
 HBM = pl.BlockSpec(memory_space=pltpu.HBM)
 
 
-def dot(a, b):
-    return lax.dot_general(a, b, (((1,), (0,)), ((), ())), precision=EXACT, preferred_element_type=jnp.float32)
-
-
-def dot_t(a, b):
-    return lax.dot_general(a, b, (((1,), (1,)), ((), ())), precision=EXACT, preferred_element_type=jnp.float32)
+def parts(x):
+    high = x.astype(jnp.bfloat16)
+    rest = x - high.astype(jnp.float32)
+    middle = rest.astype(jnp.bfloat16)
+    return high, middle, (rest - middle.astype(jnp.float32)).astype(jnp.bfloat16)
+
+
+def dot_over_rows(a, b):
+    a, b = parts(a), parts(b)
+    lhs = jnp.concatenate([a[2], a[0], a[1], a[1], a[0], a[0]], axis=0)
+    rhs = jnp.concatenate([b[0], b[2], b[1], b[0], b[1], b[0]], axis=0)
+    return lax.dot_general(lhs, rhs, (((0,), (0,)), ((), ())), preferred_element_type=jnp.float32)
 
 
 def full(row):
@@ -74,9 +81,7 @@
                 scratch[m][g + 1:until] = low
         elif until < groups:
             done = [ref[until - PANEL:until].reshape(PANEL * SUB, n) for ref in scratch]
-            update = lax.dot_general(
-                done[0], jnp.concatenate(done, axis=1), (((0,), (0,)), ((), ())), precision=EXACT,
-                preferred_element_type=jnp.float32)
+            update = dot_over_rows(done[0], jnp.concatenate(done, axis=1))
             for m in sides:
                 part = update[until * SUB:, m * n:(m + 1) * n]
                 scratch[m][until:] = scratch[m][until:] - part.reshape(groups - until, SUB, n)
@@ -86,13 +91,6 @@
 
 def is_odd_row():
     return lax.rem(lax.axis_index("row"), 2) == 1
-
-
-def parts(x):
-    high = x.astype(jnp.bfloat16)
-    rest = x - high.astype(jnp.float32)
-    middle = rest.astype(jnp.bfloat16)
-    return high, middle, (rest - middle.astype(jnp.float32)).astype(jnp.bfloat16)
 
 
 def dot_parts(a, b, dims=((1,), (0,))):
@@ -155,6 +153,48 @@
     )(matrix)
 
 
+def pick_kernel(bit, new_ref, old_ref, out_ref):
+    out_ref[...] = jnp.where(bit_set(lax.axis_index("col"), bit), new_ref[...], old_ref[...])
+
+
+def pick(new, old, bit):
+    return pl.pallas_call(
+        functools.partial(pick_kernel, bit),
+        out_shape=jax.ShapeDtypeStruct(old.shape, old.dtype),
+        in_specs=[VMEM] * 2,
+        out_specs=VMEM,
+        compiler_params=pltpu.CompilerParams(vmem_limit_bytes=2 * MIB),
+        cost_estimate=estimate(8 * 10**9, 2 * MIB),
+        name="pick",
+    )(new, old)
+
+
+def pack_kernel(across_ref, block_ref, both_ref, message_ref):
+    n = block_ref.shape[0]
+    odd = is_odd_row()
+    right = bit_set(lax.axis_index("col"), 0)
+    across, block = across_ref[...], block_ref[...]
+    left_block = jnp.where(right, across, block)
+    right_block = jnp.where(right, block, across)
+    both_ref[0] = left_block
+    both_ref[1] = right_block
+    message_ref[:n] = jnp.where(odd, right_block, left_block)
+    message_ref[n:] = jnp.where(odd, left_block.T[n // 2:], right_block[:n // 2])
+
+
+def pack(across, block):
+    n = block.shape[0]
+    return pl.pallas_call(
+        pack_kernel,
+        out_shape=[jax.ShapeDtypeStruct((2, n, n), jnp.float32), jax.ShapeDtypeStruct((n + n // 2, n), jnp.float32)],
+        in_specs=[VMEM] * 2,
+        out_specs=[VMEM] * 2,
+        compiler_params=pltpu.CompilerParams(vmem_limit_bytes=2 * MIB),
+        cost_estimate=estimate(1000, 1000),
+        name="pack",
+    )(across, block)
+
+
 def first_factor_kernel(a_ref, side_ref, f_ref, w_ref, cross_ref, *scratch):
     f_ref[...], w_ref[...], cross_ref[...] = eliminate(a_ref[...], side_ref[...], scratch)
 
@@ -188,7 +228,7 @@
     odd = is_odd_row()
     w0 = w0_ref[...]
     cross = cross_ref[...]
-    both = dot(cross.T, jnp.concatenate([cross, w0], axis=1))
+    both = dot_over_rows(cross, jnp.concatenate([cross, w0], axis=1))
     f1, w1, w10 = eliminate(a_ref[...] - both[:, :n], -both[:, n:], scratch[:-1])
     f_ref[...] = f1
     zero = jnp.zeros((n, n), jnp.float32)
@@ -309,16 +349,6 @@
     return held
 
 
-def region(run, *values):
-    shapes = jax.eval_shape(run, *values)
-
-    def skip(*_):
-        return jax.tree.map(lambda leaf: jnp.zeros(leaf.shape, leaf.dtype), shapes)
-
-    everywhere = lax.axis_index("row") < lax.axis_size("row")
-    return lax.cond(everywhere, run, skip, *values)
-
-
 def after(value, *others):
     return lax.optimization_barrier((value,) + others)
 
@@ -331,7 +361,6 @@
     row_bits = list(range(1, n_row.bit_length() - 1))
     col_bits = list(range(1, n_col.bit_length() - 1))
     odd = (grid_row % 2) == 1
-    right = (grid_col % 2) == 1
 
     block = corner_block(kernel)
     column, upper, lower = panels(kernel)
@@ -341,32 +370,30 @@
     upper_moved = exchange(upper, "row", 1 << first_bit, n_row)
     lower_moved = exchange(lower, "row", 1 << last_bit, n_row)
 
-    def along_col(new, old):
-        block = jnp.where(bit_set(grid_col, col_bits[0]), new, old)
-        return spread(block, "col", grid_col, n_col, col_bits[1:])
-
-    block = region(along_col, moved, block)
+    block = pick(moved, block, col_bits[0])
+    block = spread(block, "col", grid_col, n_col, col_bits[1:])
     across = exchange(block, "col", 1, n_col)
     ha = jnp.where(bit_set(grid_row, first_bit), upper_moved, upper)
     hb = jnp.where(bit_set(grid_row, last_bit), lower_moved, lower)
     across, block, ha, hb, column = after(across, block, ha, hb, column)
 
-    pair = jnp.stack([jnp.where(right, across, block), jnp.where(right, block, across)])
-    first_rows = pair
+    first_rows, pair = pack(across, block)
     moved = exchange(pair, "row", 1 << first_bit, n_row)
     column_moved = exchange(column, "col", 1 << col_bits[0], n_col)
     pair = jnp.where(bit_set(grid_row, first_bit), moved, pair)
-    pair = spread(pair, "row", grid_row, n_row, row_bits[1:])
-    pair, ha, hb = after(pair, ha, hb)
+    moved = exchange(pair, "row", 1 << row_bits[1], n_row)
+    rows = jnp.where(bit_set(grid_col, col_bits[0]), column_moved, column)
+    moved, pair, rows, ha, hb = after(moved, pair, rows, ha, hb)
+    pair = jnp.where(bit_set(grid_row, row_bits[1]), moved, pair)
+    pair = spread(pair, "row", grid_row, n_row, row_bits[2:])
     ha_moved = exchange(ha, "row", 1 << row_bits[1], n_row)
     hb_moved = exchange(hb, "row", 1 << row_bits[-2], n_row)
-    rows = jnp.where(bit_set(grid_col, col_bits[0]), column_moved, column)
-    pair, rows = after(pair, rows)
     other = exchange(pair, "row", 1, n_row)
 
-    a00 = jnp.where(odd, other[0], pair[0])
-    a01 = jnp.where(odd, other[1], pair[1])
-    a11 = jnp.where(odd, pair[1], other[1])
+    n = block.shape[0]
+    a00 = jnp.where(odd, other[:n], pair[:n])
+    a11 = jnp.where(odd, pair[:n], other[:n])
+    a01 = jnp.concatenate([jnp.where(odd, other[n:], pair[n:]), jnp.where(odd, pair[n:], other[n:])], axis=0)
     f0, w0, cross = first_factor(a00, a01)
 
     w0, rows, row_then, col_then = after(w0, rows, grid_row, grid_col)

time: 50.2 us -> 51.9 us (1.034)
  starting transfers between devices: 16.3 us -> 17.8 us
  Pallas kernels: 19.1 us -> 18 us
  waiting for transfers between devices: 12.7 us -> 13.8 us
    ppermute x13, starting transfers between devices: 16.3 us -> 17.8 us  [exchange(): return lax.ppermute(value, axis, [(i, i ^ mask) for i in range(size)])]
    ppermute x13, waiting for transfers between devices: 12.7 us -> 13.8 us  [exchange(): return lax.ppermute(value, axis, [(i, i ^ mask) for i in range(size)])]
    pallas_call x1, Pallas kernels: 6.69 us -> 6.03 us  [second_factor(): pl.pallas_call(second_factor_kernel, out_shape=[square, double, double, b...]
  transfers between devices with their start and end apart: 13 -> 13, of which waited for: 6 -> 6; matrix products, arithmetic and copies ran while one was open for 0% -> 0% of each run, Pallas kernels for 23% -> 21%
where the time goes in v16:
time: 51.9 us; the launch traced here: 51.6 us
  Pallas kernels  18 us (35%)
  starting transfers between devices  17.8 us (34%)
  waiting for transfers between devices  13.8 us (27%)
  local copies, waits for them, and re-layouts  1.59 us (3%)
    ppermute x13, starting transfers between devices, exchange(): return lax.ppermute(value, axis, [(i, i ^ mask) for i in range(size)])  17.8 us
    ppermute x13, waiting for transfers between devices, exchange(): return lax.ppermute(value, axis, [(i, i ^ mask) for i in range(size)])  13.8 us
    pallas_call x1, Pallas kernels, settle(): pl.pallas_call(settle_kernel, out_shape=jax.ShapeDtypeStruct((local_rows,...  6.9 us
    pallas_call x1, Pallas kernels, second_factor(): pl.pallas_call(second_factor_kernel, out_shape=[square, double, double, b...  6.03 us
    pallas_call x1, Pallas kernels, first_factor(): pl.pallas_call(first_factor_kernel, out_shape=[square] * 3, in_specs=[VME...  4.26 us
    unnamed x4, local copies, waits for them, and re-layouts  1.59 us
  transfers between devices with their start and end apart: 13, of which 6 were waited for; matrix products, arithmetic and copies ran while one was open for 0% of the time, Pallas kernels for 21%

profile of v16, /device:TPU:0, one launch (start us, length us, event | category | flops | bytes accessed | tf_op | source)
XLA Modules:
  0.0 51.6 jit_solution(10050950425570052321)
XLA Ops:
  0.0 0.0 copy-start
  0.0 1.6 %copy-done = f32[4,128,8,128]{3,2,1,0:T(8,128)S(1)} copy-done((f32[4,128,8,128]{3,2,1,0:T(8,128)S(1)}, f32[4,128,8,128]{3,2,1,0:T(8,128)}, u32[]{:S(2)}) %copy-start) | copy-done | bytes 2097176
  1.6 0.0 copy-start.1
  1.6 0.1 corner_block.1.old_ref
  1.7 4.1 %collective-permute-start = (f32[128,128]{1,0:T(8,128)S(1)}, f32[128,128]{1,0:T(8,128)S(1)}, u32[]{:S(2)}, u32[]{:S(2)}) collective-permute-start(f32[128,128]{1,0:T(8,128)S(1)} %corner_block.1.old_ref), channel_id=1, source_target_pairs={{0,2},{1,3},{2,0},{3,1},{4,6},{5,7},{6,4},{7,5},{8,10},{9,11},{10,... | collective-permute-start | bytes 196616 | tf_op jit(solution)/shard_map/ppermute | solution.py:338
  5.8 0.0 copy-done.1
  5.8 0.7 %panels.1 = (f32[3,128,128]{2,1,0:T(8,128)S(1)}, f32[8,64,128]{2,1,0:T(8,128)S(1)}, f32[8,64,128]{2,1,0:T(8,128)S(1)}) custom-call(f32[4,128,8,128]{3,2,1,0:T(8,128)S(1)} %copy-done.1), custom_call_target="tpu_custom_call" | custom-call | bytes 4194304 | tf_op jit(solution)/shard_map/panels/pallas_call | solution.py:144
  6.5 1.6 %collective-permute-start.2 = (f32[8,64,128]{2,1,0:T(8,128)S(1)}, f32[8,64,128]{2,1,0:T(8,128)}, u32[]{:S(2)}, u32[]{:S(2)}) collective-permute-start(f32[8,64,128]{2,1,0:T(8,128)S(1)} %get-tuple-element.30), channel_id=1, source_target_pairs={{0,8},{4,12},{8,0},{12,4},{16,24},{20,28},{24,16},{28,20},{1,9},{5... | collective-permute-start | bytes 786440 | tf_op jit(solution)/shard_map/ppermute | solution.py:338
  8.0 1.5 %collective-permute-start.3 = (f32[8,64,128]{2,1,0:T(8,128)S(1)}, f32[8,64,128]{2,1,0:T(8,128)}, u32[]{:S(2)}, u32[]{:S(2)}) collective-permute-start(f32[8,64,128]{2,1,0:T(8,128)S(1)} %get-tuple-element.31), channel_id=1, source_target_pairs={{0,16},{4,20},{8,24},{12,28},{16,0},{20,4},{24,8},{28,12},{1,17},{... | collective-permute-start | bytes 786440 | tf_op jit(solution)/shard_map/ppermute | solution.py:338
  9.5 0.0 collective-permute-done.new_ref
  9.6 1.6 %collective-permute-start.1 = (f32[128,128]{1,0:T(8,128)S(1)}, f32[128,128]{1,0:T(8,128)S(1)}, u32[]{:S(2)}, u32[]{:S(2)}) collective-permute-start(f32[128,128]{1,0:T(8,128)S(1)} %pick.1.block_ref), channel_id=1, source_target_pairs={{0,1},{1,0},{2,3},{3,2},{4,5},{5,4},{6,7},{7,6},{8,9},{9,8},{10,11... | collective-permute-start | bytes 196616 | tf_op jit(solution)/shard_map/ppermute | solution.py:338
  11.2 3.2 %collective-permute-done.2 = f32[8,64,128]{2,1,0:T(8,128)} collective-permute-done((f32[8,64,128]{2,1,0:T(8,128)S(1)}, f32[8,64,128]{2,1,0:T(8,128)}, u32[]{:S(2)}, u32[]{:S(2)}) %collective-permute-start.2) | collective-permute-done | bytes 262176 | tf_op jit(solution)/shard_map/ppermute | solution.py:338
  14.4 1.2 %collective-permute-done.3 = f32[8,64,128]{2,1,0:T(8,128)} collective-permute-done((f32[8,64,128]{2,1,0:T(8,128)S(1)}, f32[8,64,128]{2,1,0:T(8,128)}, u32[]{:S(2)}, u32[]{:S(2)}) %collective-permute-start.3) | collective-permute-done | bytes 262176 | tf_op jit(solution)/shard_map/ppermute | solution.py:338
  15.6 0.0 collective-permute-done.1.across_ref
  15.7 0.1 pack.1
  15.8 1.4 %collective-permute-start.4 = (f32[192,128]{1,0:T(8,128)S(1)}, f32[192,128]{1,0:T(8,128)S(1)}, u32[]{:S(2)}, u32[]{:S(2)}) collective-permute-start(f32[192,128]{1,0:T(8,128)S(1)} %get-tuple-element.35), channel_id=1, source_target_pairs={{0,8},{4,12},{8,0},{12,4},{16,24},{20,28},{24,16},{28,20},{1,9},{5... | collective-permute-start | bytes 294920 | tf_op jit(solution)/shard_map/ppermute | solution.py:338
  17.1 1.7 %collective-permute-start.6 = (f32[3,128,128]{2,1,0:T(8,128)S(1)}, f32[3,128,128]{2,1,0:T(8,128)S(1)}, u32[]{:S(2)}, u32[]{:S(2)}) collective-permute-start(f32[3,128,128]{2,1,0:T(8,128)S(1)} %get-tuple-element.36), channel_id=1, source_target_pairs={{0,2},{1,3},{2,0},{3,1},{4,6},{5,7},{6,4},{7,5},{8,10},{9,11},{10,... | collective-permute-start | bytes 589832 | tf_op jit(solution)/shard_map/ppermute | solution.py:338
  18.9 1.6 %collective-permute-done.4 = f32[192,128]{1,0:T(8,128)S(1)} collective-permute-done((f32[192,128]{1,0:T(8,128)S(1)}, f32[192,128]{1,0:T(8,128)S(1)}, u32[]{:S(2)}, u32[]{:S(2)}) %collective-permute-start.4) | collective-permute-done | bytes 98336 | tf_op jit(solution)/shard_map/ppermute | solution.py:338
  20.5 2.5 %collective-permute-start.5 = (f32[192,128]{1,0:T(8,128)S(1)}, f32[192,128]{1,0:T(8,128)S(1)}, u32[]{:S(2)}, u32[]{:S(2)}) collective-permute-start(f32[192,128]{1,0:T(8,128)S(1)} %broadcast_select_fusion.5), channel_id=1, source_target_pairs={{0,16},{4,20},{8,24},{12,28},{16,0},{20,4},{24,8},{28,12},{1,17},{... | collective-permute-start | bytes 294920 | tf_op jit(solution)/shard_map/ppermute | solution.py:338
  23.0 4.4 %collective-permute-done.6 = f32[3,128,128]{2,1,0:T(8,128)S(1)} collective-permute-done((f32[3,128,128]{2,1,0:T(8,128)S(1)}, f32[3,128,128]{2,1,0:T(8,128)S(1)}, u32[]{:S(2)}, u32[]{:S(2)}) %collective-permute-start.6) | collective-permute-done | bytes 196640 | tf_op jit(solution)/shard_map/ppermute | solution.py:338
  27.4 0.0 collective-permute-done.5
  27.5 0.1 collective-permute-start.7
  27.6 2.5 %collective-permute-start.9 = (f32[8,64,128]{2,1,0:T(8,128)S(1)}, f32[8,64,128]{2,1,0:T(8,128)}, u32[]{:S(2)}, u32[]{:S(2)}) collective-permute-start(f32[8,64,128]{2,1,0:T(8,128)S(1)} %broadcast_select_fusion.3), channel_id=1, source_target_pairs={{0,16},{4,20},{8,24},{12,28},{16,0},{20,4},{24,8},{28,12},{1,17},{... | collective-permute-start | bytes 786440 | tf_op jit(solution)/shard_map/ppermute | solution.py:338
  30.1 0.4 collective-permute-start.10
  30.5 0.0 collective-permute-done.7
  30.6 4.3 %first_factor.1 = (f32[128,128]{1,0:T(8,128)S(1)}, f32[128,128]{1,0:T(8,128)S(1)}, f32[128,128]{1,0:T(8,128)S(1)}) custom-call(f32[128,128]{1,0:T(8,128)S(1)} %get-tuple-element.56.a_ref, f32[128,128]{1,0:T(8,128)S(1)} %get-tuple-element.59.side_ref), custom_call_target="tpu_custom_call" | custom-call | flops 8000000000 | bytes 2097152 | tf_op jit(solution)/shard_map/first_factor/pallas_call | solution.py:209
  34.8 0.2 collective-permute-start.8
  35.0 2.1 %collective-permute-done.9 = f32[8,64,128]{2,1,0:T(8,128)} collective-permute-done((f32[8,64,128]{2,1,0:T(8,128)S(1)}, f32[8,64,128]{2,1,0:T(8,128)}, u32[]{:S(2)}, u32[]{:S(2)}) %collective-permute-start.9) | collective-permute-done | bytes 262176 | tf_op jit(solution)/shard_map/ppermute | solution.py:338
  37.1 0.1 collective-permute-start.11
  37.2 1.4 %collective-permute-done.10 = f32[8,64,128]{2,1,0:T(8,128)} collective-permute-done((f32[8,64,128]{2,1,0:T(8,128)S(1)}, f32[8,64,128]{2,1,0:T(8,128)}, u32[]{:S(2)}, u32[]{:S(2)}) %collective-permute-start.10) | collective-permute-done | bytes 262176 | tf_op jit(solution)/shard_map/ppermute | solution.py:338
  38.6 0.1 collective-permute-start.12
  38.7 6.0 %second_factor.1 = (f32[128,128]{1,0:T(8,128)S(1)}, f32[256,256]{1,0:T(8,128)S(1)}, f32[256,256]{1,0:T(8,128)S(1)}, f32[8,4,128,128]{3,2,1,0:T(8,128)S(1)}) custom-call(f32[128,128]{1,0:T(8,128)S(1)} %get-tuple-element.55.a_ref, f32[128,128]{1,0:T(8,128)S(1)} %get-tuple-element.42.cross_ref, f32[128,128]{1,0:T(8,128)S(1)} %get-tuple-element.45.w0_ref, ...), custom_call_target="tpu_custom_call" | custom-call | flops 8000000000 | bytes 4194304 | tf_op jit(solution)/shard_map/second_factor/pallas_call | solution.py:252
  44.7 0.0 collective-permute-done.8.rows_other_ref
  44.7 0.0 collective-permute-done.11.oa_ref
  44.7 0.0 collective-permute-done.12.ob_ref
  44.7 6.9 %settle.1 = f32[4,128,8,128]{3,2,1,0:T(8,128)} custom-call(f32[128,128]{1,0:T(8,128)S(1)} %get-tuple-element.41.f0_ref, f32[128,128]{1,0:T(8,128)S(1)} %get-tuple-element.46.f1_ref, f32[256,256]{1,0:T(8,128)S(1)} %get-tuple-element.47.w_ref, f32[256,256]{1,0:T(8,128)S(1)} %get-tuple-element.48.mixed_ref, f32[2,128,128]{2,1,0:T(8,128)S(1)} %get-tuple-element.49.first_ref, ...), custom_call_target="tpu_custom_call" | custom-call | flops 4000000000 | bytes 6291456 | tf_op jit(solution)/shard_map/settle/pallas_call | solution.py:325
  (10 shorter events, 0.2 us)
Async XLA Ops:
  0.0 1.6 %copy-start = (f32[4,128,8,128]{3,2,1,0:T(8,128)S(1)}, f32[4,128,8,128]{3,2,1,0:T(8,128)}, u32[]{:S(2)}) copy-start(f32[4,128,8,128]{3,2,1,0:T(8,128)} %matrix_ref.5) | copy-start | bytes 6291460
  1.6 4.2 %copy-start.1 = (f32[4,128,8,128]{3,2,1,0:T(8,128)S(1)}, f32[4,128,8,128]{3,2,1,0:T(8,128)}, u32[]{:S(2)}) copy-start(f32[4,128,8,128]{3,2,1,0:T(8,128)} %matrix_ref.5) | copy-start | bytes 6291460
  1.7 7.9 %collective-permute-start = (f32[128,128]{1,0:T(8,128)S(1)}, f32[128,128]{1,0:T(8,128)S(1)}, u32[]{:S(2)}, u32[]{:S(2)}) collective-permute-start(f32[128,128]{1,0:T(8,128)S(1)} %corner_block.1.old_ref), channel_id=1, source_target_pairs={{0,2},{1,3},{2,0},{3,1},{4,6},{5,7},{6,4},{7,5},{8,10},{9,11},{10,... | collective-permute-start | bytes 196616 | tf_op jit(solution)/shard_map/ppermute | solution.py:338
  6.5 7.9 %collective-permute-start.2 = (f32[8,64,128]{2,1,0:T(8,128)S(1)}, f32[8,64,128]{2,1,0:T(8,128)}, u32[]{:S(2)}, u32[]{:S(2)}) collective-permute-start(f32[8,64,128]{2,1,0:T(8,128)S(1)} %get-tuple-element.30), channel_id=1, source_target_pairs={{0,8},{4,12},{8,0},{12,4},{16,24},{20,28},{24,16},{28,20},{1,9},{5... | collective-permute-start | bytes 786440 | tf_op jit(solution)/shard_map/ppermute | solution.py:338
  8.0 7.6 %collective-permute-start.3 = (f32[8,64,128]{2,1,0:T(8,128)S(1)}, f32[8,64,128]{2,1,0:T(8,128)}, u32[]{:S(2)}, u32[]{:S(2)}) collective-permute-start(f32[8,64,128]{2,1,0:T(8,128)S(1)} %get-tuple-element.31), channel_id=1, source_target_pairs={{0,16},{4,20},{8,24},{12,28},{16,0},{20,4},{24,8},{28,12},{1,17},{... | collective-permute-start | bytes 786440 | tf_op jit(solution)/shard_map/ppermute | solution.py:338
  9.6 6.1 %collective-permute-start.1 = (f32[128,128]{1,0:T(8,128)S(1)}, f32[128,128]{1,0:T(8,128)S(1)}, u32[]{:S(2)}, u32[]{:S(2)}) collective-permute-start(f32[128,128]{1,0:T(8,128)S(1)} %pick.1.block_ref), channel_id=1, source_target_pairs={{0,1},{1,0},{2,3},{3,2},{4,5},{5,4},{6,7},{7,6},{8,9},{9,8},{10,11... | collective-permute-start | bytes 196616 | tf_op jit(solution)/shard_map/ppermute | solution.py:338
  15.8 4.7 %collective-permute-start.4 = (f32[192,128]{1,0:T(8,128)S(1)}, f32[192,128]{1,0:T(8,128)S(1)}, u32[]{:S(2)}, u32[]{:S(2)}) collective-permute-start(f32[192,128]{1,0:T(8,128)S(1)} %get-tuple-element.35), channel_id=1, source_target_pairs={{0,8},{4,12},{8,0},{12,4},{16,24},{20,28},{24,16},{28,20},{1,9},{5... | collective-permute-start | bytes 294920 | tf_op jit(solution)/shard_map/ppermute | solution.py:338
  17.1 10.3 %collective-permute-start.6 = (f32[3,128,128]{2,1,0:T(8,128)S(1)}, f32[3,128,128]{2,1,0:T(8,128)S(1)}, u32[]{:S(2)}, u32[]{:S(2)}) collective-permute-start(f32[3,128,128]{2,1,0:T(8,128)S(1)} %get-tuple-element.36), channel_id=1, source_target_pairs={{0,2},{1,3},{2,0},{3,1},{4,6},{5,7},{6,4},{7,5},{8,10},{9,11},{10,... | collective-permute-start | bytes 589832 | tf_op jit(solution)/shard_map/ppermute | solution.py:338
  20.5 7.0 %collective-permute-start.5 = (f32[192,128]{1,0:T(8,128)S(1)}, f32[192,128]{1,0:T(8,128)S(1)}, u32[]{:S(2)}, u32[]{:S(2)}) collective-permute-start(f32[192,128]{1,0:T(8,128)S(1)} %broadcast_select_fusion.5), channel_id=1, source_target_pairs={{0,16},{4,20},{8,24},{12,28},{16,0},{20,4},{24,8},{28,12},{1,17},{... | collective-permute-start | bytes 294920 | tf_op jit(solution)/shard_map/ppermute | solution.py:338
  27.5 3.1 %collective-permute-start.7 = (f32[192,128]{1,0:T(8,128)S(1)}, f32[192,128]{1,0:T(8,128)S(1)}, u32[]{:S(2)}, u32[]{:S(2)}) collective-permute-start(f32[192,128]{1,0:T(8,128)S(1)} %broadcast_select_fusion.6), channel_id=1, source_target_pairs={{0,4},{4,0},{8,12},{12,8},{16,20},{20,16},{24,28},{28,24},{1,5},{5... | collective-permute-start | bytes 294920 | tf_op jit(solution)/shard_map/ppermute | solution.py:338
  27.6 9.5 %collective-permute-start.9 = (f32[8,64,128]{2,1,0:T(8,128)S(1)}, f32[8,64,128]{2,1,0:T(8,128)}, u32[]{:S(2)}, u32[]{:S(2)}) collective-permute-start(f32[8,64,128]{2,1,0:T(8,128)S(1)} %broadcast_select_fusion.3), channel_id=1, source_target_pairs={{0,16},{4,20},{8,24},{12,28},{16,0},{20,4},{24,8},{28,12},{1,17},{... | collective-permute-start | bytes 786440 | tf_op jit(solution)/shard_map/ppermute | solution.py:338
  30.1 8.5 %collective-permute-start.10 = (f32[8,64,128]{2,1,0:T(8,128)S(1)}, f32[8,64,128]{2,1,0:T(8,128)}, u32[]{:S(2)}, u32[]{:S(2)}) collective-permute-start(f32[8,64,128]{2,1,0:T(8,128)S(1)} %broadcast_select_fusion.2), channel_id=1, source_target_pairs={{0,8},{4,12},{8,0},{12,4},{16,24},{20,28},{24,16},{28,20},{1,9},{5... | collective-permute-start | bytes 786440 | tf_op jit(solution)/shard_map/ppermute | solution.py:338
  34.8 9.9 %collective-permute-start.8 = (f32[3,128,128]{2,1,0:T(8,128)S(1)}, f32[3,128,128]{2,1,0:T(8,128)S(1)}, u32[]{:S(2)}, u32[]{:S(2)}) collective-permute-start(f32[3,128,128]{2,1,0:T(8,128)S(1)} %broadcast_select_fusion.4.rows_ref), channel_id=1, source_target_pairs={{0,1},{1,0},{2,3},{3,2},{4,5},{5,4},{6,7},{7,6},{8,9},{9,8},{10,11... | collective-permute-start | bytes 589832 | tf_op jit(solution)/shard_map/ppermute | solution.py:338
  37.1 7.6 %collective-permute-start.11 = (f32[8,64,128]{2,1,0:T(8,128)S(1)}, f32[8,64,128]{2,1,0:T(8,128)S(1)}, u32[]{:S(2)}, u32[]{:S(2)}) collective-permute-start(f32[8,64,128]{2,1,0:T(8,128)S(1)} %broadcast_select_fusion.1.ha_ref), channel_id=1, source_target_pairs={{0,4},{4,0},{8,12},{12,8},{16,20},{20,16},{24,28},{28,24},{1,5},{5... | collective-permute-start | bytes 786440 | tf_op jit(solution)/shard_map/ppermute | solution.py:338
  38.6 6.1 %collective-permute-start.12 = (f32[8,64,128]{2,1,0:T(8,128)S(1)}, f32[8,64,128]{2,1,0:T(8,128)S(1)}, u32[]{:S(2)}, u32[]{:S(2)}) collective-permute-start(f32[8,64,128]{2,1,0:T(8,128)S(1)} %broadcast_select_fusion.hb_ref), channel_id=1, source_target_pairs={{0,4},{4,0},{8,12},{12,8},{16,20},{20,16},{24,28},{28,24},{1,5},{5... | collective-permute-start | bytes 786440 | tf_op jit(solution)/shard_map/ppermute | solution.py:338

commit v17 on v16

--- a/solution.py
+++ b/solution.py
@@ -1,5 +1,3 @@
-import functools
-
 import jax
 import jax.numpy as jnp
 from jax import lax
@@ -153,22 +151,6 @@
     )(matrix)
 
 
-def pick_kernel(bit, new_ref, old_ref, out_ref):
-    out_ref[...] = jnp.where(bit_set(lax.axis_index("col"), bit), new_ref[...], old_ref[...])
-
-
-def pick(new, old, bit):
-    return pl.pallas_call(
-        functools.partial(pick_kernel, bit),
-        out_shape=jax.ShapeDtypeStruct(old.shape, old.dtype),
-        in_specs=[VMEM] * 2,
-        out_specs=VMEM,
-        compiler_params=pltpu.CompilerParams(vmem_limit_bytes=2 * MIB),
-        cost_estimate=estimate(8 * 10**9, 2 * MIB),
-        name="pick",
-    )(new, old)
-
-
 def pack_kernel(across_ref, block_ref, both_ref, message_ref):
     n = block_ref.shape[0]
     odd = is_odd_row()
@@ -349,6 +331,16 @@
     return held
 
 
+def region(run, *values):
+    shapes = jax.eval_shape(run, *values)
+
+    def skip(*_):
+        return jax.tree.map(lambda leaf: jnp.zeros(leaf.shape, leaf.dtype), shapes)
+
+    everywhere = lax.axis_index("row") < lax.axis_size("row")
+    return lax.cond(everywhere, run, skip, *values)
+
+
 def after(value, *others):
     return lax.optimization_barrier((value,) + others)
 
@@ -370,8 +362,11 @@
     upper_moved = exchange(upper, "row", 1 << first_bit, n_row)
     lower_moved = exchange(lower, "row", 1 << last_bit, n_row)
 
-    block = pick(moved, block, col_bits[0])
-    block = spread(block, "col", grid_col, n_col, col_bits[1:])
+    def along_col(new, old):
+        block = jnp.where(bit_set(grid_col, col_bits[0]), new, old)
+        return spread(block, "col", grid_col, n_col, col_bits[1:])
+
+    block = region(along_col, moved, block)
     across = exchange(block, "col", 1, n_col)
     ha = jnp.where(bit_set(grid_row, first_bit), upper_moved, upper)
     hb = jnp.where(bit_set(grid_row, last_bit), lower_moved, lower)

time: 51.9 us -> 49.6 us (0.956)
  starting transfers between devices: 17.8 us -> 16.2 us
  waiting for transfers between devices: 13.8 us -> 13.2 us
    ppermute x13, starting transfers between devices: 17.8 us -> 16.2 us  [exchange(): return lax.ppermute(value, axis, [(i, i ^ mask) for i in range(size)])]
    ppermute x13, waiting for transfers between devices: 13.8 us -> 13.2 us  [exchange(): return lax.ppermute(value, axis, [(i, i ^ mask) for i in range(size)])]
where the time goes in v17:
time: 49.6 us; the launch traced here: 49.4 us
  Pallas kernels  18 us (36%)
  starting transfers between devices  16.2 us (33%)
  waiting for transfers between devices  13.2 us (27%)
  local copies, waits for them, and re-layouts  1.6 us (3%)
    ppermute x13, starting transfers between devices, exchange(): return lax.ppermute(value, axis, [(i, i ^ mask) for i in range(size)])  16.2 us
    ppermute x13, waiting for transfers between devices, exchange(): return lax.ppermute(value, axis, [(i, i ^ mask) for i in range(size)])  13.2 us
    pallas_call x1, Pallas kernels, settle(): pl.pallas_call(settle_kernel, out_shape=jax.ShapeDtypeStruct((local_rows,...  6.91 us
    pallas_call x1, Pallas kernels, second_factor(): pl.pallas_call(second_factor_kernel, out_shape=[square, double, double, b...  6.03 us
    pallas_call x1, Pallas kernels, first_factor(): pl.pallas_call(first_factor_kernel, out_shape=[square] * 3, in_specs=[VME...  4.26 us
    unnamed x4, local copies, waits for them, and re-layouts  1.6 us
  transfers between devices with their start and end apart: 13, of which 6 were waited for; matrix products, arithmetic and copies ran while one was open for 0% of the time, Pallas kernels for 21%

profile of v17, /device:TPU:0, one launch (start us, length us, event | category | flops | bytes accessed | tf_op | source)
XLA Modules:
  0.0 49.4 jit_solution(11785836217239612660)
XLA Ops:
  0.0 0.0 copy-start
  0.0 1.6 %copy-done = f32[4,128,8,128]{3,2,1,0:T(8,128)S(1)} copy-done((f32[4,128,8,128]{3,2,1,0:T(8,128)S(1)}, f32[4,128,8,128]{3,2,1,0:T(8,128)}, u32[]{:S(2)}) %copy-start) | copy-done | bytes 2097176
  1.6 0.7 %panels.1 = (f32[3,128,128]{2,1,0:T(8,128)S(1)}, f32[8,64,128]{2,1,0:T(8,128)S(1)}, f32[8,64,128]{2,1,0:T(8,128)S(1)}) custom-call(f32[4,128,8,128]{3,2,1,0:T(8,128)S(1)} %copy-done), custom_call_target="tpu_custom_call" | custom-call | bytes 4194304 | tf_op jit(solution)/shard_map/panels/pallas_call | solution.py:142
  2.3 3.0 %collective-permute-start.2 = (f32[8,64,128]{2,1,0:T(8,128)S(1)}, f32[8,64,128]{2,1,0:T(8,128)S(1)}, u32[]{:S(2)}, u32[]{:S(2)}) collective-permute-start(f32[8,64,128]{2,1,0:T(8,128)S(1)} %get-tuple-element.42), channel_id=1, source_target_pairs={{0,8},{4,12},{8,0},{12,4},{16,24},{20,28},{24,16},{28,20},{1,9},{5... | collective-permute-start | bytes 786440 | tf_op jit(solution)/shard_map/ppermute | solution.py:320
  5.3 0.1 corner_block.1
  5.4 2.7 %collective-permute-start = (f32[128,128]{1,0:T(8,128)S(1)}, f32[128,128]{1,0:T(8,128)S(1)}, u32[]{:S(2)}, u32[]{:S(2)}) collective-permute-start(f32[128,128]{1,0:T(8,128)S(1)} %corner_block.1), channel_id=1, source_target_pairs={{0,2},{1,3},{2,0},{3,1},{4,6},{5,7},{6,4},{7,5},{8,10},{9,11},{10,... | collective-permute-start | bytes 196616 | tf_op jit(solution)/shard_map/ppermute | solution.py:320
  8.0 1.5 %collective-permute-start.3 = (f32[8,64,128]{2,1,0:T(8,128)S(1)}, f32[8,64,128]{2,1,0:T(8,128)S(1)}, u32[]{:S(2)}, u32[]{:S(2)}) collective-permute-start(f32[8,64,128]{2,1,0:T(8,128)S(1)} %get-tuple-element.43), channel_id=1, source_target_pairs={{0,16},{4,20},{8,24},{12,28},{16,0},{20,4},{24,8},{28,12},{1,17},{... | collective-permute-start | bytes 786440 | tf_op jit(solution)/shard_map/ppermute | solution.py:320
  9.5 1.4 %collective-permute-done = f32[128,128]{1,0:T(8,128)S(1)} collective-permute-done((f32[128,128]{1,0:T(8,128)S(1)}, f32[128,128]{1,0:T(8,128)S(1)}, u32[]{:S(2)}, u32[]{:S(2)}) %collective-permute-start) | collective-permute-done | bytes 65568 | tf_op jit(solution)/shard_map/ppermute | solution.py:320
  10.9 1.3 %collective-permute-start.1 = (f32[128,128]{1,0:T(8,128)S(1)}, f32[128,128]{1,0:T(8,128)S(1)}, u32[]{:S(2)}, u32[]{:S(2)}) collective-permute-start(f32[128,128]{1,0:T(8,128)S(1)} %get-tuple-element.72.block_ref), channel_id=1, source_target_pairs={{0,1},{1,0},{2,3},{3,2},{4,5},{5,4},{6,7},{7,6},{8,9},{9,8},{10,11... | collective-permute-start | bytes 196616 | tf_op jit(solution)/shard_map/ppermute | solution.py:320
  12.2 0.0 collective-permute-done.2
  12.3 3.2 %collective-permute-done.3 = f32[8,64,128]{2,1,0:T(8,128)S(1)} collective-permute-done((f32[8,64,128]{2,1,0:T(8,128)S(1)}, f32[8,64,128]{2,1,0:T(8,128)S(1)}, u32[]{:S(2)}, u32[]{:S(2)}) %collective-permute-start.3) | collective-permute-done | bytes 262176 | tf_op jit(solution)/shard_map/ppermute | solution.py:320
  15.5 0.0 collective-permute-done.1.across_ref
  15.5 0.1 pack.1
  15.6 0.6 %collective-permute-start.4 = (f32[192,128]{1,0:T(8,128)S(1)}, f32[192,128]{1,0:T(8,128)S(1)}, u32[]{:S(2)}, u32[]{:S(2)}) collective-permute-start(f32[192,128]{1,0:T(8,128)S(1)} %get-tuple-element.47), channel_id=1, source_target_pairs={{0,8},{4,12},{8,0},{12,4},{16,24},{20,28},{24,16},{28,20},{1,9},{5... | collective-permute-start | bytes 294920 | tf_op jit(solution)/shard_map/ppermute | solution.py:320
  16.2 2.1 %collective-permute-start.6 = (f32[3,128,128]{2,1,0:T(8,128)S(1)}, f32[3,128,128]{2,1,0:T(8,128)S(1)}, u32[]{:S(2)}, u32[]{:S(2)}) collective-permute-start(f32[3,128,128]{2,1,0:T(8,128)S(1)} %get-tuple-element.48), channel_id=1, source_target_pairs={{0,2},{1,3},{2,0},{3,1},{4,6},{5,7},{6,4},{7,5},{8,10},{9,11},{10,... | collective-permute-start | bytes 589832 | tf_op jit(solution)/shard_map/ppermute | solution.py:320
  18.4 2.0 %collective-permute-done.4 = f32[192,128]{1,0:T(8,128)S(1)} collective-permute-done((f32[192,128]{1,0:T(8,128)S(1)}, f32[192,128]{1,0:T(8,128)S(1)}, u32[]{:S(2)}, u32[]{:S(2)}) %collective-permute-start.4) | collective-permute-done | bytes 98336 | tf_op jit(solution)/shard_map/ppermute | solution.py:320
  20.3 1.6 %collective-permute-start.5 = (f32[192,128]{1,0:T(8,128)S(1)}, f32[192,128]{1,0:T(8,128)S(1)}, u32[]{:S(2)}, u32[]{:S(2)}) collective-permute-start(f32[192,128]{1,0:T(8,128)S(1)} %broadcast_select_fusion.6), channel_id=1, source_target_pairs={{0,16},{4,20},{8,24},{12,28},{16,0},{20,4},{24,8},{28,12},{1,17},{... | collective-permute-start | bytes 294920 | tf_op jit(solution)/shard_map/ppermute | solution.py:320
  21.9 4.3 %collective-permute-done.6 = f32[3,128,128]{2,1,0:T(8,128)S(1)} collective-permute-done((f32[3,128,128]{2,1,0:T(8,128)S(1)}, f32[3,128,128]{2,1,0:T(8,128)S(1)}, u32[]{:S(2)}, u32[]{:S(2)}) %collective-permute-start.6) | collective-permute-done | bytes 196640 | tf_op jit(solution)/shard_map/ppermute | solution.py:320
  26.3 0.0 collective-permute-done.5
  26.3 0.1 collective-permute-start.7
  26.4 1.6 %collective-permute-start.9 = (f32[8,64,128]{2,1,0:T(8,128)S(1)}, f32[8,64,128]{2,1,0:T(8,128)}, u32[]{:S(2)}, u32[]{:S(2)}) collective-permute-start(f32[8,64,128]{2,1,0:T(8,128)S(1)} %broadcast_select_fusion.4), channel_id=1, source_target_pairs={{0,16},{4,20},{8,24},{12,28},{16,0},{20,4},{24,8},{28,12},{1,17},{... | collective-permute-start | bytes 786440 | tf_op jit(solution)/shard_map/ppermute | solution.py:320
  28.0 1.5 %collective-permute-start.10 = (f32[8,64,128]{2,1,0:T(8,128)S(1)}, f32[8,64,128]{2,1,0:T(8,128)S(1)}, u32[]{:S(2)}, u32[]{:S(2)}) collective-permute-start(f32[8,64,128]{2,1,0:T(8,128)S(1)} %broadcast_select_fusion.3), channel_id=1, source_target_pairs={{0,8},{4,12},{8,0},{12,4},{16,24},{20,28},{24,16},{28,20},{1,9},{5... | collective-permute-start | bytes 786440 | tf_op jit(solution)/shard_map/ppermute | solution.py:320
  29.5 0.0 collective-permute-done.7
  29.5 0.0 copy-start.1
  29.5 4.3 %first_factor.1 = (f32[128,128]{1,0:T(8,128)S(1)}, f32[128,128]{1,0:T(8,128)S(1)}, f32[128,128]{1,0:T(8,128)S(1)}) custom-call(f32[128,128]{1,0:T(8,128)S(1)} %get-tuple-element.68.a_ref, f32[128,128]{1,0:T(8,128)S(1)} %get-tuple-element.71.side_ref), custom_call_target="tpu_custom_call" | custom-call | flops 8000000000 | bytes 2097152 | tf_op jit(solution)/shard_map/first_factor/pallas_call | solution.py:191
  33.8 0.1 collective-permute-start.8
  33.9 1.3 %collective-permute-done.9 = f32[8,64,128]{2,1,0:T(8,128)} collective-permute-done((f32[8,64,128]{2,1,0:T(8,128)S(1)}, f32[8,64,128]{2,1,0:T(8,128)}, u32[]{:S(2)}, u32[]{:S(2)}) %collective-permute-start.9) | collective-permute-done | bytes 262176 | tf_op jit(solution)/shard_map/ppermute | solution.py:320
  35.2 0.1 collective-permute-start.11
  35.3 1.0 %collective-permute-done.10 = f32[8,64,128]{2,1,0:T(8,128)S(1)} collective-permute-done((f32[8,64,128]{2,1,0:T(8,128)S(1)}, f32[8,64,128]{2,1,0:T(8,128)S(1)}, u32[]{:S(2)}, u32[]{:S(2)}) %collective-permute-start.10) | collective-permute-done | bytes 262176 | tf_op jit(solution)/shard_map/ppermute | solution.py:320
  36.4 0.1 collective-permute-start.12
  36.4 0.0 copy-done.1
  36.5 6.0 %second_factor.1 = (f32[128,128]{1,0:T(8,128)S(1)}, f32[256,256]{1,0:T(8,128)S(1)}, f32[256,256]{1,0:T(8,128)S(1)}, f32[8,4,128,128]{3,2,1,0:T(8,128)S(1)}) custom-call(f32[128,128]{1,0:T(8,128)S(1)} %get-tuple-element.67.a_ref, f32[128,128]{1,0:T(8,128)S(1)} %get-tuple-element.54.cross_ref, f32[128,128]{1,0:T(8,128)S(1)} %get-tuple-element.57.w0_ref, ...), custom_call_target="tpu_custom_call" | custom-call | flops 8000000000 | bytes 4194304 | tf_op jit(solution)/shard_map/second_factor/pallas_call | solution.py:234
  42.5 0.0 collective-permute-done.8.rows_other_ref
  42.5 0.0 collective-permute-done.11.oa_ref
  42.5 0.0 collective-permute-done.12.ob_ref
  42.5 6.9 %settle.1 = f32[4,128,8,128]{3,2,1,0:T(8,128)} custom-call(f32[128,128]{1,0:T(8,128)S(1)} %get-tuple-element.53.f0_ref, f32[128,128]{1,0:T(8,128)S(1)} %get-tuple-element.58.f1_ref, f32[256,256]{1,0:T(8,128)S(1)} %get-tuple-element.59.w_ref, f32[256,256]{1,0:T(8,128)S(1)} %get-tuple-element.60.mixed_ref, f32[2,128,128]{2,1,0:T(8,128)S(1)} %get-tuple-element.61.first_ref, ...), custom_call_target="tpu_custom_call" | custom-call | flops 4000000000 | bytes 6291456 | tf_op jit(solution)/shard_map/settle/pallas_call | solution.py:307
  (11 shorter events, 0.2 us)
Async XLA Ops:
  0.0 1.6 %copy-start = (f32[4,128,8,128]{3,2,1,0:T(8,128)S(1)}, f32[4,128,8,128]{3,2,1,0:T(8,128)}, u32[]{:S(2)}) copy-start(f32[4,128,8,128]{3,2,1,0:T(8,128)} %matrix_ref.5) | copy-start | bytes 6291460
  2.3 10.0 %collective-permute-start.2 = (f32[8,64,128]{2,1,0:T(8,128)S(1)}, f32[8,64,128]{2,1,0:T(8,128)S(1)}, u32[]{:S(2)}, u32[]{:S(2)}) collective-permute-start(f32[8,64,128]{2,1,0:T(8,128)S(1)} %get-tuple-element.42), channel_id=1, source_target_pairs={{0,8},{4,12},{8,0},{12,4},{16,24},{20,28},{24,16},{28,20},{1,9},{5... | collective-permute-start | bytes 786440 | tf_op jit(solution)/shard_map/ppermute | solution.py:320
  5.4 5.5 %collective-permute-start = (f32[128,128]{1,0:T(8,128)S(1)}, f32[128,128]{1,0:T(8,128)S(1)}, u32[]{:S(2)}, u32[]{:S(2)}) collective-permute-start(f32[128,128]{1,0:T(8,128)S(1)} %corner_block.1), channel_id=1, source_target_pairs={{0,2},{1,3},{2,0},{3,1},{4,6},{5,7},{6,4},{7,5},{8,10},{9,11},{10,... | collective-permute-start | bytes 196616 | tf_op jit(solution)/shard_map/ppermute | solution.py:320
  8.0 7.5 %collective-permute-start.3 = (f32[8,64,128]{2,1,0:T(8,128)S(1)}, f32[8,64,128]{2,1,0:T(8,128)S(1)}, u32[]{:S(2)}, u32[]{:S(2)}) collective-permute-start(f32[8,64,128]{2,1,0:T(8,128)S(1)} %get-tuple-element.43), channel_id=1, source_target_pairs={{0,16},{4,20},{8,24},{12,28},{16,0},{20,4},{24,8},{28,12},{1,17},{... | collective-permute-start | bytes 786440 | tf_op jit(solution)/shard_map/ppermute | solution.py:320
  10.9 4.6 %collective-permute-start.1 = (f32[128,128]{1,0:T(8,128)S(1)}, f32[128,128]{1,0:T(8,128)S(1)}, u32[]{:S(2)}, u32[]{:S(2)}) collective-permute-start(f32[128,128]{1,0:T(8,128)S(1)} %get-tuple-element.72.block_ref), channel_id=1, source_target_pairs={{0,1},{1,0},{2,3},{3,2},{4,5},{5,4},{6,7},{7,6},{8,9},{9,8},{10,11... | collective-permute-start | bytes 196616 | tf_op jit(solution)/shard_map/ppermute | solution.py:320
  15.6 4.7 %collective-permute-start.4 = (f32[192,128]{1,0:T(8,128)S(1)}, f32[192,128]{1,0:T(8,128)S(1)}, u32[]{:S(2)}, u32[]{:S(2)}) collective-permute-start(f32[192,128]{1,0:T(8,128)S(1)} %get-tuple-element.47), channel_id=1, source_target_pairs={{0,8},{4,12},{8,0},{12,4},{16,24},{20,28},{24,16},{28,20},{1,9},{5... | collective-permute-start | bytes 294920 | tf_op jit(solution)/shard_map/ppermute | solution.py:320
  16.2 10.0 %collective-permute-start.6 = (f32[3,128,128]{2,1,0:T(8,128)S(1)}, f32[3,128,128]{2,1,0:T(8,128)S(1)}, u32[]{:S(2)}, u32[]{:S(2)}) collective-permute-start(f32[3,128,128]{2,1,0:T(8,128)S(1)} %get-tuple-element.48), channel_id=1, source_target_pairs={{0,2},{1,3},{2,0},{3,1},{4,6},{5,7},{6,4},{7,5},{8,10},{9,11},{10,... | collective-permute-start | bytes 589832 | tf_op jit(solution)/shard_map/ppermute | solution.py:320
  20.3 5.9 %collective-permute-start.5 = (f32[192,128]{1,0:T(8,128)S(1)}, f32[192,128]{1,0:T(8,128)S(1)}, u32[]{:S(2)}, u32[]{:S(2)}) collective-permute-start(f32[192,128]{1,0:T(8,128)S(1)} %broadcast_select_fusion.6), channel_id=1, source_target_pairs={{0,16},{4,20},{8,24},{12,28},{16,0},{20,4},{24,8},{28,12},{1,17},{... | collective-permute-start | bytes 294920 | tf_op jit(solution)/shard_map/ppermute | solution.py:320
  26.3 3.2 %collective-permute-start.7 = (f32[192,128]{1,0:T(8,128)S(1)}, f32[192,128]{1,0:T(8,128)S(1)}, u32[]{:S(2)}, u32[]{:S(2)}) collective-permute-start(f32[192,128]{1,0:T(8,128)S(1)} %broadcast_select_fusion.7), channel_id=1, source_target_pairs={{0,4},{4,0},{8,12},{12,8},{16,20},{20,16},{24,28},{28,24},{1,5},{5... | collective-permute-start | bytes 294920 | tf_op jit(solution)/shard_map/ppermute | solution.py:320
  26.4 8.8 %collective-permute-start.9 = (f32[8,64,128]{2,1,0:T(8,128)S(1)}, f32[8,64,128]{2,1,0:T(8,128)}, u32[]{:S(2)}, u32[]{:S(2)}) collective-permute-start(f32[8,64,128]{2,1,0:T(8,128)S(1)} %broadcast_select_fusion.4), channel_id=1, source_target_pairs={{0,16},{4,20},{8,24},{12,28},{16,0},{20,4},{24,8},{28,12},{1,17},{... | collective-permute-start | bytes 786440 | tf_op jit(solution)/shard_map/ppermute | solution.py:320
  28.0 8.4 %collective-permute-start.10 = (f32[8,64,128]{2,1,0:T(8,128)S(1)}, f32[8,64,128]{2,1,0:T(8,128)S(1)}, u32[]{:S(2)}, u32[]{:S(2)}) collective-permute-start(f32[8,64,128]{2,1,0:T(8,128)S(1)} %broadcast_select_fusion.3), channel_id=1, source_target_pairs={{0,8},{4,12},{8,0},{12,4},{16,24},{20,28},{24,16},{28,20},{1,9},{5... | collective-permute-start | bytes 786440 | tf_op jit(solution)/shard_map/ppermute | solution.py:320
  29.5 6.9 %copy-start.1 = (f32[4,128,8,128]{3,2,1,0:T(8,128)S(1)}, f32[4,128,8,128]{3,2,1,0:T(8,128)}, u32[]{:S(2)}) copy-start(f32[4,128,8,128]{3,2,1,0:T(8,128)} %matrix_ref.5) | copy-start | bytes 6291460
  33.8 8.7 %collective-permute-start.8 = (f32[3,128,128]{2,1,0:T(8,128)S(1)}, f32[3,128,128]{2,1,0:T(8,128)S(1)}, u32[]{:S(2)}, u32[]{:S(2)}) collective-permute-start(f32[3,128,128]{2,1,0:T(8,128)S(1)} %broadcast_select_fusion.5.rows_ref), channel_id=1, source_target_pairs={{0,1},{1,0},{2,3},{3,2},{4,5},{5,4},{6,7},{7,6},{8,9},{9,8},{10,11... | collective-permute-start | bytes 589832 | tf_op jit(solution)/shard_map/ppermute | solution.py:320
  35.2 7.3 %collective-permute-start.11 = (f32[8,64,128]{2,1,0:T(8,128)S(1)}, f32[8,64,128]{2,1,0:T(8,128)S(1)}, u32[]{:S(2)}, u32[]{:S(2)}) collective-permute-start(f32[8,64,128]{2,1,0:T(8,128)S(1)} %broadcast_select_fusion.2.ha_ref), channel_id=1, source_target_pairs={{0,4},{4,0},{8,12},{12,8},{16,20},{20,16},{24,28},{28,24},{1,5},{5... | collective-permute-start | bytes 786440 | tf_op jit(solution)/shard_map/ppermute | solution.py:320
  36.4 6.2 %collective-permute-start.12 = (f32[8,64,128]{2,1,0:T(8,128)S(1)}, f32[8,64,128]{2,1,0:T(8,128)S(1)}, u32[]{:S(2)}, u32[]{:S(2)}) collective-permute-start(f32[8,64,128]{2,1,0:T(8,128)S(1)} %broadcast_select_fusion.1.hb_ref), channel_id=1, source_target_pairs={{0,4},{4,0},{8,12},{12,8},{16,20},{20,16},{24,28},{28,24},{1,5},{5... | collective-permute-start | bytes 786440 | tf_op jit(solution)/shard_map/ppermute | solution.py:320

commit v18 on v17

--- a/solution.py
+++ b/solution.py
@@ -91,12 +91,16 @@
     return lax.rem(lax.axis_index("row"), 2) == 1
 
 
+def stacked(a):
+    return jnp.concatenate(parts(a)[::-1], axis=0)
+
+
 def dot_parts(a, b, dims=((1,), (0,))):
-    total = None
-    for i, j in ((2, 0), (0, 2), (1, 1), (1, 0), (0, 1), (0, 0)):
-        term = lax.dot_general(a[i], b[j], (dims, ((), ())), preferred_element_type=jnp.float32)
-        total = term if total is None else total + term
-    return total
+    m = a.shape[0] // 3
+    high, middle, low = [
+        lax.dot_general(a[i * m:], b[i], (dims, ((), ())), preferred_element_type=jnp.float32) for i in range(3)]
+    small = high[:m] + middle[:m] + low
+    return small + (high[m:2 * m] + middle[m:]) + high[2 * m:]
 
 
 def estimate(flops, nbytes):
@@ -256,15 +260,15 @@
     rows = jnp.concatenate([
         jnp.concatenate([first_ref[0], jnp.where(swapped, other, own)], axis=0),
         jnp.concatenate([first_ref[1], jnp.where(swapped, own, other)], axis=0)], axis=1)
-    solved = dot_parts(parts(rows), parts(w_ref[...]), ((1,), (1,)))
-    left = parts(solved)
-    mixed = parts(mixed_ref[...])
+    solved = dot_parts(stacked(rows), parts(w_ref[...]), ((1,), (1,)))
+    left = stacked(solved)
+    mixed = stacked(mixed_ref[...])
     copies = []
     for j in range(0, local_cols, 2):
         pair = (j, j + 1)
-        stacked = jnp.concatenate(
+        tops = jnp.concatenate(
             [jnp.concatenate([ha_ref[b], hb_ref[b], oa_ref[b], ob_ref[b]], axis=0) for b in pair], axis=1)
-        update = dot_parts(left, parts(dot_parts(mixed, parts(stacked))))
+        update = dot_parts(left, parts(dot_parts(mixed, parts(tops))))
         for b in pair:
             part = update[:, (b - j) * n:(b - j + 1) * n].reshape(local_rows, n, n)
             result[b] = blocks_ref[b] - part
@@ -391,15 +395,16 @@
     a01 = jnp.concatenate([jnp.where(odd, other[n:], pair[n:]), jnp.where(odd, pair[n:], other[n:])], axis=0)
     f0, w0, cross = first_factor(a00, a01)
 
-    w0, rows, row_then, col_then = after(w0, rows, grid_row, grid_col)
+    rows = spread(rows, "col", grid_col, n_col, col_bits[1:])
+    rows_other = exchange(rows, "col", 1, n_col)
+    w0, row_then = after(w0, grid_row)
     ha = jnp.where(bit_set(row_then, row_bits[1]), ha_moved, ha)
     ha = spread(ha, "row", row_then, n_row, row_bits[2:])
     hb = jnp.where(bit_set(row_then, row_bits[-2]), hb_moved, hb)
     hb = spread(hb, "row", row_then, n_row, row_bits[:-2][::-1])
-    rows = spread(rows, "col", col_then, n_col, col_bits[1:])
-    rows_other = exchange(rows, "col", 1, n_col)
     oa = exchange(ha, "row", 1, n_row)
     ob = exchange(hb, "row", 1, n_row)
+    a11, rows_other = after(a11, rows_other)
     f1, w, mixed, blocks = second_factor(a11, cross, w0, kernel)
     return settle(f0, f1, w, mixed, first_rows, rows, rows_other, ha, hb, oa, ob, blocks)
 

time: 49.6 us -> 49.9 us (level)
  no operation moved by 1% of the time
where the time goes in v18:
time: 49.9 us; the launch traced here: 49.5 us
  Pallas kernels  17.9 us (36%)
  starting transfers between devices  16.2 us (32%)
  waiting for transfers between devices  13.3 us (27%)
  local copies, waits for them, and re-layouts  1.6 us (3%)
    ppermute x13, starting transfers between devices, exchange(): return lax.ppermute(value, axis, [(i, i ^ mask) for i in range(size)])  16.2 us
    ppermute x13, waiting for transfers between devices, exchange(): return lax.ppermute(value, axis, [(i, i ^ mask) for i in range(size)])  13.3 us
    pallas_call x1, Pallas kernels, settle(): pl.pallas_call(settle_kernel, out_shape=jax.ShapeDtypeStruct((local_rows,...  6.77 us
    pallas_call x1, Pallas kernels, second_factor(): pl.pallas_call(second_factor_kernel, out_shape=[square, double, double, b...  6.03 us
    pallas_call x1, Pallas kernels, first_factor(): pl.pallas_call(first_factor_kernel, out_shape=[square] * 3, in_specs=[VME...  4.26 us
    unnamed x4, local copies, waits for them, and re-layouts  1.6 us
  transfers between devices with their start and end apart: 13, of which 6 were waited for; matrix products, arithmetic and copies ran while one was open for 0% of the time, Pallas kernels for 21%

profile of v18, /device:TPU:0, one launch (start us, length us, event | category | flops | bytes accessed | tf_op | source)
XLA Modules:
  0.0 49.5 jit_solution(886139979894209131)
XLA Ops:
  0.0 0.0 copy-start
  0.0 1.6 %copy-done = f32[4,128,8,128]{3,2,1,0:T(8,128)S(1)} copy-done((f32[4,128,8,128]{3,2,1,0:T(8,128)S(1)}, f32[4,128,8,128]{3,2,1,0:T(8,128)}, u32[]{:S(2)}) %copy-start) | copy-done | bytes 2097176
  1.6 0.7 %panels.1 = (f32[3,128,128]{2,1,0:T(8,128)S(1)}, f32[8,64,128]{2,1,0:T(8,128)S(1)}, f32[8,64,128]{2,1,0:T(8,128)S(1)}) custom-call(f32[4,128,8,128]{3,2,1,0:T(8,128)S(1)} %copy-done), custom_call_target="tpu_custom_call" | custom-call | bytes 4194304 | tf_op jit(solution)/shard_map/panels/pallas_call | solution.py:146
  2.3 3.0 %collective-permute-start.2 = (f32[8,64,128]{2,1,0:T(8,128)S(1)}, f32[8,64,128]{2,1,0:T(8,128)S(1)}, u32[]{:S(2)}, u32[]{:S(2)}) collective-permute-start(f32[8,64,128]{2,1,0:T(8,128)S(1)} %get-tuple-element.43), channel_id=1, source_target_pairs={{0,8},{4,12},{8,0},{12,4},{16,24},{20,28},{24,16},{28,20},{1,9},{5... | collective-permute-start | bytes 786440 | tf_op jit(solution)/shard_map/ppermute | solution.py:324
  5.3 0.1 corner_block.1
  5.4 2.7 %collective-permute-start = (f32[128,128]{1,0:T(8,128)S(1)}, f32[128,128]{1,0:T(8,128)S(1)}, u32[]{:S(2)}, u32[]{:S(2)}) collective-permute-start(f32[128,128]{1,0:T(8,128)S(1)} %corner_block.1), channel_id=1, source_target_pairs={{0,2},{1,3},{2,0},{3,1},{4,6},{5,7},{6,4},{7,5},{8,10},{9,11},{10,... | collective-permute-start | bytes 196616 | tf_op jit(solution)/shard_map/ppermute | solution.py:324
  8.0 1.5 %collective-permute-start.3 = (f32[8,64,128]{2,1,0:T(8,128)S(1)}, f32[8,64,128]{2,1,0:T(8,128)S(1)}, u32[]{:S(2)}, u32[]{:S(2)}) collective-permute-start(f32[8,64,128]{2,1,0:T(8,128)S(1)} %get-tuple-element.44), channel_id=1, source_target_pairs={{0,16},{4,20},{8,24},{12,28},{16,0},{20,4},{24,8},{28,12},{1,17},{... | collective-permute-start | bytes 786440 | tf_op jit(solution)/shard_map/ppermute | solution.py:324
  9.5 1.4 %collective-permute-done = f32[128,128]{1,0:T(8,128)S(1)} collective-permute-done((f32[128,128]{1,0:T(8,128)S(1)}, f32[128,128]{1,0:T(8,128)S(1)}, u32[]{:S(2)}, u32[]{:S(2)}) %collective-permute-start) | collective-permute-done | bytes 65568 | tf_op jit(solution)/shard_map/ppermute | solution.py:324
  10.9 1.3 %collective-permute-start.1 = (f32[128,128]{1,0:T(8,128)S(1)}, f32[128,128]{1,0:T(8,128)S(1)}, u32[]{:S(2)}, u32[]{:S(2)}) collective-permute-start(f32[128,128]{1,0:T(8,128)S(1)} %get-tuple-element.73.block_ref), channel_id=1, source_target_pairs={{0,1},{1,0},{2,3},{3,2},{4,5},{5,4},{6,7},{7,6},{8,9},{9,8},{10,11... | collective-permute-start | bytes 196616 | tf_op jit(solution)/shard_map/ppermute | solution.py:324
  12.2 0.0 collective-permute-done.2
  12.3 3.2 %collective-permute-done.3 = f32[8,64,128]{2,1,0:T(8,128)S(1)} collective-permute-done((f32[8,64,128]{2,1,0:T(8,128)S(1)}, f32[8,64,128]{2,1,0:T(8,128)S(1)}, u32[]{:S(2)}, u32[]{:S(2)}) %collective-permute-start.3) | collective-permute-done | bytes 262176 | tf_op jit(solution)/shard_map/ppermute | solution.py:324
  15.5 0.0 collective-permute-done.1.across_ref
  15.5 0.1 pack.1
  15.6 0.6 %collective-permute-start.4 = (f32[192,128]{1,0:T(8,128)S(1)}, f32[192,128]{1,0:T(8,128)S(1)}, u32[]{:S(2)}, u32[]{:S(2)}) collective-permute-start(f32[192,128]{1,0:T(8,128)S(1)} %get-tuple-element.48), channel_id=1, source_target_pairs={{0,8},{4,12},{8,0},{12,4},{16,24},{20,28},{24,16},{28,20},{1,9},{5... | collective-permute-start | bytes 294920 | tf_op jit(solution)/shard_map/ppermute | solution.py:324
  16.2 2.1 %collective-permute-start.6 = (f32[3,128,128]{2,1,0:T(8,128)S(1)}, f32[3,128,128]{2,1,0:T(8,128)S(1)}, u32[]{:S(2)}, u32[]{:S(2)}) collective-permute-start(f32[3,128,128]{2,1,0:T(8,128)S(1)} %get-tuple-element.49), channel_id=1, source_target_pairs={{0,2},{1,3},{2,0},{3,1},{4,6},{5,7},{6,4},{7,5},{8,10},{9,11},{10,... | collective-permute-start | bytes 589832 | tf_op jit(solution)/shard_map/ppermute | solution.py:324
  18.4 2.0 %collective-permute-done.4 = f32[192,128]{1,0:T(8,128)S(1)} collective-permute-done((f32[192,128]{1,0:T(8,128)S(1)}, f32[192,128]{1,0:T(8,128)S(1)}, u32[]{:S(2)}, u32[]{:S(2)}) %collective-permute-start.4) | collective-permute-done | bytes 98336 | tf_op jit(solution)/shard_map/ppermute | solution.py:324
  20.3 1.6 %collective-permute-start.5 = (f32[192,128]{1,0:T(8,128)S(1)}, f32[192,128]{1,0:T(8,128)S(1)}, u32[]{:S(2)}, u32[]{:S(2)}) collective-permute-start(f32[192,128]{1,0:T(8,128)S(1)} %broadcast_select_fusion.6), channel_id=1, source_target_pairs={{0,16},{4,20},{8,24},{12,28},{16,0},{20,4},{24,8},{28,12},{1,17},{... | collective-permute-start | bytes 294920 | tf_op jit(solution)/shard_map/ppermute | solution.py:324
  21.9 4.3 %collective-permute-done.6 = f32[3,128,128]{2,1,0:T(8,128)S(1)} collective-permute-done((f32[3,128,128]{2,1,0:T(8,128)S(1)}, f32[3,128,128]{2,1,0:T(8,128)S(1)}, u32[]{:S(2)}, u32[]{:S(2)}) %collective-permute-start.6) | collective-permute-done | bytes 196640 | tf_op jit(solution)/shard_map/ppermute | solution.py:324
  26.3 0.0 collective-permute-done.5
  26.3 0.1 collective-permute-start.7
  26.4 0.4 collective-permute-start.8
  26.8 1.5 %collective-permute-start.9 = (f32[8,64,128]{2,1,0:T(8,128)S(1)}, f32[8,64,128]{2,1,0:T(8,128)}, u32[]{:S(2)}, u32[]{:S(2)}) collective-permute-start(f32[8,64,128]{2,1,0:T(8,128)S(1)} %broadcast_select_fusion.4), channel_id=1, source_target_pairs={{0,16},{4,20},{8,24},{12,28},{16,0},{20,4},{24,8},{28,12},{1,17},{... | collective-permute-start | bytes 786440 | tf_op jit(solution)/shard_map/ppermute | solution.py:324
  28.3 1.2 %collective-permute-start.10 = (f32[8,64,128]{2,1,0:T(8,128)S(1)}, f32[8,64,128]{2,1,0:T(8,128)}, u32[]{:S(2)}, u32[]{:S(2)}) collective-permute-start(f32[8,64,128]{2,1,0:T(8,128)S(1)} %broadcast_select_fusion.3), channel_id=1, source_target_pairs={{0,8},{4,12},{8,0},{12,4},{16,24},{20,28},{24,16},{28,20},{1,9},{5... | collective-permute-start | bytes 786440 | tf_op jit(solution)/shard_map/ppermute | solution.py:324
  29.5 0.0 collective-permute-done.7
  29.6 0.0 copy-start.1
  29.6 4.3 %first_factor.1 = (f32[128,128]{1,0:T(8,128)S(1)}, f32[128,128]{1,0:T(8,128)S(1)}, f32[128,128]{1,0:T(8,128)S(1)}) custom-call(f32[128,128]{1,0:T(8,128)S(1)} %get-tuple-element.70.a_ref, f32[128,128]{1,0:T(8,128)S(1)} %pad_maximum_fusion.side_ref), custom_call_target="tpu_custom_call" | custom-call | flops 8000000000 | bytes 2097152 | tf_op jit(solution)/shard_map/first_factor/pallas_call | solution.py:195
  33.9 0.0 collective-permute-done.8.rows_other_ref
  33.9 1.4 %collective-permute-done.9 = f32[8,64,128]{2,1,0:T(8,128)} collective-permute-done((f32[8,64,128]{2,1,0:T(8,128)S(1)}, f32[8,64,128]{2,1,0:T(8,128)}, u32[]{:S(2)}, u32[]{:S(2)}) %collective-permute-start.9) | collective-permute-done | bytes 262176 | tf_op jit(solution)/shard_map/ppermute | solution.py:324
  35.3 0.1 collective-permute-start.11
  35.4 1.1 %collective-permute-done.10 = f32[8,64,128]{2,1,0:T(8,128)} collective-permute-done((f32[8,64,128]{2,1,0:T(8,128)S(1)}, f32[8,64,128]{2,1,0:T(8,128)}, u32[]{:S(2)}, u32[]{:S(2)}) %collective-permute-start.10) | collective-permute-done | bytes 262176 | tf_op jit(solution)/shard_map/ppermute | solution.py:324
  36.5 0.1 collective-permute-start.12
  36.6 0.0 copy-done.1
  36.6 6.0 %second_factor.1 = (f32[128,128]{1,0:T(8,128)S(1)}, f32[256,256]{1,0:T(8,128)S(1)}, f32[256,256]{1,0:T(8,128)S(1)}, f32[8,4,128,128]{3,2,1,0:T(8,128)S(1)}) custom-call(f32[128,128]{1,0:T(8,128)S(1)} %get-tuple-element.56.a_ref, f32[128,128]{1,0:T(8,128)S(1)} %get-tuple-element.57.cross_ref, f32[128,128]{1,0:T(8,128)S(1)} %get-tuple-element.59.w0_ref, ...), custom_call_target="tpu_custom_call" | custom-call | flops 8000000000 | bytes 4194304 | tf_op jit(solution)/shard_map/second_factor/pallas_call | solution.py:238
  42.7 0.0 collective-permute-done.11.oa_ref
  42.7 0.0 collective-permute-done.12.ob_ref
  42.7 6.8 %settle.1 = f32[4,128,8,128]{3,2,1,0:T(8,128)} custom-call(f32[128,128]{1,0:T(8,128)S(1)} %get-tuple-element.54.f0_ref, f32[128,128]{1,0:T(8,128)S(1)} %get-tuple-element.60.f1_ref, f32[256,256]{1,0:T(8,128)S(1)} %get-tuple-element.61.w_ref, f32[256,256]{1,0:T(8,128)S(1)} %get-tuple-element.62.mixed_ref, f32[2,128,128]{2,1,0:T(8,128)S(1)} %get-tuple-element.63.first_ref, ...), custom_call_target="tpu_custom_call" | custom-call | flops 4000000000 | bytes 6291456 | tf_op jit(solution)/shard_map/settle/pallas_call | solution.py:311
  (12 shorter events, 0.2 us)
Async XLA Ops:
  0.0 1.6 %copy-start = (f32[4,128,8,128]{3,2,1,0:T(8,128)S(1)}, f32[4,128,8,128]{3,2,1,0:T(8,128)}, u32[]{:S(2)}) copy-start(f32[4,128,8,128]{3,2,1,0:T(8,128)} %matrix_ref.5) | copy-start | bytes 6291460
  2.3 10.0 %collective-permute-start.2 = (f32[8,64,128]{2,1,0:T(8,128)S(1)}, f32[8,64,128]{2,1,0:T(8,128)S(1)}, u32[]{:S(2)}, u32[]{:S(2)}) collective-permute-start(f32[8,64,128]{2,1,0:T(8,128)S(1)} %get-tuple-element.43), channel_id=1, source_target_pairs={{0,8},{4,12},{8,0},{12,4},{16,24},{20,28},{24,16},{28,20},{1,9},{5... | collective-permute-start | bytes 786440 | tf_op jit(solution)/shard_map/ppermute | solution.py:324
  5.4 5.5 %collective-permute-start = (f32[128,128]{1,0:T(8,128)S(1)}, f32[128,128]{1,0:T(8,128)S(1)}, u32[]{:S(2)}, u32[]{:S(2)}) collective-permute-start(f32[128,128]{1,0:T(8,128)S(1)} %corner_block.1), channel_id=1, source_target_pairs={{0,2},{1,3},{2,0},{3,1},{4,6},{5,7},{6,4},{7,5},{8,10},{9,11},{10,... | collective-permute-start | bytes 196616 | tf_op jit(solution)/shard_map/ppermute | solution.py:324
  8.0 7.5 %collective-permute-start.3 = (f32[8,64,128]{2,1,0:T(8,128)S(1)}, f32[8,64,128]{2,1,0:T(8,128)S(1)}, u32[]{:S(2)}, u32[]{:S(2)}) collective-permute-start(f32[8,64,128]{2,1,0:T(8,128)S(1)} %get-tuple-element.44), channel_id=1, source_target_pairs={{0,16},{4,20},{8,24},{12,28},{16,0},{20,4},{24,8},{28,12},{1,17},{... | collective-permute-start | bytes 786440 | tf_op jit(solution)/shard_map/ppermute | solution.py:324
  10.9 4.6 %collective-permute-start.1 = (f32[128,128]{1,0:T(8,128)S(1)}, f32[128,128]{1,0:T(8,128)S(1)}, u32[]{:S(2)}, u32[]{:S(2)}) collective-permute-start(f32[128,128]{1,0:T(8,128)S(1)} %get-tuple-element.73.block_ref), channel_id=1, source_target_pairs={{0,1},{1,0},{2,3},{3,2},{4,5},{5,4},{6,7},{7,6},{8,9},{9,8},{10,11... | collective-permute-start | bytes 196616 | tf_op jit(solution)/shard_map/ppermute | solution.py:324
  15.6 4.7 %collective-permute-start.4 = (f32[192,128]{1,0:T(8,128)S(1)}, f32[192,128]{1,0:T(8,128)S(1)}, u32[]{:S(2)}, u32[]{:S(2)}) collective-permute-start(f32[192,128]{1,0:T(8,128)S(1)} %get-tuple-element.48), channel_id=1, source_target_pairs={{0,8},{4,12},{8,0},{12,4},{16,24},{20,28},{24,16},{28,20},{1,9},{5... | collective-permute-start | bytes 294920 | tf_op jit(solution)/shard_map/ppermute | solution.py:324
  16.2 10.0 %collective-permute-start.6 = (f32[3,128,128]{2,1,0:T(8,128)S(1)}, f32[3,128,128]{2,1,0:T(8,128)S(1)}, u32[]{:S(2)}, u32[]{:S(2)}) collective-permute-start(f32[3,128,128]{2,1,0:T(8,128)S(1)} %get-tuple-element.49), channel_id=1, source_target_pairs={{0,2},{1,3},{2,0},{3,1},{4,6},{5,7},{6,4},{7,5},{8,10},{9,11},{10,... | collective-permute-start | bytes 589832 | tf_op jit(solution)/shard_map/ppermute | solution.py:324
  20.3 5.9 %collective-permute-start.5 = (f32[192,128]{1,0:T(8,128)S(1)}, f32[192,128]{1,0:T(8,128)S(1)}, u32[]{:S(2)}, u32[]{:S(2)}) collective-permute-start(f32[192,128]{1,0:T(8,128)S(1)} %broadcast_select_fusion.6), channel_id=1, source_target_pairs={{0,16},{4,20},{8,24},{12,28},{16,0},{20,4},{24,8},{28,12},{1,17},{... | collective-permute-start | bytes 294920 | tf_op jit(solution)/shard_map/ppermute | solution.py:324
  26.3 3.2 %collective-permute-start.7 = (f32[192,128]{1,0:T(8,128)S(1)}, f32[192,128]{1,0:T(8,128)S(1)}, u32[]{:S(2)}, u32[]{:S(2)}) collective-permute-start(f32[192,128]{1,0:T(8,128)S(1)} %broadcast_select_fusion.7), channel_id=1, source_target_pairs={{0,4},{4,0},{8,12},{12,8},{16,20},{20,16},{24,28},{28,24},{1,5},{5... | collective-permute-start | bytes 294920 | tf_op jit(solution)/shard_map/ppermute | solution.py:324
  26.4 7.5 %collective-permute-start.8 = (f32[3,128,128]{2,1,0:T(8,128)S(1)}, f32[3,128,128]{2,1,0:T(8,128)S(1)}, u32[]{:S(2)}, u32[]{:S(2)}) collective-permute-start(f32[3,128,128]{2,1,0:T(8,128)S(1)} %broadcast_select_fusion.5.rows_ref), channel_id=1, source_target_pairs={{0,1},{1,0},{2,3},{3,2},{4,5},{5,4},{6,7},{7,6},{8,9},{9,8},{10,11... | collective-permute-start | bytes 589832 | tf_op jit(solution)/shard_map/ppermute | solution.py:324
  26.8 8.5 %collective-permute-start.9 = (f32[8,64,128]{2,1,0:T(8,128)S(1)}, f32[8,64,128]{2,1,0:T(8,128)}, u32[]{:S(2)}, u32[]{:S(2)}) collective-permute-start(f32[8,64,128]{2,1,0:T(8,128)S(1)} %broadcast_select_fusion.4), channel_id=1, source_target_pairs={{0,16},{4,20},{8,24},{12,28},{16,0},{20,4},{24,8},{28,12},{1,17},{... | collective-permute-start | bytes 786440 | tf_op jit(solution)/shard_map/ppermute | solution.py:324
  28.3 8.2 %collective-permute-start.10 = (f32[8,64,128]{2,1,0:T(8,128)S(1)}, f32[8,64,128]{2,1,0:T(8,128)}, u32[]{:S(2)}, u32[]{:S(2)}) collective-permute-start(f32[8,64,128]{2,1,0:T(8,128)S(1)} %broadcast_select_fusion.3), channel_id=1, source_target_pairs={{0,8},{4,12},{8,0},{12,4},{16,24},{20,28},{24,16},{28,20},{1,9},{5... | collective-permute-start | bytes 786440 | tf_op jit(solution)/shard_map/ppermute | solution.py:324
  29.6 7.0 %copy-start.1 = (f32[4,128,8,128]{3,2,1,0:T(8,128)S(1)}, f32[4,128,8,128]{3,2,1,0:T(8,128)}, u32[]{:S(2)}) copy-start(f32[4,128,8,128]{3,2,1,0:T(8,128)} %matrix_ref.5) | copy-start | bytes 6291460
  35.3 7.4 %collective-permute-start.11 = (f32[8,64,128]{2,1,0:T(8,128)S(1)}, f32[8,64,128]{2,1,0:T(8,128)S(1)}, u32[]{:S(2)}, u32[]{:S(2)}) collective-permute-start(f32[8,64,128]{2,1,0:T(8,128)S(1)} %broadcast_select_fusion.2.ha_ref), channel_id=1, source_target_pairs={{0,4},{4,0},{8,12},{12,8},{16,20},{20,16},{24,28},{28,24},{1,5},{5... | collective-permute-start | bytes 786440 | tf_op jit(solution)/shard_map/ppermute | solution.py:324
  36.5 6.1 %collective-permute-start.12 = (f32[8,64,128]{2,1,0:T(8,128)S(1)}, f32[8,64,128]{2,1,0:T(8,128)S(1)}, u32[]{:S(2)}, u32[]{:S(2)}) collective-permute-start(f32[8,64,128]{2,1,0:T(8,128)S(1)} %broadcast_select_fusion.1.hb_ref), channel_id=1, source_target_pairs={{0,4},{4,0},{8,12},{12,8},{16,20},{20,16},{24,28},{28,24},{1,5},{5... | collective-permute-start | bytes 786440 | tf_op jit(solution)/shard_map/ppermute | solution.py:324

commit v19 on v18

--- a/solution.py
+++ b/solution.py
@@ -380,14 +380,18 @@
     moved = exchange(pair, "row", 1 << first_bit, n_row)
     column_moved = exchange(column, "col", 1 << col_bits[0], n_col)
     pair = jnp.where(bit_set(grid_row, first_bit), moved, pair)
+    pair, ha, hb = after(pair, ha, hb)
     moved = exchange(pair, "row", 1 << row_bits[1], n_row)
+    ha_moved = exchange(ha, "row", 1 << row_bits[1], n_row)
+    hb_moved = exchange(hb, "row", 1 << row_bits[-2], n_row)
     rows = jnp.where(bit_set(grid_col, col_bits[0]), column_moved, column)
-    moved, pair, rows, ha, hb = after(moved, pair, rows, ha, hb)
+    moved, pair, rows = after(moved, pair, rows)
     pair = jnp.where(bit_set(grid_row, row_bits[1]), moved, pair)
     pair = spread(pair, "row", grid_row, n_row, row_bits[2:])
-    ha_moved = exchange(ha, "row", 1 << row_bits[1], n_row)
-    hb_moved = exchange(hb, "row", 1 << row_bits[-2], n_row)
     other = exchange(pair, "row", 1, n_row)
+    ha = jnp.where(bit_set(grid_row, row_bits[1]), ha_moved, ha)
+    hb = jnp.where(bit_set(grid_row, row_bits[-2]), hb_moved, hb)
+    other, pair, ha, hb = after(other, pair, ha, hb)
 
     n = block.shape[0]
     a00 = jnp.where(odd, other[:n], pair[:n])
@@ -397,10 +401,8 @@
 
     rows = spread(rows, "col", grid_col, n_col, col_bits[1:])
     rows_other = exchange(rows, "col", 1, n_col)
-    w0, row_then = after(w0, grid_row)
-    ha = jnp.where(bit_set(row_then, row_bits[1]), ha_moved, ha)
+    w0, row_then, ha, hb = after(w0, grid_row, ha, hb)
     ha = spread(ha, "row", row_then, n_row, row_bits[2:])
-    hb = jnp.where(bit_set(row_then, row_bits[-2]), hb_moved, hb)
     hb = spread(hb, "row", row_then, n_row, row_bits[:-2][::-1])
     oa = exchange(ha, "row", 1, n_row)
     ob = exchange(hb, "row", 1, n_row)

time: 49.9 us -> 46.7 us (0.936)
  waiting for transfers between devices: 13.3 us -> 11.5 us
  starting transfers between devices: 16.2 us -> 15.2 us
    ppermute x13, waiting for transfers between devices: 13.3 us -> 11.5 us  [exchange(): return lax.ppermute(value, axis, [(i, i ^ mask) for i in range(size)])]
    ppermute x13, starting transfers between devices: 16.2 us -> 15.2 us  [exchange(): return lax.ppermute(value, axis, [(i, i ^ mask) for i in range(size)])]
  transfers between devices with their start and end apart: 13 -> 13, of which waited for: 6 -> 6; matrix products, arithmetic and copies ran while one was open for 0% -> 0% of each run, Pallas kernels for 21% -> 22%
where the time goes in v19:
time: 46.7 us; the launch traced here: 46.6 us
  Pallas kernels  17.9 us (38%)
  starting transfers between devices  15.2 us (33%)
  waiting for transfers between devices  11.5 us (25%)
  local copies, waits for them, and re-layouts  1.6 us (3%)
    ppermute x13, starting transfers between devices, exchange(): return lax.ppermute(value, axis, [(i, i ^ mask) for i in range(size)])  15.2 us
    ppermute x13, waiting for transfers between devices, exchange(): return lax.ppermute(value, axis, [(i, i ^ mask) for i in range(size)])  11.5 us
    pallas_call x1, Pallas kernels, settle(): pl.pallas_call(settle_kernel, out_shape=jax.ShapeDtypeStruct((local_rows,...  6.77 us
    pallas_call x1, Pallas kernels, second_factor(): pl.pallas_call(second_factor_kernel, out_shape=[square, double, double, b...  6.03 us
    pallas_call x1, Pallas kernels, first_factor(): pl.pallas_call(first_factor_kernel, out_shape=[square] * 3, in_specs=[VME...  4.26 us
    unnamed x4, local copies, waits for them, and re-layouts  1.6 us
  transfers between devices with their start and end apart: 13, of which 6 were waited for; matrix products, arithmetic and copies ran while one was open for 0% of the time, Pallas kernels for 22%

profile of v19, /device:TPU:0, one launch (start us, length us, event | category | flops | bytes accessed | tf_op | source)
XLA Modules:
  0.0 46.6 jit_solution(706677797424448599)
XLA Ops:
  0.0 0.0 copy-start
  0.0 1.6 %copy-done = f32[4,128,8,128]{3,2,1,0:T(8,128)S(1)} copy-done((f32[4,128,8,128]{3,2,1,0:T(8,128)S(1)}, f32[4,128,8,128]{3,2,1,0:T(8,128)}, u32[]{:S(2)}) %copy-start) | copy-done | bytes 2097176
  1.6 0.7 %panels.1 = (f32[3,128,128]{2,1,0:T(8,128)S(1)}, f32[8,64,128]{2,1,0:T(8,128)S(1)}, f32[8,64,128]{2,1,0:T(8,128)S(1)}) custom-call(f32[4,128,8,128]{3,2,1,0:T(8,128)S(1)} %copy-done), custom_call_target="tpu_custom_call" | custom-call | bytes 4194304 | tf_op jit(solution)/shard_map/panels/pallas_call | solution.py:146
  2.3 3.0 %collective-permute-start.2 = (f32[8,64,128]{2,1,0:T(8,128)S(1)}, f32[8,64,128]{2,1,0:T(8,128)S(1)}, u32[]{:S(2)}, u32[]{:S(2)}) collective-permute-start(f32[8,64,128]{2,1,0:T(8,128)S(1)} %get-tuple-element.49), channel_id=1, source_target_pairs={{0,8},{4,12},{8,0},{12,4},{16,24},{20,28},{24,16},{28,20},{1,9},{5... | collective-permute-start | bytes 786440 | tf_op jit(solution)/shard_map/ppermute | solution.py:324
  5.3 0.1 corner_block.1
  5.4 2.7 %collective-permute-start = (f32[128,128]{1,0:T(8,128)S(1)}, f32[128,128]{1,0:T(8,128)S(1)}, u32[]{:S(2)}, u32[]{:S(2)}) collective-permute-start(f32[128,128]{1,0:T(8,128)S(1)} %corner_block.1), channel_id=1, source_target_pairs={{0,2},{1,3},{2,0},{3,1},{4,6},{5,7},{6,4},{7,5},{8,10},{9,11},{10,... | collective-permute-start | bytes 196616 | tf_op jit(solution)/shard_map/ppermute | solution.py:324
  8.0 1.5 %collective-permute-start.3 = (f32[8,64,128]{2,1,0:T(8,128)S(1)}, f32[8,64,128]{2,1,0:T(8,128)S(1)}, u32[]{:S(2)}, u32[]{:S(2)}) collective-permute-start(f32[8,64,128]{2,1,0:T(8,128)S(1)} %get-tuple-element.50), channel_id=1, source_target_pairs={{0,16},{4,20},{8,24},{12,28},{16,0},{20,4},{24,8},{28,12},{1,17},{... | collective-permute-start | bytes 786440 | tf_op jit(solution)/shard_map/ppermute | solution.py:324
  9.5 1.4 %collective-permute-done = f32[128,128]{1,0:T(8,128)S(1)} collective-permute-done((f32[128,128]{1,0:T(8,128)S(1)}, f32[128,128]{1,0:T(8,128)S(1)}, u32[]{:S(2)}, u32[]{:S(2)}) %collective-permute-start) | collective-permute-done | bytes 65568 | tf_op jit(solution)/shard_map/ppermute | solution.py:324
  10.9 1.3 %collective-permute-start.1 = (f32[128,128]{1,0:T(8,128)S(1)}, f32[128,128]{1,0:T(8,128)S(1)}, u32[]{:S(2)}, u32[]{:S(2)}) collective-permute-start(f32[128,128]{1,0:T(8,128)S(1)} %get-tuple-element.85.block_ref), channel_id=1, source_target_pairs={{0,1},{1,0},{2,3},{3,2},{4,5},{5,4},{6,7},{7,6},{8,9},{9,8},{10,11... | collective-permute-start | bytes 196616 | tf_op jit(solution)/shard_map/ppermute | solution.py:324
  12.2 0.0 collective-permute-done.2
  12.3 3.2 %collective-permute-done.3 = f32[8,64,128]{2,1,0:T(8,128)S(1)} collective-permute-done((f32[8,64,128]{2,1,0:T(8,128)S(1)}, f32[8,64,128]{2,1,0:T(8,128)S(1)}, u32[]{:S(2)}, u32[]{:S(2)}) %collective-permute-start.3) | collective-permute-done | bytes 262176 | tf_op jit(solution)/shard_map/ppermute | solution.py:324
  15.5 0.0 collective-permute-done.1.across_ref
  15.5 0.1 pack.1
  15.6 0.6 %collective-permute-start.4 = (f32[192,128]{1,0:T(8,128)S(1)}, f32[192,128]{1,0:T(8,128)S(1)}, u32[]{:S(2)}, u32[]{:S(2)}) collective-permute-start(f32[192,128]{1,0:T(8,128)S(1)} %get-tuple-element.54), channel_id=1, source_target_pairs={{0,8},{4,12},{8,0},{12,4},{16,24},{20,28},{24,16},{28,20},{1,9},{5... | collective-permute-start | bytes 294920 | tf_op jit(solution)/shard_map/ppermute | solution.py:324
  16.2 2.1 %collective-permute-start.6 = (f32[3,128,128]{2,1,0:T(8,128)S(1)}, f32[3,128,128]{2,1,0:T(8,128)S(1)}, u32[]{:S(2)}, u32[]{:S(2)}) collective-permute-start(f32[3,128,128]{2,1,0:T(8,128)S(1)} %get-tuple-element.58), channel_id=1, source_target_pairs={{0,2},{1,3},{2,0},{3,1},{4,6},{5,7},{6,4},{7,5},{8,10},{9,11},{10,... | collective-permute-start | bytes 589832 | tf_op jit(solution)/shard_map/ppermute | solution.py:324
  18.4 2.0 %collective-permute-done.4 = f32[192,128]{1,0:T(8,128)S(1)} collective-permute-done((f32[192,128]{1,0:T(8,128)S(1)}, f32[192,128]{1,0:T(8,128)S(1)}, u32[]{:S(2)}, u32[]{:S(2)}) %collective-permute-start.4) | collective-permute-done | bytes 98336 | tf_op jit(solution)/shard_map/ppermute | solution.py:324
  20.3 1.6 %collective-permute-start.5 = (f32[192,128]{1,0:T(8,128)S(1)}, f32[192,128]{1,0:T(8,128)S(1)}, u32[]{:S(2)}, u32[]{:S(2)}) collective-permute-start(f32[192,128]{1,0:T(8,128)S(1)} %broadcast_select_fusion.6), channel_id=1, source_target_pairs={{0,16},{4,20},{8,24},{12,28},{16,0},{20,4},{24,8},{28,12},{1,17},{... | collective-permute-start | bytes 294920 | tf_op jit(solution)/shard_map/ppermute | solution.py:324
  21.9 0.5 %collective-permute-start.8 = (f32[8,64,128]{2,1,0:T(8,128)S(1)}, f32[8,64,128]{2,1,0:T(8,128)S(1)}, u32[]{:S(2)}, u32[]{:S(2)}) collective-permute-start(f32[8,64,128]{2,1,0:T(8,128)S(1)} %broadcast_select_fusion.4), channel_id=1, source_target_pairs={{0,16},{4,20},{8,24},{12,28},{16,0},{20,4},{24,8},{28,12},{1,17},{... | collective-permute-start | bytes 786440 | tf_op jit(solution)/shard_map/ppermute | solution.py:324
  22.4 0.5 %collective-permute-start.9 = (f32[8,64,128]{2,1,0:T(8,128)S(1)}, f32[8,64,128]{2,1,0:T(8,128)S(1)}, u32[]{:S(2)}, u32[]{:S(2)}) collective-permute-start(f32[8,64,128]{2,1,0:T(8,128)S(1)} %broadcast_select_fusion.2), channel_id=1, source_target_pairs={{0,8},{4,12},{8,0},{12,4},{16,24},{20,28},{24,16},{28,20},{1,9},{5... | collective-permute-start | bytes 786440 | tf_op jit(solution)/shard_map/ppermute | solution.py:324
  23.0 3.3 %collective-permute-done.6 = f32[3,128,128]{2,1,0:T(8,128)S(1)} collective-permute-done((f32[3,128,128]{2,1,0:T(8,128)S(1)}, f32[3,128,128]{2,1,0:T(8,128)S(1)}, u32[]{:S(2)}, u32[]{:S(2)}) %collective-permute-start.6) | collective-permute-done | bytes 196640 | tf_op jit(solution)/shard_map/ppermute | solution.py:324
  26.3 0.0 collective-permute-done.5
  26.3 0.1 collective-permute-start.7
  26.4 0.7 %collective-permute-start.10 = (f32[3,128,128]{2,1,0:T(8,128)S(1)}, f32[3,128,128]{2,1,0:T(8,128)S(1)}, u32[]{:S(2)}, u32[]{:S(2)}) collective-permute-start(f32[3,128,128]{2,1,0:T(8,128)S(1)} %broadcast_select_fusion.5.rows_ref), channel_id=1, source_target_pairs={{0,1},{1,0},{2,3},{3,2},{4,5},{5,4},{6,7},{7,6},{8,9},{9,8},{10,11... | collective-permute-start | bytes 589832 | tf_op jit(solution)/shard_map/ppermute | solution.py:324
  27.0 1.3 %collective-permute-done.8 = f32[8,64,128]{2,1,0:T(8,128)S(1)} collective-permute-done((f32[8,64,128]{2,1,0:T(8,128)S(1)}, f32[8,64,128]{2,1,0:T(8,128)S(1)}, u32[]{:S(2)}, u32[]{:S(2)}) %collective-permute-start.8) | collective-permute-done | bytes 262176 | tf_op jit(solution)/shard_map/ppermute | solution.py:324
  28.3 0.5 %collective-permute-done.9 = f32[8,64,128]{2,1,0:T(8,128)S(1)} collective-permute-done((f32[8,64,128]{2,1,0:T(8,128)S(1)}, f32[8,64,128]{2,1,0:T(8,128)S(1)}, u32[]{:S(2)}, u32[]{:S(2)}) %collective-permute-start.9) | collective-permute-done | bytes 262176 | tf_op jit(solution)/shard_map/ppermute | solution.py:324
  28.8 0.0 collective-permute-done.7
  28.9 0.0 copy-start.1
  28.9 4.3 %first_factor.1 = (f32[128,128]{1,0:T(8,128)S(1)}, f32[128,128]{1,0:T(8,128)S(1)}, f32[128,128]{1,0:T(8,128)S(1)}) custom-call(f32[128,128]{1,0:T(8,128)S(1)} %get-tuple-element.82.a_ref, f32[128,128]{1,0:T(8,128)S(1)} %pad_maximum_fusion.side_ref), custom_call_target="tpu_custom_call" | custom-call | flops 8000000000 | bytes 2097152 | tf_op jit(solution)/shard_map/first_factor/pallas_call | solution.py:195
  33.2 0.1 collective-permute-start.11
  33.3 0.5 %collective-permute-start.12 = (f32[8,64,128]{2,1,0:T(8,128)S(1)}, f32[8,64,128]{2,1,0:T(8,128)S(1)}, u32[]{:S(2)}, u32[]{:S(2)}) collective-permute-start(f32[8,64,128]{2,1,0:T(8,128)S(1)} %broadcast_select_fusion.3.hb_ref), channel_id=1, source_target_pairs={{0,4},{4,0},{8,12},{12,8},{16,20},{20,16},{24,28},{28,24},{1,5},{5... | collective-permute-start | bytes 786440 | tf_op jit(solution)/shard_map/ppermute | solution.py:324
  33.8 0.0 collective-permute-done.10.rows_other_ref
  33.8 0.0 copy-done.1
  33.8 6.0 %second_factor.1 = (f32[128,128]{1,0:T(8,128)S(1)}, f32[256,256]{1,0:T(8,128)S(1)}, f32[256,256]{1,0:T(8,128)S(1)}, f32[8,4,128,128]{3,2,1,0:T(8,128)S(1)}) custom-call(f32[128,128]{1,0:T(8,128)S(1)} %get-tuple-element.67.a_ref, f32[128,128]{1,0:T(8,128)S(1)} %get-tuple-element.68.cross_ref, f32[128,128]{1,0:T(8,128)S(1)} %get-tuple-element.72.w0_ref, ...), custom_call_target="tpu_custom_call" | custom-call | flops 8000000000 | bytes 4194304 | tf_op jit(solution)/shard_map/second_factor/pallas_call | solution.py:238
  39.8 0.0 collective-permute-done.11.oa_ref
  39.8 0.0 collective-permute-done.12.ob_ref
  39.8 6.8 %settle.1 = f32[4,128,8,128]{3,2,1,0:T(8,128)} custom-call(f32[128,128]{1,0:T(8,128)S(1)} %get-tuple-element.65.f0_ref, f32[128,128]{1,0:T(8,128)S(1)} %get-tuple-element.73.f1_ref, f32[256,256]{1,0:T(8,128)S(1)} %get-tuple-element.74.w_ref, f32[256,256]{1,0:T(8,128)S(1)} %get-tuple-element.75.mixed_ref, f32[2,128,128]{2,1,0:T(8,128)S(1)} %get-tuple-element.76.first_ref, ...), custom_call_target="tpu_custom_call" | custom-call | flops 4000000000 | bytes 6291456 | tf_op jit(solution)/shard_map/settle/pallas_call | solution.py:311
  (12 shorter events, 0.2 us)
Async XLA Ops:
  0.0 1.6 %copy-start = (f32[4,128,8,128]{3,2,1,0:T(8,128)S(1)}, f32[4,128,8,128]{3,2,1,0:T(8,128)}, u32[]{:S(2)}) copy-start(f32[4,128,8,128]{3,2,1,0:T(8,128)} %matrix_ref.5) | copy-start | bytes 6291460
  2.3 10.0 %collective-permute-start.2 = (f32[8,64,128]{2,1,0:T(8,128)S(1)}, f32[8,64,128]{2,1,0:T(8,128)S(1)}, u32[]{:S(2)}, u32[]{:S(2)}) collective-permute-start(f32[8,64,128]{2,1,0:T(8,128)S(1)} %get-tuple-element.49), channel_id=1, source_target_pairs={{0,8},{4,12},{8,0},{12,4},{16,24},{20,28},{24,16},{28,20},{1,9},{5... | collective-permute-start | bytes 786440 | tf_op jit(solution)/shard_map/ppermute | solution.py:324
  5.4 5.5 %collective-permute-start = (f32[128,128]{1,0:T(8,128)S(1)}, f32[128,128]{1,0:T(8,128)S(1)}, u32[]{:S(2)}, u32[]{:S(2)}) collective-permute-start(f32[128,128]{1,0:T(8,128)S(1)} %corner_block.1), channel_id=1, source_target_pairs={{0,2},{1,3},{2,0},{3,1},{4,6},{5,7},{6,4},{7,5},{8,10},{9,11},{10,... | collective-permute-start | bytes 196616 | tf_op jit(solution)/shard_map/ppermute | solution.py:324
  8.0 7.5 %collective-permute-start.3 = (f32[8,64,128]{2,1,0:T(8,128)S(1)}, f32[8,64,128]{2,1,0:T(8,128)S(1)}, u32[]{:S(2)}, u32[]{:S(2)}) collective-permute-start(f32[8,64,128]{2,1,0:T(8,128)S(1)} %get-tuple-element.50), channel_id=1, source_target_pairs={{0,16},{4,20},{8,24},{12,28},{16,0},{20,4},{24,8},{28,12},{1,17},{... | collective-permute-start | bytes 786440 | tf_op jit(solution)/shard_map/ppermute | solution.py:324
  10.9 4.6 %collective-permute-start.1 = (f32[128,128]{1,0:T(8,128)S(1)}, f32[128,128]{1,0:T(8,128)S(1)}, u32[]{:S(2)}, u32[]{:S(2)}) collective-permute-start(f32[128,128]{1,0:T(8,128)S(1)} %get-tuple-element.85.block_ref), channel_id=1, source_target_pairs={{0,1},{1,0},{2,3},{3,2},{4,5},{5,4},{6,7},{7,6},{8,9},{9,8},{10,11... | collective-permute-start | bytes 196616 | tf_op jit(solution)/shard_map/ppermute | solution.py:324
  15.6 4.7 %collective-permute-start.4 = (f32[192,128]{1,0:T(8,128)S(1)}, f32[192,128]{1,0:T(8,128)S(1)}, u32[]{:S(2)}, u32[]{:S(2)}) collective-permute-start(f32[192,128]{1,0:T(8,128)S(1)} %get-tuple-element.54), channel_id=1, source_target_pairs={{0,8},{4,12},{8,0},{12,4},{16,24},{20,28},{24,16},{28,20},{1,9},{5... | collective-permute-start | bytes 294920 | tf_op jit(solution)/shard_map/ppermute | solution.py:324
  16.2 10.0 %collective-permute-start.6 = (f32[3,128,128]{2,1,0:T(8,128)S(1)}, f32[3,128,128]{2,1,0:T(8,128)S(1)}, u32[]{:S(2)}, u32[]{:S(2)}) collective-permute-start(f32[3,128,128]{2,1,0:T(8,128)S(1)} %get-tuple-element.58), channel_id=1, source_target_pairs={{0,2},{1,3},{2,0},{3,1},{4,6},{5,7},{6,4},{7,5},{8,10},{9,11},{10,... | collective-permute-start | bytes 589832 | tf_op jit(solution)/shard_map/ppermute | solution.py:324
  20.3 5.9 %collective-permute-start.5 = (f32[192,128]{1,0:T(8,128)S(1)}, f32[192,128]{1,0:T(8,128)S(1)}, u32[]{:S(2)}, u32[]{:S(2)}) collective-permute-start(f32[192,128]{1,0:T(8,128)S(1)} %broadcast_select_fusion.6), channel_id=1, source_target_pairs={{0,16},{4,20},{8,24},{12,28},{16,0},{20,4},{24,8},{28,12},{1,17},{... | collective-permute-start | bytes 294920 | tf_op jit(solution)/shard_map/ppermute | solution.py:324
  21.9 6.4 %collective-permute-start.8 = (f32[8,64,128]{2,1,0:T(8,128)S(1)}, f32[8,64,128]{2,1,0:T(8,128)S(1)}, u32[]{:S(2)}, u32[]{:S(2)}) collective-permute-start(f32[8,64,128]{2,1,0:T(8,128)S(1)} %broadcast_select_fusion.4), channel_id=1, source_target_pairs={{0,16},{4,20},{8,24},{12,28},{16,0},{20,4},{24,8},{28,12},{1,17},{... | collective-permute-start | bytes 786440 | tf_op jit(solution)/shard_map/ppermute | solution.py:324
  22.4 6.4 %collective-permute-start.9 = (f32[8,64,128]{2,1,0:T(8,128)S(1)}, f32[8,64,128]{2,1,0:T(8,128)S(1)}, u32[]{:S(2)}, u32[]{:S(2)}) collective-permute-start(f32[8,64,128]{2,1,0:T(8,128)S(1)} %broadcast_select_fusion.2), channel_id=1, source_target_pairs={{0,8},{4,12},{8,0},{12,4},{16,24},{20,28},{24,16},{28,20},{1,9},{5... | collective-permute-start | bytes 786440 | tf_op jit(solution)/shard_map/ppermute | solution.py:324
  26.3 2.6 %collective-permute-start.7 = (f32[192,128]{1,0:T(8,128)S(1)}, f32[192,128]{1,0:T(8,128)S(1)}, u32[]{:S(2)}, u32[]{:S(2)}) collective-permute-start(f32[192,128]{1,0:T(8,128)S(1)} %broadcast_select_fusion.7), channel_id=1, source_target_pairs={{0,4},{4,0},{8,12},{12,8},{16,20},{20,16},{24,28},{28,24},{1,5},{5... | collective-permute-start | bytes 294920 | tf_op jit(solution)/shard_map/ppermute | solution.py:324
  26.4 7.4 %collective-permute-start.10 = (f32[3,128,128]{2,1,0:T(8,128)S(1)}, f32[3,128,128]{2,1,0:T(8,128)S(1)}, u32[]{:S(2)}, u32[]{:S(2)}) collective-permute-start(f32[3,128,128]{2,1,0:T(8,128)S(1)} %broadcast_select_fusion.5.rows_ref), channel_id=1, source_target_pairs={{0,1},{1,0},{2,3},{3,2},{4,5},{5,4},{6,7},{7,6},{8,9},{9,8},{10,11... | collective-permute-start | bytes 589832 | tf_op jit(solution)/shard_map/ppermute | solution.py:324
  28.9 4.8 %copy-start.1 = (f32[4,128,8,128]{3,2,1,0:T(8,128)S(1)}, f32[4,128,8,128]{3,2,1,0:T(8,128)}, u32[]{:S(2)}) copy-start(f32[4,128,8,128]{3,2,1,0:T(8,128)} %matrix_ref.5) | copy-start | bytes 6291460
  33.2 6.6 %collective-permute-start.11 = (f32[8,64,128]{2,1,0:T(8,128)S(1)}, f32[8,64,128]{2,1,0:T(8,128)S(1)}, u32[]{:S(2)}, u32[]{:S(2)}) collective-permute-start(f32[8,64,128]{2,1,0:T(8,128)S(1)} %broadcast_select_fusion.1.ha_ref), channel_id=1, source_target_pairs={{0,4},{4,0},{8,12},{12,8},{16,20},{20,16},{24,28},{28,24},{1,5},{5... | collective-permute-start | bytes 786440 | tf_op jit(solution)/shard_map/ppermute | solution.py:324
  33.3 6.6 %collective-permute-start.12 = (f32[8,64,128]{2,1,0:T(8,128)S(1)}, f32[8,64,128]{2,1,0:T(8,128)S(1)}, u32[]{:S(2)}, u32[]{:S(2)}) collective-permute-start(f32[8,64,128]{2,1,0:T(8,128)S(1)} %broadcast_select_fusion.3.hb_ref), channel_id=1, source_target_pairs={{0,4},{4,0},{8,12},{12,8},{16,20},{20,16},{24,28},{28,24},{1,5},{5... | collective-permute-start | bytes 786440 | tf_op jit(solution)/shard_map/ppermute | solution.py:324

commit v20 on v19

--- a/solution.py
+++ b/solution.py
@@ -26,11 +26,33 @@
     return lax.dot_general(lhs, rhs, (((0,), (0,)), ((), ())), preferred_element_type=jnp.float32)
 
 
+def wide(a):
+    a = parts(a)
+    return jnp.concatenate([a[2], a[0], a[1], a[1], a[0], a[0]], axis=1)
+
+
+def tall(b):
+    b = parts(b)
+    return jnp.concatenate([b[0], b[2], b[1], b[0], b[1], b[0]], axis=0)
+
+
+def times(a, b):
+    return jnp.dot(a, b, preferred_element_type=jnp.float32)
+
+
+def panel_rows(panel, first_ref, rows_ref, rows_other_ref):
+    n = rows_ref.shape[-1]
+    flat = rows_ref.shape[0] * n
+    here = lax.rem(lax.axis_index("col"), 2) == panel
+    rest = jnp.where(here, rows_ref[...].reshape(flat, n), rows_other_ref[...].reshape(flat, n))
+    return jnp.concatenate([first_ref[panel], rest], axis=0)
+
+
 def full(row):
     return jnp.broadcast_to(row, (SUB, row.shape[-1]))
 
 
-def eliminate(s, extra, scratch):
+def eliminate(s, extra, scratch, beside=()):
     n = s.shape[0]
     groups = n // SUB
     sub = lax.broadcasted_iota(jnp.int32, (SUB, n), 0)
@@ -83,6 +105,8 @@
             for m in sides:
                 part = update[until * SUB:, m * n:(m + 1) * n]
                 scratch[m][until:] = scratch[m][until:] - part.reshape(groups - until, SUB, n)
+        if g < len(beside):
+            beside[g]()
     upper, inverse, product = [ref[...].reshape(n, n) for ref in scratch]
     return upper.T, inverse, product
 
@@ -204,82 +228,115 @@
     )(a, side)
 
 
-def second_factor_kernel(a_ref, cross_ref, w0_ref, matrix_ref, f_ref, w_ref, mixed_ref, blocks_ref, *scratch):
+def second_factor_kernel(a_ref, cross_ref, w0_ref, first_ref, rows_ref, rows_other_ref, ha_ref, hb_ref, oa_ref, ob_ref, matrix_ref,
+                         f_ref, low_ref, mixed_ref, solved_ref, blocks_ref, left, right, sems, *scratch):
     n = w0_ref.shape[0]
     local_cols = matrix_ref.shape[2]
-    sems = scratch[-1]
+    local_rows = matrix_ref.shape[0]
     copies = [pltpu.make_async_copy(matrix_ref.at[:, :, j, :], blocks_ref.at[j], sems.at[j]) for j in range(local_cols)]
     for copy in copies:
         copy.start()
     odd = is_odd_row()
     w0 = w0_ref[...]
     cross = cross_ref[...]
+
+    def solve_rows():
+        solved = times(wide(panel_rows(0, first_ref, rows_ref, rows_other_ref)), tall(w0.T))
+        solved_ref[...] = solved
+        left[...] = wide(solved)
+
+    def solve_top(j):
+        def step():
+            top = jnp.concatenate([
+                jnp.concatenate([jnp.where(odd, oa_ref[b], ha_ref[b]), jnp.where(odd, ob_ref[b], hb_ref[b])], axis=0)
+                for b in (j, j + 1)], axis=1)
+            right[...] = tall(times(wide(w0), tall(top)))
+        return step
+
+    def update(j, i):
+        def step():
+            if i == 0:
+                copies[j].wait()
+                copies[j + 1].wait()
+            change = times(left[i * n:(i + 2) * n], right[...])
+            for b in range(2):
+                part = change[:, b * n:(b + 1) * n].reshape(2, n, n)
+                blocks_ref[j + b, i:i + 2] = blocks_ref[j + b, i:i + 2] - part
+        return step
+
+    steps = [solve_rows]
+    for j in range(0, local_cols, 2):
+        steps.append(solve_top(j))
+        steps.extend(update(j, i) for i in range(0, local_rows, 2))
+
     both = dot_over_rows(cross, jnp.concatenate([cross, w0], axis=1))
-    f1, w1, w10 = eliminate(a_ref[...] - both[:, :n], -both[:, n:], scratch[:-1])
+    groups = n // SUB
+    each = -(-len(steps) // groups)
+
+    def several(some):
+        def run():
+            for step in some:
+                step()
+        return run
+
+    beside = [several(steps[at:at + each]) for at in range(0, len(steps), each)]
+    f1, w1, w10 = eliminate(a_ref[...] - both[:, :n], -both[:, n:], scratch, beside)
     f_ref[...] = f1
-    zero = jnp.zeros((n, n), jnp.float32)
-    w_ref[:n, :n] = w0
-    w_ref[:n, n:] = zero
-    w_ref[n:, :n] = w10
-    w_ref[n:, n:] = w1
-    mixed_ref[:n, :n] = jnp.where(odd, zero, w0)
-    mixed_ref[:n, n:] = jnp.where(odd, w0, zero)
-    mixed_ref[n:, :n] = jnp.where(odd, w1, w10)
-    mixed_ref[n:, n:] = jnp.where(odd, w10, w1)
-    for copy in copies:
-        copy.wait()
-
-
-def second_factor(a, cross, w0, matrix):
+    low_ref[:, :n] = w10
+    low_ref[:, n:] = w1
+    mixed_ref[:, :n] = jnp.where(odd, w1, w10)
+    mixed_ref[:, n:] = jnp.where(odd, w10, w1)
+
+
+def second_factor(a, cross, w0, first_rows, rows, rows_other, ha, hb, oa, ob, matrix):
     local_rows, n, local_cols, _ = matrix.shape
     square = jax.ShapeDtypeStruct((n, n), jnp.float32)
-    double = jax.ShapeDtypeStruct((2 * n, 2 * n), jnp.float32)
+    half = jax.ShapeDtypeStruct((n, 2 * n), jnp.float32)
+    solved = jax.ShapeDtypeStruct((local_rows * n, n), jnp.float32)
     blocks = jax.ShapeDtypeStruct((local_cols, local_rows, n, n), jnp.float32)
     return pl.pallas_call(
         second_factor_kernel,
-        out_shape=[square, double, double, blocks],
-        in_specs=[VMEM] * 3 + [HBM],
-        out_specs=[VMEM] * 4,
-        scratch_shapes=elimination_scratch(n) + [pltpu.SemaphoreType.DMA((local_cols,))],
-        compiler_params=pltpu.CompilerParams(vmem_limit_bytes=12 * MIB),
+        out_shape=[square, half, half, solved, blocks],
+        in_specs=[VMEM] * 10 + [HBM],
+        out_specs=[VMEM] * 5,
+        scratch_shapes=[
+            pltpu.VMEM((local_rows * n, 6 * n), jnp.bfloat16),
+            pltpu.VMEM((6 * n, 2 * n), jnp.bfloat16),
+            pltpu.SemaphoreType.DMA((local_cols,)),
+        ] + elimination_scratch(n),
+        compiler_params=pltpu.CompilerParams(vmem_limit_bytes=20 * MIB),
         cost_estimate=estimate(8 * 10**9, 4 * MIB),
         name="second_factor",
-    )(a, cross, w0, matrix)
-
-
-def settle_kernel(f0_ref, f1_ref, w_ref, mixed_ref, first_ref, rows_ref, rows_other_ref, ha_ref, hb_ref, oa_ref, ob_ref,
+    )(a, cross, w0, first_rows, rows, rows_other, ha, hb, oa, ob, matrix)
+
+
+def settle_kernel(f0_ref, f1_ref, low_ref, mixed_ref, solved_ref, first_ref, rows_ref, rows_other_ref, ha_ref, hb_ref, oa_ref, ob_ref,
                   blocks_ref, out_ref, result, sems):
     grid_row = lax.axis_index("row")
     grid_col = lax.axis_index("col")
     n = f0_ref.shape[0]
     local_cols, local_rows, _, _ = blocks_ref.shape
-    flat = (local_rows - 1) * n
-    own = rows_ref[...].reshape(flat, n)
-    other = rows_other_ref[...].reshape(flat, n)
-    swapped = lax.rem(grid_col, 2) == 1
-    rows = jnp.concatenate([
-        jnp.concatenate([first_ref[0], jnp.where(swapped, other, own)], axis=0),
-        jnp.concatenate([first_ref[1], jnp.where(swapped, own, other)], axis=0)], axis=1)
-    solved = dot_parts(stacked(rows), parts(w_ref[...]), ((1,), (1,)))
-    left = stacked(solved)
+    rows = jnp.concatenate([panel_rows(p, first_ref, rows_ref, rows_other_ref) for p in range(2)], axis=1)
+    solved = dot_parts(stacked(rows), parts(low_ref[...]), ((1,), (1,)))
+    left = wide(solved)
     mixed = stacked(mixed_ref[...])
     copies = []
     for j in range(0, local_cols, 2):
         pair = (j, j + 1)
         tops = jnp.concatenate(
             [jnp.concatenate([ha_ref[b], hb_ref[b], oa_ref[b], ob_ref[b]], axis=0) for b in pair], axis=1)
-        update = dot_parts(left, parts(dot_parts(mixed, parts(tops))))
+        update = times(left, tall(dot_parts(mixed, parts(tops))))
         for b in pair:
             part = update[:, (b - j) * n:(b - j + 1) * n].reshape(local_rows, n, n)
             result[b] = blocks_ref[b] - part
         if j == 0:
             @pl.when(grid_col == 0)
             def _():
-                result[0] = solved[:, :n].reshape(local_rows, n, n)
+                result[0] = solved_ref[...].reshape(local_rows, n, n)
 
             @pl.when(grid_col == 1)
             def _():
-                result[0] = solved[:, n:].reshape(local_rows, n, n)
+                result[0] = solved.reshape(local_rows, n, n)
 
         @pl.when(grid_row <= 1)
         def _():
@@ -306,18 +363,18 @@
         copy.wait()
 
 
-def settle(f0, f1, w, mixed, first_rows, rows, rows_other, ha, hb, oa, ob, blocks):
+def settle(f0, f1, low, mixed, solved, first_rows, rows, rows_other, ha, hb, oa, ob, blocks):
     local_cols, local_rows, n, _ = blocks.shape
     return pl.pallas_call(
         settle_kernel,
         out_shape=jax.ShapeDtypeStruct((local_rows, n, local_cols, n), jnp.float32),
-        in_specs=[VMEM] * 12,
+        in_specs=[VMEM] * 13,
         out_specs=HBM,
         scratch_shapes=[pltpu.VMEM(blocks.shape, jnp.float32), pltpu.SemaphoreType.DMA((local_cols,))],
         compiler_params=pltpu.CompilerParams(vmem_limit_bytes=32 * MIB),
         cost_estimate=estimate(4 * 10**9, 6 * MIB),
         name="settle",
-    )(f0, f1, w, mixed, first_rows, rows, rows_other, ha, hb, oa, ob, blocks)
+    )(f0, f1, low, mixed, solved, first_rows, rows, rows_other, ha, hb, oa, ob, blocks)
 
 
 def exchange(value, axis, mask, size):
@@ -391,7 +448,11 @@
     other = exchange(pair, "row", 1, n_row)
     ha = jnp.where(bit_set(grid_row, row_bits[1]), ha_moved, ha)
     hb = jnp.where(bit_set(grid_row, row_bits[-2]), hb_moved, hb)
+    ha = spread(ha, "row", grid_row, n_row, row_bits[2:])
+    hb = spread(hb, "row", grid_row, n_row, row_bits[:-2][::-1])
     other, pair, ha, hb = after(other, pair, ha, hb)
+    oa = exchange(ha, "row", 1, n_row)
+    ob = exchange(hb, "row", 1, n_row)
 
     n = block.shape[0]
     a00 = jnp.where(odd, other[:n], pair[:n])
@@ -401,14 +462,8 @@
 
     rows = spread(rows, "col", grid_col, n_col, col_bits[1:])
     rows_other = exchange(rows, "col", 1, n_col)
-    w0, row_then, ha, hb = after(w0, grid_row, ha, hb)
-    ha = spread(ha, "row", row_then, n_row, row_bits[2:])
-    hb = spread(hb, "row", row_then, n_row, row_bits[:-2][::-1])
-    oa = exchange(ha, "row", 1, n_row)
-    ob = exchange(hb, "row", 1, n_row)
-    a11, rows_other = after(a11, rows_other)
-    f1, w, mixed, blocks = second_factor(a11, cross, w0, kernel)
-    return settle(f0, f1, w, mixed, first_rows, rows, rows_other, ha, hb, oa, ob, blocks)
+    f1, low, mixed, solved, blocks = second_factor(a11, cross, w0, first_rows, rows, rows_other, ha, hb, oa, ob, kernel)
+    return settle(f0, f1, low, mixed, solved, first_rows, rows, rows_other, ha, hb, oa, ob, blocks)
 
 
 def solution(mesh):

time: 46.7 us -> 45 us (0.964)
  Pallas kernels: 17.9 us -> 16.2 us
    pallas_call x1, Pallas kernels: 6.77 us -> 4.75 us  [settle(): pl.pallas_call(settle_kernel, out_shape=jax.ShapeDtypeStruct((local_rows,...]
  transfers between devices with their start and end apart: 13 -> 13, of which waited for: 6 -> 6; matrix products, arithmetic and copies ran while one was open for 0% -> 0% of each run, Pallas kernels for 22% -> 10%
where the time goes in v20:
time: 45 us; the launch traced here: 44.8 us
  Pallas kernels  16.2 us (36%)
  starting transfers between devices  15.2 us (34%)
  waiting for transfers between devices  11.5 us (26%)
  local copies, waits for them, and re-layouts  1.59 us (4%)
    ppermute x13, starting transfers between devices, exchange(): return lax.ppermute(value, axis, [(i, i ^ mask) for i in range(size)])  15.2 us
    ppermute x13, waiting for transfers between devices, exchange(): return lax.ppermute(value, axis, [(i, i ^ mask) for i in range(size)])  11.5 us
    pallas_call x1, Pallas kernels, second_factor(): pl.pallas_call(second_factor_kernel, out_shape=[square, half, half, solve...  6.3 us
    pallas_call x1, Pallas kernels, settle(): pl.pallas_call(settle_kernel, out_shape=jax.ShapeDtypeStruct((local_rows,...  4.75 us
    pallas_call x1, Pallas kernels, first_factor(): pl.pallas_call(first_factor_kernel, out_shape=[square] * 3, in_specs=[VME...  4.25 us
    unnamed x4, local copies, waits for them, and re-layouts  1.59 us
  transfers between devices with their start and end apart: 13, of which 6 were waited for; matrix products, arithmetic and copies ran while one was open for 0% of the time, Pallas kernels for 10%

profile of v20, /device:TPU:0, one launch (start us, length us, event | category | flops | bytes accessed | tf_op | source)
XLA Modules:
  0.0 44.8 jit_solution(15641654441293243789)
XLA Ops:
  0.0 0.0 copy-start
  0.0 1.6 %copy-done = f32[4,128,8,128]{3,2,1,0:T(8,128)S(1)} copy-done((f32[4,128,8,128]{3,2,1,0:T(8,128)S(1)}, f32[4,128,8,128]{3,2,1,0:T(8,128)}, u32[]{:S(2)}) %copy-start) | copy-done | bytes 2097176
  1.6 0.7 %panels.1 = (f32[3,128,128]{2,1,0:T(8,128)S(1)}, f32[8,64,128]{2,1,0:T(8,128)S(1)}, f32[8,64,128]{2,1,0:T(8,128)S(1)}) custom-call(f32[4,128,8,128]{3,2,1,0:T(8,128)S(1)} %copy-done), custom_call_target="tpu_custom_call" | custom-call | bytes 4194304 | tf_op jit(solution)/shard_map/panels/pallas_call | solution.py:170
  2.3 3.0 %collective-permute-start.2 = (f32[8,64,128]{2,1,0:T(8,128)S(1)}, f32[8,64,128]{2,1,0:T(8,128)S(1)}, u32[]{:S(2)}, u32[]{:S(2)}) collective-permute-start(f32[8,64,128]{2,1,0:T(8,128)S(1)} %get-tuple-element.45), channel_id=1, source_target_pairs={{0,8},{4,12},{8,0},{12,4},{16,24},{20,28},{24,16},{28,20},{1,9},{5... | collective-permute-start | bytes 786440 | tf_op jit(solution)/shard_map/ppermute | solution.py:381
  5.3 0.1 corner_block.1
  5.4 2.7 %collective-permute-start = (f32[128,128]{1,0:T(8,128)S(1)}, f32[128,128]{1,0:T(8,128)S(1)}, u32[]{:S(2)}, u32[]{:S(2)}) collective-permute-start(f32[128,128]{1,0:T(8,128)S(1)} %corner_block.1), channel_id=1, source_target_pairs={{0,2},{1,3},{2,0},{3,1},{4,6},{5,7},{6,4},{7,5},{8,10},{9,11},{10,... | collective-permute-start | bytes 196616 | tf_op jit(solution)/shard_map/ppermute | solution.py:381
  8.0 1.5 %collective-permute-start.3 = (f32[8,64,128]{2,1,0:T(8,128)S(1)}, f32[8,64,128]{2,1,0:T(8,128)S(1)}, u32[]{:S(2)}, u32[]{:S(2)}) collective-permute-start(f32[8,64,128]{2,1,0:T(8,128)S(1)} %get-tuple-element.46), channel_id=1, source_target_pairs={{0,16},{4,20},{8,24},{12,28},{16,0},{20,4},{24,8},{28,12},{1,17},{... | collective-permute-start | bytes 786440 | tf_op jit(solution)/shard_map/ppermute | solution.py:381
  9.5 1.4 %collective-permute-done = f32[128,128]{1,0:T(8,128)S(1)} collective-permute-done((f32[128,128]{1,0:T(8,128)S(1)}, f32[128,128]{1,0:T(8,128)S(1)}, u32[]{:S(2)}, u32[]{:S(2)}) %collective-permute-start) | collective-permute-done | bytes 65568 | tf_op jit(solution)/shard_map/ppermute | solution.py:381
  10.9 1.3 %collective-permute-start.1 = (f32[128,128]{1,0:T(8,128)S(1)}, f32[128,128]{1,0:T(8,128)S(1)}, u32[]{:S(2)}, u32[]{:S(2)}) collective-permute-start(f32[128,128]{1,0:T(8,128)S(1)} %get-tuple-element.77.block_ref), channel_id=1, source_target_pairs={{0,1},{1,0},{2,3},{3,2},{4,5},{5,4},{6,7},{7,6},{8,9},{9,8},{10,11... | collective-permute-start | bytes 196616 | tf_op jit(solution)/shard_map/ppermute | solution.py:381
  12.2 0.0 collective-permute-done.2
  12.3 3.2 %collective-permute-done.3 = f32[8,64,128]{2,1,0:T(8,128)S(1)} collective-permute-done((f32[8,64,128]{2,1,0:T(8,128)S(1)}, f32[8,64,128]{2,1,0:T(8,128)S(1)}, u32[]{:S(2)}, u32[]{:S(2)}) %collective-permute-start.3) | collective-permute-done | bytes 262176 | tf_op jit(solution)/shard_map/ppermute | solution.py:381
  15.5 0.0 collective-permute-done.1.across_ref
  15.5 0.1 pack.1
  15.6 0.6 %collective-permute-start.4 = (f32[192,128]{1,0:T(8,128)S(1)}, f32[192,128]{1,0:T(8,128)S(1)}, u32[]{:S(2)}, u32[]{:S(2)}) collective-permute-start(f32[192,128]{1,0:T(8,128)S(1)} %get-tuple-element.50), channel_id=1, source_target_pairs={{0,8},{4,12},{8,0},{12,4},{16,24},{20,28},{24,16},{28,20},{1,9},{5... | collective-permute-start | bytes 294920 | tf_op jit(solution)/shard_map/ppermute | solution.py:381
  16.2 2.1 %collective-permute-start.6 = (f32[3,128,128]{2,1,0:T(8,128)S(1)}, f32[3,128,128]{2,1,0:T(8,128)S(1)}, u32[]{:S(2)}, u32[]{:S(2)}) collective-permute-start(f32[3,128,128]{2,1,0:T(8,128)S(1)} %get-tuple-element.54), channel_id=1, source_target_pairs={{0,2},{1,3},{2,0},{3,1},{4,6},{5,7},{6,4},{7,5},{8,10},{9,11},{10,... | collective-permute-start | bytes 589832 | tf_op jit(solution)/shard_map/ppermute | solution.py:381
  18.4 2.0 %collective-permute-done.4 = f32[192,128]{1,0:T(8,128)S(1)} collective-permute-done((f32[192,128]{1,0:T(8,128)S(1)}, f32[192,128]{1,0:T(8,128)S(1)}, u32[]{:S(2)}, u32[]{:S(2)}) %collective-permute-start.4) | collective-permute-done | bytes 98336 | tf_op jit(solution)/shard_map/ppermute | solution.py:381
  20.3 1.6 %collective-permute-start.5 = (f32[192,128]{1,0:T(8,128)S(1)}, f32[192,128]{1,0:T(8,128)S(1)}, u32[]{:S(2)}, u32[]{:S(2)}) collective-permute-start(f32[192,128]{1,0:T(8,128)S(1)} %broadcast_select_fusion.6), channel_id=1, source_target_pairs={{0,16},{4,20},{8,24},{12,28},{16,0},{20,4},{24,8},{28,12},{1,17},{... | collective-permute-start | bytes 294920 | tf_op jit(solution)/shard_map/ppermute | solution.py:381
  21.9 0.5 %collective-permute-start.8 = (f32[8,64,128]{2,1,0:T(8,128)S(1)}, f32[8,64,128]{2,1,0:T(8,128)S(1)}, u32[]{:S(2)}, u32[]{:S(2)}) collective-permute-start(f32[8,64,128]{2,1,0:T(8,128)S(1)} %broadcast_select_fusion.4), channel_id=1, source_target_pairs={{0,16},{4,20},{8,24},{12,28},{16,0},{20,4},{24,8},{28,12},{1,17},{... | collective-permute-start | bytes 786440 | tf_op jit(solution)/shard_map/ppermute | solution.py:381
  22.4 0.5 %collective-permute-start.9 = (f32[8,64,128]{2,1,0:T(8,128)S(1)}, f32[8,64,128]{2,1,0:T(8,128)S(1)}, u32[]{:S(2)}, u32[]{:S(2)}) collective-permute-start(f32[8,64,128]{2,1,0:T(8,128)S(1)} %broadcast_select_fusion.2), channel_id=1, source_target_pairs={{0,8},{4,12},{8,0},{12,4},{16,24},{20,28},{24,16},{28,20},{1,9},{5... | collective-permute-start | bytes 786440 | tf_op jit(solution)/shard_map/ppermute | solution.py:381
  23.0 3.3 %collective-permute-done.6 = f32[3,128,128]{2,1,0:T(8,128)S(1)} collective-permute-done((f32[3,128,128]{2,1,0:T(8,128)S(1)}, f32[3,128,128]{2,1,0:T(8,128)S(1)}, u32[]{:S(2)}, u32[]{:S(2)}) %collective-permute-start.6) | collective-permute-done | bytes 196640 | tf_op jit(solution)/shard_map/ppermute | solution.py:381
  26.3 0.0 collective-permute-done.5
  26.3 0.1 collective-permute-start.7
  26.4 0.7 %collective-permute-start.10 = (f32[3,128,128]{2,1,0:T(8,128)S(1)}, f32[3,128,128]{2,1,0:T(8,128)S(1)}, u32[]{:S(2)}, u32[]{:S(2)}) collective-permute-start(f32[3,128,128]{2,1,0:T(8,128)S(1)} %broadcast_select_fusion.5.rows_ref), channel_id=1, source_target_pairs={{0,1},{1,0},{2,3},{3,2},{4,5},{5,4},{6,7},{7,6},{8,9},{9,8},{10,11... | collective-permute-start | bytes 589832 | tf_op jit(solution)/shard_map/ppermute | solution.py:381
  27.0 1.3 %collective-permute-done.8 = f32[8,64,128]{2,1,0:T(8,128)S(1)} collective-permute-done((f32[8,64,128]{2,1,0:T(8,128)S(1)}, f32[8,64,128]{2,1,0:T(8,128)S(1)}, u32[]{:S(2)}, u32[]{:S(2)}) %collective-permute-start.8) | collective-permute-done | bytes 262176 | tf_op jit(solution)/shard_map/ppermute | solution.py:381
  28.3 0.5 %collective-permute-done.9 = f32[8,64,128]{2,1,0:T(8,128)S(1)} collective-permute-done((f32[8,64,128]{2,1,0:T(8,128)S(1)}, f32[8,64,128]{2,1,0:T(8,128)S(1)}, u32[]{:S(2)}, u32[]{:S(2)}) %collective-permute-start.9) | collective-permute-done | bytes 262176 | tf_op jit(solution)/shard_map/ppermute | solution.py:381
  28.8 0.0 collective-permute-done.7
  28.9 0.1 collective-permute-start.11
  29.0 0.5 %collective-permute-start.12 = (f32[8,64,128]{2,1,0:T(8,128)S(1)}, f32[8,64,128]{2,1,0:T(8,128)S(1)}, u32[]{:S(2)}, u32[]{:S(2)}) collective-permute-start(f32[8,64,128]{2,1,0:T(8,128)S(1)} %broadcast_select_fusion.3.hb_ref), channel_id=1, source_target_pairs={{0,4},{4,0},{8,12},{12,8},{16,20},{20,16},{24,28},{28,24},{1,5},{5... | collective-permute-start | bytes 786440 | tf_op jit(solution)/shard_map/ppermute | solution.py:381
  29.5 0.0 copy-start.1
  29.5 4.3 %first_factor.1 = (f32[128,128]{1,0:T(8,128)S(1)}, f32[128,128]{1,0:T(8,128)S(1)}, f32[128,128]{1,0:T(8,128)S(1)}) custom-call(f32[128,128]{1,0:T(8,128)S(1)} %get-tuple-element.74.a_ref, f32[128,128]{1,0:T(8,128)S(1)} %pad_maximum_fusion.side_ref), custom_call_target="tpu_custom_call" | custom-call | flops 8000000000 | bytes 2097152 | tf_op jit(solution)/shard_map/first_factor/pallas_call | solution.py:219
  33.7 0.0 collective-permute-done.10.rows_other_ref
  33.7 0.0 collective-permute-done.11.oa_ref
  33.8 0.0 collective-permute-done.12.ob_ref
  33.8 0.0 copy-done.1
  33.8 6.3 %second_factor.1 = (f32[128,128]{1,0:T(8,128)S(1)}, f32[128,256]{1,0:T(8,128)S(1)}, f32[128,256]{1,0:T(8,128)S(1)}, f32[512,128]{1,0:T(8,128)S(1)}, f32[8,4,128,128]{3,2,1,0:T(8,128)S(1)}) custom-call(f32[128,128]{1,0:T(8,128)S(1)} %get-tuple-element.73.a_ref, f32[128,128]{1,0:T(8,128)S(1)} %get-tuple-element.62.cross_ref, ...), custom_call_target="tpu_custom_call" | custom-call | flops 8000000000 | bytes 4194304 | tf_op jit(solution)/shard_map/second_factor/pallas_call | solution.py:297
  40.1 4.8 %settle.1 = f32[4,128,8,128]{3,2,1,0:T(8,128)} custom-call(f32[128,128]{1,0:T(8,128)S(1)} %get-tuple-element.61.f0_ref, f32[128,128]{1,0:T(8,128)S(1)} %get-tuple-element.68.f1_ref, f32[128,256]{1,0:T(8,128)S(1)} %get-tuple-element.69.low_ref, f32[128,256]{1,0:T(8,128)S(1)} %get-tuple-element.70.mixed_ref, f32[512,128]{1,0:T(8,128)S(1)} %get-tuple-element.71.solved_ref, ...), custom_call_target="tpu_custom_call" | custom-call | flops 4000000000 | bytes 6291456 | tf_op jit(solution)/shard_map/settle/pallas_call | solution.py:368
  (12 shorter events, 0.2 us)
Async XLA Ops:
  0.0 1.6 %copy-start = (f32[4,128,8,128]{3,2,1,0:T(8,128)S(1)}, f32[4,128,8,128]{3,2,1,0:T(8,128)}, u32[]{:S(2)}) copy-start(f32[4,128,8,128]{3,2,1,0:T(8,128)} %matrix_ref.5) | copy-start | bytes 6291460
  2.3 10.0 %collective-permute-start.2 = (f32[8,64,128]{2,1,0:T(8,128)S(1)}, f32[8,64,128]{2,1,0:T(8,128)S(1)}, u32[]{:S(2)}, u32[]{:S(2)}) collective-permute-start(f32[8,64,128]{2,1,0:T(8,128)S(1)} %get-tuple-element.45), channel_id=1, source_target_pairs={{0,8},{4,12},{8,0},{12,4},{16,24},{20,28},{24,16},{28,20},{1,9},{5... | collective-permute-start | bytes 786440 | tf_op jit(solution)/shard_map/ppermute | solution.py:381
  5.4 5.5 %collective-permute-start = (f32[128,128]{1,0:T(8,128)S(1)}, f32[128,128]{1,0:T(8,128)S(1)}, u32[]{:S(2)}, u32[]{:S(2)}) collective-permute-start(f32[128,128]{1,0:T(8,128)S(1)} %corner_block.1), channel_id=1, source_target_pairs={{0,2},{1,3},{2,0},{3,1},{4,6},{5,7},{6,4},{7,5},{8,10},{9,11},{10,... | collective-permute-start | bytes 196616 | tf_op jit(solution)/shard_map/ppermute | solution.py:381
  8.0 7.5 %collective-permute-start.3 = (f32[8,64,128]{2,1,0:T(8,128)S(1)}, f32[8,64,128]{2,1,0:T(8,128)S(1)}, u32[]{:S(2)}, u32[]{:S(2)}) collective-permute-start(f32[8,64,128]{2,1,0:T(8,128)S(1)} %get-tuple-element.46), channel_id=1, source_target_pairs={{0,16},{4,20},{8,24},{12,28},{16,0},{20,4},{24,8},{28,12},{1,17},{... | collective-permute-start | bytes 786440 | tf_op jit(solution)/shard_map/ppermute | solution.py:381
  10.9 4.6 %collective-permute-start.1 = (f32[128,128]{1,0:T(8,128)S(1)}, f32[128,128]{1,0:T(8,128)S(1)}, u32[]{:S(2)}, u32[]{:S(2)}) collective-permute-start(f32[128,128]{1,0:T(8,128)S(1)} %get-tuple-element.77.block_ref), channel_id=1, source_target_pairs={{0,1},{1,0},{2,3},{3,2},{4,5},{5,4},{6,7},{7,6},{8,9},{9,8},{10,11... | collective-permute-start | bytes 196616 | tf_op jit(solution)/shard_map/ppermute | solution.py:381
  15.6 4.7 %collective-permute-start.4 = (f32[192,128]{1,0:T(8,128)S(1)}, f32[192,128]{1,0:T(8,128)S(1)}, u32[]{:S(2)}, u32[]{:S(2)}) collective-permute-start(f32[192,128]{1,0:T(8,128)S(1)} %get-tuple-element.50), channel_id=1, source_target_pairs={{0,8},{4,12},{8,0},{12,4},{16,24},{20,28},{24,16},{28,20},{1,9},{5... | collective-permute-start | bytes 294920 | tf_op jit(solution)/shard_map/ppermute | solution.py:381
  16.2 10.0 %collective-permute-start.6 = (f32[3,128,128]{2,1,0:T(8,128)S(1)}, f32[3,128,128]{2,1,0:T(8,128)S(1)}, u32[]{:S(2)}, u32[]{:S(2)}) collective-permute-start(f32[3,128,128]{2,1,0:T(8,128)S(1)} %get-tuple-element.54), channel_id=1, source_target_pairs={{0,2},{1,3},{2,0},{3,1},{4,6},{5,7},{6,4},{7,5},{8,10},{9,11},{10,... | collective-permute-start | bytes 589832 | tf_op jit(solution)/shard_map/ppermute | solution.py:381
  20.3 5.9 %collective-permute-start.5 = (f32[192,128]{1,0:T(8,128)S(1)}, f32[192,128]{1,0:T(8,128)S(1)}, u32[]{:S(2)}, u32[]{:S(2)}) collective-permute-start(f32[192,128]{1,0:T(8,128)S(1)} %broadcast_select_fusion.6), channel_id=1, source_target_pairs={{0,16},{4,20},{8,24},{12,28},{16,0},{20,4},{24,8},{28,12},{1,17},{... | collective-permute-start | bytes 294920 | tf_op jit(solution)/shard_map/ppermute | solution.py:381
  21.9 6.4 %collective-permute-start.8 = (f32[8,64,128]{2,1,0:T(8,128)S(1)}, f32[8,64,128]{2,1,0:T(8,128)S(1)}, u32[]{:S(2)}, u32[]{:S(2)}) collective-permute-start(f32[8,64,128]{2,1,0:T(8,128)S(1)} %broadcast_select_fusion.4), channel_id=1, source_target_pairs={{0,16},{4,20},{8,24},{12,28},{16,0},{20,4},{24,8},{28,12},{1,17},{... | collective-permute-start | bytes 786440 | tf_op jit(solution)/shard_map/ppermute | solution.py:381
  22.4 6.4 %collective-permute-start.9 = (f32[8,64,128]{2,1,0:T(8,128)S(1)}, f32[8,64,128]{2,1,0:T(8,128)S(1)}, u32[]{:S(2)}, u32[]{:S(2)}) collective-permute-start(f32[8,64,128]{2,1,0:T(8,128)S(1)} %broadcast_select_fusion.2), channel_id=1, source_target_pairs={{0,8},{4,12},{8,0},{12,4},{16,24},{20,28},{24,16},{28,20},{1,9},{5... | collective-permute-start | bytes 786440 | tf_op jit(solution)/shard_map/ppermute | solution.py:381
  26.3 2.6 %collective-permute-start.7 = (f32[192,128]{1,0:T(8,128)S(1)}, f32[192,128]{1,0:T(8,128)S(1)}, u32[]{:S(2)}, u32[]{:S(2)}) collective-permute-start(f32[192,128]{1,0:T(8,128)S(1)} %broadcast_select_fusion.7), channel_id=1, source_target_pairs={{0,4},{4,0},{8,12},{12,8},{16,20},{20,16},{24,28},{28,24},{1,5},{5... | collective-permute-start | bytes 294920 | tf_op jit(solution)/shard_map/ppermute | solution.py:381
  26.4 7.4 %collective-permute-start.10 = (f32[3,128,128]{2,1,0:T(8,128)S(1)}, f32[3,128,128]{2,1,0:T(8,128)S(1)}, u32[]{:S(2)}, u32[]{:S(2)}) collective-permute-start(f32[3,128,128]{2,1,0:T(8,128)S(1)} %broadcast_select_fusion.5.rows_ref), channel_id=1, source_target_pairs={{0,1},{1,0},{2,3},{3,2},{4,5},{5,4},{6,7},{7,6},{8,9},{9,8},{10,11... | collective-permute-start | bytes 589832 | tf_op jit(solution)/shard_map/ppermute | solution.py:381
  28.9 4.9 %collective-permute-start.11 = (f32[8,64,128]{2,1,0:T(8,128)S(1)}, f32[8,64,128]{2,1,0:T(8,128)S(1)}, u32[]{:S(2)}, u32[]{:S(2)}) collective-permute-start(f32[8,64,128]{2,1,0:T(8,128)S(1)} %broadcast_select_fusion.1.ha_ref), channel_id=1, source_target_pairs={{0,4},{4,0},{8,12},{12,8},{16,20},{20,16},{24,28},{28,24},{1,5},{5... | collective-permute-start | bytes 786440 | tf_op jit(solution)/shard_map/ppermute | solution.py:381
  29.0 4.8 %collective-permute-start.12 = (f32[8,64,128]{2,1,0:T(8,128)S(1)}, f32[8,64,128]{2,1,0:T(8,128)S(1)}, u32[]{:S(2)}, u32[]{:S(2)}) collective-permute-start(f32[8,64,128]{2,1,0:T(8,128)S(1)} %broadcast_select_fusion.3.hb_ref), channel_id=1, source_target_pairs={{0,4},{4,0},{8,12},{12,8},{16,20},{20,16},{24,28},{28,24},{1,5},{5... | collective-permute-start | bytes 786440 | tf_op jit(solution)/shard_map/ppermute | solution.py:381
  29.5 4.3 %copy-start.1 = (f32[4,128,8,128]{3,2,1,0:T(8,128)S(1)}, f32[4,128,8,128]{3,2,1,0:T(8,128)}, u32[]{:S(2)}) copy-start(f32[4,128,8,128]{3,2,1,0:T(8,128)} %matrix_ref.5) | copy-start | bytes 6291460

commit v21 on v20

--- a/solution.py
+++ b/solution.py
@@ -59,7 +59,7 @@
     lane = lax.broadcasted_iota(jnp.int32, (SUB, n), 1)
     rows = lax.broadcasted_iota(jnp.int32, (n, n), 0)
     cols = lax.broadcasted_iota(jnp.int32, (n, n), 1)
-    for ref, value in zip(scratch, (s, jnp.where(rows == cols, 1.0, 0.0), extra)):
+    for ref, value in zip(scratch, [s, jnp.where(rows == cols, 1.0, 0.0)] + list(extra)):
         ref[...] = value.reshape(groups, SUB, n)
     sides = range(len(scratch))
     for g in range(groups):
@@ -107,24 +107,12 @@
                 scratch[m][until:] = scratch[m][until:] - part.reshape(groups - until, SUB, n)
         if g < len(beside):
             beside[g]()
-    upper, inverse, product = [ref[...].reshape(n, n) for ref in scratch]
-    return upper.T, inverse, product
+    upper, *others = [ref[...].reshape(n, n) for ref in scratch]
+    return [upper.T] + others
 
 
 def is_odd_row():
     return lax.rem(lax.axis_index("row"), 2) == 1
-
-
-def stacked(a):
-    return jnp.concatenate(parts(a)[::-1], axis=0)
-
-
-def dot_parts(a, b, dims=((1,), (0,))):
-    m = a.shape[0] // 3
-    high, middle, low = [
-        lax.dot_general(a[i * m:], b[i], (dims, ((), ())), preferred_element_type=jnp.float32) for i in range(3)]
-    small = high[:m] + middle[:m] + low
-    return small + (high[m:2 * m] + middle[m:]) + high[2 * m:]
 
 
 def estimate(flops, nbytes):
@@ -206,11 +194,11 @@
 
 
 def first_factor_kernel(a_ref, side_ref, f_ref, w_ref, cross_ref, *scratch):
-    f_ref[...], w_ref[...], cross_ref[...] = eliminate(a_ref[...], side_ref[...], scratch)
-
-
-def elimination_scratch(n):
-    return [pltpu.VMEM((n // SUB, SUB, n), jnp.float32)] * 3
+    f_ref[...], w_ref[...], cross_ref[...] = eliminate(a_ref[...], [side_ref[...]], scratch)
+
+
+def elimination_scratch(n, matrices):
+    return [pltpu.VMEM((n // SUB, SUB, n), jnp.float32)] * matrices
 
 
 def first_factor(a, side):
@@ -221,7 +209,7 @@
         out_shape=[square] * 3,
         in_specs=[VMEM] * 2,
         out_specs=[VMEM] * 3,
-        scratch_shapes=elimination_scratch(n),
+        scratch_shapes=elimination_scratch(n, 3),
         compiler_params=pltpu.CompilerParams(vmem_limit_bytes=4 * MIB),
         cost_estimate=estimate(8 * 10**9, 2 * MIB),
         name="first_factor",
@@ -229,7 +217,7 @@
 
 
 def second_factor_kernel(a_ref, cross_ref, w0_ref, first_ref, rows_ref, rows_other_ref, ha_ref, hb_ref, oa_ref, ob_ref, matrix_ref,
-                         f_ref, low_ref, mixed_ref, solved_ref, blocks_ref, left, right, sems, *scratch):
+                         f_ref, w_ref, solved_ref, rows_left_ref, top_left_ref, blocks_ref, left, right, sems, *scratch):
     n = w0_ref.shape[0]
     local_cols = matrix_ref.shape[2]
     local_rows = matrix_ref.shape[0]
@@ -245,12 +233,19 @@
         solved_ref[...] = solved
         left[...] = wide(solved)
 
+    def update_rows():
+        rows_left_ref[...] = wide(panel_rows(1, first_ref, rows_ref, rows_other_ref) - times(left[...], tall(cross)))
+
+    def top(panel, j):
+        here = odd == (panel == 1)
+        return jnp.concatenate([
+            jnp.concatenate([jnp.where(here, ha_ref[b], oa_ref[b]), jnp.where(here, hb_ref[b], ob_ref[b])], axis=0)
+            for b in (j, j + 1)], axis=1)
+
     def solve_top(j):
         def step():
-            top = jnp.concatenate([
-                jnp.concatenate([jnp.where(odd, oa_ref[b], ha_ref[b]), jnp.where(odd, ob_ref[b], hb_ref[b])], axis=0)
-                for b in (j, j + 1)], axis=1)
-            right[...] = tall(times(wide(w0), tall(top)))
+            right[...] = tall(times(wide(w0), tall(top(0, j))))
+            top_left_ref[:, j * n:(j + 2) * n] = tall(top(1, j) - times(wide(cross.T), right[...]))
         return step
 
     def update(j, i):
@@ -264,12 +259,11 @@
                 blocks_ref[j + b, i:i + 2] = blocks_ref[j + b, i:i + 2] - part
         return step
 
-    steps = [solve_rows]
+    steps = [solve_rows, update_rows]
     for j in range(0, local_cols, 2):
         steps.append(solve_top(j))
         steps.extend(update(j, i) for i in range(0, local_rows, 2))
 
-    both = dot_over_rows(cross, jnp.concatenate([cross, w0], axis=1))
     groups = n // SUB
     each = -(-len(steps) // groups)
 
@@ -280,52 +274,45 @@
         return run
 
     beside = [several(steps[at:at + each]) for at in range(0, len(steps), each)]
-    f1, w1, w10 = eliminate(a_ref[...] - both[:, :n], -both[:, n:], scratch, beside)
-    f_ref[...] = f1
-    low_ref[:, :n] = w10
-    low_ref[:, n:] = w1
-    mixed_ref[:, :n] = jnp.where(odd, w1, w10)
-    mixed_ref[:, n:] = jnp.where(odd, w10, w1)
+    f_ref[...], w_ref[...] = eliminate(a_ref[...] - dot_over_rows(cross, cross), [], scratch, beside)
 
 
 def second_factor(a, cross, w0, first_rows, rows, rows_other, ha, hb, oa, ob, matrix):
     local_rows, n, local_cols, _ = matrix.shape
     square = jax.ShapeDtypeStruct((n, n), jnp.float32)
-    half = jax.ShapeDtypeStruct((n, 2 * n), jnp.float32)
     solved = jax.ShapeDtypeStruct((local_rows * n, n), jnp.float32)
+    rows_left = jax.ShapeDtypeStruct((local_rows * n, 6 * n), jnp.bfloat16)
+    top_left = jax.ShapeDtypeStruct((6 * n, local_cols * n), jnp.bfloat16)
     blocks = jax.ShapeDtypeStruct((local_cols, local_rows, n, n), jnp.float32)
     return pl.pallas_call(
         second_factor_kernel,
-        out_shape=[square, half, half, solved, blocks],
+        out_shape=[square, square, solved, rows_left, top_left, blocks],
         in_specs=[VMEM] * 10 + [HBM],
-        out_specs=[VMEM] * 5,
+        out_specs=[VMEM] * 6,
         scratch_shapes=[
             pltpu.VMEM((local_rows * n, 6 * n), jnp.bfloat16),
             pltpu.VMEM((6 * n, 2 * n), jnp.bfloat16),
             pltpu.SemaphoreType.DMA((local_cols,)),
-        ] + elimination_scratch(n),
+        ] + elimination_scratch(n, 2),
         compiler_params=pltpu.CompilerParams(vmem_limit_bytes=20 * MIB),
         cost_estimate=estimate(8 * 10**9, 4 * MIB),
         name="second_factor",
     )(a, cross, w0, first_rows, rows, rows_other, ha, hb, oa, ob, matrix)
 
 
-def settle_kernel(f0_ref, f1_ref, low_ref, mixed_ref, solved_ref, first_ref, rows_ref, rows_other_ref, ha_ref, hb_ref, oa_ref, ob_ref,
-                  blocks_ref, out_ref, result, sems):
+def settle_kernel(f0_ref, f1_ref, w_ref, solved_ref, rows_left_ref, top_left_ref, blocks_ref, out_ref, result, sems):
     grid_row = lax.axis_index("row")
     grid_col = lax.axis_index("col")
     n = f0_ref.shape[0]
     local_cols, local_rows, _, _ = blocks_ref.shape
-    rows = jnp.concatenate([panel_rows(p, first_ref, rows_ref, rows_other_ref) for p in range(2)], axis=1)
-    solved = dot_parts(stacked(rows), parts(low_ref[...]), ((1,), (1,)))
+    w1 = w_ref[...]
+    solved = times(rows_left_ref[...], tall(w1.T))
     left = wide(solved)
-    mixed = stacked(mixed_ref[...])
+    inverse = wide(w1)
     copies = []
     for j in range(0, local_cols, 2):
         pair = (j, j + 1)
-        tops = jnp.concatenate(
-            [jnp.concatenate([ha_ref[b], hb_ref[b], oa_ref[b], ob_ref[b]], axis=0) for b in pair], axis=1)
-        update = times(left, tall(dot_parts(mixed, parts(tops))))
+        update = times(left, tall(times(inverse, top_left_ref[:, j * n:(j + 2) * n])))
         for b in pair:
             part = update[:, (b - j) * n:(b - j + 1) * n].reshape(local_rows, n, n)
             result[b] = blocks_ref[b] - part
@@ -363,18 +350,18 @@
         copy.wait()
 
 
-def settle(f0, f1, low, mixed, solved, first_rows, rows, rows_other, ha, hb, oa, ob, blocks):
+def settle(f0, f1, w1, solved, rows_left, top_left, blocks):
     local_cols, local_rows, n, _ = blocks.shape
     return pl.pallas_call(
         settle_kernel,
         out_shape=jax.ShapeDtypeStruct((local_rows, n, local_cols, n), jnp.float32),
-        in_specs=[VMEM] * 13,
+        in_specs=[VMEM] * 7,
         out_specs=HBM,
         scratch_shapes=[pltpu.VMEM(blocks.shape, jnp.float32), pltpu.SemaphoreType.DMA((local_cols,))],
         compiler_params=pltpu.CompilerParams(vmem_limit_bytes=32 * MIB),
         cost_estimate=estimate(4 * 10**9, 6 * MIB),
         name="settle",
-    )(f0, f1, low, mixed, solved, first_rows, rows, rows_other, ha, hb, oa, ob, blocks)
+    )(f0, f1, w1, solved, rows_left, top_left, blocks)
 
 
 def exchange(value, axis, mask, size):
@@ -462,8 +449,9 @@
 
     rows = spread(rows, "col", grid_col, n_col, col_bits[1:])
     rows_other = exchange(rows, "col", 1, n_col)
-    f1, low, mixed, solved, blocks = second_factor(a11, cross, w0, first_rows, rows, rows_other, ha, hb, oa, ob, kernel)
-    return settle(f0, f1, low, mixed, solved, first_rows, rows, rows_other, ha, hb, oa, ob, blocks)
+    f1, w1, solved, rows_left, top_left, blocks = second_factor(
+        a11, cross, w0, first_rows, rows, rows_other, ha, hb, oa, ob, kernel)
+    return settle(f0, f1, w1, solved, rows_left, top_left, blocks)
 
 
 def solution(mesh):

time: 45 us -> 44.8 us (level)
  no operation moved by 1% of the time
where the time goes in v21:
time: 44.8 us; the launch traced here: 44.6 us
  Pallas kernels  16 us (36%)
  starting transfers between devices  15.2 us (34%)
  waiting for transfers between devices  11.5 us (26%)
  local copies, waits for them, and re-layouts  1.59 us (4%)
    ppermute x13, starting transfers between devices, exchange(): return lax.ppermute(value, axis, [(i, i ^ mask) for i in range(size)])  15.2 us
    ppermute x13, waiting for transfers between devices, exchange(): return lax.ppermute(value, axis, [(i, i ^ mask) for i in range(size)])  11.5 us
    pallas_call x1, Pallas kernels, second_factor(): pl.pallas_call(second_factor_kernel, out_shape=[square, square, solved, r...  6.5 us
    pallas_call x1, Pallas kernels, settle(): pl.pallas_call(settle_kernel, out_shape=jax.ShapeDtypeStruct((local_rows,...  4.36 us
    pallas_call x1, Pallas kernels, first_factor(): pl.pallas_call(first_factor_kernel, out_shape=[square] * 3, in_specs=[VME...  4.25 us
    unnamed x4, local copies, waits for them, and re-layouts  1.59 us
  transfers between devices with their start and end apart: 13, of which 6 were waited for; matrix products, arithmetic and copies ran while one was open for 0% of the time, Pallas kernels for 10%

profile of v21, /device:TPU:0, one launch (start us, length us, event | category | flops | bytes accessed | tf_op | source)
XLA Modules:
  0.0 44.6 jit_solution(5974830442521348015)
XLA Ops:
  0.0 0.0 copy-start
  0.0 1.6 %copy-done = f32[4,128,8,128]{3,2,1,0:T(8,128)S(1)} copy-done((f32[4,128,8,128]{3,2,1,0:T(8,128)S(1)}, f32[4,128,8,128]{3,2,1,0:T(8,128)}, u32[]{:S(2)}) %copy-start) | copy-done | bytes 2097176
  1.6 0.7 %panels.1 = (f32[3,128,128]{2,1,0:T(8,128)S(1)}, f32[8,64,128]{2,1,0:T(8,128)S(1)}, f32[8,64,128]{2,1,0:T(8,128)S(1)}) custom-call(f32[4,128,8,128]{3,2,1,0:T(8,128)S(1)} %copy-done), custom_call_target="tpu_custom_call" | custom-call | bytes 4194304 | tf_op jit(solution)/shard_map/panels/pallas_call | solution.py:158
  2.3 3.0 %collective-permute-start.2 = (f32[8,64,128]{2,1,0:T(8,128)S(1)}, f32[8,64,128]{2,1,0:T(8,128)S(1)}, u32[]{:S(2)}, u32[]{:S(2)}) collective-permute-start(f32[8,64,128]{2,1,0:T(8,128)S(1)} %get-tuple-element.46), channel_id=1, source_target_pairs={{0,8},{4,12},{8,0},{12,4},{16,24},{20,28},{24,16},{28,20},{1,9},{5... | collective-permute-start | bytes 786440 | tf_op jit(solution)/shard_map/ppermute | solution.py:368
  5.3 0.1 corner_block.1
  5.4 2.7 %collective-permute-start = (f32[128,128]{1,0:T(8,128)S(1)}, f32[128,128]{1,0:T(8,128)S(1)}, u32[]{:S(2)}, u32[]{:S(2)}) collective-permute-start(f32[128,128]{1,0:T(8,128)S(1)} %corner_block.1), channel_id=1, source_target_pairs={{0,2},{1,3},{2,0},{3,1},{4,6},{5,7},{6,4},{7,5},{8,10},{9,11},{10,... | collective-permute-start | bytes 196616 | tf_op jit(solution)/shard_map/ppermute | solution.py:368
  8.0 1.5 %collective-permute-start.3 = (f32[8,64,128]{2,1,0:T(8,128)S(1)}, f32[8,64,128]{2,1,0:T(8,128)S(1)}, u32[]{:S(2)}, u32[]{:S(2)}) collective-permute-start(f32[8,64,128]{2,1,0:T(8,128)S(1)} %get-tuple-element.47), channel_id=1, source_target_pairs={{0,16},{4,20},{8,24},{12,28},{16,0},{20,4},{24,8},{28,12},{1,17},{... | collective-permute-start | bytes 786440 | tf_op jit(solution)/shard_map/ppermute | solution.py:368
  9.5 1.4 %collective-permute-done = f32[128,128]{1,0:T(8,128)S(1)} collective-permute-done((f32[128,128]{1,0:T(8,128)S(1)}, f32[128,128]{1,0:T(8,128)S(1)}, u32[]{:S(2)}, u32[]{:S(2)}) %collective-permute-start) | collective-permute-done | bytes 65568 | tf_op jit(solution)/shard_map/ppermute | solution.py:368
  10.9 1.3 %collective-permute-start.1 = (f32[128,128]{1,0:T(8,128)S(1)}, f32[128,128]{1,0:T(8,128)S(1)}, u32[]{:S(2)}, u32[]{:S(2)}) collective-permute-start(f32[128,128]{1,0:T(8,128)S(1)} %get-tuple-element.79.block_ref), channel_id=1, source_target_pairs={{0,1},{1,0},{2,3},{3,2},{4,5},{5,4},{6,7},{7,6},{8,9},{9,8},{10,11... | collective-permute-start | bytes 196616 | tf_op jit(solution)/shard_map/ppermute | solution.py:368
  12.2 0.0 collective-permute-done.2
  12.3 3.2 %collective-permute-done.3 = f32[8,64,128]{2,1,0:T(8,128)S(1)} collective-permute-done((f32[8,64,128]{2,1,0:T(8,128)S(1)}, f32[8,64,128]{2,1,0:T(8,128)S(1)}, u32[]{:S(2)}, u32[]{:S(2)}) %collective-permute-start.3) | collective-permute-done | bytes 262176 | tf_op jit(solution)/shard_map/ppermute | solution.py:368
  15.5 0.0 collective-permute-done.1.across_ref
  15.5 0.1 pack.1
  15.6 0.6 %collective-permute-start.4 = (f32[192,128]{1,0:T(8,128)S(1)}, f32[192,128]{1,0:T(8,128)S(1)}, u32[]{:S(2)}, u32[]{:S(2)}) collective-permute-start(f32[192,128]{1,0:T(8,128)S(1)} %get-tuple-element.51), channel_id=1, source_target_pairs={{0,8},{4,12},{8,0},{12,4},{16,24},{20,28},{24,16},{28,20},{1,9},{5... | collective-permute-start | bytes 294920 | tf_op jit(solution)/shard_map/ppermute | solution.py:368
  16.2 2.1 %collective-permute-start.6 = (f32[3,128,128]{2,1,0:T(8,128)S(1)}, f32[3,128,128]{2,1,0:T(8,128)S(1)}, u32[]{:S(2)}, u32[]{:S(2)}) collective-permute-start(f32[3,128,128]{2,1,0:T(8,128)S(1)} %get-tuple-element.55), channel_id=1, source_target_pairs={{0,2},{1,3},{2,0},{3,1},{4,6},{5,7},{6,4},{7,5},{8,10},{9,11},{10,... | collective-permute-start | bytes 589832 | tf_op jit(solution)/shard_map/ppermute | solution.py:368
  18.4 2.0 %collective-permute-done.4 = f32[192,128]{1,0:T(8,128)S(1)} collective-permute-done((f32[192,128]{1,0:T(8,128)S(1)}, f32[192,128]{1,0:T(8,128)S(1)}, u32[]{:S(2)}, u32[]{:S(2)}) %collective-permute-start.4) | collective-permute-done | bytes 98336 | tf_op jit(solution)/shard_map/ppermute | solution.py:368
  20.3 1.6 %collective-permute-start.5 = (f32[192,128]{1,0:T(8,128)S(1)}, f32[192,128]{1,0:T(8,128)S(1)}, u32[]{:S(2)}, u32[]{:S(2)}) collective-permute-start(f32[192,128]{1,0:T(8,128)S(1)} %broadcast_select_fusion.6), channel_id=1, source_target_pairs={{0,16},{4,20},{8,24},{12,28},{16,0},{20,4},{24,8},{28,12},{1,17},{... | collective-permute-start | bytes 294920 | tf_op jit(solution)/shard_map/ppermute | solution.py:368
  21.9 0.5 %collective-permute-start.8 = (f32[8,64,128]{2,1,0:T(8,128)S(1)}, f32[8,64,128]{2,1,0:T(8,128)S(1)}, u32[]{:S(2)}, u32[]{:S(2)}) collective-permute-start(f32[8,64,128]{2,1,0:T(8,128)S(1)} %broadcast_select_fusion.4), channel_id=1, source_target_pairs={{0,16},{4,20},{8,24},{12,28},{16,0},{20,4},{24,8},{28,12},{1,17},{... | collective-permute-start | bytes 786440 | tf_op jit(solution)/shard_map/ppermute | solution.py:368
  22.4 0.5 %collective-permute-start.9 = (f32[8,64,128]{2,1,0:T(8,128)S(1)}, f32[8,64,128]{2,1,0:T(8,128)S(1)}, u32[]{:S(2)}, u32[]{:S(2)}) collective-permute-start(f32[8,64,128]{2,1,0:T(8,128)S(1)} %broadcast_select_fusion.2), channel_id=1, source_target_pairs={{0,8},{4,12},{8,0},{12,4},{16,24},{20,28},{24,16},{28,20},{1,9},{5... | collective-permute-start | bytes 786440 | tf_op jit(solution)/shard_map/ppermute | solution.py:368
  23.0 3.3 %collective-permute-done.6 = f32[3,128,128]{2,1,0:T(8,128)S(1)} collective-permute-done((f32[3,128,128]{2,1,0:T(8,128)S(1)}, f32[3,128,128]{2,1,0:T(8,128)S(1)}, u32[]{:S(2)}, u32[]{:S(2)}) %collective-permute-start.6) | collective-permute-done | bytes 196640 | tf_op jit(solution)/shard_map/ppermute | solution.py:368
  26.3 0.0 collective-permute-done.5
  26.3 0.1 collective-permute-start.7
  26.4 0.7 %collective-permute-start.10 = (f32[3,128,128]{2,1,0:T(8,128)S(1)}, f32[3,128,128]{2,1,0:T(8,128)S(1)}, u32[]{:S(2)}, u32[]{:S(2)}) collective-permute-start(f32[3,128,128]{2,1,0:T(8,128)S(1)} %broadcast_select_fusion.5.rows_ref), channel_id=1, source_target_pairs={{0,1},{1,0},{2,3},{3,2},{4,5},{5,4},{6,7},{7,6},{8,9},{9,8},{10,11... | collective-permute-start | bytes 589832 | tf_op jit(solution)/shard_map/ppermute | solution.py:368
  27.0 1.3 %collective-permute-done.8 = f32[8,64,128]{2,1,0:T(8,128)S(1)} collective-permute-done((f32[8,64,128]{2,1,0:T(8,128)S(1)}, f32[8,64,128]{2,1,0:T(8,128)S(1)}, u32[]{:S(2)}, u32[]{:S(2)}) %collective-permute-start.8) | collective-permute-done | bytes 262176 | tf_op jit(solution)/shard_map/ppermute | solution.py:368
  28.3 0.5 %collective-permute-done.9 = f32[8,64,128]{2,1,0:T(8,128)S(1)} collective-permute-done((f32[8,64,128]{2,1,0:T(8,128)S(1)}, f32[8,64,128]{2,1,0:T(8,128)S(1)}, u32[]{:S(2)}, u32[]{:S(2)}) %collective-permute-start.9) | collective-permute-done | bytes 262176 | tf_op jit(solution)/shard_map/ppermute | solution.py:368
  28.8 0.0 collective-permute-done.7
  28.9 0.1 collective-permute-start.11
  29.0 0.5 %collective-permute-start.12 = (f32[8,64,128]{2,1,0:T(8,128)S(1)}, f32[8,64,128]{2,1,0:T(8,128)S(1)}, u32[]{:S(2)}, u32[]{:S(2)}) collective-permute-start(f32[8,64,128]{2,1,0:T(8,128)S(1)} %broadcast_select_fusion.3.hb_ref), channel_id=1, source_target_pairs={{0,4},{4,0},{8,12},{12,8},{16,20},{20,16},{24,28},{28,24},{1,5},{5... | collective-permute-start | bytes 786440 | tf_op jit(solution)/shard_map/ppermute | solution.py:368
  29.5 0.0 copy-start.1
  29.5 4.3 %first_factor.1 = (f32[128,128]{1,0:T(8,128)S(1)}, f32[128,128]{1,0:T(8,128)S(1)}, f32[128,128]{1,0:T(8,128)S(1)}) custom-call(f32[128,128]{1,0:T(8,128)S(1)} %get-tuple-element.76.a_ref, f32[128,128]{1,0:T(8,128)S(1)} %pad_maximum_fusion.side_ref), custom_call_target="tpu_custom_call" | custom-call | flops 8000000000 | bytes 2097152 | tf_op jit(solution)/shard_map/first_factor/pallas_call | solution.py:207
  33.7 0.0 collective-permute-done.10.rows_other_ref
  33.7 0.0 collective-permute-done.11.oa_ref
  33.8 0.0 collective-permute-done.12.ob_ref
  33.8 0.0 copy-done.1
  33.8 6.5 %second_factor.1 = (f32[128,128]{1,0:T(8,128)S(1)}, f32[128,128]{1,0:T(8,128)S(1)}, f32[512,128]{1,0:T(8,128)S(1)}, bf16[512,768]{1,0:T(8,128)(2,1)S(1)}, bf16[7...) custom-call(f32[128,128]{1,0:T(8,128)S(1)} %get-tuple-element.75.a_ref, ...), custom_call_target="tpu_custom_call" | custom-call | flops 8000000000 | bytes 4194304 | tf_op jit(solution)/shard_map/second_factor/pallas_call | solution.py:287
  40.3 4.4 %settle.1 = f32[4,128,8,128]{3,2,1,0:T(8,128)} custom-call(f32[128,128]{1,0:T(8,128)S(1)} %get-tuple-element.62.f0_ref, f32[128,128]{1,0:T(8,128)S(1)} %get-tuple-element.69.f1_ref, f32[128,128]{1,0:T(8,128)S(1)} %get-tuple-element.70.w_ref, f32[512,128]{1,0:T(8,128)S(1)} %get-tuple-element.71.solved_ref, ...), custom_call_target="tpu_custom_call" | custom-call | flops 4000000000 | bytes 6291456 | tf_op jit(solution)/shard_map/settle/pallas_call | solution.py:355
  (12 shorter events, 0.2 us)
Async XLA Ops:
  0.0 1.6 %copy-start = (f32[4,128,8,128]{3,2,1,0:T(8,128)S(1)}, f32[4,128,8,128]{3,2,1,0:T(8,128)}, u32[]{:S(2)}) copy-start(f32[4,128,8,128]{3,2,1,0:T(8,128)} %matrix_ref.5) | copy-start | bytes 6291460
  2.3 10.0 %collective-permute-start.2 = (f32[8,64,128]{2,1,0:T(8,128)S(1)}, f32[8,64,128]{2,1,0:T(8,128)S(1)}, u32[]{:S(2)}, u32[]{:S(2)}) collective-permute-start(f32[8,64,128]{2,1,0:T(8,128)S(1)} %get-tuple-element.46), channel_id=1, source_target_pairs={{0,8},{4,12},{8,0},{12,4},{16,24},{20,28},{24,16},{28,20},{1,9},{5... | collective-permute-start | bytes 786440 | tf_op jit(solution)/shard_map/ppermute | solution.py:368
  5.4 5.5 %collective-permute-start = (f32[128,128]{1,0:T(8,128)S(1)}, f32[128,128]{1,0:T(8,128)S(1)}, u32[]{:S(2)}, u32[]{:S(2)}) collective-permute-start(f32[128,128]{1,0:T(8,128)S(1)} %corner_block.1), channel_id=1, source_target_pairs={{0,2},{1,3},{2,0},{3,1},{4,6},{5,7},{6,4},{7,5},{8,10},{9,11},{10,... | collective-permute-start | bytes 196616 | tf_op jit(solution)/shard_map/ppermute | solution.py:368
  8.0 7.5 %collective-permute-start.3 = (f32[8,64,128]{2,1,0:T(8,128)S(1)}, f32[8,64,128]{2,1,0:T(8,128)S(1)}, u32[]{:S(2)}, u32[]{:S(2)}) collective-permute-start(f32[8,64,128]{2,1,0:T(8,128)S(1)} %get-tuple-element.47), channel_id=1, source_target_pairs={{0,16},{4,20},{8,24},{12,28},{16,0},{20,4},{24,8},{28,12},{1,17},{... | collective-permute-start | bytes 786440 | tf_op jit(solution)/shard_map/ppermute | solution.py:368
  10.9 4.6 %collective-permute-start.1 = (f32[128,128]{1,0:T(8,128)S(1)}, f32[128,128]{1,0:T(8,128)S(1)}, u32[]{:S(2)}, u32[]{:S(2)}) collective-permute-start(f32[128,128]{1,0:T(8,128)S(1)} %get-tuple-element.79.block_ref), channel_id=1, source_target_pairs={{0,1},{1,0},{2,3},{3,2},{4,5},{5,4},{6,7},{7,6},{8,9},{9,8},{10,11... | collective-permute-start | bytes 196616 | tf_op jit(solution)/shard_map/ppermute | solution.py:368
  15.6 4.7 %collective-permute-start.4 = (f32[192,128]{1,0:T(8,128)S(1)}, f32[192,128]{1,0:T(8,128)S(1)}, u32[]{:S(2)}, u32[]{:S(2)}) collective-permute-start(f32[192,128]{1,0:T(8,128)S(1)} %get-tuple-element.51), channel_id=1, source_target_pairs={{0,8},{4,12},{8,0},{12,4},{16,24},{20,28},{24,16},{28,20},{1,9},{5... | collective-permute-start | bytes 294920 | tf_op jit(solution)/shard_map/ppermute | solution.py:368
  16.2 10.0 %collective-permute-start.6 = (f32[3,128,128]{2,1,0:T(8,128)S(1)}, f32[3,128,128]{2,1,0:T(8,128)S(1)}, u32[]{:S(2)}, u32[]{:S(2)}) collective-permute-start(f32[3,128,128]{2,1,0:T(8,128)S(1)} %get-tuple-element.55), channel_id=1, source_target_pairs={{0,2},{1,3},{2,0},{3,1},{4,6},{5,7},{6,4},{7,5},{8,10},{9,11},{10,... | collective-permute-start | bytes 589832 | tf_op jit(solution)/shard_map/ppermute | solution.py:368
  20.3 5.9 %collective-permute-start.5 = (f32[192,128]{1,0:T(8,128)S(1)}, f32[192,128]{1,0:T(8,128)S(1)}, u32[]{:S(2)}, u32[]{:S(2)}) collective-permute-start(f32[192,128]{1,0:T(8,128)S(1)} %broadcast_select_fusion.6), channel_id=1, source_target_pairs={{0,16},{4,20},{8,24},{12,28},{16,0},{20,4},{24,8},{28,12},{1,17},{... | collective-permute-start | bytes 294920 | tf_op jit(solution)/shard_map/ppermute | solution.py:368
  21.9 6.4 %collective-permute-start.8 = (f32[8,64,128]{2,1,0:T(8,128)S(1)}, f32[8,64,128]{2,1,0:T(8,128)S(1)}, u32[]{:S(2)}, u32[]{:S(2)}) collective-permute-start(f32[8,64,128]{2,1,0:T(8,128)S(1)} %broadcast_select_fusion.4), channel_id=1, source_target_pairs={{0,16},{4,20},{8,24},{12,28},{16,0},{20,4},{24,8},{28,12},{1,17},{... | collective-permute-start | bytes 786440 | tf_op jit(solution)/shard_map/ppermute | solution.py:368
  22.4 6.4 %collective-permute-start.9 = (f32[8,64,128]{2,1,0:T(8,128)S(1)}, f32[8,64,128]{2,1,0:T(8,128)S(1)}, u32[]{:S(2)}, u32[]{:S(2)}) collective-permute-start(f32[8,64,128]{2,1,0:T(8,128)S(1)} %broadcast_select_fusion.2), channel_id=1, source_target_pairs={{0,8},{4,12},{8,0},{12,4},{16,24},{20,28},{24,16},{28,20},{1,9},{5... | collective-permute-start | bytes 786440 | tf_op jit(solution)/shard_map/ppermute | solution.py:368
  26.3 2.6 %collective-permute-start.7 = (f32[192,128]{1,0:T(8,128)S(1)}, f32[192,128]{1,0:T(8,128)S(1)}, u32[]{:S(2)}, u32[]{:S(2)}) collective-permute-start(f32[192,128]{1,0:T(8,128)S(1)} %broadcast_select_fusion.7), channel_id=1, source_target_pairs={{0,4},{4,0},{8,12},{12,8},{16,20},{20,16},{24,28},{28,24},{1,5},{5... | collective-permute-start | bytes 294920 | tf_op jit(solution)/shard_map/ppermute | solution.py:368
  26.4 7.4 %collective-permute-start.10 = (f32[3,128,128]{2,1,0:T(8,128)S(1)}, f32[3,128,128]{2,1,0:T(8,128)S(1)}, u32[]{:S(2)}, u32[]{:S(2)}) collective-permute-start(f32[3,128,128]{2,1,0:T(8,128)S(1)} %broadcast_select_fusion.5.rows_ref), channel_id=1, source_target_pairs={{0,1},{1,0},{2,3},{3,2},{4,5},{5,4},{6,7},{7,6},{8,9},{9,8},{10,11... | collective-permute-start | bytes 589832 | tf_op jit(solution)/shard_map/ppermute | solution.py:368
  28.9 4.9 %collective-permute-start.11 = (f32[8,64,128]{2,1,0:T(8,128)S(1)}, f32[8,64,128]{2,1,0:T(8,128)S(1)}, u32[]{:S(2)}, u32[]{:S(2)}) collective-permute-start(f32[8,64,128]{2,1,0:T(8,128)S(1)} %broadcast_select_fusion.1.ha_ref), channel_id=1, source_target_pairs={{0,4},{4,0},{8,12},{12,8},{16,20},{20,16},{24,28},{28,24},{1,5},{5... | collective-permute-start | bytes 786440 | tf_op jit(solution)/shard_map/ppermute | solution.py:368
  29.0 4.8 %collective-permute-start.12 = (f32[8,64,128]{2,1,0:T(8,128)S(1)}, f32[8,64,128]{2,1,0:T(8,128)S(1)}, u32[]{:S(2)}, u32[]{:S(2)}) collective-permute-start(f32[8,64,128]{2,1,0:T(8,128)S(1)} %broadcast_select_fusion.3.hb_ref), channel_id=1, source_target_pairs={{0,4},{4,0},{8,12},{12,8},{16,20},{20,16},{24,28},{28,24},{1,5},{5... | collective-permute-start | bytes 786440 | tf_op jit(solution)/shard_map/ppermute | solution.py:368
  29.5 4.3 %copy-start.1 = (f32[4,128,8,128]{3,2,1,0:T(8,128)S(1)}, f32[4,128,8,128]{3,2,1,0:T(8,128)}, u32[]{:S(2)}) copy-start(f32[4,128,8,128]{3,2,1,0:T(8,128)} %matrix_ref.5) | copy-start | bytes 6291460

commit v22 on v21

--- a/solution.py
+++ b/solution.py
@@ -78,10 +78,13 @@
             rest_of = 2.0 - pivot * guess
             recip = guess * rest_of
             root = lax.rsqrt(pivot)
+            factors = {j: unit[j, k] * recip for j in range(k + 1, SUB)}
             for j in range(k + 1, SUB):
                 for i in range(j, SUB):
-                    unit[i, j] = unit[i, j] - (unit[i, k] * unit[j, k] * guess) * rest_of
-            factors = {j: unit[j, k] * recip for j in range(k + 1, SUB)}
+                    if i == j == k + 1:
+                        unit[i, j] = unit[i, j] - (unit[i, k] * unit[j, k] * guess) * rest_of
+                    else:
+                        unit[i, j] = unit[i, j] - unit[i, k] * factors[j]
             for j in range(k + 1, SUB):
                 spread[j] = spread[j] - spread[k] * factors[j][None]
             for m in sides:
@@ -309,40 +312,30 @@
     solved = times(rows_left_ref[...], tall(w1.T))
     left = wide(solved)
     inverse = wide(w1)
+
+    def solve_top(j):
+        return tall(times(inverse, top_left_ref[:, j * n:(j + 2) * n]))
+
     copies = []
+    top = solve_top(0)
     for j in range(0, local_cols, 2):
-        pair = (j, j + 1)
-        update = times(left, tall(times(inverse, top_left_ref[:, j * n:(j + 2) * n])))
-        for b in pair:
-            part = update[:, (b - j) * n:(b - j + 1) * n].reshape(local_rows, n, n)
-            result[b] = blocks_ref[b] - part
-        if j == 0:
-            @pl.when(grid_col == 0)
-            def _():
-                result[0] = solved_ref[...].reshape(local_rows, n, n)
-
-            @pl.when(grid_col == 1)
-            def _():
-                result[0] = solved.reshape(local_rows, n, n)
-
-        @pl.when(grid_row <= 1)
-        def _():
-            for b in pair:
-                if b > 0:
-                    result[b, 0] = jnp.zeros((n, n), jnp.float32)
-            if j == 0:
-                @pl.when(grid_col > grid_row)
-                def _():
-                    result[0, 0] = jnp.zeros((n, n), jnp.float32)
-
-                @pl.when((grid_row == 0) & (grid_col == 0))
-                def _():
-                    result[0, 0] = f0_ref[...]
-
-                @pl.when((grid_row == 1) & (grid_col == 1))
-                def _():
-                    result[0, 0] = f1_ref[...]
-        for b in pair:
+        now = top
+        if j + 2 < local_cols:
+            top = solve_top(j + 2)
+        update = times(left, now)
+        for b in (j, j + 1):
+            value = blocks_ref[b] - update[:, (b - j) * n:(b - j + 1) * n].reshape(local_rows, n, n)
+            zero = jnp.zeros((n, n), jnp.float32)
+            if b == 0:
+                value = jnp.where(grid_col == 0, solved_ref[...].reshape(local_rows, n, n), value)
+                value = jnp.where(grid_col == 1, solved.reshape(local_rows, n, n), value)
+                head = jnp.where((grid_row <= 1) & (grid_col > grid_row), zero, value[0])
+                head = jnp.where((grid_row == 0) & (grid_col == 0), f0_ref[...], head)
+                head = jnp.where((grid_row == 1) & (grid_col == 1), f1_ref[...], head)
+            else:
+                head = jnp.where(grid_row <= 1, zero, value[0])
+            result[b, 0] = head
+            result[b, 1:] = value[1:]
             copy = pltpu.make_async_copy(result.at[b], out_ref.at[:, :, b, :], sems.at[b])
             copy.start()
             copies.append(copy)

time: 44.8 us -> 42.8 us (0.955)
  Pallas kernels: 16 us -> 13.8 us
    pallas_call x1, Pallas kernels: 4.36 us -> 2.62 us  [settle(): pl.pallas_call(settle_kernel, out_shape=jax.ShapeDtypeStruct((local_rows,...]
  transfers between devices with their start and end apart: 13 -> 13, of which waited for: 6 -> 7; matrix products, arithmetic and copies ran while one was open for 0% -> 0% of each run, Pallas kernels for 10% -> 10%
where the time goes in v22:
time: 42.8 us; the launch traced here: 42.7 us
  starting transfers between devices  15.2 us (36%)
  Pallas kernels  13.8 us (32%)
  waiting for transfers between devices  11.7 us (27%)
  local copies, waits for them, and re-layouts  1.59 us (4%)
    ppermute x13, starting transfers between devices, exchange(): return lax.ppermute(value, axis, [(i, i ^ mask) for i in range(size)])  15.2 us
    ppermute x13, waiting for transfers between devices, exchange(): return lax.ppermute(value, axis, [(i, i ^ mask) for i in range(size)])  11.7 us
    pallas_call x1, Pallas kernels, second_factor(): pl.pallas_call(second_factor_kernel, out_shape=[square, square, solved, r...  6.34 us
    pallas_call x1, Pallas kernels, first_factor(): pl.pallas_call(first_factor_kernel, out_shape=[square] * 3, in_specs=[VME...  4.05 us
    pallas_call x1, Pallas kernels, settle(): pl.pallas_call(settle_kernel, out_shape=jax.ShapeDtypeStruct((local_rows,...  2.62 us
    unnamed x4, local copies, waits for them, and re-layouts  1.59 us
  transfers between devices with their start and end apart: 13, of which 7 were waited for; matrix products, arithmetic and copies ran while one was open for 0% of the time, Pallas kernels for 10%

profile of v22, /device:TPU:0, one launch (start us, length us, event | category | flops | bytes accessed | tf_op | source)
XLA Modules:
  0.0 42.7 jit_solution(736962340728369985)
XLA Ops:
  0.0 0.0 copy-start
  0.0 1.6 %copy-done = f32[4,128,8,128]{3,2,1,0:T(8,128)S(1)} copy-done((f32[4,128,8,128]{3,2,1,0:T(8,128)S(1)}, f32[4,128,8,128]{3,2,1,0:T(8,128)}, u32[]{:S(2)}) %copy-start) | copy-done | bytes 2097176
  1.6 0.7 %panels.1 = (f32[3,128,128]{2,1,0:T(8,128)S(1)}, f32[8,64,128]{2,1,0:T(8,128)S(1)}, f32[8,64,128]{2,1,0:T(8,128)S(1)}) custom-call(f32[4,128,8,128]{3,2,1,0:T(8,128)S(1)} %copy-done), custom_call_target="tpu_custom_call" | custom-call | bytes 4194304 | tf_op jit(solution)/shard_map/panels/pallas_call | solution.py:161
  2.3 3.0 %collective-permute-start.2 = (f32[8,64,128]{2,1,0:T(8,128)S(1)}, f32[8,64,128]{2,1,0:T(8,128)S(1)}, u32[]{:S(2)}, u32[]{:S(2)}) collective-permute-start(f32[8,64,128]{2,1,0:T(8,128)S(1)} %get-tuple-element.46), channel_id=1, source_target_pairs={{0,8},{4,12},{8,0},{12,4},{16,24},{20,28},{24,16},{28,20},{1,9},{5... | collective-permute-start | bytes 786440 | tf_op jit(solution)/shard_map/ppermute | solution.py:361
  5.3 0.1 corner_block.1
  5.4 2.7 %collective-permute-start = (f32[128,128]{1,0:T(8,128)S(1)}, f32[128,128]{1,0:T(8,128)S(1)}, u32[]{:S(2)}, u32[]{:S(2)}) collective-permute-start(f32[128,128]{1,0:T(8,128)S(1)} %corner_block.1), channel_id=1, source_target_pairs={{0,2},{1,3},{2,0},{3,1},{4,6},{5,7},{6,4},{7,5},{8,10},{9,11},{10,... | collective-permute-start | bytes 196616 | tf_op jit(solution)/shard_map/ppermute | solution.py:361
  8.0 1.5 %collective-permute-start.3 = (f32[8,64,128]{2,1,0:T(8,128)S(1)}, f32[8,64,128]{2,1,0:T(8,128)S(1)}, u32[]{:S(2)}, u32[]{:S(2)}) collective-permute-start(f32[8,64,128]{2,1,0:T(8,128)S(1)} %get-tuple-element.47), channel_id=1, source_target_pairs={{0,16},{4,20},{8,24},{12,28},{16,0},{20,4},{24,8},{28,12},{1,17},{... | collective-permute-start | bytes 786440 | tf_op jit(solution)/shard_map/ppermute | solution.py:361
  9.5 1.4 %collective-permute-done = f32[128,128]{1,0:T(8,128)S(1)} collective-permute-done((f32[128,128]{1,0:T(8,128)S(1)}, f32[128,128]{1,0:T(8,128)S(1)}, u32[]{:S(2)}, u32[]{:S(2)}) %collective-permute-start) | collective-permute-done | bytes 65568 | tf_op jit(solution)/shard_map/ppermute | solution.py:361
  10.9 1.3 %collective-permute-start.1 = (f32[128,128]{1,0:T(8,128)S(1)}, f32[128,128]{1,0:T(8,128)S(1)}, u32[]{:S(2)}, u32[]{:S(2)}) collective-permute-start(f32[128,128]{1,0:T(8,128)S(1)} %get-tuple-element.79.block_ref), channel_id=1, source_target_pairs={{0,1},{1,0},{2,3},{3,2},{4,5},{5,4},{6,7},{7,6},{8,9},{9,8},{10,11... | collective-permute-start | bytes 196616 | tf_op jit(solution)/shard_map/ppermute | solution.py:361
  12.2 0.0 collective-permute-done.2
  12.3 3.2 %collective-permute-done.3 = f32[8,64,128]{2,1,0:T(8,128)S(1)} collective-permute-done((f32[8,64,128]{2,1,0:T(8,128)S(1)}, f32[8,64,128]{2,1,0:T(8,128)S(1)}, u32[]{:S(2)}, u32[]{:S(2)}) %collective-permute-start.3) | collective-permute-done | bytes 262176 | tf_op jit(solution)/shard_map/ppermute | solution.py:361
  15.5 0.0 collective-permute-done.1.across_ref
  15.5 0.1 pack.1
  15.6 0.6 %collective-permute-start.4 = (f32[192,128]{1,0:T(8,128)S(1)}, f32[192,128]{1,0:T(8,128)S(1)}, u32[]{:S(2)}, u32[]{:S(2)}) collective-permute-start(f32[192,128]{1,0:T(8,128)S(1)} %get-tuple-element.51), channel_id=1, source_target_pairs={{0,8},{4,12},{8,0},{12,4},{16,24},{20,28},{24,16},{28,20},{1,9},{5... | collective-permute-start | bytes 294920 | tf_op jit(solution)/shard_map/ppermute | solution.py:361
  16.2 2.1 %collective-permute-start.6 = (f32[3,128,128]{2,1,0:T(8,128)S(1)}, f32[3,128,128]{2,1,0:T(8,128)S(1)}, u32[]{:S(2)}, u32[]{:S(2)}) collective-permute-start(f32[3,128,128]{2,1,0:T(8,128)S(1)} %get-tuple-element.55), channel_id=1, source_target_pairs={{0,2},{1,3},{2,0},{3,1},{4,6},{5,7},{6,4},{7,5},{8,10},{9,11},{10,... | collective-permute-start | bytes 589832 | tf_op jit(solution)/shard_map/ppermute | solution.py:361
  18.4 2.0 %collective-permute-done.4 = f32[192,128]{1,0:T(8,128)S(1)} collective-permute-done((f32[192,128]{1,0:T(8,128)S(1)}, f32[192,128]{1,0:T(8,128)S(1)}, u32[]{:S(2)}, u32[]{:S(2)}) %collective-permute-start.4) | collective-permute-done | bytes 98336 | tf_op jit(solution)/shard_map/ppermute | solution.py:361
  20.3 1.6 %collective-permute-start.5 = (f32[192,128]{1,0:T(8,128)S(1)}, f32[192,128]{1,0:T(8,128)S(1)}, u32[]{:S(2)}, u32[]{:S(2)}) collective-permute-start(f32[192,128]{1,0:T(8,128)S(1)} %broadcast_select_fusion.6), channel_id=1, source_target_pairs={{0,16},{4,20},{8,24},{12,28},{16,0},{20,4},{24,8},{28,12},{1,17},{... | collective-permute-start | bytes 294920 | tf_op jit(solution)/shard_map/ppermute | solution.py:361
  21.9 0.5 %collective-permute-start.8 = (f32[8,64,128]{2,1,0:T(8,128)S(1)}, f32[8,64,128]{2,1,0:T(8,128)S(1)}, u32[]{:S(2)}, u32[]{:S(2)}) collective-permute-start(f32[8,64,128]{2,1,0:T(8,128)S(1)} %broadcast_select_fusion.4), channel_id=1, source_target_pairs={{0,16},{4,20},{8,24},{12,28},{16,0},{20,4},{24,8},{28,12},{1,17},{... | collective-permute-start | bytes 786440 | tf_op jit(solution)/shard_map/ppermute | solution.py:361
  22.4 0.5 %collective-permute-start.9 = (f32[8,64,128]{2,1,0:T(8,128)S(1)}, f32[8,64,128]{2,1,0:T(8,128)S(1)}, u32[]{:S(2)}, u32[]{:S(2)}) collective-permute-start(f32[8,64,128]{2,1,0:T(8,128)S(1)} %broadcast_select_fusion.2), channel_id=1, source_target_pairs={{0,8},{4,12},{8,0},{12,4},{16,24},{20,28},{24,16},{28,20},{1,9},{5... | collective-permute-start | bytes 786440 | tf_op jit(solution)/shard_map/ppermute | solution.py:361
  23.0 3.3 %collective-permute-done.6 = f32[3,128,128]{2,1,0:T(8,128)S(1)} collective-permute-done((f32[3,128,128]{2,1,0:T(8,128)S(1)}, f32[3,128,128]{2,1,0:T(8,128)S(1)}, u32[]{:S(2)}, u32[]{:S(2)}) %collective-permute-start.6) | collective-permute-done | bytes 196640 | tf_op jit(solution)/shard_map/ppermute | solution.py:361
  26.3 0.0 collective-permute-done.5
  26.3 0.1 collective-permute-start.7
  26.4 0.7 %collective-permute-start.10 = (f32[3,128,128]{2,1,0:T(8,128)S(1)}, f32[3,128,128]{2,1,0:T(8,128)S(1)}, u32[]{:S(2)}, u32[]{:S(2)}) collective-permute-start(f32[3,128,128]{2,1,0:T(8,128)S(1)} %broadcast_select_fusion.5.rows_ref), channel_id=1, source_target_pairs={{0,1},{1,0},{2,3},{3,2},{4,5},{5,4},{6,7},{7,6},{8,9},{9,8},{10,11... | collective-permute-start | bytes 589832 | tf_op jit(solution)/shard_map/ppermute | solution.py:361
  27.0 1.3 %collective-permute-done.8 = f32[8,64,128]{2,1,0:T(8,128)S(1)} collective-permute-done((f32[8,64,128]{2,1,0:T(8,128)S(1)}, f32[8,64,128]{2,1,0:T(8,128)S(1)}, u32[]{:S(2)}, u32[]{:S(2)}) %collective-permute-start.8) | collective-permute-done | bytes 262176 | tf_op jit(solution)/shard_map/ppermute | solution.py:361
  28.3 0.5 %collective-permute-done.9 = f32[8,64,128]{2,1,0:T(8,128)S(1)} collective-permute-done((f32[8,64,128]{2,1,0:T(8,128)S(1)}, f32[8,64,128]{2,1,0:T(8,128)S(1)}, u32[]{:S(2)}, u32[]{:S(2)}) %collective-permute-start.9) | collective-permute-done | bytes 262176 | tf_op jit(solution)/shard_map/ppermute | solution.py:361
  28.8 0.0 collective-permute-done.7
  28.9 0.1 collective-permute-start.11
  29.0 0.5 %collective-permute-start.12 = (f32[8,64,128]{2,1,0:T(8,128)S(1)}, f32[8,64,128]{2,1,0:T(8,128)S(1)}, u32[]{:S(2)}, u32[]{:S(2)}) collective-permute-start(f32[8,64,128]{2,1,0:T(8,128)S(1)} %broadcast_select_fusion.3.hb_ref), channel_id=1, source_target_pairs={{0,4},{4,0},{8,12},{12,8},{16,20},{20,16},{24,28},{28,24},{1,5},{5... | collective-permute-start | bytes 786440 | tf_op jit(solution)/shard_map/ppermute | solution.py:361
  29.5 0.0 copy-start.1
  29.5 4.0 %first_factor.1 = (f32[128,128]{1,0:T(8,128)S(1)}, f32[128,128]{1,0:T(8,128)S(1)}, f32[128,128]{1,0:T(8,128)S(1)}) custom-call(f32[128,128]{1,0:T(8,128)S(1)} %get-tuple-element.76.a_ref, f32[128,128]{1,0:T(8,128)S(1)} %pad_maximum_fusion.side_ref), custom_call_target="tpu_custom_call" | custom-call | flops 8000000000 | bytes 2097152 | tf_op jit(solution)/shard_map/first_factor/pallas_call | solution.py:210
  33.5 0.2 collective-permute-done.10.rows_other_ref
  33.7 0.0 collective-permute-done.11.oa_ref
  33.7 0.0 collective-permute-done.12.ob_ref
  33.7 0.0 copy-done.1
  33.7 6.3 %second_factor.1 = (f32[128,128]{1,0:T(8,128)S(1)}, f32[128,128]{1,0:T(8,128)S(1)}, f32[512,128]{1,0:T(8,128)S(1)}, bf16[512,768]{1,0:T(8,128)(2,1)S(1)}, bf16[7...) custom-call(f32[128,128]{1,0:T(8,128)S(1)} %get-tuple-element.75.a_ref, ...), custom_call_target="tpu_custom_call" | custom-call | flops 8000000000 | bytes 4194304 | tf_op jit(solution)/shard_map/second_factor/pallas_call | solution.py:290
  40.1 2.6 %settle.1 = f32[4,128,8,128]{3,2,1,0:T(8,128)} custom-call(f32[128,128]{1,0:T(8,128)S(1)} %get-tuple-element.62.f0_ref, f32[128,128]{1,0:T(8,128)S(1)} %get-tuple-element.69.f1_ref, f32[128,128]{1,0:T(8,128)S(1)} %get-tuple-element.70.w_ref, f32[512,128]{1,0:T(8,128)S(1)} %get-tuple-element.71.solved_ref, ...), custom_call_target="tpu_custom_call" | custom-call | flops 4000000000 | bytes 6291456 | tf_op jit(solution)/shard_map/settle/pallas_call | solution.py:348
  (12 shorter events, 0.2 us)
Async XLA Ops:
  0.0 1.6 %copy-start = (f32[4,128,8,128]{3,2,1,0:T(8,128)S(1)}, f32[4,128,8,128]{3,2,1,0:T(8,128)}, u32[]{:S(2)}) copy-start(f32[4,128,8,128]{3,2,1,0:T(8,128)} %matrix_ref.5) | copy-start | bytes 6291460
  2.3 10.0 %collective-permute-start.2 = (f32[8,64,128]{2,1,0:T(8,128)S(1)}, f32[8,64,128]{2,1,0:T(8,128)S(1)}, u32[]{:S(2)}, u32[]{:S(2)}) collective-permute-start(f32[8,64,128]{2,1,0:T(8,128)S(1)} %get-tuple-element.46), channel_id=1, source_target_pairs={{0,8},{4,12},{8,0},{12,4},{16,24},{20,28},{24,16},{28,20},{1,9},{5... | collective-permute-start | bytes 786440 | tf_op jit(solution)/shard_map/ppermute | solution.py:361
  5.4 5.5 %collective-permute-start = (f32[128,128]{1,0:T(8,128)S(1)}, f32[128,128]{1,0:T(8,128)S(1)}, u32[]{:S(2)}, u32[]{:S(2)}) collective-permute-start(f32[128,128]{1,0:T(8,128)S(1)} %corner_block.1), channel_id=1, source_target_pairs={{0,2},{1,3},{2,0},{3,1},{4,6},{5,7},{6,4},{7,5},{8,10},{9,11},{10,... | collective-permute-start | bytes 196616 | tf_op jit(solution)/shard_map/ppermute | solution.py:361
  8.0 7.5 %collective-permute-start.3 = (f32[8,64,128]{2,1,0:T(8,128)S(1)}, f32[8,64,128]{2,1,0:T(8,128)S(1)}, u32[]{:S(2)}, u32[]{:S(2)}) collective-permute-start(f32[8,64,128]{2,1,0:T(8,128)S(1)} %get-tuple-element.47), channel_id=1, source_target_pairs={{0,16},{4,20},{8,24},{12,28},{16,0},{20,4},{24,8},{28,12},{1,17},{... | collective-permute-start | bytes 786440 | tf_op jit(solution)/shard_map/ppermute | solution.py:361
  10.9 4.6 %collective-permute-start.1 = (f32[128,128]{1,0:T(8,128)S(1)}, f32[128,128]{1,0:T(8,128)S(1)}, u32[]{:S(2)}, u32[]{:S(2)}) collective-permute-start(f32[128,128]{1,0:T(8,128)S(1)} %get-tuple-element.79.block_ref), channel_id=1, source_target_pairs={{0,1},{1,0},{2,3},{3,2},{4,5},{5,4},{6,7},{7,6},{8,9},{9,8},{10,11... | collective-permute-start | bytes 196616 | tf_op jit(solution)/shard_map/ppermute | solution.py:361
  15.6 4.7 %collective-permute-start.4 = (f32[192,128]{1,0:T(8,128)S(1)}, f32[192,128]{1,0:T(8,128)S(1)}, u32[]{:S(2)}, u32[]{:S(2)}) collective-permute-start(f32[192,128]{1,0:T(8,128)S(1)} %get-tuple-element.51), channel_id=1, source_target_pairs={{0,8},{4,12},{8,0},{12,4},{16,24},{20,28},{24,16},{28,20},{1,9},{5... | collective-permute-start | bytes 294920 | tf_op jit(solution)/shard_map/ppermute | solution.py:361
  16.2 10.0 %collective-permute-start.6 = (f32[3,128,128]{2,1,0:T(8,128)S(1)}, f32[3,128,128]{2,1,0:T(8,128)S(1)}, u32[]{:S(2)}, u32[]{:S(2)}) collective-permute-start(f32[3,128,128]{2,1,0:T(8,128)S(1)} %get-tuple-element.55), channel_id=1, source_target_pairs={{0,2},{1,3},{2,0},{3,1},{4,6},{5,7},{6,4},{7,5},{8,10},{9,11},{10,... | collective-permute-start | bytes 589832 | tf_op jit(solution)/shard_map/ppermute | solution.py:361
  20.3 5.9 %collective-permute-start.5 = (f32[192,128]{1,0:T(8,128)S(1)}, f32[192,128]{1,0:T(8,128)S(1)}, u32[]{:S(2)}, u32[]{:S(2)}) collective-permute-start(f32[192,128]{1,0:T(8,128)S(1)} %broadcast_select_fusion.6), channel_id=1, source_target_pairs={{0,16},{4,20},{8,24},{12,28},{16,0},{20,4},{24,8},{28,12},{1,17},{... | collective-permute-start | bytes 294920 | tf_op jit(solution)/shard_map/ppermute | solution.py:361
  21.9 6.4 %collective-permute-start.8 = (f32[8,64,128]{2,1,0:T(8,128)S(1)}, f32[8,64,128]{2,1,0:T(8,128)S(1)}, u32[]{:S(2)}, u32[]{:S(2)}) collective-permute-start(f32[8,64,128]{2,1,0:T(8,128)S(1)} %broadcast_select_fusion.4), channel_id=1, source_target_pairs={{0,16},{4,20},{8,24},{12,28},{16,0},{20,4},{24,8},{28,12},{1,17},{... | collective-permute-start | bytes 786440 | tf_op jit(solution)/shard_map/ppermute | solution.py:361
  22.4 6.4 %collective-permute-start.9 = (f32[8,64,128]{2,1,0:T(8,128)S(1)}, f32[8,64,128]{2,1,0:T(8,128)S(1)}, u32[]{:S(2)}, u32[]{:S(2)}) collective-permute-start(f32[8,64,128]{2,1,0:T(8,128)S(1)} %broadcast_select_fusion.2), channel_id=1, source_target_pairs={{0,8},{4,12},{8,0},{12,4},{16,24},{20,28},{24,16},{28,20},{1,9},{5... | collective-permute-start | bytes 786440 | tf_op jit(solution)/shard_map/ppermute | solution.py:361
  26.3 2.6 %collective-permute-start.7 = (f32[192,128]{1,0:T(8,128)S(1)}, f32[192,128]{1,0:T(8,128)S(1)}, u32[]{:S(2)}, u32[]{:S(2)}) collective-permute-start(f32[192,128]{1,0:T(8,128)S(1)} %broadcast_select_fusion.7), channel_id=1, source_target_pairs={{0,4},{4,0},{8,12},{12,8},{16,20},{20,16},{24,28},{28,24},{1,5},{5... | collective-permute-start | bytes 294920 | tf_op jit(solution)/shard_map/ppermute | solution.py:361
  26.4 7.3 %collective-permute-start.10 = (f32[3,128,128]{2,1,0:T(8,128)S(1)}, f32[3,128,128]{2,1,0:T(8,128)S(1)}, u32[]{:S(2)}, u32[]{:S(2)}) collective-permute-start(f32[3,128,128]{2,1,0:T(8,128)S(1)} %broadcast_select_fusion.5.rows_ref), channel_id=1, source_target_pairs={{0,1},{1,0},{2,3},{3,2},{4,5},{5,4},{6,7},{7,6},{8,9},{9,8},{10,11... | collective-permute-start | bytes 589832 | tf_op jit(solution)/shard_map/ppermute | solution.py:361
  28.9 4.8 %collective-permute-start.11 = (f32[8,64,128]{2,1,0:T(8,128)S(1)}, f32[8,64,128]{2,1,0:T(8,128)S(1)}, u32[]{:S(2)}, u32[]{:S(2)}) collective-permute-start(f32[8,64,128]{2,1,0:T(8,128)S(1)} %broadcast_select_fusion.1.ha_ref), channel_id=1, source_target_pairs={{0,4},{4,0},{8,12},{12,8},{16,20},{20,16},{24,28},{28,24},{1,5},{5... | collective-permute-start | bytes 786440 | tf_op jit(solution)/shard_map/ppermute | solution.py:361
  29.0 4.7 %collective-permute-start.12 = (f32[8,64,128]{2,1,0:T(8,128)S(1)}, f32[8,64,128]{2,1,0:T(8,128)S(1)}, u32[]{:S(2)}, u32[]{:S(2)}) collective-permute-start(f32[8,64,128]{2,1,0:T(8,128)S(1)} %broadcast_select_fusion.3.hb_ref), channel_id=1, source_target_pairs={{0,4},{4,0},{8,12},{12,8},{16,20},{20,16},{24,28},{28,24},{1,5},{5... | collective-permute-start | bytes 786440 | tf_op jit(solution)/shard_map/ppermute | solution.py:361
  29.5 4.2 %copy-start.1 = (f32[4,128,8,128]{3,2,1,0:T(8,128)S(1)}, f32[4,128,8,128]{3,2,1,0:T(8,128)}, u32[]{:S(2)}) copy-start(f32[4,128,8,128]{3,2,1,0:T(8,128)} %matrix_ref.5) | copy-start | bytes 6291460

commit v23 on v22

--- a/solution.py
+++ b/solution.py
@@ -1,3 +1,5 @@
+import functools
+
 import jax
 import jax.numpy as jnp
 from jax import lax
@@ -122,29 +124,11 @@
     return pl.CostEstimate(flops=flops, bytes_accessed=nbytes, transcendentals=0)
 
 
-def corner_kernel(matrix_ref, block_ref, sem):
-    copy = pltpu.make_async_copy(matrix_ref.at[0, :, 0, :], block_ref, sem)
-    copy.start()
-    copy.wait()
-
-
-def corner_block(matrix):
-    n = matrix.shape[1]
-    return pl.pallas_call(
-        corner_kernel,
-        out_shape=jax.ShapeDtypeStruct((n, n), jnp.float32),
-        in_specs=[HBM],
-        out_specs=VMEM,
-        scratch_shapes=[pltpu.SemaphoreType.DMA(())],
-        compiler_params=pltpu.CompilerParams(vmem_limit_bytes=2 * MIB),
-        cost_estimate=estimate(0, 3 * MIB),
-        name="corner_block",
-    )(matrix)
-
-
-def panels_kernel(matrix_ref, column_ref, upper_ref, lower_ref, sems):
+def panels_kernel(matrix_ref, block_ref, column_ref, upper_ref, lower_ref, sems):
     local_cols, half, _ = upper_ref.shape
-    copies = [pltpu.make_async_copy(matrix_ref.at[pl.ds(1, column_ref.shape[0]), :, 0, :], column_ref, sems.at[0])]
+    copies = [
+        pltpu.make_async_copy(matrix_ref.at[0, :, 0, :], block_ref, sems.at[2 * local_cols + 1]),
+        pltpu.make_async_copy(matrix_ref.at[pl.ds(1, column_ref.shape[0]), :, 0, :], column_ref, sems.at[0])]
     for j in range(local_cols):
         copies.append(pltpu.make_async_copy(matrix_ref.at[0, pl.ds(0, half), j, :], upper_ref.at[j], sems.at[1 + j]))
         copies.append(pltpu.make_async_copy(
@@ -160,14 +144,31 @@
     strip = jax.ShapeDtypeStruct((local_cols, n // 2, n), jnp.float32)
     return pl.pallas_call(
         panels_kernel,
-        out_shape=[jax.ShapeDtypeStruct((local_rows - 1, n, n), jnp.float32), strip, strip],
+        out_shape=[
+            jax.ShapeDtypeStruct((n, n), jnp.float32), jax.ShapeDtypeStruct((local_rows - 1, n, n), jnp.float32), strip, strip],
         in_specs=[HBM],
-        out_specs=[VMEM] * 3,
-        scratch_shapes=[pltpu.SemaphoreType.DMA((1 + 2 * local_cols,))],
+        out_specs=[VMEM] * 4,
+        scratch_shapes=[pltpu.SemaphoreType.DMA((2 + 2 * local_cols,))],
         compiler_params=pltpu.CompilerParams(vmem_limit_bytes=4 * MIB),
         cost_estimate=estimate(0, 4 * MIB),
         name="panels",
     )(matrix)
+
+
+def pick_kernel(bit, new_ref, old_ref, out_ref):
+    out_ref[...] = jnp.where(bit_set(lax.axis_index("col"), bit), new_ref[...], old_ref[...])
+
+
+def pick(new, old, bit):
+    return pl.pallas_call(
+        functools.partial(pick_kernel, bit),
+        out_shape=jax.ShapeDtypeStruct(old.shape, old.dtype),
+        in_specs=[VMEM] * 2,
+        out_specs=VMEM,
+        compiler_params=pltpu.CompilerParams(vmem_limit_bytes=2 * MIB),
+        cost_estimate=estimate(8 * 10**9, 2 * MIB),
+        name="pick",
+    )(new, old)
 
 
 def pack_kernel(across_ref, block_ref, both_ref, message_ref):
@@ -247,25 +248,25 @@
 
     def solve_top(j):
         def step():
-            right[...] = tall(times(wide(w0), tall(top(0, j))))
-            top_left_ref[:, j * n:(j + 2) * n] = tall(top(1, j) - times(wide(cross.T), right[...]))
+            solved = tall(times(wide(w0), tall(top(0, j))))
+            right[:, j * n:(j + 2) * n] = solved
+            top_left_ref[:, j * n:(j + 2) * n] = tall(top(1, j) - times(wide(cross.T), solved))
         return step
 
     def update(j, i):
         def step():
-            if i == 0:
-                copies[j].wait()
-                copies[j + 1].wait()
-            change = times(left[i * n:(i + 2) * n], right[...])
+            if i == 0 and j == 0:
+                for copy in copies:
+                    copy.wait()
+            change = times(left[i * n:(i + 2) * n], right[:, j * n:(j + 2) * n])
             for b in range(2):
                 part = change[:, b * n:(b + 1) * n].reshape(2, n, n)
                 blocks_ref[j + b, i:i + 2] = blocks_ref[j + b, i:i + 2] - part
         return step
 
     steps = [solve_rows, update_rows]
-    for j in range(0, local_cols, 2):
-        steps.append(solve_top(j))
-        steps.extend(update(j, i) for i in range(0, local_rows, 2))
+    steps.extend(solve_top(j) for j in range(0, local_cols, 2))
+    steps.extend(update(j, i) for j in range(0, local_cols, 2) for i in range(0, local_rows, 2))
 
     groups = n // SUB
     each = -(-len(steps) // groups)
@@ -294,7 +295,7 @@
         out_specs=[VMEM] * 6,
         scratch_shapes=[
             pltpu.VMEM((local_rows * n, 6 * n), jnp.bfloat16),
-            pltpu.VMEM((6 * n, 2 * n), jnp.bfloat16),
+            pltpu.VMEM((6 * n, local_cols * n), jnp.bfloat16),
             pltpu.SemaphoreType.DMA((local_cols,)),
         ] + elimination_scratch(n, 2),
         compiler_params=pltpu.CompilerParams(vmem_limit_bytes=20 * MIB),
@@ -372,16 +373,6 @@
     return held
 
 
-def region(run, *values):
-    shapes = jax.eval_shape(run, *values)
-
-    def skip(*_):
-        return jax.tree.map(lambda leaf: jnp.zeros(leaf.shape, leaf.dtype), shapes)
-
-    everywhere = lax.axis_index("row") < lax.axis_size("row")
-    return lax.cond(everywhere, run, skip, *values)
-
-
 def after(value, *others):
     return lax.optimization_barrier((value,) + others)
 
@@ -395,19 +386,15 @@
     col_bits = list(range(1, n_col.bit_length() - 1))
     odd = (grid_row % 2) == 1
 
-    block = corner_block(kernel)
-    column, upper, lower = panels(kernel)
+    block, column, upper, lower = panels(kernel)
     first_bit, last_bit = row_bits[0], row_bits[-1]
 
     moved = exchange(block, "col", 1 << col_bits[0], n_col)
     upper_moved = exchange(upper, "row", 1 << first_bit, n_row)
     lower_moved = exchange(lower, "row", 1 << last_bit, n_row)
 
-    def along_col(new, old):
-        block = jnp.where(bit_set(grid_col, col_bits[0]), new, old)
-        return spread(block, "col", grid_col, n_col, col_bits[1:])
-
-    block = region(along_col, moved, block)
+    block = pick(moved, block, col_bits[0])
+    block = spread(block, "col", grid_col, n_col, col_bits[1:])
     across = exchange(block, "col", 1, n_col)
     ha = jnp.where(bit_set(grid_row, first_bit), upper_moved, upper)
     hb = jnp.where(bit_set(grid_row, last_bit), lower_moved, lower)

time: 42.8 us -> 42.6 us (level)
  waiting for transfers between devices: 11.7 us -> 12.3 us
  starting transfers between devices: 15.2 us -> 14.6 us
    ppermute x13, waiting for transfers between devices: 11.7 us -> 12.3 us  [exchange(): return lax.ppermute(value, axis, [(i, i ^ mask) for i in range(size)])]
    ppermute x13, starting transfers between devices: 15.2 us -> 14.6 us  [exchange(): return lax.ppermute(value, axis, [(i, i ^ mask) for i in range(size)])]
  transfers between devices with their start and end apart: 13 -> 13, of which waited for: 7 -> 8; matrix products, arithmetic and copies ran while one was open for 0% -> 0% of each run, Pallas kernels for 10% -> 10%
where the time goes in v23:
time: 42.6 us; the launch traced here: 42.4 us
  starting transfers between devices  14.6 us (34%)
  Pallas kernels  13.6 us (32%)
  waiting for transfers between devices  12.3 us (29%)
  local copies, waits for them, and re-layouts  1.59 us (4%)
    ppermute x13, starting transfers between devices, exchange(): return lax.ppermute(value, axis, [(i, i ^ mask) for i in range(size)])  14.6 us
    ppermute x13, waiting for transfers between devices, exchange(): return lax.ppermute(value, axis, [(i, i ^ mask) for i in range(size)])  12.3 us
    pallas_call x1, Pallas kernels, second_factor(): pl.pallas_call(second_factor_kernel, out_shape=[square, square, solved, r...  6.07 us
    pallas_call x1, Pallas kernels, first_factor(): pl.pallas_call(first_factor_kernel, out_shape=[square] * 3, in_specs=[VME...  4.05 us
    pallas_call x1, Pallas kernels, settle(): pl.pallas_call(settle_kernel, out_shape=jax.ShapeDtypeStruct((local_rows,...  2.62 us
    unnamed x4, local copies, waits for them, and re-layouts  1.59 us
  transfers between devices with their start and end apart: 13, of which 8 were waited for; matrix products, arithmetic and copies ran while one was open for 0% of the time, Pallas kernels for 10%

profile of v23, /device:TPU:0, one launch (start us, length us, event | category | flops | bytes accessed | tf_op | source)
XLA Modules:
  0.0 42.4 jit_solution(13709181012541544710)
XLA Ops:
  0.0 0.0 copy-start
  0.0 1.6 %copy-done = f32[4,128,8,128]{3,2,1,0:T(8,128)S(1)} copy-done((f32[4,128,8,128]{3,2,1,0:T(8,128)S(1)}, f32[4,128,8,128]{3,2,1,0:T(8,128)}, u32[]{:S(2)}) %copy-start) | copy-done | bytes 2097176
  1.6 0.7 %panels.1 = (f32[128,128]{1,0:T(8,128)S(1)}, f32[3,128,128]{2,1,0:T(8,128)S(1)}, f32[8,64,128]{2,1,0:T(8,128)S(1)}, f32[8,64,128]{2,1,0:T(8,128)S(1)}) custom-call(f32[4,128,8,128]{3,2,1,0:T(8,128)S(1)} %copy-done), custom_call_target="tpu_custom_call" | custom-call | bytes 4194304 | tf_op jit(solution)/shard_map/panels/pallas_call | solution.py:145
  2.3 4.1 %collective-permute-start = (f32[128,128]{1,0:T(8,128)S(1)}, f32[128,128]{1,0:T(8,128)S(1)}, u32[]{:S(2)}, u32[]{:S(2)}) collective-permute-start(f32[128,128]{1,0:T(8,128)S(1)} %get-tuple-element.35.old_ref), channel_id=1, source_target_pairs={{0,2},{1,3},{2,0},{3,1},{4,6},{5,7},{6,4},{7,5},{8,10},{9,11},{10,... | collective-permute-start | bytes 196616 | tf_op jit(solution)/shard_map/ppermute | solution.py:362
  6.4 1.5 %collective-permute-start.2 = (f32[8,64,128]{2,1,0:T(8,128)S(1)}, f32[8,64,128]{2,1,0:T(8,128)S(1)}, u32[]{:S(2)}, u32[]{:S(2)}) collective-permute-start(f32[8,64,128]{2,1,0:T(8,128)S(1)} %get-tuple-element.36), channel_id=1, source_target_pairs={{0,8},{4,12},{8,0},{12,4},{16,24},{20,28},{24,16},{28,20},{1,9},{5... | collective-permute-start | bytes 786440 | tf_op jit(solution)/shard_map/ppermute | solution.py:362
  7.9 1.5 %collective-permute-start.3 = (f32[8,64,128]{2,1,0:T(8,128)S(1)}, f32[8,64,128]{2,1,0:T(8,128)S(1)}, u32[]{:S(2)}, u32[]{:S(2)}) collective-permute-start(f32[8,64,128]{2,1,0:T(8,128)S(1)} %get-tuple-element.37), channel_id=1, source_target_pairs={{0,16},{4,20},{8,24},{12,28},{16,0},{20,4},{24,8},{28,12},{1,17},{... | collective-permute-start | bytes 786440 | tf_op jit(solution)/shard_map/ppermute | solution.py:362
  9.5 0.6 %collective-permute-done.new_ref = f32[128,128]{1,0:T(8,128)S(1)} collective-permute-done((f32[128,128]{1,0:T(8,128)S(1)}, f32[128,128]{1,0:T(8,128)S(1)}, u32[]{:S(2)}, u32[]{:S(2)}) %collective-permute-start) | collective-permute-done | bytes 65568 | tf_op jit(solution)/shard_map/ppermute | solution.py:362
  10.1 1.0 %collective-permute-start.1 = (f32[128,128]{1,0:T(8,128)S(1)}, f32[128,128]{1,0:T(8,128)S(1)}, u32[]{:S(2)}, u32[]{:S(2)}) collective-permute-start(f32[128,128]{1,0:T(8,128)S(1)} %pick.1.block_ref), channel_id=1, source_target_pairs={{0,1},{1,0},{2,3},{3,2},{4,5},{5,4},{6,7},{7,6},{8,9},{9,8},{10,11... | collective-permute-start | bytes 196616 | tf_op jit(solution)/shard_map/ppermute | solution.py:362
  11.1 3.1 %collective-permute-done.2 = f32[8,64,128]{2,1,0:T(8,128)S(1)} collective-permute-done((f32[8,64,128]{2,1,0:T(8,128)S(1)}, f32[8,64,128]{2,1,0:T(8,128)S(1)}, u32[]{:S(2)}, u32[]{:S(2)}) %collective-permute-start.2) | collective-permute-done | bytes 262176 | tf_op jit(solution)/shard_map/ppermute | solution.py:362
  14.2 1.2 %collective-permute-done.3 = f32[8,64,128]{2,1,0:T(8,128)S(1)} collective-permute-done((f32[8,64,128]{2,1,0:T(8,128)S(1)}, f32[8,64,128]{2,1,0:T(8,128)S(1)}, u32[]{:S(2)}, u32[]{:S(2)}) %collective-permute-start.3) | collective-permute-done | bytes 262176 | tf_op jit(solution)/shard_map/ppermute | solution.py:362
  15.5 0.0 collective-permute-done.1.across_ref
  15.5 0.1 pack.1
  15.6 0.7 %collective-permute-start.4 = (f32[192,128]{1,0:T(8,128)S(1)}, f32[192,128]{1,0:T(8,128)S(1)}, u32[]{:S(2)}, u32[]{:S(2)}) collective-permute-start(f32[192,128]{1,0:T(8,128)S(1)} %get-tuple-element.41), channel_id=1, source_target_pairs={{0,8},{4,12},{8,0},{12,4},{16,24},{20,28},{24,16},{28,20},{1,9},{5... | collective-permute-start | bytes 294920 | tf_op jit(solution)/shard_map/ppermute | solution.py:362
  16.3 1.7 %collective-permute-start.6 = (f32[3,128,128]{2,1,0:T(8,128)S(1)}, f32[3,128,128]{2,1,0:T(8,128)S(1)}, u32[]{:S(2)}, u32[]{:S(2)}) collective-permute-start(f32[3,128,128]{2,1,0:T(8,128)S(1)} %get-tuple-element.45), channel_id=1, source_target_pairs={{0,2},{1,3},{2,0},{3,1},{4,6},{5,7},{6,4},{7,5},{8,10},{9,11},{10,... | collective-permute-start | bytes 589832 | tf_op jit(solution)/shard_map/ppermute | solution.py:362
  18.0 2.2 %collective-permute-done.4 = f32[192,128]{1,0:T(8,128)S(1)} collective-permute-done((f32[192,128]{1,0:T(8,128)S(1)}, f32[192,128]{1,0:T(8,128)S(1)}, u32[]{:S(2)}, u32[]{:S(2)}) %collective-permute-start.4) | collective-permute-done | bytes 98336 | tf_op jit(solution)/shard_map/ppermute | solution.py:362
  20.3 1.6 %collective-permute-start.5 = (f32[192,128]{1,0:T(8,128)S(1)}, f32[192,128]{1,0:T(8,128)S(1)}, u32[]{:S(2)}, u32[]{:S(2)}) collective-permute-start(f32[192,128]{1,0:T(8,128)S(1)} %broadcast_select_fusion.5), channel_id=1, source_target_pairs={{0,16},{4,20},{8,24},{12,28},{16,0},{20,4},{24,8},{28,12},{1,17},{... | collective-permute-start | bytes 294920 | tf_op jit(solution)/shard_map/ppermute | solution.py:362
  21.9 0.5 %collective-permute-start.8 = (f32[8,64,128]{2,1,0:T(8,128)S(1)}, f32[8,64,128]{2,1,0:T(8,128)S(1)}, u32[]{:S(2)}, u32[]{:S(2)}) collective-permute-start(f32[8,64,128]{2,1,0:T(8,128)S(1)} %broadcast_select_fusion.3), channel_id=1, source_target_pairs={{0,16},{4,20},{8,24},{12,28},{16,0},{20,4},{24,8},{28,12},{1,17},{... | collective-permute-start | bytes 786440 | tf_op jit(solution)/shard_map/ppermute | solution.py:362
  22.4 0.7 %collective-permute-start.9 = (f32[8,64,128]{2,1,0:T(8,128)S(1)}, f32[8,64,128]{2,1,0:T(8,128)S(1)}, u32[]{:S(2)}, u32[]{:S(2)}) collective-permute-start(f32[8,64,128]{2,1,0:T(8,128)S(1)} %broadcast_select_fusion.1), channel_id=1, source_target_pairs={{0,8},{4,12},{8,0},{12,4},{16,24},{20,28},{24,16},{28,20},{1,9},{5... | collective-permute-start | bytes 786440 | tf_op jit(solution)/shard_map/ppermute | solution.py:362
  23.0 3.2 %collective-permute-done.6 = f32[3,128,128]{2,1,0:T(8,128)S(1)} collective-permute-done((f32[3,128,128]{2,1,0:T(8,128)S(1)}, f32[3,128,128]{2,1,0:T(8,128)S(1)}, u32[]{:S(2)}, u32[]{:S(2)}) %collective-permute-start.6) | collective-permute-done | bytes 196640 | tf_op jit(solution)/shard_map/ppermute | solution.py:362
  26.3 0.0 collective-permute-done.5
  26.3 0.1 collective-permute-start.7
  26.4 0.6 %collective-permute-start.10 = (f32[3,128,128]{2,1,0:T(8,128)S(1)}, f32[3,128,128]{2,1,0:T(8,128)S(1)}, u32[]{:S(2)}, u32[]{:S(2)}) collective-permute-start(f32[3,128,128]{2,1,0:T(8,128)S(1)} %broadcast_select_fusion.4.rows_ref), channel_id=1, source_target_pairs={{0,1},{1,0},{2,3},{3,2},{4,5},{5,4},{6,7},{7,6},{8,9},{9,8},{10,11... | collective-permute-start | bytes 589832 | tf_op jit(solution)/shard_map/ppermute | solution.py:362
  27.0 1.3 %collective-permute-done.8 = f32[8,64,128]{2,1,0:T(8,128)S(1)} collective-permute-done((f32[8,64,128]{2,1,0:T(8,128)S(1)}, f32[8,64,128]{2,1,0:T(8,128)S(1)}, u32[]{:S(2)}, u32[]{:S(2)}) %collective-permute-start.8) | collective-permute-done | bytes 262176 | tf_op jit(solution)/shard_map/ppermute | solution.py:362
  28.3 0.5 %collective-permute-done.9 = f32[8,64,128]{2,1,0:T(8,128)S(1)} collective-permute-done((f32[8,64,128]{2,1,0:T(8,128)S(1)}, f32[8,64,128]{2,1,0:T(8,128)S(1)}, u32[]{:S(2)}, u32[]{:S(2)}) %collective-permute-start.9) | collective-permute-done | bytes 262176 | tf_op jit(solution)/shard_map/ppermute | solution.py:362
  28.8 0.0 collective-permute-done.7
  28.8 0.1 collective-permute-start.11
  28.9 0.5 %collective-permute-start.12 = (f32[8,64,128]{2,1,0:T(8,128)S(1)}, f32[8,64,128]{2,1,0:T(8,128)S(1)}, u32[]{:S(2)}, u32[]{:S(2)}) collective-permute-start(f32[8,64,128]{2,1,0:T(8,128)S(1)} %broadcast_select_fusion.2.hb_ref), channel_id=1, source_target_pairs={{0,4},{4,0},{8,12},{12,8},{16,20},{20,16},{24,28},{28,24},{1,5},{5... | collective-permute-start | bytes 786440 | tf_op jit(solution)/shard_map/ppermute | solution.py:362
  29.4 0.0 copy-start.1
  29.4 4.1 %first_factor.1 = (f32[128,128]{1,0:T(8,128)S(1)}, f32[128,128]{1,0:T(8,128)S(1)}, f32[128,128]{1,0:T(8,128)S(1)}) custom-call(f32[128,128]{1,0:T(8,128)S(1)} %get-tuple-element.66.a_ref, f32[128,128]{1,0:T(8,128)S(1)} %pad_maximum_fusion.side_ref), custom_call_target="tpu_custom_call" | custom-call | flops 8000000000 | bytes 2097152 | tf_op jit(solution)/shard_map/first_factor/pallas_call | solution.py:211
  33.5 0.3 collective-permute-done.10.rows_other_ref
  33.7 0.0 collective-permute-done.11.oa_ref
  33.7 0.0 collective-permute-done.12.ob_ref
  33.7 0.0 copy-done.1
  33.7 6.1 %second_factor.1 = (f32[128,128]{1,0:T(8,128)S(1)}, f32[128,128]{1,0:T(8,128)S(1)}, f32[512,128]{1,0:T(8,128)S(1)}, bf16[512,768]{1,0:T(8,128)(2,1)S(1)}, bf16[7...) custom-call(f32[128,128]{1,0:T(8,128)S(1)} %get-tuple-element.65.a_ref, ...), custom_call_target="tpu_custom_call" | custom-call | flops 8000000000 | bytes 4194304 | tf_op jit(solution)/shard_map/second_factor/pallas_call | solution.py:291
  39.8 2.6 %settle.1 = f32[4,128,8,128]{3,2,1,0:T(8,128)} custom-call(f32[128,128]{1,0:T(8,128)S(1)} %get-tuple-element.52.f0_ref, f32[128,128]{1,0:T(8,128)S(1)} %get-tuple-element.59.f1_ref, f32[128,128]{1,0:T(8,128)S(1)} %get-tuple-element.60.w_ref, f32[512,128]{1,0:T(8,128)S(1)} %get-tuple-element.61.solved_ref, ...), custom_call_target="tpu_custom_call" | custom-call | flops 4000000000 | bytes 6291456 | tf_op jit(solution)/shard_map/settle/pallas_call | solution.py:349
  (11 shorter events, 0.2 us)
Async XLA Ops:
  0.0 1.6 %copy-start = (f32[4,128,8,128]{3,2,1,0:T(8,128)S(1)}, f32[4,128,8,128]{3,2,1,0:T(8,128)}, u32[]{:S(2)}) copy-start(f32[4,128,8,128]{3,2,1,0:T(8,128)} %matrix_ref.3) | copy-start | bytes 6291460
  2.3 7.8 %collective-permute-start = (f32[128,128]{1,0:T(8,128)S(1)}, f32[128,128]{1,0:T(8,128)S(1)}, u32[]{:S(2)}, u32[]{:S(2)}) collective-permute-start(f32[128,128]{1,0:T(8,128)S(1)} %get-tuple-element.35.old_ref), channel_id=1, source_target_pairs={{0,2},{1,3},{2,0},{3,1},{4,6},{5,7},{6,4},{7,5},{8,10},{9,11},{10,... | collective-permute-start | bytes 196616 | tf_op jit(solution)/shard_map/ppermute | solution.py:362
  6.4 7.8 %collective-permute-start.2 = (f32[8,64,128]{2,1,0:T(8,128)S(1)}, f32[8,64,128]{2,1,0:T(8,128)S(1)}, u32[]{:S(2)}, u32[]{:S(2)}) collective-permute-start(f32[8,64,128]{2,1,0:T(8,128)S(1)} %get-tuple-element.36), channel_id=1, source_target_pairs={{0,8},{4,12},{8,0},{12,4},{16,24},{20,28},{24,16},{28,20},{1,9},{5... | collective-permute-start | bytes 786440 | tf_op jit(solution)/shard_map/ppermute | solution.py:362
  7.9 7.5 %collective-permute-start.3 = (f32[8,64,128]{2,1,0:T(8,128)S(1)}, f32[8,64,128]{2,1,0:T(8,128)S(1)}, u32[]{:S(2)}, u32[]{:S(2)}) collective-permute-start(f32[8,64,128]{2,1,0:T(8,128)S(1)} %get-tuple-element.37), channel_id=1, source_target_pairs={{0,16},{4,20},{8,24},{12,28},{16,0},{20,4},{24,8},{28,12},{1,17},{... | collective-permute-start | bytes 786440 | tf_op jit(solution)/shard_map/ppermute | solution.py:362
  10.1 5.3 %collective-permute-start.1 = (f32[128,128]{1,0:T(8,128)S(1)}, f32[128,128]{1,0:T(8,128)S(1)}, u32[]{:S(2)}, u32[]{:S(2)}) collective-permute-start(f32[128,128]{1,0:T(8,128)S(1)} %pick.1.block_ref), channel_id=1, source_target_pairs={{0,1},{1,0},{2,3},{3,2},{4,5},{5,4},{6,7},{7,6},{8,9},{9,8},{10,11... | collective-permute-start | bytes 196616 | tf_op jit(solution)/shard_map/ppermute | solution.py:362
  15.6 4.7 %collective-permute-start.4 = (f32[192,128]{1,0:T(8,128)S(1)}, f32[192,128]{1,0:T(8,128)S(1)}, u32[]{:S(2)}, u32[]{:S(2)}) collective-permute-start(f32[192,128]{1,0:T(8,128)S(1)} %get-tuple-element.41), channel_id=1, source_target_pairs={{0,8},{4,12},{8,0},{12,4},{16,24},{20,28},{24,16},{28,20},{1,9},{5... | collective-permute-start | bytes 294920 | tf_op jit(solution)/shard_map/ppermute | solution.py:362
  16.3 9.9 %collective-permute-start.6 = (f32[3,128,128]{2,1,0:T(8,128)S(1)}, f32[3,128,128]{2,1,0:T(8,128)S(1)}, u32[]{:S(2)}, u32[]{:S(2)}) collective-permute-start(f32[3,128,128]{2,1,0:T(8,128)S(1)} %get-tuple-element.45), channel_id=1, source_target_pairs={{0,2},{1,3},{2,0},{3,1},{4,6},{5,7},{6,4},{7,5},{8,10},{9,11},{10,... | collective-permute-start | bytes 589832 | tf_op jit(solution)/shard_map/ppermute | solution.py:362
  20.3 6.0 %collective-permute-start.5 = (f32[192,128]{1,0:T(8,128)S(1)}, f32[192,128]{1,0:T(8,128)S(1)}, u32[]{:S(2)}, u32[]{:S(2)}) collective-permute-start(f32[192,128]{1,0:T(8,128)S(1)} %broadcast_select_fusion.5), channel_id=1, source_target_pairs={{0,16},{4,20},{8,24},{12,28},{16,0},{20,4},{24,8},{28,12},{1,17},{... | collective-permute-start | bytes 294920 | tf_op jit(solution)/shard_map/ppermute | solution.py:362
  21.9 6.4 %collective-permute-start.8 = (f32[8,64,128]{2,1,0:T(8,128)S(1)}, f32[8,64,128]{2,1,0:T(8,128)S(1)}, u32[]{:S(2)}, u32[]{:S(2)}) collective-permute-start(f32[8,64,128]{2,1,0:T(8,128)S(1)} %broadcast_select_fusion.3), channel_id=1, source_target_pairs={{0,16},{4,20},{8,24},{12,28},{16,0},{20,4},{24,8},{28,12},{1,17},{... | collective-permute-start | bytes 786440 | tf_op jit(solution)/shard_map/ppermute | solution.py:362
  22.4 6.4 %collective-permute-start.9 = (f32[8,64,128]{2,1,0:T(8,128)S(1)}, f32[8,64,128]{2,1,0:T(8,128)S(1)}, u32[]{:S(2)}, u32[]{:S(2)}) collective-permute-start(f32[8,64,128]{2,1,0:T(8,128)S(1)} %broadcast_select_fusion.1), channel_id=1, source_target_pairs={{0,8},{4,12},{8,0},{12,4},{16,24},{20,28},{24,16},{28,20},{1,9},{5... | collective-permute-start | bytes 786440 | tf_op jit(solution)/shard_map/ppermute | solution.py:362
  26.3 2.5 %collective-permute-start.7 = (f32[192,128]{1,0:T(8,128)S(1)}, f32[192,128]{1,0:T(8,128)S(1)}, u32[]{:S(2)}, u32[]{:S(2)}) collective-permute-start(f32[192,128]{1,0:T(8,128)S(1)} %broadcast_select_fusion.6), channel_id=1, source_target_pairs={{0,4},{4,0},{8,12},{12,8},{16,20},{20,16},{24,28},{28,24},{1,5},{5... | collective-permute-start | bytes 294920 | tf_op jit(solution)/shard_map/ppermute | solution.py:362
  26.4 7.3 %collective-permute-start.10 = (f32[3,128,128]{2,1,0:T(8,128)S(1)}, f32[3,128,128]{2,1,0:T(8,128)S(1)}, u32[]{:S(2)}, u32[]{:S(2)}) collective-permute-start(f32[3,128,128]{2,1,0:T(8,128)S(1)} %broadcast_select_fusion.4.rows_ref), channel_id=1, source_target_pairs={{0,1},{1,0},{2,3},{3,2},{4,5},{5,4},{6,7},{7,6},{8,9},{9,8},{10,11... | collective-permute-start | bytes 589832 | tf_op jit(solution)/shard_map/ppermute | solution.py:362
  28.8 4.9 %collective-permute-start.11 = (f32[8,64,128]{2,1,0:T(8,128)S(1)}, f32[8,64,128]{2,1,0:T(8,128)S(1)}, u32[]{:S(2)}, u32[]{:S(2)}) collective-permute-start(f32[8,64,128]{2,1,0:T(8,128)S(1)} %broadcast_select_fusion.ha_ref), channel_id=1, source_target_pairs={{0,4},{4,0},{8,12},{12,8},{16,20},{20,16},{24,28},{28,24},{1,5},{5... | collective-permute-start | bytes 786440 | tf_op jit(solution)/shard_map/ppermute | solution.py:362
  28.9 4.8 %collective-permute-start.12 = (f32[8,64,128]{2,1,0:T(8,128)S(1)}, f32[8,64,128]{2,1,0:T(8,128)S(1)}, u32[]{:S(2)}, u32[]{:S(2)}) collective-permute-start(f32[8,64,128]{2,1,0:T(8,128)S(1)} %broadcast_select_fusion.2.hb_ref), channel_id=1, source_target_pairs={{0,4},{4,0},{8,12},{12,8},{16,20},{20,16},{24,28},{28,24},{1,5},{5... | collective-permute-start | bytes 786440 | tf_op jit(solution)/shard_map/ppermute | solution.py:362
  29.4 4.3 %copy-start.1 = (f32[4,128,8,128]{3,2,1,0:T(8,128)S(1)}, f32[4,128,8,128]{3,2,1,0:T(8,128)}, u32[]{:S(2)}) copy-start(f32[4,128,8,128]{3,2,1,0:T(8,128)} %matrix_ref.3) | copy-start | bytes 6291460

commit v24 on v23

--- a/solution.py
+++ b/solution.py
@@ -395,20 +395,27 @@
 
     block = pick(moved, block, col_bits[0])
     block = spread(block, "col", grid_col, n_col, col_bits[1:])
+    part = (column.shape[0] + 1) // 2
+    block, early = after(block, column[:part])
+    early_moved = exchange(early, "col", 1 << col_bits[0], n_col)
     across = exchange(block, "col", 1, n_col)
     ha = jnp.where(bit_set(grid_row, first_bit), upper_moved, upper)
     hb = jnp.where(bit_set(grid_row, last_bit), lower_moved, lower)
-    across, block, ha, hb, column = after(across, block, ha, hb, column)
+    across, block, ha, hb, late = after(across, block, ha, hb, column[part:])
 
     first_rows, pair = pack(across, block)
+    pair, col_then = after(pair, grid_col)
     moved = exchange(pair, "row", 1 << first_bit, n_row)
-    column_moved = exchange(column, "col", 1 << col_bits[0], n_col)
+    late_moved = exchange(late, "col", 1 << col_bits[0], n_col)
+    early = jnp.where(bit_set(col_then, col_bits[0]), early_moved, early)
     pair = jnp.where(bit_set(grid_row, first_bit), moved, pair)
-    pair, ha, hb = after(pair, ha, hb)
+    pair, ha, hb, early = after(pair, ha, hb, early)
     moved = exchange(pair, "row", 1 << row_bits[1], n_row)
     ha_moved = exchange(ha, "row", 1 << row_bits[1], n_row)
     hb_moved = exchange(hb, "row", 1 << row_bits[-2], n_row)
-    rows = jnp.where(bit_set(grid_col, col_bits[0]), column_moved, column)
+    moved, col_then = after(moved, grid_col)
+    late = jnp.where(bit_set(col_then, col_bits[0]), late_moved, late)
+    rows = jnp.concatenate([early, late], axis=0)
     moved, pair, rows = after(moved, pair, rows)
     pair = jnp.where(bit_set(grid_row, row_bits[1]), moved, pair)
     pair = spread(pair, "row", grid_row, n_row, row_bits[2:])

time: 42.6 us -> 43.9 us (1.031)
  starting transfers between devices: 14.6 us -> 19.8 us
  waiting for transfers between devices: 12.3 us -> 8.36 us
    ppermute x13 -> x14, starting transfers between devices: 14.6 us -> 19.8 us  [exchange(): return lax.ppermute(value, axis, [(i, i ^ mask) for i in range(size)])]
    ppermute x13 -> x14, waiting for transfers between devices: 12.3 us -> 8.36 us  [exchange(): return lax.ppermute(value, axis, [(i, i ^ mask) for i in range(size)])]
  transfers between devices with their start and end apart: 13 -> 14, of which waited for: 8 -> 9; matrix products, arithmetic and copies ran while one was open for 0% -> 0% of each run, Pallas kernels for 10% -> 10%
where the time goes in v24:
time: 43.9 us; the launch traced here: 43.8 us
  starting transfers between devices  19.8 us (45%)
  Pallas kernels  13.6 us (31%)
  waiting for transfers between devices  8.36 us (19%)
  local copies, waits for them, and re-layouts  1.61 us (4%)
    ppermute x14, starting transfers between devices, exchange(): return lax.ppermute(value, axis, [(i, i ^ mask) for i in range(size)])  19.8 us
    ppermute x14, waiting for transfers between devices, exchange(): return lax.ppermute(value, axis, [(i, i ^ mask) for i in range(size)])  8.36 us
    pallas_call x1, Pallas kernels, second_factor(): pl.pallas_call(second_factor_kernel, out_shape=[square, square, solved, r...  6.07 us
    pallas_call x1, Pallas kernels, first_factor(): pl.pallas_call(first_factor_kernel, out_shape=[square] * 3, in_specs=[VME...  4.05 us
    pallas_call x1, Pallas kernels, settle(): pl.pallas_call(settle_kernel, out_shape=jax.ShapeDtypeStruct((local_rows,...  2.62 us
    unnamed x4, local copies, waits for them, and re-layouts  1.59 us
  transfers between devices with their start and end apart: 14, of which 9 were waited for; matrix products, arithmetic and copies ran while one was open for 0% of the time, Pallas kernels for 10%

profile of v24, /device:TPU:0, one launch (start us, length us, event | category | flops | bytes accessed | tf_op | source)
XLA Modules:
  0.0 43.8 jit_solution(6489669756554518042)
XLA Ops:
  0.0 0.0 copy-start
  0.0 1.6 %copy-done = f32[4,128,8,128]{3,2,1,0:T(8,128)S(1)} copy-done((f32[4,128,8,128]{3,2,1,0:T(8,128)S(1)}, f32[4,128,8,128]{3,2,1,0:T(8,128)}, u32[]{:S(2)}) %copy-start) | copy-done | bytes 2097176
  1.6 0.7 %panels.1 = (f32[128,128]{1,0:T(8,128)S(1)}, f32[3,128,128]{2,1,0:T(8,128)S(1)}, f32[8,64,128]{2,1,0:T(8,128)S(1)}, f32[8,64,128]{2,1,0:T(8,128)S(1)}) custom-call(f32[4,128,8,128]{3,2,1,0:T(8,128)S(1)} %copy-done), custom_call_target="tpu_custom_call" | custom-call | bytes 4194304 | tf_op jit(solution)/shard_map/panels/pallas_call | solution.py:145
  2.3 4.1 %collective-permute-start = (f32[128,128]{1,0:T(8,128)S(1)}, f32[128,128]{1,0:T(8,128)S(1)}, u32[]{:S(2)}, u32[]{:S(2)}) collective-permute-start(f32[128,128]{1,0:T(8,128)S(1)} %get-tuple-element.42.old_ref), channel_id=1, source_target_pairs={{0,2},{1,3},{2,0},{3,1},{4,6},{5,7},{6,4},{7,5},{8,10},{9,11},{10,... | collective-permute-start | bytes 196616 | tf_op jit(solution)/shard_map/ppermute | solution.py:362
  6.4 1.5 %collective-permute-start.2 = (f32[8,64,128]{2,1,0:T(8,128)S(1)}, f32[8,64,128]{2,1,0:T(8,128)S(1)}, u32[]{:S(2)}, u32[]{:S(2)}) collective-permute-start(f32[8,64,128]{2,1,0:T(8,128)S(1)} %get-tuple-element.45), channel_id=1, source_target_pairs={{0,8},{4,12},{8,0},{12,4},{16,24},{20,28},{24,16},{28,20},{1,9},{5... | collective-permute-start | bytes 786440 | tf_op jit(solution)/shard_map/ppermute | solution.py:362
  7.9 1.5 %collective-permute-start.3 = (f32[8,64,128]{2,1,0:T(8,128)S(1)}, f32[8,64,128]{2,1,0:T(8,128)S(1)}, u32[]{:S(2)}, u32[]{:S(2)}) collective-permute-start(f32[8,64,128]{2,1,0:T(8,128)S(1)} %get-tuple-element.46), channel_id=1, source_target_pairs={{0,16},{4,20},{8,24},{12,28},{16,0},{20,4},{24,8},{28,12},{1,17},{... | collective-permute-start | bytes 786440 | tf_op jit(solution)/shard_map/ppermute | solution.py:362
  9.5 0.6 %collective-permute-done.new_ref = f32[128,128]{1,0:T(8,128)S(1)} collective-permute-done((f32[128,128]{1,0:T(8,128)S(1)}, f32[128,128]{1,0:T(8,128)S(1)}, u32[]{:S(2)}, u32[]{:S(2)}) %collective-permute-start) | collective-permute-done | bytes 65568 | tf_op jit(solution)/shard_map/ppermute | solution.py:362
  10.1 1.0 %collective-permute-start.1 = (f32[128,128]{1,0:T(8,128)S(1)}, f32[128,128]{1,0:T(8,128)S(1)}, u32[]{:S(2)}, u32[]{:S(2)}) collective-permute-start(f32[128,128]{1,0:T(8,128)S(1)} %pick.1.block_ref), channel_id=1, source_target_pairs={{0,1},{1,0},{2,3},{3,2},{4,5},{5,4},{6,7},{7,6},{8,9},{9,8},{10,11... | collective-permute-start | bytes 196616 | tf_op jit(solution)/shard_map/ppermute | solution.py:362
  11.2 3.0 %collective-permute-start.5 = (f32[2,128,128]{2,1,0:T(8,128)S(1)}, f32[2,128,128]{2,1,0:T(8,128)S(1)}, u32[]{:S(2)}, u32[]{:S(2)}) collective-permute-start(f32[2,128,128]{2,1,0:T(8,128)S(1)} %slice.22), channel_id=1, source_target_pairs={{0,2},{1,3},{2,0},{3,1},{4,6},{5,7},{6,4},{7,5},{8,10},{9,11},{10,... | collective-permute-start | bytes 393224 | tf_op jit(solution)/shard_map/ppermute | solution.py:362
  14.1 0.1 collective-permute-done.2
  14.2 1.2 %collective-permute-done.3 = f32[8,64,128]{2,1,0:T(8,128)S(1)} collective-permute-done((f32[8,64,128]{2,1,0:T(8,128)S(1)}, f32[8,64,128]{2,1,0:T(8,128)S(1)}, u32[]{:S(2)}, u32[]{:S(2)}) %collective-permute-start.3) | collective-permute-done | bytes 262176 | tf_op jit(solution)/shard_map/ppermute | solution.py:362
  15.5 0.0 collective-permute-done.1.across_ref
  15.5 0.1 pack.1
  15.6 1.3 %collective-permute-start.4 = (f32[192,128]{1,0:T(8,128)S(1)}, f32[192,128]{1,0:T(8,128)S(1)}, u32[]{:S(2)}, u32[]{:S(2)}) collective-permute-start(f32[192,128]{1,0:T(8,128)S(1)} %get-tuple-element.50), channel_id=1, source_target_pairs={{0,8},{4,12},{8,0},{12,4},{16,24},{20,28},{24,16},{28,20},{1,9},{5... | collective-permute-start | bytes 294920 | tf_op jit(solution)/shard_map/ppermute | solution.py:362
  16.8 3.1 %collective-permute-done.5 = f32[2,128,128]{2,1,0:T(8,128)S(1)} collective-permute-done((f32[2,128,128]{2,1,0:T(8,128)S(1)}, f32[2,128,128]{2,1,0:T(8,128)S(1)}, u32[]{:S(2)}, u32[]{:S(2)}) %collective-permute-start.5) | collective-permute-done | bytes 131104 | tf_op jit(solution)/shard_map/ppermute | solution.py:362
  20.0 0.3 collective-permute-done.4
  20.3 1.6 %collective-permute-start.6 = (f32[192,128]{1,0:T(8,128)S(1)}, f32[192,128]{1,0:T(8,128)S(1)}, u32[]{:S(2)}, u32[]{:S(2)}) collective-permute-start(f32[192,128]{1,0:T(8,128)S(1)} %broadcast_select_fusion.5), channel_id=1, source_target_pairs={{0,16},{4,20},{8,24},{12,28},{16,0},{20,4},{24,8},{28,12},{1,17},{... | collective-permute-start | bytes 294920 | tf_op jit(solution)/shard_map/ppermute | solution.py:362
  21.9 1.6 %collective-permute-start.7 = (f32[1,128,128]{2,1,0:T(8,128)S(1)}, f32[1,128,128]{2,1,0:T(8,128)S(1)}, u32[]{:S(2)}, u32[]{:S(2)}) collective-permute-start(f32[1,128,128]{2,1,0:T(8,128)S(1)} %slice.23), channel_id=1, source_target_pairs={{0,2},{1,3},{2,0},{3,1},{4,6},{5,7},{6,4},{7,5},{8,10},{9,11},{10,... | collective-permute-start | bytes 196616 | tf_op jit(solution)/shard_map/ppermute | solution.py:362
  23.5 0.5 %collective-permute-start.9 = (f32[8,64,128]{2,1,0:T(8,128)S(1)}, f32[8,64,128]{2,1,0:T(8,128)S(1)}, u32[]{:S(2)}, u32[]{:S(2)}) collective-permute-start(f32[8,64,128]{2,1,0:T(8,128)S(1)} %broadcast_select_fusion.3), channel_id=1, source_target_pairs={{0,16},{4,20},{8,24},{12,28},{16,0},{20,4},{24,8},{28,12},{1,17},{... | collective-permute-start | bytes 786440 | tf_op jit(solution)/shard_map/ppermute | solution.py:362
  24.0 1.5 %collective-permute-start.10 = (f32[8,64,128]{2,1,0:T(8,128)S(1)}, f32[8,64,128]{2,1,0:T(8,128)S(1)}, u32[]{:S(2)}, u32[]{:S(2)}) collective-permute-start(f32[8,64,128]{2,1,0:T(8,128)S(1)} %broadcast_select_fusion.1), channel_id=1, source_target_pairs={{0,8},{4,12},{8,0},{12,4},{16,24},{20,28},{24,16},{28,20},{1,9},{5... | collective-permute-start | bytes 786440 | tf_op jit(solution)/shard_map/ppermute | solution.py:362
  25.5 0.5 %collective-permute-done.6 = f32[192,128]{1,0:T(8,128)S(1)} collective-permute-done((f32[192,128]{1,0:T(8,128)S(1)}, f32[192,128]{1,0:T(8,128)S(1)}, u32[]{:S(2)}, u32[]{:S(2)}) %collective-permute-start.6) | collective-permute-done | bytes 98336 | tf_op jit(solution)/shard_map/ppermute | solution.py:362
  26.0 1.1 %collective-permute-done.7 = f32[1,128,128]{2,1,0:T(8,128)S(1)} collective-permute-done((f32[1,128,128]{2,1,0:T(8,128)S(1)}, f32[1,128,128]{2,1,0:T(8,128)S(1)}, u32[]{:S(2)}, u32[]{:S(2)}) %collective-permute-start.7) | collective-permute-done | bytes 65568 | tf_op jit(solution)/shard_map/ppermute | solution.py:362
  27.1 0.1 collective-permute-start.8
  27.2 1.6 %collective-permute-start.11 = (f32[3,128,128]{2,1,0:T(8,128)S(1)}, f32[3,128,128]{2,1,0:T(8,128)S(1)}, u32[]{:S(2)}, u32[]{:S(2)}) collective-permute-start(f32[3,128,128]{2,1,0:T(8,128)S(1)} %pad_maximum_fusion.rows_ref), channel_id=1, source_target_pairs={{0,1},{1,0},{2,3},{3,2},{4,5},{5,4},{6,7},{7,6},{8,9},{9,8},{10,11... | collective-permute-start | bytes 589832 | tf_op jit(solution)/shard_map/ppermute | solution.py:362
  28.8 1.2 %collective-permute-done.9 = f32[8,64,128]{2,1,0:T(8,128)S(1)} collective-permute-done((f32[8,64,128]{2,1,0:T(8,128)S(1)}, f32[8,64,128]{2,1,0:T(8,128)S(1)}, u32[]{:S(2)}, u32[]{:S(2)}) %collective-permute-start.9) | collective-permute-done | bytes 262176 | tf_op jit(solution)/shard_map/ppermute | solution.py:362
  30.0 0.3 collective-permute-done.10
  30.4 0.0 collective-permute-done.8
  30.4 0.1 collective-permute-start.12
  30.5 0.5 %collective-permute-start.13 = (f32[8,64,128]{2,1,0:T(8,128)S(1)}, f32[8,64,128]{2,1,0:T(8,128)S(1)}, u32[]{:S(2)}, u32[]{:S(2)}) collective-permute-start(f32[8,64,128]{2,1,0:T(8,128)S(1)} %broadcast_select_fusion.2.hb_ref), channel_id=1, source_target_pairs={{0,4},{4,0},{8,12},{12,8},{16,20},{20,16},{24,28},{28,24},{1,5},{5... | collective-permute-start | bytes 786440 | tf_op jit(solution)/shard_map/ppermute | solution.py:362
  31.0 0.0 copy-start.1
  31.0 4.0 %first_factor.1 = (f32[128,128]{1,0:T(8,128)S(1)}, f32[128,128]{1,0:T(8,128)S(1)}, f32[128,128]{1,0:T(8,128)S(1)}) custom-call(f32[128,128]{1,0:T(8,128)S(1)} %get-tuple-element.80.a_ref, f32[128,128]{1,0:T(8,128)S(1)} %pad_maximum_fusion.1.side_ref), custom_call_target="tpu_custom_call" | custom-call | flops 8000000000 | bytes 2097152 | tf_op jit(solution)/shard_map/first_factor/pallas_call | solution.py:211
  35.1 0.0 collective-permute-done.11.rows_other_ref
  35.1 0.0 collective-permute-done.12.oa_ref
  35.1 0.0 collective-permute-done.13.ob_ref
  35.1 0.0 copy-done.1
  35.1 6.1 %second_factor.1 = (f32[128,128]{1,0:T(8,128)S(1)}, f32[128,128]{1,0:T(8,128)S(1)}, f32[512,128]{1,0:T(8,128)S(1)}, bf16[512,768]{1,0:T(8,128)(2,1)S(1)}, bf16[7...) custom-call(f32[128,128]{1,0:T(8,128)S(1)} %get-tuple-element.79.a_ref, ...), custom_call_target="tpu_custom_call" | custom-call | flops 8000000000 | bytes 4194304 | tf_op jit(solution)/shard_map/second_factor/pallas_call | solution.py:291
  41.2 2.6 %settle.1 = f32[4,128,8,128]{3,2,1,0:T(8,128)} custom-call(f32[128,128]{1,0:T(8,128)S(1)} %get-tuple-element.66.f0_ref, f32[128,128]{1,0:T(8,128)S(1)} %get-tuple-element.73.f1_ref, f32[128,128]{1,0:T(8,128)S(1)} %get-tuple-element.74.w_ref, f32[512,128]{1,0:T(8,128)S(1)} %get-tuple-element.75.solved_ref, ...), custom_call_target="tpu_custom_call" | custom-call | flops 4000000000 | bytes 6291456 | tf_op jit(solution)/shard_map/settle/pallas_call | solution.py:349
  (15 shorter events, 0.2 us)
Async XLA Ops:
  0.0 1.6 %copy-start = (f32[4,128,8,128]{3,2,1,0:T(8,128)S(1)}, f32[4,128,8,128]{3,2,1,0:T(8,128)}, u32[]{:S(2)}) copy-start(f32[4,128,8,128]{3,2,1,0:T(8,128)} %matrix_ref.3) | copy-start | bytes 6291460
  2.3 7.8 %collective-permute-start = (f32[128,128]{1,0:T(8,128)S(1)}, f32[128,128]{1,0:T(8,128)S(1)}, u32[]{:S(2)}, u32[]{:S(2)}) collective-permute-start(f32[128,128]{1,0:T(8,128)S(1)} %get-tuple-element.42.old_ref), channel_id=1, source_target_pairs={{0,2},{1,3},{2,0},{3,1},{4,6},{5,7},{6,4},{7,5},{8,10},{9,11},{10,... | collective-permute-start | bytes 196616 | tf_op jit(solution)/shard_map/ppermute | solution.py:362
  6.4 7.8 %collective-permute-start.2 = (f32[8,64,128]{2,1,0:T(8,128)S(1)}, f32[8,64,128]{2,1,0:T(8,128)S(1)}, u32[]{:S(2)}, u32[]{:S(2)}) collective-permute-start(f32[8,64,128]{2,1,0:T(8,128)S(1)} %get-tuple-element.45), channel_id=1, source_target_pairs={{0,8},{4,12},{8,0},{12,4},{16,24},{20,28},{24,16},{28,20},{1,9},{5... | collective-permute-start | bytes 786440 | tf_op jit(solution)/shard_map/ppermute | solution.py:362
  7.9 7.5 %collective-permute-start.3 = (f32[8,64,128]{2,1,0:T(8,128)S(1)}, f32[8,64,128]{2,1,0:T(8,128)S(1)}, u32[]{:S(2)}, u32[]{:S(2)}) collective-permute-start(f32[8,64,128]{2,1,0:T(8,128)S(1)} %get-tuple-element.46), channel_id=1, source_target_pairs={{0,16},{4,20},{8,24},{12,28},{16,0},{20,4},{24,8},{28,12},{1,17},{... | collective-permute-start | bytes 786440 | tf_op jit(solution)/shard_map/ppermute | solution.py:362
  10.1 5.3 %collective-permute-start.1 = (f32[128,128]{1,0:T(8,128)S(1)}, f32[128,128]{1,0:T(8,128)S(1)}, u32[]{:S(2)}, u32[]{:S(2)}) collective-permute-start(f32[128,128]{1,0:T(8,128)S(1)} %pick.1.block_ref), channel_id=1, source_target_pairs={{0,1},{1,0},{2,3},{3,2},{4,5},{5,4},{6,7},{7,6},{8,9},{9,8},{10,11... | collective-permute-start | bytes 196616 | tf_op jit(solution)/shard_map/ppermute | solution.py:362
  11.2 8.8 %collective-permute-start.5 = (f32[2,128,128]{2,1,0:T(8,128)S(1)}, f32[2,128,128]{2,1,0:T(8,128)S(1)}, u32[]{:S(2)}, u32[]{:S(2)}) collective-permute-start(f32[2,128,128]{2,1,0:T(8,128)S(1)} %slice.22), channel_id=1, source_target_pairs={{0,2},{1,3},{2,0},{3,1},{4,6},{5,7},{6,4},{7,5},{8,10},{9,11},{10,... | collective-permute-start | bytes 393224 | tf_op jit(solution)/shard_map/ppermute | solution.py:362
  15.6 4.7 %collective-permute-start.4 = (f32[192,128]{1,0:T(8,128)S(1)}, f32[192,128]{1,0:T(8,128)S(1)}, u32[]{:S(2)}, u32[]{:S(2)}) collective-permute-start(f32[192,128]{1,0:T(8,128)S(1)} %get-tuple-element.50), channel_id=1, source_target_pairs={{0,8},{4,12},{8,0},{12,4},{16,24},{20,28},{24,16},{28,20},{1,9},{5... | collective-permute-start | bytes 294920 | tf_op jit(solution)/shard_map/ppermute | solution.py:362
  20.3 5.7 %collective-permute-start.6 = (f32[192,128]{1,0:T(8,128)S(1)}, f32[192,128]{1,0:T(8,128)S(1)}, u32[]{:S(2)}, u32[]{:S(2)}) collective-permute-start(f32[192,128]{1,0:T(8,128)S(1)} %broadcast_select_fusion.5), channel_id=1, source_target_pairs={{0,16},{4,20},{8,24},{12,28},{16,0},{20,4},{24,8},{28,12},{1,17},{... | collective-permute-start | bytes 294920 | tf_op jit(solution)/shard_map/ppermute | solution.py:362
  21.9 5.2 %collective-permute-start.7 = (f32[1,128,128]{2,1,0:T(8,128)S(1)}, f32[1,128,128]{2,1,0:T(8,128)S(1)}, u32[]{:S(2)}, u32[]{:S(2)}) collective-permute-start(f32[1,128,128]{2,1,0:T(8,128)S(1)} %slice.23), channel_id=1, source_target_pairs={{0,2},{1,3},{2,0},{3,1},{4,6},{5,7},{6,4},{7,5},{8,10},{9,11},{10,... | collective-permute-start | bytes 196616 | tf_op jit(solution)/shard_map/ppermute | solution.py:362
  23.5 6.5 %collective-permute-start.9 = (f32[8,64,128]{2,1,0:T(8,128)S(1)}, f32[8,64,128]{2,1,0:T(8,128)S(1)}, u32[]{:S(2)}, u32[]{:S(2)}) collective-permute-start(f32[8,64,128]{2,1,0:T(8,128)S(1)} %broadcast_select_fusion.3), channel_id=1, source_target_pairs={{0,16},{4,20},{8,24},{12,28},{16,0},{20,4},{24,8},{28,12},{1,17},{... | collective-permute-start | bytes 786440 | tf_op jit(solution)/shard_map/ppermute | solution.py:362
  24.0 6.4 %collective-permute-start.10 = (f32[8,64,128]{2,1,0:T(8,128)S(1)}, f32[8,64,128]{2,1,0:T(8,128)S(1)}, u32[]{:S(2)}, u32[]{:S(2)}) collective-permute-start(f32[8,64,128]{2,1,0:T(8,128)S(1)} %broadcast_select_fusion.1), channel_id=1, source_target_pairs={{0,8},{4,12},{8,0},{12,4},{16,24},{20,28},{24,16},{28,20},{1,9},{5... | collective-permute-start | bytes 786440 | tf_op jit(solution)/shard_map/ppermute | solution.py:362
  27.1 3.3 %collective-permute-start.8 = (f32[192,128]{1,0:T(8,128)S(1)}, f32[192,128]{1,0:T(8,128)S(1)}, u32[]{:S(2)}, u32[]{:S(2)}) collective-permute-start(f32[192,128]{1,0:T(8,128)S(1)} %broadcast_select_fusion.6), channel_id=1, source_target_pairs={{0,4},{4,0},{8,12},{12,8},{16,20},{20,16},{24,28},{28,24},{1,5},{5... | collective-permute-start | bytes 294920 | tf_op jit(solution)/shard_map/ppermute | solution.py:362
  27.2 7.9 %collective-permute-start.11 = (f32[3,128,128]{2,1,0:T(8,128)S(1)}, f32[3,128,128]{2,1,0:T(8,128)S(1)}, u32[]{:S(2)}, u32[]{:S(2)}) collective-permute-start(f32[3,128,128]{2,1,0:T(8,128)S(1)} %pad_maximum_fusion.rows_ref), channel_id=1, source_target_pairs={{0,1},{1,0},{2,3},{3,2},{4,5},{5,4},{6,7},{7,6},{8,9},{9,8},{10,11... | collective-permute-start | bytes 589832 | tf_op jit(solution)/shard_map/ppermute | solution.py:362
  30.4 4.6 %collective-permute-start.12 = (f32[8,64,128]{2,1,0:T(8,128)S(1)}, f32[8,64,128]{2,1,0:T(8,128)S(1)}, u32[]{:S(2)}, u32[]{:S(2)}) collective-permute-start(f32[8,64,128]{2,1,0:T(8,128)S(1)} %broadcast_select_fusion.ha_ref), channel_id=1, source_target_pairs={{0,4},{4,0},{8,12},{12,8},{16,20},{20,16},{24,28},{28,24},{1,5},{5... | collective-permute-start | bytes 786440 | tf_op jit(solution)/shard_map/ppermute | solution.py:362
  30.5 4.6 %collective-permute-start.13 = (f32[8,64,128]{2,1,0:T(8,128)S(1)}, f32[8,64,128]{2,1,0:T(8,128)S(1)}, u32[]{:S(2)}, u32[]{:S(2)}) collective-permute-start(f32[8,64,128]{2,1,0:T(8,128)S(1)} %broadcast_select_fusion.2.hb_ref), channel_id=1, source_target_pairs={{0,4},{4,0},{8,12},{12,8},{16,20},{20,16},{24,28},{28,24},{1,5},{5... | collective-permute-start | bytes 786440 | tf_op jit(solution)/shard_map/ppermute | solution.py:362
  31.0 4.1 %copy-start.1 = (f32[4,128,8,128]{3,2,1,0:T(8,128)S(1)}, f32[4,128,8,128]{3,2,1,0:T(8,128)}, u32[]{:S(2)}) copy-start(f32[4,128,8,128]{3,2,1,0:T(8,128)} %matrix_ref.3) | copy-start | bytes 6291460
